TPU v7x, 128 devices: a whole 4x4x4 slice. The times are simulated.
128 devices in a mesh: blk: 8 (over y_hi, z), dp: 16 (over x, y_lo, core).
Axes of the slice: x: 4, y: 4 (y_hi: 2, y_lo: 2; y = y_hi * 2 + y_lo), z: 4, core: 2. Of those that a mesh axis runs over, the one named last changes fastest.
Arguments:
- image_embeds: bfloat16 [20480, 1152], P(('blk', 'dp')), may hold values from -6 to 6
- text_embeds: bfloat16 [20480, 1152], P(('blk', 'dp')), may hold values from -6 to 6
- log_scale: float32 [1], replicated, may hold values from 3 to 4.1
- logit_bias: float32 [1], replicated, may hold values from -2 to 0
Outputs:
- image_grad: bfloat16 [20480, 1152], P(('blk', 'dp'))
- text_grad: bfloat16 [20480, 1152], P(('blk', 'dp'))
All inputs are finite; a program needn't handle non-finite values.
Results may differ from a plain program's by a relative error of at most 0.011.
Values may be sent and summed in bfloat16 or wider, within the bound.
No kernel may reach another device: no remote copies, remote signals or barrier semaphores. Data moves between devices by JAX's collectives and lax.ppermute only.
A program may use at most 128 MiB of HBM per device.

v0:
```python
import jax
import jax.numpy as jnp
from jax import lax
from jax.sharding import PartitionSpec as P

norm_eps = 1e-06


def passed_along(value, axis, steps):
    count = lax.axis_size(axis)
    pairs = [(source, (source + steps) % count) for source in range(count)]
    return lax.ppermute(value, axis, pairs)


def normalize(embeds):
    values = embeds.astype(jnp.float32)
    inverse = lax.rsqrt(jnp.sum(values * values, axis=1, keepdims=True) + norm_eps)
    return (values * inverse, inverse)


def project_back(direction, unit_float, inverse):
    along = jnp.sum(unit_float * direction, axis=1, keepdims=True)
    return inverse * (direction - unit_float * along)


def move_texts(pieces):
    return [passed_along(pieces[0], "blk", 1)]


def move_partials(partials):
    return [passed_along(partials[0], "blk", 1)]


def on_device(image_embeds, text_embeds, log_scale, logit_bias):
    row_count, feature_width = image_embeds.shape
    blk_count = lax.axis_size("blk")
    dp_count = lax.axis_size("dp")
    group_rows = row_count * dp_count
    blk_index = lax.axis_index("blk")
    dp_index = lax.axis_index("dp")
    logit_scale = jnp.exp(log_scale[0])
    bias_value = logit_bias[0]
    image_float, image_inverse = normalize(image_embeds)
    text_float, text_inverse = normalize(text_embeds)
    text_unit = text_float.astype(jnp.bfloat16)
    gathered = lax.all_gather(image_float.astype(jnp.bfloat16), "dp", axis=0, tiled=True)
    image_ids = blk_index * group_rows + jnp.arange(group_rows, dtype=jnp.int32)
    offsets = [0]
    lengths = [row_count]
    moves = [1]
    pieces = [text_unit for offset, length in zip(offsets, lengths)]
    partials = [jnp.zeros((length, feature_width), jnp.float32) for length in lengths]
    image_total = jnp.zeros((group_rows, feature_width), jnp.float32)
    for visit in range(blk_count):
        anchors = [(blk_index - step * visit) % blk_count for step in moves]
        current = pieces[0]
        column_ids = jnp.concatenate(
            [
                (anchor * dp_count + dp_index) * row_count
                + offset
                + jnp.arange(length, dtype=jnp.int32)
                for anchor, offset, length in zip(anchors, offsets, lengths)
            ],
            axis=0,
        )
        logits = (
            logit_scale
            * lax.dot_general(
                gathered, current, (((1,), (1,)), ((), ())), preferred_element_type=jnp.float32
            )
            + bias_value
        )
        positive = (image_ids[:, None] == column_ids[None, :]).astype(jnp.float32)
        weights = (jax.nn.sigmoid(logits) - positive).astype(jnp.bfloat16)
        image_total = image_total + jnp.dot(weights, current, preferred_element_type=jnp.float32)
        text_part = lax.dot_general(
            weights, gathered, (((0,), (0,)), ((), ())), preferred_element_type=jnp.float32
        )
        partials = [partial_value + text_part for partial_value in partials]
        if visit + 1 < blk_count:
            pieces = move_texts(pieces)
        partials = move_partials(partials)
    text_total = partials[0]
    image_dir = lax.psum_scatter(image_total, "dp", scatter_dimension=0, tiled=True)
    image_grad = project_back(logit_scale * image_dir, image_float, image_inverse).astype(
        jnp.bfloat16
    )
    text_grad = project_back(logit_scale * text_total, text_float, text_inverse).astype(
        jnp.bfloat16
    )
    return (image_grad, text_grad)


def solution(mesh):
    return jax.shard_map(
        on_device,
        mesh=mesh,
        in_specs=(P(("blk", "dp"), None), P(("blk", "dp"), None), P(), P()),
        out_specs=(P(("blk", "dp"), None), P(("blk", "dp"), None)),
        check_vma=False,
    )
```

profile of v0, /device:TPU:8, one launch (start us, length us, event | category | flops | bytes accessed | tf_op | source)
XLA Modules:
  0.0 444.7 jit_solution(12562521516052154068)
XLA Ops:
  7.2 1.2 fusion.66
  8.4 0.6 copy-done.22
  9.0 1.9 fusion.61
  10.9 0.2 fusion.71
  11.1 0.1 fusion.58
  11.2 2.0 collective-permute-start
  13.2 12.4 %collective-permute-done = bf16[160,1152]{1,0:T(8,128)(2,1)S(1)} collective-permute-done((bf16[160,1152]{1,0:T(8,128)(2,1)S(1)}, bf16[160,1152]{1,0:T(8,128)(2,1)S(1)}, u32[]{:S(2)}, u32[]{:S(2)}) %collective-permute-start) | collective-permute-done | bytes 368672 | tf_op jit(solution)/shard_map/ppermute | solution.py:12
  25.7 22.2 %collective-permute-done.1 = bf16[160,1152]{1,0:T(8,128)(2,1)S(1)} collective-permute-done((bf16[160,1152]{1,0:T(8,128)(2,1)S(1)}, bf16[160,1152]{1,0:T(8,128)(2,1)S(1)}, u32[]{:S(2)}, u32[]{:S(2)}) %collective-permute-start.1) | collective-permute-done | bytes 368672 | tf_op jit(solution)/shard_map/ppermute | solution.py:12
  47.8 0.7 copy-done.11
  48.6 22.1 %collective-permute-done.2 = bf16[160,1152]{1,0:T(8,128)(2,1)S(1)} collective-permute-done((bf16[160,1152]{1,0:T(8,128)(2,1)S(1)}, bf16[160,1152]{1,0:T(8,128)(2,1)S(1)}, u32[]{:S(2)}, u32[]{:S(2)}) %collective-permute-start.2) | collective-permute-done | bytes 368672 | tf_op jit(solution)/shard_map/ppermute | solution.py:12
  70.7 12.0 %collective-permute-done.3 = bf16[160,1152]{1,0:T(8,128)(2,1)S(1)} collective-permute-done((bf16[160,1152]{1,0:T(8,128)(2,1)S(1)}, bf16[160,1152]{1,0:T(8,128)(2,1)S(1)}, u32[]{:S(2)}, u32[]{:S(2)}) %collective-permute-start.3) | collective-permute-done | bytes 368672 | tf_op jit(solution)/shard_map/ppermute | solution.py:12
  82.8 11.0 %collective-permute-done.4 = bf16[160,1152]{1,0:T(8,128)(2,1)S(1)} collective-permute-done((bf16[160,1152]{1,0:T(8,128)(2,1)S(1)}, bf16[160,1152]{1,0:T(8,128)(2,1)S(1)}, u32[]{:S(2)}, u32[]{:S(2)}) %collective-permute-start.4) | collective-permute-done | bytes 368672 | tf_op jit(solution)/shard_map/ppermute | solution.py:12
  95.3 9.8 %collective-permute-done.5 = bf16[160,1152]{1,0:T(8,128)(2,1)} collective-permute-done((bf16[160,1152]{1,0:T(8,128)(2,1)S(1)}, bf16[160,1152]{1,0:T(8,128)(2,1)}, u32[]{:S(2)}, u32[]{:S(2)}) %collective-permute-start.5) | collective-permute-done | bytes 368672 | tf_op jit(solution)/shard_map/ppermute | solution.py:12
  105.0 0.2 collective-permute-start.6
  105.2 4.8 %fusion.48 = bf16[2560,160]{0,1:T(8,128)(2,1)S(1)} fusion(bf16[2560,1152]{1,0:T(8,128)(2,1)} %all-gather.2.cloned.1.call-done, bf16[160,1152]{1,0:T(8,128)(2,1)S(1)} %fusion.58, s32[2560]{0:T(1024)S(1)} %iota_add_fusion, f32[]{:T(128)} %bitcast.50, f32[]{:T(128)} %bitcast, s32[160]{0:T(256)S(1)} %iota_add_fusion.8), kind=kOutput, calls=%fused_computation.63 | convolution fusion | flops 947404800 | bytes 7096968 | tf_op jit(solution)/shard_map/dot_general | solution.py:68
  110.1 1.9 fusion.72
  112.1 1.0 copy-done
  113.1 3.2 fusion.54
  116.4 2.2 fusion.53
  118.6 3.1 fusion.52
  121.6 3.1 fusion.51
  124.7 3.1 fusion.50
  127.8 3.1 fusion.49
  130.9 3.6 convolution_add_fusion.6
  134.4 3.2 convolution_add_fusion.5
  137.6 3.2 convolution_add_fusion.4
  140.8 3.2 convolution_add_fusion.3
  144.0 6.3 %convolution_add_fusion.2 = f32[2560,1152]{1,0:T(8,128)} fusion(f32[2560,1152]{1,0:T(8,128)S(1)} %convolution_add_fusion.3, bf16[2560,160]{0,1:T(8,128)(2,1)S(1)} %fusion.53, bf16[160,1152]{1,0:T(8,128)(2,1)S(1)} %copy-done.21), kind=kOutput, calls=%fused_computation.2 | convolution fusion | flops 946667520 | bytes 24780800 | tf_op jit(solution)/shard_map/dot_general | solution.py:75
  150.3 6.4 %convolution_add_fusion.1 = f32[2560,1152]{1,0:T(8,128)S(1)} fusion(f32[2560,1152]{1,0:T(8,128)} %convolution_add_fusion.2, bf16[2560,160]{0,1:T(8,128)(2,1)S(1)} %fusion.54, bf16[160,1152]{1,0:T(8,128)(2,1)} %collective-permute-done.5), kind=kOutput, calls=%fused_computation.1 | convolution fusion | flops 946667520 | bytes 24780800 | tf_op jit(solution)/shard_map/dot_general | solution.py:75
  156.8 3.2 fusion.55
  160.0 0.9 copy-done.1
  160.9 7.5 %convolution_add_fusion = f32[2560,1152]{1,0:T(8,128)} fusion(f32[2560,1152]{1,0:T(8,128)S(1)} %convolution_add_fusion.1, bf16[2560,160]{0,1:T(8,128)(2,1)S(1)} %fusion.55, bf16[160,1152]{1,0:T(8,128)(2,1)} %collective-permute-done.6), kind=kOutput, calls=%fused_computation | convolution fusion | flops 946667520 | bytes 24780800 | tf_op jit(solution)/shard_map/dot_general | solution.py:75
  168.4 4.3 fusion.73
  172.7 0.1 collective-permute-start.7
  172.8 37.1 %collective-permute-done.7 = f32[160,1152]{1,0:T(8,128)S(1)} collective-permute-done((f32[160,1152]{1,0:T(8,128)S(1)}, f32[160,1152]{1,0:T(8,128)S(1)}, u32[]{:S(2)}, u32[]{:S(2)}) %collective-permute-start.7) | collective-permute-done | bytes 737312 | tf_op jit(solution)/shard_map/ppermute | solution.py:12
  209.9 1.2 convolution_add_fusion.7
  211.2 0.1 collective-permute-start.8
  211.3 1.2 fusion.74
  212.5 37.3 %collective-permute-done.8 = f32[160,1152]{1,0:T(8,128)S(1)} collective-permute-done((f32[160,1152]{1,0:T(8,128)S(1)}, f32[160,1152]{1,0:T(8,128)S(1)}, u32[]{:S(2)}, u32[]{:S(2)}) %collective-permute-start.8) | collective-permute-done | bytes 737312 | tf_op jit(solution)/shard_map/ppermute | solution.py:12
  249.8 0.1 add.325
  249.9 0.1 collective-permute-start.9
  250.0 1.3 fusion.75
  251.3 36.0 %collective-permute-done.9 = f32[160,1152]{1,0:T(8,128)S(1)} collective-permute-done((f32[160,1152]{1,0:T(8,128)S(1)}, f32[160,1152]{1,0:T(8,128)S(1)}, u32[]{:S(2)}, u32[]{:S(2)}) %collective-permute-start.9) | collective-permute-done | bytes 737312 | tf_op jit(solution)/shard_map/ppermute | solution.py:12
  287.3 0.1 add.326
  287.4 0.1 collective-permute-start.10
  287.5 1.3 fusion.76
  288.8 38.7 %collective-permute-done.10 = f32[160,1152]{1,0:T(8,128)S(1)} collective-permute-done((f32[160,1152]{1,0:T(8,128)S(1)}, f32[160,1152]{1,0:T(8,128)S(1)}, u32[]{:S(2)}, u32[]{:S(2)}) %collective-permute-start.10) | collective-permute-done | bytes 737312 | tf_op jit(solution)/shard_map/ppermute | solution.py:12
  327.4 0.1 add.327
  327.5 0.1 collective-permute-start.11
  327.6 1.2 fusion.77
  328.8 38.5 %collective-permute-done.11 = f32[160,1152]{1,0:T(8,128)S(1)} collective-permute-done((f32[160,1152]{1,0:T(8,128)S(1)}, f32[160,1152]{1,0:T(8,128)S(1)}, u32[]{:S(2)}, u32[]{:S(2)}) %collective-permute-start.11) | collective-permute-done | bytes 737312 | tf_op jit(solution)/shard_map/ppermute | solution.py:12
  367.3 0.1 add.328
  367.5 1.2 fusion.78
  368.8 26.6 %collective-permute-done.12 = f32[160,1152]{1,0:T(8,128)S(1)} collective-permute-done((f32[160,1152]{1,0:T(8,128)S(1)}, f32[160,1152]{1,0:T(8,128)S(1)}, u32[]{:S(2)}, u32[]{:S(2)}) %collective-permute-start.12) | collective-permute-done | bytes 737312 | tf_op jit(solution)/shard_map/ppermute | solution.py:12
  395.4 0.1 add.329
  395.5 0.3 collective-permute-start.13
  395.8 1.3 fusion.79
  397.1 20.6 %collective-permute-done.13 = f32[160,1152]{1,0:T(8,128)S(1)} collective-permute-done((f32[160,1152]{1,0:T(8,128)S(1)}, f32[160,1152]{1,0:T(8,128)S(1)}, u32[]{:S(2)}, u32[]{:S(2)}) %collective-permute-start.13) | collective-permute-done | bytes 737312 | tf_op jit(solution)/shard_map/ppermute | solution.py:12
  417.7 0.1 add.330
  417.9 15.1 %collective-permute-done.14 = f32[160,1152]{1,0:T(8,128)S(1)} collective-permute-done((f32[160,1152]{1,0:T(8,128)S(1)}, f32[160,1152]{1,0:T(8,128)S(1)}, u32[]{:S(2)}, u32[]{:S(2)}) %collective-permute-start.14) | collective-permute-done | bytes 737312 | tf_op jit(solution)/shard_map/ppermute | solution.py:12
  432.9 0.3 fusion.67
  433.2 1.0 fusion.70
  434.2 1.4 fusion.62
  435.6 2.1 fusion.65
  (78 shorter events, 0.5 us)
Async XLA Ops:
  7.2 3.8 copy-start.8
  7.2 98.0 %all-gather.2.cloned.1.call-start = ((), (), s32[]{:S(2)}) async-start(), calls=%async_computation.1 | async-start | bytes 6266880 | tf_op jit(solution)/shard_map/all_gather | solution.py:46
  8.4 0.6 copy-start.22
  10.9 423.3 %reduce-scatter.2.cloned.1.call-start = ((), (), s32[]{:S(2)}) async-start(), calls=%async_computation.2 | async-start | bytes 12533760 | tf_op jit(solution)/shard_map/reduce_scatter | solution.py:84
  11.1 37.5 %copy-start.24 = (f32[160]{0:T(256)}, f32[160]{0:T(256)S(1)}, u32[]{:S(2)}) copy-start(f32[160]{0:T(256)S(1)} %add_rsqrt_fusion) | copy-start | bytes 1924
  11.2 14.4 %collective-permute-start = (bf16[160,1152]{1,0:T(8,128)(2,1)S(1)}, bf16[160,1152]{1,0:T(8,128)(2,1)S(1)}, u32[]{:S(2)}, u32[]{:S(2)}) collective-permute-start(bf16[160,1152]{1,0:T(8,128)(2,1)S(1)} %fusion.58), channel_id=1, source_target_pairs={{0,16},{16,32},{32,48},{48,64},{64,80},{80,96},{96,112},{112,0},{1... | collective-permute-start | bytes 1105928 | tf_op jit(solution)/shard_map/ppermute | solution.py:12
  25.7 22.2 %collective-permute-start.1 = (bf16[160,1152]{1,0:T(8,128)(2,1)S(1)}, bf16[160,1152]{1,0:T(8,128)(2,1)S(1)}, u32[]{:S(2)}, u32[]{:S(2)}) collective-permute-start(bf16[160,1152]{1,0:T(8,128)(2,1)S(1)} %collective-permute-done), channel_id=1, source_target_pairs={{0,16},{16,32},{32,48},{48,64},{64,80},{80,96},{96,112},{112,0},{1... | collective-permute-start | bytes 1105928 | tf_op jit(solution)/shard_map/ppermute | solution.py:12
  47.8 0.7 copy-start.11
  48.6 22.1 %collective-permute-start.2 = (bf16[160,1152]{1,0:T(8,128)(2,1)S(1)}, bf16[160,1152]{1,0:T(8,128)(2,1)S(1)}, u32[]{:S(2)}, u32[]{:S(2)}) collective-permute-start(bf16[160,1152]{1,0:T(8,128)(2,1)S(1)} %collective-permute-done.1), channel_id=1, source_target_pairs={{0,16},{16,32},{32,48},{48,64},{64,80},{80,96},{96,112},{112,0},{1... | collective-permute-start | bytes 1105928 | tf_op jit(solution)/shard_map/ppermute | solution.py:12
  70.6 34.6 %copy-start.13 = (bf16[160,1152]{1,0:T(8,128)(2,1)}, bf16[160,1152]{1,0:T(8,128)(2,1)S(1)}, u32[]{:S(2)}) copy-start(bf16[160,1152]{1,0:T(8,128)(2,1)S(1)} %collective-permute-done.2) | copy-start | bytes 1105924
  70.6 12.0 %collective-permute-start.3 = (bf16[160,1152]{1,0:T(8,128)(2,1)S(1)}, bf16[160,1152]{1,0:T(8,128)(2,1)S(1)}, u32[]{:S(2)}, u32[]{:S(2)}) collective-permute-start(bf16[160,1152]{1,0:T(8,128)(2,1)S(1)} %collective-permute-done.2), channel_id=1, source_target_pairs={{0,16},{16,32},{32,48},{48,64},{64,80},{80,96},{96,112},{112,0},{1... | collective-permute-start | bytes 1105928 | tf_op jit(solution)/shard_map/ppermute | solution.py:12
  82.7 22.6 %copy-start.16 = (bf16[160,1152]{1,0:T(8,128)(2,1)}, bf16[160,1152]{1,0:T(8,128)(2,1)S(1)}, u32[]{:S(2)}) copy-start(bf16[160,1152]{1,0:T(8,128)(2,1)S(1)} %collective-permute-done.3) | copy-start | bytes 1105924
  82.7 11.1 %collective-permute-start.4 = (bf16[160,1152]{1,0:T(8,128)(2,1)S(1)}, bf16[160,1152]{1,0:T(8,128)(2,1)S(1)}, u32[]{:S(2)}, u32[]{:S(2)}) collective-permute-start(bf16[160,1152]{1,0:T(8,128)(2,1)S(1)} %collective-permute-done.3), channel_id=1, source_target_pairs={{0,16},{16,32},{32,48},{48,64},{64,80},{80,96},{96,112},{112,0},{1... | collective-permute-start | bytes 1105928 | tf_op jit(solution)/shard_map/ppermute | solution.py:12
  93.8 16.3 %copy-start.19 = (bf16[160,1152]{1,0:T(8,128)(2,1)}, bf16[160,1152]{1,0:T(8,128)(2,1)S(1)}, u32[]{:S(2)}) copy-start(bf16[160,1152]{1,0:T(8,128)(2,1)S(1)} %collective-permute-done.4) | copy-start | bytes 1105924
  93.8 11.2 %collective-permute-start.5 = (bf16[160,1152]{1,0:T(8,128)(2,1)S(1)}, bf16[160,1152]{1,0:T(8,128)(2,1)}, u32[]{:S(2)}, u32[]{:S(2)}) collective-permute-start(bf16[160,1152]{1,0:T(8,128)(2,1)S(1)} %collective-permute-done.4), channel_id=1, source_target_pairs={{0,16},{16,32},{32,48},{48,64},{64,80},{80,96},{96,112},{112,0},{1... | collective-permute-start | bytes 1105928 | tf_op jit(solution)/shard_map/ppermute | solution.py:12
  105.0 51.7 %collective-permute-start.6 = (bf16[160,1152]{1,0:T(8,128)(2,1)}, bf16[160,1152]{1,0:T(8,128)(2,1)}, u32[]{:S(2)}, u32[]{:S(2)}) collective-permute-start(bf16[160,1152]{1,0:T(8,128)(2,1)} %collective-permute-done.5), channel_id=1, source_target_pairs={{0,16},{16,32},{32,48},{48,64},{64,80},{80,96},{96,112},{112,0},{1... | collective-permute-start | bytes 1105928 | tf_op jit(solution)/shard_map/ppermute | solution.py:12
  110.1 2.0 copy-start.6
  110.1 3.0 copy-start
  113.1 3.2 copy-start.20
  116.3 2.2 copy-start.17
  118.5 3.1 copy-start.14
  121.6 3.1 copy-start.12
  134.4 3.2 copy-start.15
  137.6 3.2 copy-start.18
  140.8 3.2 copy-start.21
  160.0 0.9 copy-start.1
  168.3 41.6 %slice-start = ((s8[5898240]{0:T(1024)(128)(4,1)}), s8[1703936]{0:T(1024)(128)(4,1)S(1)}, s32[]{:S(2)}) async-start(s8[5898240]{0:T(1024)(128)(4,1)} %bitcast.58), calls=%async_computation.3 | async-start | bytes 3407872
  168.4 41.6 %slice-start.1 = ((s8[5898240]{0:T(1024)(128)(4,1)}), s8[4194304]{0:T(1024)(128)(4,1)S(1)}, s32[]{:S(2)}) async-start(s8[5898240]{0:T(1024)(128)(4,1)} %bitcast.58), calls=%async_computation.4 | async-start | bytes 8388608
  168.4 41.5 %copy-start.7 = (bf16[2560,160]{0,1:T(8,128)(2,1)S(1)}, bf16[2560,160]{0,1:T(8,128)(2,1)}, u32[]{:S(2)}) copy-start(bf16[2560,160]{0,1:T(8,128)(2,1)} %fusion.49) | copy-start | bytes 2457604
  172.7 38.6 %copy-start.5 = (bf16[2560,160]{0,1:T(8,128)(2,1)S(1)}, bf16[2560,160]{0,1:T(8,128)(2,1)}, u32[]{:S(2)}) copy-start(bf16[2560,160]{0,1:T(8,128)(2,1)} %fusion.50) | copy-start | bytes 2457604
  172.7 37.2 %collective-permute-start.7 = (f32[160,1152]{1,0:T(8,128)S(1)}, f32[160,1152]{1,0:T(8,128)S(1)}, u32[]{:S(2)}, u32[]{:S(2)}) collective-permute-start(f32[160,1152]{1,0:T(8,128)S(1)} %fusion.73), channel_id=1, source_target_pairs={{0,16},{16,32},{32,48},{48,64},{64,80},{80,96},{96,112},{112,0},{1... | collective-permute-start | bytes 2211848 | tf_op jit(solution)/shard_map/ppermute | solution.py:12
  211.2 38.6 %collective-permute-start.8 = (f32[160,1152]{1,0:T(8,128)S(1)}, f32[160,1152]{1,0:T(8,128)S(1)}, u32[]{:S(2)}, u32[]{:S(2)}) collective-permute-start(f32[160,1152]{1,0:T(8,128)S(1)} %convolution_add_fusion.7), channel_id=1, source_target_pairs={{0,16},{16,32},{32,48},{48,64},{64,80},{80,96},{96,112},{112,0},{1... | collective-permute-start | bytes 2211848 | tf_op jit(solution)/shard_map/ppermute | solution.py:12
  212.5 37.5 %copy-start.4 = (bf16[2560,160]{0,1:T(8,128)(2,1)S(1)}, bf16[2560,160]{0,1:T(8,128)(2,1)}, u32[]{:S(2)}) copy-start(bf16[2560,160]{0,1:T(8,128)(2,1)} %fusion.51) | copy-start | bytes 2457604
  249.9 37.4 %collective-permute-start.9 = (f32[160,1152]{1,0:T(8,128)S(1)}, f32[160,1152]{1,0:T(8,128)S(1)}, u32[]{:S(2)}, u32[]{:S(2)}) collective-permute-start(f32[160,1152]{1,0:T(8,128)S(1)} %add.325), channel_id=1, source_target_pairs={{0,16},{16,32},{32,48},{48,64},{64,80},{80,96},{96,112},{112,0},{1... | collective-permute-start | bytes 2211848 | tf_op jit(solution)/shard_map/ppermute | solution.py:12
  251.3 36.2 %copy-start.3 = (bf16[2560,160]{0,1:T(8,128)(2,1)S(1)}, bf16[2560,160]{0,1:T(8,128)(2,1)}, u32[]{:S(2)}) copy-start(bf16[2560,160]{0,1:T(8,128)(2,1)} %fusion.52) | copy-start | bytes 2457604
  287.4 40.1 %collective-permute-start.10 = (f32[160,1152]{1,0:T(8,128)S(1)}, f32[160,1152]{1,0:T(8,128)S(1)}, u32[]{:S(2)}, u32[]{:S(2)}) collective-permute-start(f32[160,1152]{1,0:T(8,128)S(1)} %add.326), channel_id=1, source_target_pairs={{0,16},{16,32},{32,48},{48,64},{64,80},{80,96},{96,112},{112,0},{1... | collective-permute-start | bytes 2211848 | tf_op jit(solution)/shard_map/ppermute | solution.py:12
  327.5 39.8 %collective-permute-start.11 = (f32[160,1152]{1,0:T(8,128)S(1)}, f32[160,1152]{1,0:T(8,128)S(1)}, u32[]{:S(2)}, u32[]{:S(2)}) collective-permute-start(f32[160,1152]{1,0:T(8,128)S(1)} %add.327), channel_id=1, source_target_pairs={{0,16},{16,32},{32,48},{48,64},{64,80},{80,96},{96,112},{112,0},{1... | collective-permute-start | bytes 2211848 | tf_op jit(solution)/shard_map/ppermute | solution.py:12
  367.4 27.9 %collective-permute-start.12 = (f32[160,1152]{1,0:T(8,128)S(1)}, f32[160,1152]{1,0:T(8,128)S(1)}, u32[]{:S(2)}, u32[]{:S(2)}) collective-permute-start(f32[160,1152]{1,0:T(8,128)S(1)} %add.328), channel_id=1, source_target_pairs={{0,16},{16,32},{32,48},{48,64},{64,80},{80,96},{96,112},{112,0},{1... | collective-permute-start | bytes 2211848 | tf_op jit(solution)/shard_map/ppermute | solution.py:12
  368.7 27.0 %copy-start.2 = (bf16[2560,160]{0,1:T(8,128)(2,1)S(1)}, bf16[2560,160]{0,1:T(8,128)(2,1)}, u32[]{:S(2)}) copy-start(bf16[2560,160]{0,1:T(8,128)(2,1)} %copy-done.1) | copy-start | bytes 2457604
  395.5 22.2 %collective-permute-start.13 = (f32[160,1152]{1,0:T(8,128)S(1)}, f32[160,1152]{1,0:T(8,128)S(1)}, u32[]{:S(2)}, u32[]{:S(2)}) collective-permute-start(f32[160,1152]{1,0:T(8,128)S(1)} %add.329), channel_id=1, source_target_pairs={{0,16},{16,32},{32,48},{48,64},{64,80},{80,96},{96,112},{112,0},{1... | collective-permute-start | bytes 2211848 | tf_op jit(solution)/shard_map/ppermute | solution.py:12
  397.1 35.9 %copy-start.9 = (bf16[160,1152]{1,0:T(8,128)(2,1)S(1)}, bf16[160,1152]{1,0:T(8,128)(2,1)}, u32[]{:S(2)}) copy-start(bf16[160,1152]{1,0:T(8,128)(2,1)} %param.5) | copy-start | bytes 1105924
  397.1 35.8 %copy-start.25 = (f32[160]{0:T(256)S(1)}, f32[160]{0:T(256)}, u32[]{:S(2)}) copy-start(f32[160]{0:T(256)} %copy-done.24) | copy-start | bytes 1924
  417.7 16.4 %copy-start.10 = (bf16[160,1152]{1,0:T(8,128)(2,1)S(1)}, bf16[160,1152]{1,0:T(8,128)(2,1)}, u32[]{:S(2)}) copy-start(bf16[160,1152]{1,0:T(8,128)(2,1)} %param.4) | copy-start | bytes 1105924
  417.8 16.4 %copy-start.23 = (f32[160]{0:T(256)S(1)}, f32[160]{0:T(256)}, u32[]{:S(2)}) copy-start(f32[160]{0:T(256)} %copy-done.22) | copy-start | bytes 1924
  417.8 15.1 %collective-permute-start.14 = (f32[160,1152]{1,0:T(8,128)S(1)}, f32[160,1152]{1,0:T(8,128)S(1)}, u32[]{:S(2)}, u32[]{:S(2)}) collective-permute-start(f32[160,1152]{1,0:T(8,128)S(1)} %add.330), channel_id=1, source_target_pairs={{0,16},{16,32},{32,48},{48,64},{64,80},{80,96},{96,112},{112,0},{1... | collective-permute-start | bytes 2211848 | tf_op jit(solution)/shard_map/ppermute | solution.py:12
Sparse Core Ops, SparseCore 0:
  11.0 42.8 all-gather.1
  168.5 131.4 reduce-scatter.1
where the time goes:
time: 448 us; the launch traced here: 445 us
  waiting for transfers between devices  339 us (76%)
  matrix products  74.1 us (17%)
  between operations  16.3 us (4%)
  other arithmetic  8.61 us (2%)
    ppermute x15, waiting for transfers between devices, passed_along(): return lax.ppermute(value, axis, pairs)  339 us
    dot_general x8, matrix products, on_device(): jnp.dot(weights, current, preferred_element_type=jnp.float32)  35.2 us
    dot_general x8, matrix products, on_device(): lax.dot_general(gathered, current, (((1,), (1,)), ((), ())), preferred_el...  25.8 us
    dot_general x8, matrix products, on_device(): lax.dot_general(weights, gathered, (((0,), (0,)), ((), ())), preferred_el...  13.1 us
  transfers between devices with their start and end apart: 17, of which 14 were waited for; matrix products, arithmetic and copies ran while one was open for 15% of the time, Pallas kernels for 0%

commit v1 on v0

v1 whole, which is shorter than its diff:
```python
import functools

import jax
import jax.numpy as jnp
from jax import lax
from jax.experimental import pallas as pl
from jax.experimental.pallas import tpu as pltpu
from jax.sharding import Mesh, PartitionSpec as P

norm_eps = 1e-06
log2_e = 1.4426950408889634
axes = ("yh", "z", "x", "yl", "core")
extents = (2, 4, 4, 2, 2)
rows = 160
chip_rows = 2 * rows
chunk = 256


def pairs_of(move):
    pairs = []
    for yh in range(2):
        for z in range(4):
            for x in range(4):
                for yl in range(2):
                    for core in range(2):
                        place = (yh, z, x, yl, core)
                        pairs.append((linear(place), linear(move(*place))))
    return pairs


def linear(place):
    index = 0
    for value, extent in zip(place, extents):
        index = index * extent + value
    return index


def ring_move(steps):
    def move(yh, z, x, yl, core):
        if core == 0:
            return (yh, z, (x + steps) % 4, yl, core)
        return (yh, (z + steps) % 4, x, yl, core)

    return pairs_of(move)


def ring(value, steps):
    return lax.ppermute(value, axes, ring_move(steps))


def pair(value):
    def move(yh, z, x, yl, core):
        if core == 0:
            return (yh, z, x, 1 - yl, core)
        return (1 - yh, z, x, yl, core)

    return lax.ppermute(value, axes, pairs_of(move))


def swap(value):
    return lax.ppermute(value, "core", [(0, 1), (1, 0)])


def unit_rows(values):
    inverse = lax.rsqrt(jnp.sum(values * values, axis=1, keepdims=True) + norm_eps)
    return values * inverse, inverse


def pack_kernel(core_ref, image_ref, text_ref, got_ref, unit_ref, raw_ref):
    first_core = core_ref[0] == 0
    image = image_ref[...].astype(jnp.float32)
    text = text_ref[...].astype(jnp.float32)
    got = got_ref[...].astype(jnp.float32)
    low = jnp.where(first_core, image, got)
    high = jnp.where(first_core, got, text)
    for half, values in enumerate((low, high)):
        place = pl.ds(half * rows, rows)
        unit_ref[place, :] = unit_rows(values)[0].astype(jnp.bfloat16)
        raw_ref[place, :] = values.astype(jnp.bfloat16)


def pair_kernel(chips, scale_ref, core_ref, *refs):
    mine_in, other_in = refs[:chips], refs[chips : 2 * chips]
    mine_out, other_out = refs[2 * chips : 3 * chips], refs[3 * chips : 4 * chips]
    mine, other, weights, mine_sum, other_sum, in_sem, out_sem = refs[4 * chips :]
    count = chips * rows
    core = core_ref[0]
    half = pl.program_id(0)
    opposite = jnp.where(core == 0, half, 1 - half)

    def half_rows(which):
        return pl.ds(pl.multiple_of(which * rows, rows), rows)

    def loads(which, group):
        arrays, held, sems = (
            (mine_in, mine, 0) if group == 0 else (other_in, other, 1)
        )
        return [
            pltpu.make_async_copy(
                arrays[chip].at[half_rows(which)],
                held.at[which, pl.ds(chip * rows, rows)],
                in_sem.at[sems, which, chip],
            )
            for chip in range(chips)
        ]

    def stores(which, group):
        arrays, held, sems = (
            (mine_out, mine_sum, 0) if group == 0 else (other_out, other_sum, 1)
        )
        return [
            pltpu.make_async_copy(
                held.at[which, pl.ds(chip * rows, rows)],
                arrays[chip].at[half_rows(which)],
                out_sem.at[sems, which, chip],
            )
            for chip in range(chips)
        ]

    @pl.when(half == 0)
    def _():
        for which, far in ((0, opposite), (1, 1 - opposite)):
            for copy in loads(which, 0):
                copy.start()
            for copy in loads(far, 1):
                copy.start()

    for copy in loads(half, 0):
        copy.wait()
    for copy in loads(opposite, 1):
        copy.wait()

    slope = scale_ref[0]
    shift = scale_ref[1]
    mine_rows = mine[half]
    for begin in range(0, count, chunk):
        place = pl.ds(begin, chunk)
        dots = lax.dot_general(
            mine_rows,
            other[opposite, place, :],
            (((1,), (1,)), ((), ())),
            preferred_element_type=jnp.float32,
        )
        power = jnp.exp2(dots * slope + shift)
        share = pl.reciprocal(1.0 + power, approx=True)
        if begin == 0:
            row = lax.broadcasted_iota(jnp.int32, dots.shape, 0)
            column = lax.broadcasted_iota(jnp.int32, dots.shape, 1)
            matched = (row == column) & (row < rows) & (core == 0)
            share = jnp.where(matched, -power * share, share)
        weights[:, place] = share.astype(jnp.bfloat16)
    for begin in range(0, count, chunk):
        place = pl.ds(begin, chunk)
        other_sum[opposite, place, :] = lax.dot_general(
            weights[:, place],
            mine_rows,
            (((0,), (0,)), ((), ())),
            preferred_element_type=jnp.float32,
        ).astype(jnp.bfloat16)
    for copy in stores(opposite, 1):
        copy.start()
    other_rows = other[opposite]
    for begin in range(0, count, chunk):
        place = pl.ds(begin, chunk)
        mine_sum[half, place, :] = jnp.dot(
            weights[place, :], other_rows, preferred_element_type=jnp.float32
        ).astype(jnp.bfloat16)
    for copy in stores(half, 0):
        copy.start()

    @pl.when(half == 1)
    def _():
        for which in range(2):
            for group in range(2):
                for copy in stores(which, group):
                    copy.wait()


def pair_sums(scale, core, mine, other):
    chips = len(mine)
    width = mine[0].shape[1]
    count = chips * rows
    hbm = pl.BlockSpec(memory_space=pl.ANY)
    smem = pl.BlockSpec(memory_space=pltpu.SMEM)
    sums = pl.pallas_call(
        functools.partial(pair_kernel, chips),
        grid=(2,),
        in_specs=[smem, smem] + [hbm] * (2 * chips),
        out_specs=[hbm] * (2 * chips),
        out_shape=[jax.ShapeDtypeStruct((chip_rows, width), jnp.bfloat16)] * (2 * chips),
        scratch_shapes=[
            pltpu.VMEM((2, count, width), jnp.bfloat16),
            pltpu.VMEM((2, count, width), jnp.bfloat16),
            pltpu.VMEM((count, count), jnp.bfloat16),
            pltpu.VMEM((2, count, width), jnp.bfloat16),
            pltpu.VMEM((2, count, width), jnp.bfloat16),
            pltpu.SemaphoreType.DMA((2, 2, chips)),
            pltpu.SemaphoreType.DMA((2, 2, chips)),
        ],
        compiler_params=pltpu.CompilerParams(vmem_limit_bytes=50 * 2**20),
        cost_estimate=pl.CostEstimate(
            flops=12 * count * count * width,
            bytes_accessed=8 * chips * chip_rows * width,
            transcendentals=4 * count * count,
        ),
    )(scale, core, *mine, *other)
    return sums[:chips], sums[chips:]


def final_kernel(scale_ref, core_ref, raw_ref, *refs):
    parts, (keep_ref, give_ref) = refs[:-2], refs[-2:]
    first_core = core_ref[0] == 0
    grads = []
    for half in range(2):
        place = pl.ds(half * rows, rows)
        unit, inverse = unit_rows(raw_ref[place, :].astype(jnp.float32))
        direction = parts[0][place, :].astype(jnp.float32)
        for part in parts[1:]:
            direction = direction + part[place, :].astype(jnp.float32)
        direction = direction * scale_ref[0]
        along = jnp.sum(unit * direction, axis=1, keepdims=True)
        grads.append(inverse * (direction - unit * along))
    low, high = grads
    keep_ref[...] = jnp.where(first_core, low, high).astype(jnp.bfloat16)
    give_ref[...] = jnp.where(first_core, high, low).astype(jnp.bfloat16)


def small_call(kernel, out_shape, scalars, arrays):
    return pl.pallas_call(
        kernel,
        in_specs=[pl.BlockSpec(memory_space=pltpu.SMEM)] * len(scalars)
        + [pl.BlockSpec(memory_space=pltpu.VMEM)] * len(arrays),
        out_specs=[pl.BlockSpec(memory_space=pltpu.VMEM)] * len(out_shape),
        out_shape=[jax.ShapeDtypeStruct(shape, jnp.bfloat16) for shape in out_shape],
        compiler_params=pltpu.CompilerParams(vmem_limit_bytes=32 * 2**20),
    )(*scalars, *arrays)


def add(*parts):
    total = parts[0].astype(jnp.float32)
    for part in parts[1:]:
        total = total + part.astype(jnp.float32)
    return total.astype(jnp.bfloat16)


def on_device(image_embeds, text_embeds, log_scale, logit_bias):
    width = image_embeds.shape[1]
    core = lax.axis_index("core")
    first_core = core == 0
    cores = core.astype(jnp.int32).reshape(1)
    logit_scale = jnp.exp(log_scale)
    factors = jnp.concatenate([-log2_e * logit_scale, -log2_e * logit_bias])
    got = swap(jnp.where(first_core, text_embeds, image_embeds))
    unit, raw = small_call(
        pack_kernel,
        [(chip_rows, width)] * 2,
        (cores,),
        (image_embeds, text_embeds, got),
    )
    near = [unit, ring(unit, 1), ring(unit, -1), ring(unit, 2)]
    across = pair(unit)
    far = [across, ring(across, 1), ring(across, -1), ring(across, 2)]
    mine = near + far
    other = [swap(value) for value in mine]
    mine_sums, other_sums = pair_sums(factors, cores, mine, other)
    sums = [add(one, swap(two)) for one, two in zip(mine_sums, other_sums)]
    near_sums, far_sums = sums[:4], sums[4:]
    back = (0, -1, 1, 2)
    far_total = add(far_sums[0], *[ring(far_sums[k], back[k]) for k in (1, 2, 3)])
    parts = [near_sums[0]] + [ring(near_sums[k], back[k]) for k in (1, 2, 3)] + [pair(far_total)]
    keep, give = small_call(
        final_kernel, [(rows, width)] * 2, (logit_scale, cores), (raw, *parts)
    )
    given = swap(give)
    image_grad = jnp.where(first_core, keep, given)
    text_grad = jnp.where(first_core, given, keep)
    return (image_grad, text_grad)


def solution(mesh):
    fine = Mesh(mesh.devices.reshape(extents), axes)
    split = P(axes, None)
    return jax.shard_map(
        on_device,
        mesh=fine,
        in_specs=(split, split, P(), P()),
        out_specs=(split, split),
        check_vma=False,
    )
```

time: 448 us -> 142 us (0.32)
  the two profiles are of different devices: /device:TPU:8 before, /device:TPU:1 now
where the time goes in v1:
time: 142 us
  waiting for transfers between devices  64.7 us (46%)
  Pallas kernels  35.2 us (25%)
  starting transfers between devices  32.4 us (23%)
  other arithmetic  3.8 us (3%)
  local copies, waits for them, and re-layouts  3.2 us (2%)
  between operations  2.25 us (2%)
    ppermute x12, waiting for transfers between devices, ring(): return lax.ppermute(value, axes, ring_move(steps))  40.8 us
    pallas_call x1, Pallas kernels, pair_sums(): pl.pallas_call(functools.partial(pair_kernel, chips), grid=(2,), in_specs...  33.8 us
    ppermute x12, starting transfers between devices, ring(): return lax.ppermute(value, axes, ring_move(steps))  18.4 us
    ppermute x2, waiting for transfers between devices, pair(): return lax.ppermute(value, axes, pairs_of(move))  13.3 us
    ppermute x18, waiting for transfers between devices, swap(): return lax.ppermute(value, 'core', [(0, 1), (1, 0)])  10.6 us
    ppermute x18, starting transfers between devices, swap(): return lax.ppermute(value, 'core', [(0, 1), (1, 0)])  7.43 us
    ppermute x2, starting transfers between devices, pair(): return lax.ppermute(value, axes, pairs_of(move))  6.55 us
    unnamed x44, local copies, waits for them, and re-layouts  3.2 us
  transfers between devices with their start and end apart: 32, of which 15 were waited for; matrix products, arithmetic and copies ran while one was open for 1% of the time, Pallas kernels for 0%

profile of v1, /device:TPU:1, one launch (start us, length us, event | category | flops | bytes accessed | tf_op | source)
XLA Modules:
  0.0 141.5 jit_solution(8791506412672900257)
XLA Ops:
  0.7 1.1 broadcast_select_fusion.2
  1.8 1.5 %collective-permute-start = (bf16[160,1152]{1,0:T(8,128)(2,1)S(1)}, bf16[160,1152]{1,0:T(8,128)(2,1)S(1)}, u32[]{:S(2)}, u32[]{:S(2)}) collective-permute-start(bf16[160,1152]{1,0:T(8,128)(2,1)S(1)} %broadcast_select_fusion.2), channel_id=1, source_target_pairs={{0,1},{1,0},{2,3},{3,2},{4,5},{5,4},{6,7},{7,6},{8,9},{9,8},{10,11... | collective-permute-start | bytes 1105928 | tf_op jit(solution)/shard_map/ppermute | solution.py:61
  3.3 1.3 collective-permute-done.got_ref
  4.6 0.4 shard_map.59
  5.0 3.1 %collective-permute-start.4 = (bf16[320,1152]{1,0:T(8,128)(2,1)S(1)}, bf16[320,1152]{1,0:T(8,128)(2,1)S(1)}, u32[]{:S(2)}, u32[]{:S(2)}) collective-permute-start(bf16[320,1152]{1,0:T(8,128)(2,1)S(1)} %get-tuple-element.23.refs_0_), channel_id=1, source_target_pairs={{0,2},{1,65},{2,0},{3,67},{4,6},{5,69},{6,4},{7,71},{8,10},{9,73},... | collective-permute-start | bytes 2211848 | tf_op jit(solution)/shard_map/ppermute | solution.py:57
  8.1 3.6 %collective-permute-start.3 = (bf16[320,1152]{1,0:T(8,128)(2,1)S(1)}, bf16[320,1152]{1,0:T(8,128)(2,1)S(1)}, u32[]{:S(2)}, u32[]{:S(2)}) collective-permute-start(bf16[320,1152]{1,0:T(8,128)(2,1)S(1)} %get-tuple-element.23.refs_0_), channel_id=1, source_target_pairs={{0,8},{1,33},{2,10},{3,35},{4,12},{5,37},{6,14},{7,39},{8,0},{9,41... | collective-permute-start | bytes 2211848 | tf_op jit(solution)/shard_map/ppermute | solution.py:48
  11.7 0.4 collective-permute-start.2
  12.1 1.0 collective-permute-start.1
  13.1 10.5 %collective-permute-done.4.refs_4_ = bf16[320,1152]{1,0:T(8,128)(2,1)S(1)} collective-permute-done((bf16[320,1152]{1,0:T(8,128)(2,1)S(1)}, bf16[320,1152]{1,0:T(8,128)(2,1)S(1)}, u32[]{:S(2)}, u32[]{:S(2)}) %collective-permute-start.4) | collective-permute-done | bytes 737312 | tf_op jit(solution)/shard_map/ppermute | solution.py:57
  23.6 0.1 collective-permute-start.12
  23.7 3.8 %collective-permute-start.7 = (bf16[320,1152]{1,0:T(8,128)(2,1)S(1)}, bf16[320,1152]{1,0:T(8,128)(2,1)S(1)}, u32[]{:S(2)}, u32[]{:S(2)}) collective-permute-start(bf16[320,1152]{1,0:T(8,128)(2,1)S(1)} %collective-permute-done.4.refs_4_), channel_id=1, source_target_pairs={{0,8},{1,33},{2,10},{3,35},{4,12},{5,37},{6,14},{7,39},{8,0},{9,41... | collective-permute-start | bytes 2211848 | tf_op jit(solution)/shard_map/ppermute | solution.py:48
  27.5 0.4 collective-permute-start.6
  27.9 1.6 %collective-permute-done.2.refs_2_ = bf16[320,1152]{1,0:T(8,128)(2,1)S(1)} collective-permute-done((bf16[320,1152]{1,0:T(8,128)(2,1)S(1)}, bf16[320,1152]{1,0:T(8,128)(2,1)S(1)}, u32[]{:S(2)}, u32[]{:S(2)}) %collective-permute-start.2) | collective-permute-done | bytes 737312 | tf_op jit(solution)/shard_map/ppermute | solution.py:48
  29.5 0.2 collective-permute-start.5
  29.7 1.2 collective-permute-start.11
  30.9 0.1 collective-permute-start.10
  31.0 5.6 %collective-permute-done.7.refs_7_ = bf16[320,1152]{1,0:T(8,128)(2,1)S(1)} collective-permute-done((bf16[320,1152]{1,0:T(8,128)(2,1)S(1)}, bf16[320,1152]{1,0:T(8,128)(2,1)S(1)}, u32[]{:S(2)}, u32[]{:S(2)}) %collective-permute-start.7) | collective-permute-done | bytes 737312 | tf_op jit(solution)/shard_map/ppermute | solution.py:48
  36.7 0.8 collective-permute-start.9
  37.5 7.5 %collective-permute-done.6.refs_6_ = bf16[320,1152]{1,0:T(8,128)(2,1)S(1)} collective-permute-done((bf16[320,1152]{1,0:T(8,128)(2,1)S(1)}, bf16[320,1152]{1,0:T(8,128)(2,1)S(1)}, u32[]{:S(2)}, u32[]{:S(2)}) %collective-permute-start.6) | collective-permute-done | bytes 737312 | tf_op jit(solution)/shard_map/ppermute | solution.py:48
  45.0 0.4 collective-permute-start.15
  45.4 0.1 collective-permute-start.14
  45.6 0.4 collective-permute-start.13
  47.3 0.1 pad_maximum_fusion.scale_ref
  47.4 2.0 %collective-permute-done.14.refs_14_ = bf16[320,1152]{1,0:T(8,128)(2,1)S(1)} collective-permute-done((bf16[320,1152]{1,0:T(8,128)(2,1)S(1)}, bf16[320,1152]{1,0:T(8,128)(2,1)S(1)}, u32[]{:S(2)}, u32[]{:S(2)}) %collective-permute-start.14) | collective-permute-done | bytes 737312 | tf_op jit(solution)/shard_map/ppermute | solution.py:61
  49.4 0.9 copy-done.21
  50.3 33.8 %shard_map.60 = (bf16[320,1152]{1,0:T(8,128)(2,1)S(1)}, bf16[320,1152]{1,0:T(8,128)(2,1)S(1)}, bf16[320,1152]{1,0:T(8,128)(2,1)S(1)}, bf16[320,1152]{1,0:T(8,128...) custom-call(f32[2]{0:T(128)S(1)} %pad_maximum_fusion.scale_ref, ...), custom_call_target="tpu_custom_call" | custom-call | flops 22649241600 | bytes 23592960 | tf_op jit(solution)/shard_map/pallas_call | solution.py:185
  84.1 0.7 collective-permute-start.17
  84.8 0.1 collective-permute-start.24
  84.9 0.4 collective-permute-start.19
  85.3 0.1 collective-permute-start.21
  85.4 0.4 collective-permute-start.23
  85.8 1.0 collective-permute-done.17
  86.8 0.4 collective-permute-start.26
  87.2 0.2 add_convert_fusion.7
  87.4 0.5 collective-permute-done.24
  87.9 0.4 copy-done.18
  88.3 0.1 collective-permute-start.28
  88.5 0.1 copy-done.5
  88.6 0.2 add_convert_fusion.3
  88.7 4.4 %collective-permute-done.26 = bf16[320,1152]{1,0:T(8,128)(2,1)S(1)} collective-permute-done((bf16[320,1152]{1,0:T(8,128)(2,1)}, bf16[320,1152]{1,0:T(8,128)(2,1)S(1)}, u32[]{:S(2)}, u32[]{:S(2)}) %collective-permute-start.26) | collective-permute-done | bytes 737312 | tf_op jit(solution)/shard_map/ppermute | solution.py:61
  93.2 3.7 %collective-permute-start.25 = (bf16[320,1152]{1,0:T(8,128)(2,1)S(1)}, bf16[320,1152]{1,0:T(8,128)(2,1)S(1)}, u32[]{:S(2)}, u32[]{:S(2)}) collective-permute-start(bf16[320,1152]{1,0:T(8,128)(2,1)S(1)} %add_convert_fusion.3), channel_id=1, source_target_pairs={{0,12},{1,49},{2,14},{3,51},{4,0},{5,53},{6,2},{7,55},{8,4},{9,57}... | collective-permute-start | bytes 2211848 | tf_op jit(solution)/shard_map/ppermute | solution.py:48
  96.9 0.2 add_convert_fusion.2
  97.1 0.1 collective-permute-start.27
  97.2 0.8 copy-done.3
  98.0 0.2 add_convert_fusion.1
  98.2 0.5 collective-permute-start.29
  98.8 0.2 add_convert_fusion.6
  99.0 0.9 copy-done.6
  99.9 0.1 collective-permute-start.16
  100.0 0.2 add_convert_fusion.5
  100.2 3.3 %collective-permute-start.18 = (bf16[320,1152]{1,0:T(8,128)(2,1)S(1)}, bf16[320,1152]{1,0:T(8,128)(2,1)S(1)}, u32[]{:S(2)}, u32[]{:S(2)}) collective-permute-start(bf16[320,1152]{1,0:T(8,128)(2,1)S(1)} %add_convert_fusion.7), channel_id=1, source_target_pairs={{0,12},{1,49},{2,14},{3,51},{4,0},{5,53},{6,2},{7,55},{8,4},{9,57}... | collective-permute-start | bytes 2211848 | tf_op jit(solution)/shard_map/ppermute | solution.py:48
  103.5 9.7 %collective-permute-done.25 = bf16[320,1152]{1,0:T(8,128)(2,1)S(1)} collective-permute-done((bf16[320,1152]{1,0:T(8,128)(2,1)S(1)}, bf16[320,1152]{1,0:T(8,128)(2,1)S(1)}, u32[]{:S(2)}, u32[]{:S(2)}) %collective-permute-start.25) | collective-permute-done | bytes 737312 | tf_op jit(solution)/shard_map/ppermute | solution.py:48
  113.2 3.4 %collective-permute-done.27 = bf16[320,1152]{1,0:T(8,128)(2,1)S(1)} collective-permute-done((bf16[320,1152]{1,0:T(8,128)(2,1)S(1)}, bf16[320,1152]{1,0:T(8,128)(2,1)S(1)}, u32[]{:S(2)}, u32[]{:S(2)}) %collective-permute-start.27) | collective-permute-done | bytes 737312 | tf_op jit(solution)/shard_map/ppermute | solution.py:48
  116.6 1.2 collective-permute-start.22
  117.8 0.5 add_convert_fusion
  118.3 3.5 %collective-permute-start.30 = (bf16[320,1152]{1,0:T(8,128)(2,1)S(1)}, bf16[320,1152]{1,0:T(8,128)(2,1)S(1)}, u32[]{:S(2)}, u32[]{:S(2)}) collective-permute-start(bf16[320,1152]{1,0:T(8,128)(2,1)S(1)} %add_convert_fusion), channel_id=1, source_target_pairs={{0,2},{1,65},{2,0},{3,67},{4,6},{5,69},{6,4},{7,71},{8,10},{9,73},... | collective-permute-start | bytes 2211848 | tf_op jit(solution)/shard_map/ppermute | solution.py:57
  121.8 0.2 add_convert_fusion.8.refs_0_
  122.0 7.1 %collective-permute-done.18.refs_1_ = bf16[320,1152]{1,0:T(8,128)(2,1)S(1)} collective-permute-done((bf16[320,1152]{1,0:T(8,128)(2,1)S(1)}, bf16[320,1152]{1,0:T(8,128)(2,1)S(1)}, u32[]{:S(2)}, u32[]{:S(2)}) %collective-permute-start.18) | collective-permute-done | bytes 737312 | tf_op jit(solution)/shard_map/ppermute | solution.py:48
  129.0 5.8 %collective-permute-done.22.refs_3_ = bf16[320,1152]{1,0:T(8,128)(2,1)S(1)} collective-permute-done((bf16[320,1152]{1,0:T(8,128)(2,1)S(1)}, bf16[320,1152]{1,0:T(8,128)(2,1)S(1)}, u32[]{:S(2)}, u32[]{:S(2)}) %collective-permute-start.22) | collective-permute-done | bytes 737312 | tf_op jit(solution)/shard_map/ppermute | solution.py:48
  134.9 2.9 %collective-permute-done.30.refs_4_ = bf16[320,1152]{1,0:T(8,128)(2,1)S(1)} collective-permute-done((bf16[320,1152]{1,0:T(8,128)(2,1)S(1)}, bf16[320,1152]{1,0:T(8,128)(2,1)S(1)}, u32[]{:S(2)}, u32[]{:S(2)}) %collective-permute-start.30) | collective-permute-done | bytes 737312 | tf_op jit(solution)/shard_map/ppermute | solution.py:57
  137.7 1.0 shard_map.61
  138.8 0.5 collective-permute-start.31
  139.3 1.3 collective-permute-done.31
  140.6 0.9 broadcast_select_fusion
  (58 shorter events, 0.1 us)
Async XLA Ops:
  0.6 4.0 %copy-start.1 = (bf16[160,1152]{1,0:T(8,128)(2,1)S(1)}, bf16[160,1152]{1,0:T(8,128)(2,1)}, u32[]{:S(2)}) copy-start(bf16[160,1152]{1,0:T(8,128)(2,1)} %text_ref.1) | copy-start | bytes 1105924
  0.6 3.9 %copy-start = (bf16[160,1152]{1,0:T(8,128)(2,1)S(1)}, bf16[160,1152]{1,0:T(8,128)(2,1)}, u32[]{:S(2)}) copy-start(bf16[160,1152]{1,0:T(8,128)(2,1)} %image_ref.1) | copy-start | bytes 1105924
  1.8 2.8 %collective-permute-start = (bf16[160,1152]{1,0:T(8,128)(2,1)S(1)}, bf16[160,1152]{1,0:T(8,128)(2,1)S(1)}, u32[]{:S(2)}, u32[]{:S(2)}) collective-permute-start(bf16[160,1152]{1,0:T(8,128)(2,1)S(1)} %broadcast_select_fusion.2), channel_id=1, source_target_pairs={{0,1},{1,0},{2,3},{3,2},{4,5},{5,4},{6,7},{7,6},{8,9},{9,8},{10,11... | collective-permute-start | bytes 1105928 | tf_op jit(solution)/shard_map/ppermute | solution.py:61
  5.0 45.3 %copy-start.2 = (bf16[320,1152]{1,0:T(8,128)(2,1)}, bf16[320,1152]{1,0:T(8,128)(2,1)S(1)}, u32[]{:S(2)}) copy-start(bf16[320,1152]{1,0:T(8,128)(2,1)S(1)} %get-tuple-element.23.refs_0_) | copy-start | bytes 2211844
  5.0 18.6 %collective-permute-start.4 = (bf16[320,1152]{1,0:T(8,128)(2,1)S(1)}, bf16[320,1152]{1,0:T(8,128)(2,1)S(1)}, u32[]{:S(2)}, u32[]{:S(2)}) collective-permute-start(bf16[320,1152]{1,0:T(8,128)(2,1)S(1)} %get-tuple-element.23.refs_0_), channel_id=1, source_target_pairs={{0,2},{1,65},{2,0},{3,67},{4,6},{5,69},{6,4},{7,71},{8,10},{9,73},... | collective-permute-start | bytes 2211848 | tf_op jit(solution)/shard_map/ppermute | solution.py:57
  8.1 15.6 %collective-permute-start.8 = (bf16[320,1152]{1,0:T(8,128)(2,1)S(1)}, bf16[320,1152]{1,0:T(8,128)(2,1)S(1)}, u32[]{:S(2)}, u32[]{:S(2)}) collective-permute-start(bf16[320,1152]{1,0:T(8,128)(2,1)S(1)} %get-tuple-element.23.refs_0_), channel_id=1, source_target_pairs={{0,1},{1,0},{2,3},{3,2},{4,5},{5,4},{6,7},{7,6},{8,9},{9,8},{10,11... | collective-permute-start | bytes 2211848 | tf_op jit(solution)/shard_map/ppermute | solution.py:61
  8.1 19.4 %collective-permute-start.3 = (bf16[320,1152]{1,0:T(8,128)(2,1)S(1)}, bf16[320,1152]{1,0:T(8,128)(2,1)S(1)}, u32[]{:S(2)}, u32[]{:S(2)}) collective-permute-start(bf16[320,1152]{1,0:T(8,128)(2,1)S(1)} %get-tuple-element.23.refs_0_), channel_id=1, source_target_pairs={{0,8},{1,33},{2,10},{3,35},{4,12},{5,37},{6,14},{7,39},{8,0},{9,41... | collective-permute-start | bytes 2211848 | tf_op jit(solution)/shard_map/ppermute | solution.py:48
  11.7 17.8 %collective-permute-start.2 = (bf16[320,1152]{1,0:T(8,128)(2,1)S(1)}, bf16[320,1152]{1,0:T(8,128)(2,1)S(1)}, u32[]{:S(2)}, u32[]{:S(2)}) collective-permute-start(bf16[320,1152]{1,0:T(8,128)(2,1)S(1)} %get-tuple-element.23.refs_0_), channel_id=1, source_target_pairs={{0,12},{1,49},{2,14},{3,51},{4,0},{5,53},{6,2},{7,55},{8,4},{9,57}... | collective-permute-start | bytes 2211848 | tf_op jit(solution)/shard_map/ppermute | solution.py:48
  12.1 17.6 %collective-permute-start.1 = (bf16[320,1152]{1,0:T(8,128)(2,1)S(1)}, bf16[320,1152]{1,0:T(8,128)(2,1)S(1)}, u32[]{:S(2)}, u32[]{:S(2)}) collective-permute-start(bf16[320,1152]{1,0:T(8,128)(2,1)S(1)} %get-tuple-element.23.refs_0_), channel_id=1, source_target_pairs={{0,4},{1,17},{2,6},{3,19},{4,8},{5,21},{6,10},{7,23},{8,12},{9,25}... | collective-permute-start | bytes 2211848 | tf_op jit(solution)/shard_map/ppermute | solution.py:48
  23.6 26.6 %copy-start.7 = (bf16[320,1152]{1,0:T(8,128)(2,1)}, bf16[320,1152]{1,0:T(8,128)(2,1)S(1)}, u32[]{:S(2)}) copy-start(bf16[320,1152]{1,0:T(8,128)(2,1)S(1)} %collective-permute-done.4.refs_4_) | copy-start | bytes 2211844
  23.6 7.4 %collective-permute-start.12 = (bf16[320,1152]{1,0:T(8,128)(2,1)S(1)}, bf16[320,1152]{1,0:T(8,128)(2,1)S(1)}, u32[]{:S(2)}, u32[]{:S(2)}) collective-permute-start(bf16[320,1152]{1,0:T(8,128)(2,1)S(1)} %collective-permute-done.4.refs_4_), channel_id=1, source_target_pairs={{0,1},{1,0},{2,3},{3,2},{4,5},{5,4},{6,7},{7,6},{8,9},{9,8},{10,11... | collective-permute-start | bytes 2211848 | tf_op jit(solution)/shard_map/ppermute | solution.py:61
  23.7 26.5 %copy-start.8 = (bf16[320,1152]{1,0:T(8,128)(2,1)}, bf16[320,1152]{1,0:T(8,128)(2,1)S(1)}, u32[]{:S(2)}) copy-start(bf16[320,1152]{1,0:T(8,128)(2,1)S(1)} %collective-permute-done.8.refs_8_) | copy-start | bytes 2211844
  23.7 13.0 %collective-permute-start.7 = (bf16[320,1152]{1,0:T(8,128)(2,1)S(1)}, bf16[320,1152]{1,0:T(8,128)(2,1)S(1)}, u32[]{:S(2)}, u32[]{:S(2)}) collective-permute-start(bf16[320,1152]{1,0:T(8,128)(2,1)S(1)} %collective-permute-done.4.refs_4_), channel_id=1, source_target_pairs={{0,8},{1,33},{2,10},{3,35},{4,12},{5,37},{6,14},{7,39},{8,0},{9,41... | collective-permute-start | bytes 2211848 | tf_op jit(solution)/shard_map/ppermute | solution.py:48
  27.5 22.8 %copy-start.9 = (bf16[320,1152]{1,0:T(8,128)(2,1)}, bf16[320,1152]{1,0:T(8,128)(2,1)S(1)}, u32[]{:S(2)}) copy-start(bf16[320,1152]{1,0:T(8,128)(2,1)S(1)} %collective-permute-done.3.refs_3_) | copy-start | bytes 2211844
  27.5 17.6 %collective-permute-start.6 = (bf16[320,1152]{1,0:T(8,128)(2,1)S(1)}, bf16[320,1152]{1,0:T(8,128)(2,1)S(1)}, u32[]{:S(2)}, u32[]{:S(2)}) collective-permute-start(bf16[320,1152]{1,0:T(8,128)(2,1)S(1)} %collective-permute-done.4.refs_4_), channel_id=1, source_target_pairs={{0,12},{1,49},{2,14},{3,51},{4,0},{5,53},{6,2},{7,55},{8,4},{9,57}... | collective-permute-start | bytes 2211848 | tf_op jit(solution)/shard_map/ppermute | solution.py:48
  29.5 20.8 %copy-start.10 = (bf16[320,1152]{1,0:T(8,128)(2,1)}, bf16[320,1152]{1,0:T(8,128)(2,1)S(1)}, u32[]{:S(2)}) copy-start(bf16[320,1152]{1,0:T(8,128)(2,1)S(1)} %collective-permute-done.2.refs_2_) | copy-start | bytes 2211844
  29.5 15.9 %collective-permute-start.5 = (bf16[320,1152]{1,0:T(8,128)(2,1)S(1)}, bf16[320,1152]{1,0:T(8,128)(2,1)S(1)}, u32[]{:S(2)}, u32[]{:S(2)}) collective-permute-start(bf16[320,1152]{1,0:T(8,128)(2,1)S(1)} %collective-permute-done.4.refs_4_), channel_id=1, source_target_pairs={{0,4},{1,17},{2,6},{3,19},{4,8},{5,21},{6,10},{7,23},{8,12},{9,25}... | collective-permute-start | bytes 2211848 | tf_op jit(solution)/shard_map/ppermute | solution.py:48
  29.7 20.5 %copy-start.11 = (bf16[320,1152]{1,0:T(8,128)(2,1)}, bf16[320,1152]{1,0:T(8,128)(2,1)S(1)}, u32[]{:S(2)}) copy-start(bf16[320,1152]{1,0:T(8,128)(2,1)S(1)} %collective-permute-done.1.refs_1_) | copy-start | bytes 2211844
  29.7 15.8 %collective-permute-start.11 = (bf16[320,1152]{1,0:T(8,128)(2,1)S(1)}, bf16[320,1152]{1,0:T(8,128)(2,1)S(1)}, u32[]{:S(2)}, u32[]{:S(2)}) collective-permute-start(bf16[320,1152]{1,0:T(8,128)(2,1)S(1)} %collective-permute-done.3.refs_3_), channel_id=1, source_target_pairs={{0,1},{1,0},{2,3},{3,2},{4,5},{5,4},{6,7},{7,6},{8,9},{9,8},{10,11... | collective-permute-start | bytes 2211848 | tf_op jit(solution)/shard_map/ppermute | solution.py:61
  30.9 19.3 %copy-start.12 = (bf16[320,1152]{1,0:T(8,128)(2,1)}, bf16[320,1152]{1,0:T(8,128)(2,1)S(1)}, u32[]{:S(2)}) copy-start(bf16[320,1152]{1,0:T(8,128)(2,1)S(1)} %collective-permute-done.12.refs_12_) | copy-start | bytes 2211844
  30.9 16.4 %collective-permute-start.10 = (bf16[320,1152]{1,0:T(8,128)(2,1)S(1)}, bf16[320,1152]{1,0:T(8,128)(2,1)S(1)}, u32[]{:S(2)}, u32[]{:S(2)}) collective-permute-start(bf16[320,1152]{1,0:T(8,128)(2,1)S(1)} %collective-permute-done.2.refs_2_), channel_id=1, source_target_pairs={{0,1},{1,0},{2,3},{3,2},{4,5},{5,4},{6,7},{7,6},{8,9},{9,8},{10,11... | collective-permute-start | bytes 2211848 | tf_op jit(solution)/shard_map/ppermute | solution.py:61
  36.7 13.6 %copy-start.13 = (bf16[320,1152]{1,0:T(8,128)(2,1)}, bf16[320,1152]{1,0:T(8,128)(2,1)S(1)}, u32[]{:S(2)}) copy-start(bf16[320,1152]{1,0:T(8,128)(2,1)S(1)} %collective-permute-done.7.refs_7_) | copy-start | bytes 2211844
  36.7 10.7 %collective-permute-start.9 = (bf16[320,1152]{1,0:T(8,128)(2,1)S(1)}, bf16[320,1152]{1,0:T(8,128)(2,1)S(1)}, u32[]{:S(2)}, u32[]{:S(2)}) collective-permute-start(bf16[320,1152]{1,0:T(8,128)(2,1)S(1)} %collective-permute-done.1.refs_1_), channel_id=1, source_target_pairs={{0,1},{1,0},{2,3},{3,2},{4,5},{5,4},{6,7},{7,6},{8,9},{9,8},{10,11... | collective-permute-start | bytes 2211848 | tf_op jit(solution)/shard_map/ppermute | solution.py:61
  45.0 5.3 %copy-start.14 = (bf16[320,1152]{1,0:T(8,128)(2,1)}, bf16[320,1152]{1,0:T(8,128)(2,1)S(1)}, u32[]{:S(2)}) copy-start(bf16[320,1152]{1,0:T(8,128)(2,1)S(1)} %collective-permute-done.6.refs_6_) | copy-start | bytes 2211844
  45.0 2.3 %collective-permute-start.15 = (bf16[320,1152]{1,0:T(8,128)(2,1)S(1)}, bf16[320,1152]{1,0:T(8,128)(2,1)S(1)}, u32[]{:S(2)}, u32[]{:S(2)}) collective-permute-start(bf16[320,1152]{1,0:T(8,128)(2,1)S(1)} %collective-permute-done.7.refs_7_), channel_id=1, source_target_pairs={{0,1},{1,0},{2,3},{3,2},{4,5},{5,4},{6,7},{7,6},{8,9},{9,8},{10,11... | collective-permute-start | bytes 2211848 | tf_op jit(solution)/shard_map/ppermute | solution.py:61
  45.4 4.9 %copy-start.15 = (bf16[320,1152]{1,0:T(8,128)(2,1)}, bf16[320,1152]{1,0:T(8,128)(2,1)S(1)}, u32[]{:S(2)}) copy-start(bf16[320,1152]{1,0:T(8,128)(2,1)S(1)} %collective-permute-done.5.refs_5_) | copy-start | bytes 2211844
  45.4 3.9 %collective-permute-start.14 = (bf16[320,1152]{1,0:T(8,128)(2,1)S(1)}, bf16[320,1152]{1,0:T(8,128)(2,1)S(1)}, u32[]{:S(2)}, u32[]{:S(2)}) collective-permute-start(bf16[320,1152]{1,0:T(8,128)(2,1)S(1)} %collective-permute-done.6.refs_6_), channel_id=1, source_target_pairs={{0,1},{1,0},{2,3},{3,2},{4,5},{5,4},{6,7},{7,6},{8,9},{9,8},{10,11... | collective-permute-start | bytes 2211848 | tf_op jit(solution)/shard_map/ppermute | solution.py:61
  45.6 4.8 %copy-start.16 = (bf16[320,1152]{1,0:T(8,128)(2,1)}, bf16[320,1152]{1,0:T(8,128)(2,1)S(1)}, u32[]{:S(2)}) copy-start(bf16[320,1152]{1,0:T(8,128)(2,1)S(1)} %collective-permute-done.11.refs_11_) | copy-start | bytes 2211844
  45.6 4.7 %collective-permute-start.13 = (bf16[320,1152]{1,0:T(8,128)(2,1)S(1)}, bf16[320,1152]{1,0:T(8,128)(2,1)}, u32[]{:S(2)}, u32[]{:S(2)}) collective-permute-start(bf16[320,1152]{1,0:T(8,128)(2,1)S(1)} %collective-permute-done.5.refs_5_), channel_id=1, source_target_pairs={{0,1},{1,0},{2,3},{3,2},{4,5},{5,4},{6,7},{7,6},{8,9},{9,8},{10,11... | collective-permute-start | bytes 2211848 | tf_op jit(solution)/shard_map/ppermute | solution.py:61
  47.3 3.0 %copy-start.17 = (bf16[320,1152]{1,0:T(8,128)(2,1)}, bf16[320,1152]{1,0:T(8,128)(2,1)S(1)}, u32[]{:S(2)}) copy-start(bf16[320,1152]{1,0:T(8,128)(2,1)S(1)} %collective-permute-done.10.refs_10_) | copy-start | bytes 2211844
  47.4 3.0 %copy-start.19 = (bf16[320,1152]{1,0:T(8,128)(2,1)}, bf16[320,1152]{1,0:T(8,128)(2,1)S(1)}, u32[]{:S(2)}) copy-start(bf16[320,1152]{1,0:T(8,128)(2,1)S(1)} %collective-permute-done.9.refs_9_) | copy-start | bytes 2211844
  47.4 2.0 %copy-start.20 = (bf16[320,1152]{1,0:T(8,128)(2,1)}, bf16[320,1152]{1,0:T(8,128)(2,1)S(1)}, u32[]{:S(2)}) copy-start(bf16[320,1152]{1,0:T(8,128)(2,1)S(1)} %collective-permute-done.15.refs_15_) | copy-start | bytes 2211844
  49.4 0.9 copy-start.21
  84.1 2.7 %collective-permute-start.17 = (bf16[320,1152]{1,0:T(8,128)(2,1)}, bf16[320,1152]{1,0:T(8,128)(2,1)S(1)}, u32[]{:S(2)}, u32[]{:S(2)}) collective-permute-start(bf16[320,1152]{1,0:T(8,128)(2,1)} %get-tuple-element.27), channel_id=1, source_target_pairs={{0,1},{1,0},{2,3},{3,2},{4,5},{5,4},{6,7},{7,6},{8,9},{9,8},{10,11... | collective-permute-start | bytes 2211848 | tf_op jit(solution)/shard_map/ppermute | solution.py:61
  84.8 3.1 %collective-permute-start.24 = (bf16[320,1152]{1,0:T(8,128)(2,1)}, bf16[320,1152]{1,0:T(8,128)(2,1)S(1)}, u32[]{:S(2)}, u32[]{:S(2)}) collective-permute-start(bf16[320,1152]{1,0:T(8,128)(2,1)} %get-tuple-element.35), channel_id=1, source_target_pairs={{0,1},{1,0},{2,3},{3,2},{4,5},{5,4},{6,7},{7,6},{8,9},{9,8},{10,11... | collective-permute-start | bytes 2211848 | tf_op jit(solution)/shard_map/ppermute | solution.py:61
  84.9 13.3 %collective-permute-start.19 = (bf16[320,1152]{1,0:T(8,128)(2,1)}, bf16[320,1152]{1,0:T(8,128)(2,1)S(1)}, u32[]{:S(2)}, u32[]{:S(2)}) collective-permute-start(bf16[320,1152]{1,0:T(8,128)(2,1)} %get-tuple-element.29), channel_id=1, source_target_pairs={{0,1},{1,0},{2,3},{3,2},{4,5},{5,4},{6,7},{7,6},{8,9},{9,8},{10,11... | collective-permute-start | bytes 2211848 | tf_op jit(solution)/shard_map/ppermute | solution.py:61
  85.3 13.7 %collective-permute-start.21 = (bf16[320,1152]{1,0:T(8,128)(2,1)}, bf16[320,1152]{1,0:T(8,128)(2,1)S(1)}, u32[]{:S(2)}, u32[]{:S(2)}) collective-permute-start(bf16[320,1152]{1,0:T(8,128)(2,1)} %get-tuple-element.31), channel_id=1, source_target_pairs={{0,1},{1,0},{2,3},{3,2},{4,5},{5,4},{6,7},{7,6},{8,9},{9,8},{10,11... | collective-permute-start | bytes 2211848 | tf_op jit(solution)/shard_map/ppermute | solution.py:61
  85.4 14.7 %collective-permute-start.23 = (bf16[320,1152]{1,0:T(8,128)(2,1)}, bf16[320,1152]{1,0:T(8,128)(2,1)S(1)}, u32[]{:S(2)}, u32[]{:S(2)}) collective-permute-start(bf16[320,1152]{1,0:T(8,128)(2,1)} %get-tuple-element.33), channel_id=1, source_target_pairs={{0,1},{1,0},{2,3},{3,2},{4,5},{5,4},{6,7},{7,6},{8,9},{9,8},{10,11... | collective-permute-start | bytes 2211848 | tf_op jit(solution)/shard_map/ppermute | solution.py:61
  86.8 6.3 %collective-permute-start.26 = (bf16[320,1152]{1,0:T(8,128)(2,1)}, bf16[320,1152]{1,0:T(8,128)(2,1)S(1)}, u32[]{:S(2)}, u32[]{:S(2)}) collective-permute-start(bf16[320,1152]{1,0:T(8,128)(2,1)} %get-tuple-element.37), channel_id=1, source_target_pairs={{0,1},{1,0},{2,3},{3,2},{4,5},{5,4},{6,7},{7,6},{8,9},{9,8},{10,11... | collective-permute-start | bytes 2211848 | tf_op jit(solution)/shard_map/ppermute | solution.py:61
  87.2 1.1 copy-start.18
  87.2 1.3 copy-start.5
  88.3 8.8 %collective-permute-start.28 = (bf16[320,1152]{1,0:T(8,128)(2,1)S(1)}, bf16[320,1152]{1,0:T(8,128)(2,1)S(1)}, u32[]{:S(2)}, u32[]{:S(2)}) collective-permute-start(bf16[320,1152]{1,0:T(8,128)(2,1)S(1)} %copy-done.18), channel_id=1, source_target_pairs={{0,1},{1,0},{2,3},{3,2},{4,5},{5,4},{6,7},{7,6},{8,9},{9,8},{10,11... | collective-permute-start | bytes 2211848 | tf_op jit(solution)/shard_map/ppermute | solution.py:61
  88.6 8.4 %copy-start.4 = (bf16[320,1152]{1,0:T(8,128)(2,1)S(1)}, bf16[320,1152]{1,0:T(8,128)(2,1)}, u32[]{:S(2)}) copy-start(bf16[320,1152]{1,0:T(8,128)(2,1)} %get-tuple-element.36) | copy-start | bytes 2211844
  93.2 20.1 %collective-permute-start.25 = (bf16[320,1152]{1,0:T(8,128)(2,1)S(1)}, bf16[320,1152]{1,0:T(8,128)(2,1)S(1)}, u32[]{:S(2)}, u32[]{:S(2)}) collective-permute-start(bf16[320,1152]{1,0:T(8,128)(2,1)S(1)} %add_convert_fusion.3), channel_id=1, source_target_pairs={{0,12},{1,49},{2,14},{3,51},{4,0},{5,53},{6,2},{7,55},{8,4},{9,57}... | collective-permute-start | bytes 2211848 | tf_op jit(solution)/shard_map/ppermute | solution.py:48
  96.9 1.1 copy-start.3
  97.1 19.5 %collective-permute-start.27 = (bf16[320,1152]{1,0:T(8,128)(2,1)S(1)}, bf16[320,1152]{1,0:T(8,128)(2,1)S(1)}, u32[]{:S(2)}, u32[]{:S(2)}) collective-permute-start(bf16[320,1152]{1,0:T(8,128)(2,1)S(1)} %add_convert_fusion.2), channel_id=1, source_target_pairs={{0,4},{1,17},{2,6},{3,19},{4,8},{5,21},{6,10},{7,23},{8,12},{9,25}... | collective-permute-start | bytes 2211848 | tf_op jit(solution)/shard_map/ppermute | solution.py:48
  98.2 19.6 %collective-permute-start.29 = (bf16[320,1152]{1,0:T(8,128)(2,1)S(1)}, bf16[320,1152]{1,0:T(8,128)(2,1)S(1)}, u32[]{:S(2)}, u32[]{:S(2)}) collective-permute-start(bf16[320,1152]{1,0:T(8,128)(2,1)S(1)} %add_convert_fusion.1), channel_id=1, source_target_pairs={{0,8},{1,33},{2,10},{3,35},{4,12},{5,37},{6,14},{7,39},{8,0},{9,41... | collective-permute-start | bytes 2211848 | tf_op jit(solution)/shard_map/ppermute | solution.py:48
  98.8 1.1 copy-start.6
  99.9 21.9 %collective-permute-start.16 = (bf16[320,1152]{1,0:T(8,128)(2,1)S(1)}, bf16[320,1152]{1,0:T(8,128)(2,1)S(1)}, u32[]{:S(2)}, u32[]{:S(2)}) collective-permute-start(bf16[320,1152]{1,0:T(8,128)(2,1)S(1)} %copy-done.6), channel_id=1, source_target_pairs={{0,1},{1,0},{2,3},{3,2},{4,5},{5,4},{6,7},{7,6},{8,9},{9,8},{10,11... | collective-permute-start | bytes 2211848 | tf_op jit(solution)/shard_map/ppermute | solution.py:61
  100.2 28.8 %collective-permute-start.18 = (bf16[320,1152]{1,0:T(8,128)(2,1)S(1)}, bf16[320,1152]{1,0:T(8,128)(2,1)S(1)}, u32[]{:S(2)}, u32[]{:S(2)}) collective-permute-start(bf16[320,1152]{1,0:T(8,128)(2,1)S(1)} %add_convert_fusion.7), channel_id=1, source_target_pairs={{0,12},{1,49},{2,14},{3,51},{4,0},{5,53},{6,2},{7,55},{8,4},{9,57}... | collective-permute-start | bytes 2211848 | tf_op jit(solution)/shard_map/ppermute | solution.py:48
  113.2 15.8 %collective-permute-start.20 = (bf16[320,1152]{1,0:T(8,128)(2,1)S(1)}, bf16[320,1152]{1,0:T(8,128)(2,1)S(1)}, u32[]{:S(2)}, u32[]{:S(2)}) collective-permute-start(bf16[320,1152]{1,0:T(8,128)(2,1)S(1)} %add_convert_fusion.6), channel_id=1, source_target_pairs={{0,4},{1,17},{2,6},{3,19},{4,8},{5,21},{6,10},{7,23},{8,12},{9,25}... | collective-permute-start | bytes 2211848 | tf_op jit(solution)/shard_map/ppermute | solution.py:48
  116.6 18.3 %collective-permute-start.22 = (bf16[320,1152]{1,0:T(8,128)(2,1)S(1)}, bf16[320,1152]{1,0:T(8,128)(2,1)S(1)}, u32[]{:S(2)}, u32[]{:S(2)}) collective-permute-start(bf16[320,1152]{1,0:T(8,128)(2,1)S(1)} %add_convert_fusion.5), channel_id=1, source_target_pairs={{0,8},{1,33},{2,10},{3,35},{4,12},{5,37},{6,14},{7,39},{8,0},{9,41... | collective-permute-start | bytes 2211848 | tf_op jit(solution)/shard_map/ppermute | solution.py:48
  118.3 19.4 %collective-permute-start.30 = (bf16[320,1152]{1,0:T(8,128)(2,1)S(1)}, bf16[320,1152]{1,0:T(8,128)(2,1)S(1)}, u32[]{:S(2)}, u32[]{:S(2)}) collective-permute-start(bf16[320,1152]{1,0:T(8,128)(2,1)S(1)} %add_convert_fusion), channel_id=1, source_target_pairs={{0,2},{1,65},{2,0},{3,67},{4,6},{5,69},{6,4},{7,71},{8,10},{9,73},... | collective-permute-start | bytes 2211848 | tf_op jit(solution)/shard_map/ppermute | solution.py:57
  138.8 1.8 %collective-permute-start.31 = (bf16[160,1152]{1,0:T(8,128)(2,1)S(1)}, bf16[160,1152]{1,0:T(8,128)(2,1)S(1)}, u32[]{:S(2)}, u32[]{:S(2)}) collective-permute-start(bf16[160,1152]{1,0:T(8,128)(2,1)S(1)} %get-tuple-element.41), channel_id=1, source_target_pairs={{0,1},{1,0},{2,3},{3,2},{4,5},{5,4},{6,7},{7,6},{8,9},{9,8},{10,11... | collective-permute-start | bytes 1105928 | tf_op jit(solution)/shard_map/ppermute | solution.py:61

commit v2 on v1

--- a/solution.py
+++ b/solution.py
@@ -52,7 +52,7 @@
     def move(yh, z, x, yl, core):
         if core == 0:
             return (yh, z, x, 1 - yl, core)
-        return (1 - yh, z, x, yl, core)
+        return (1 - yh, z, x, 1 - yl, core)
 
     return lax.ppermute(value, axes, pairs_of(move))
 
@@ -259,15 +259,21 @@
     )
     near = [unit, ring(unit, 1), ring(unit, -1), ring(unit, 2)]
     across = pair(unit)
-    far = [across, ring(across, 1), ring(across, -1), ring(across, 2)]
+    far = [across, ring(across, 1), ring(across, -1), pair(near[3])]
     mine = near + far
     other = [swap(value) for value in mine]
     mine_sums, other_sums = pair_sums(factors, cores, mine, other)
     sums = [add(one, swap(two)) for one, two in zip(mine_sums, other_sums)]
     near_sums, far_sums = sums[:4], sums[4:]
-    back = (0, -1, 1, 2)
-    far_total = add(far_sums[0], *[ring(far_sums[k], back[k]) for k in (1, 2, 3)])
-    parts = [near_sums[0]] + [ring(near_sums[k], back[k]) for k in (1, 2, 3)] + [pair(far_total)]
+    far_total = add(far_sums[0], ring(far_sums[1], -1), ring(far_sums[2], 1))
+    distant = add(near_sums[3], pair(far_sums[3]))
+    parts = [
+        near_sums[0],
+        ring(near_sums[1], -1),
+        ring(near_sums[2], 1),
+        ring(distant, 2),
+        pair(far_total),
+    ]
     keep, give = small_call(
         final_kernel, [(rows, width)] * 2, (logit_scale, cores), (raw, *parts)
     )

time: 142 us -> 127 us (0.89)
  waiting for transfers between devices: 64.7 us -> 52.9 us
  starting transfers between devices: 32.4 us -> 29.1 us
    ppermute x12 -> x10, waiting for transfers between devices: 40.8 us -> 30.5 us  [ring(): return lax.ppermute(value, axes, ring_move(steps))]
    ppermute x18, starting transfers between devices: 7.43 us -> 4.88 us  [swap(): return lax.ppermute(value, 'core', [(0, 1), (1, 0)])]
    ppermute x12 -> x10, starting transfers between devices: 18.4 us -> 17.7 us  [ring(): return lax.ppermute(value, axes, ring_move(steps))]
    ppermute x2 -> x4, waiting for transfers between devices: 13.3 us -> 13.2 us  [pair(): return lax.ppermute(value, axes, pairs_of(move))]
    ppermute x2 -> x4, starting transfers between devices: 6.55 us -> 6.48 us  [pair(): return lax.ppermute(value, axes, pairs_of(move))]
  transfers between devices with their start and end apart: 32 -> 32, of which waited for: 15 -> 12; matrix products, arithmetic and copies ran while one was open for 1% -> 1% of each run, Pallas kernels for 0% -> 0%
where the time goes in v2:
time: 127 us; the launch traced here: 126 us
  waiting for transfers between devices  52.9 us (42%)
  Pallas kernels  35.2 us (28%)
  starting transfers between devices  29.1 us (23%)
  other arithmetic  3.86 us (3%)
  local copies, waits for them, and re-layouts  2.99 us (2%)
  between operations  2.29 us (2%)
    pallas_call x1, Pallas kernels, pair_sums(): pl.pallas_call(functools.partial(pair_kernel, chips), grid=(2,), in_specs...  33.8 us
    ppermute x10, waiting for transfers between devices, ring(): return lax.ppermute(value, axes, ring_move(steps))  30.5 us
    ppermute x10, starting transfers between devices, ring(): return lax.ppermute(value, axes, ring_move(steps))  17.7 us
    ppermute x4, waiting for transfers between devices, pair(): return lax.ppermute(value, axes, pairs_of(move))  13.2 us
    ppermute x18, waiting for transfers between devices, swap(): return lax.ppermute(value, 'core', [(0, 1), (1, 0)])  9.22 us
    ppermute x4, starting transfers between devices, pair(): return lax.ppermute(value, axes, pairs_of(move))  6.48 us
    ppermute x18, starting transfers between devices, swap(): return lax.ppermute(value, 'core', [(0, 1), (1, 0)])  4.88 us
    unnamed x44, local copies, waits for them, and re-layouts  2.99 us
  transfers between devices with their start and end apart: 32, of which 12 were waited for; matrix products, arithmetic and copies ran while one was open for 1% of the time, Pallas kernels for 0%

profile of v2, /device:TPU:1, one launch (start us, length us, event | category | flops | bytes accessed | tf_op | source)
XLA Modules:
  0.0 126.3 jit_solution(2173905916142825054)
XLA Ops:
  0.7 1.1 broadcast_select_fusion.2
  1.8 1.5 %collective-permute-start = (bf16[160,1152]{1,0:T(8,128)(2,1)S(1)}, bf16[160,1152]{1,0:T(8,128)(2,1)S(1)}, u32[]{:S(2)}, u32[]{:S(2)}) collective-permute-start(bf16[160,1152]{1,0:T(8,128)(2,1)S(1)} %broadcast_select_fusion.2), channel_id=1, source_target_pairs={{0,1},{1,0},{2,3},{3,2},{4,5},{5,4},{6,7},{7,6},{8,9},{9,8},{10,11... | collective-permute-start | bytes 1105928 | tf_op jit(solution)/shard_map/ppermute | solution.py:61
  3.3 1.3 %collective-permute-done.got_ref = bf16[160,1152]{1,0:T(8,128)(2,1)S(1)} collective-permute-done((bf16[160,1152]{1,0:T(8,128)(2,1)S(1)}, bf16[160,1152]{1,0:T(8,128)(2,1)S(1)}, u32[]{:S(2)}, u32[]{:S(2)}) %collective-permute-start) | collective-permute-done | bytes 368672 | tf_op jit(solution)/shard_map/ppermute | solution.py:61
  4.6 0.4 shard_map.59
  5.0 2.9 %collective-permute-start.4 = (bf16[320,1152]{1,0:T(8,128)(2,1)S(1)}, bf16[320,1152]{1,0:T(8,128)(2,1)S(1)}, u32[]{:S(2)}, u32[]{:S(2)}) collective-permute-start(bf16[320,1152]{1,0:T(8,128)(2,1)S(1)} %get-tuple-element.23.refs_0_), channel_id=1, source_target_pairs={{0,2},{1,67},{2,0},{3,65},{4,6},{5,71},{6,4},{7,69},{8,10},{9,75},... | collective-permute-start | bytes 2211848 | tf_op jit(solution)/shard_map/ppermute | solution.py:57
  7.9 3.6 %collective-permute-start.3 = (bf16[320,1152]{1,0:T(8,128)(2,1)S(1)}, bf16[320,1152]{1,0:T(8,128)(2,1)S(1)}, u32[]{:S(2)}, u32[]{:S(2)}) collective-permute-start(bf16[320,1152]{1,0:T(8,128)(2,1)S(1)} %get-tuple-element.23.refs_0_), channel_id=1, source_target_pairs={{0,8},{1,33},{2,10},{3,35},{4,12},{5,37},{6,14},{7,39},{8,0},{9,41... | collective-permute-start | bytes 2211848 | tf_op jit(solution)/shard_map/ppermute | solution.py:48
  11.5 0.4 collective-permute-start.2
  11.9 1.0 collective-permute-start.1
  12.9 4.1 %collective-permute-done.4.refs_4_ = bf16[320,1152]{1,0:T(8,128)(2,1)S(1)} collective-permute-done((bf16[320,1152]{1,0:T(8,128)(2,1)S(1)}, bf16[320,1152]{1,0:T(8,128)(2,1)S(1)}, u32[]{:S(2)}, u32[]{:S(2)}) %collective-permute-start.4) | collective-permute-done | bytes 737312 | tf_op jit(solution)/shard_map/ppermute | solution.py:57
  17.0 3.8 %collective-permute-start.6 = (bf16[320,1152]{1,0:T(8,128)(2,1)S(1)}, bf16[320,1152]{1,0:T(8,128)(2,1)S(1)}, u32[]{:S(2)}, u32[]{:S(2)}) collective-permute-start(bf16[320,1152]{1,0:T(8,128)(2,1)S(1)} %collective-permute-done.4.refs_4_), channel_id=1, source_target_pairs={{0,12},{1,49},{2,14},{3,51},{4,0},{5,53},{6,2},{7,55},{8,4},{9,57}... | collective-permute-start | bytes 2211848 | tf_op jit(solution)/shard_map/ppermute | solution.py:48
  20.9 0.0 collective-permute-done.3.refs_3_
  20.9 0.8 collective-permute-start.5
  21.7 7.6 %collective-permute-done.2.refs_2_ = bf16[320,1152]{1,0:T(8,128)(2,1)S(1)} collective-permute-done((bf16[320,1152]{1,0:T(8,128)(2,1)S(1)}, bf16[320,1152]{1,0:T(8,128)(2,1)S(1)}, u32[]{:S(2)}, u32[]{:S(2)}) %collective-permute-start.2) | collective-permute-done | bytes 737312 | tf_op jit(solution)/shard_map/ppermute | solution.py:48
  29.3 0.1 collective-permute-start.11
  29.4 1.1 collective-permute-start.7
  30.5 0.0 collective-permute-done.12.refs_12_
  30.5 0.0 collective-permute-start.10
  30.5 6.7 %collective-permute-done.6.refs_6_ = bf16[320,1152]{1,0:T(8,128)(2,1)S(1)} collective-permute-done((bf16[320,1152]{1,0:T(8,128)(2,1)S(1)}, bf16[320,1152]{1,0:T(8,128)(2,1)S(1)}, u32[]{:S(2)}, u32[]{:S(2)}) %collective-permute-start.6) | collective-permute-done | bytes 737312 | tf_op jit(solution)/shard_map/ppermute | solution.py:48
  37.2 0.1 collective-permute-start.9
  37.3 0.4 collective-permute-start.14
  37.7 0.0 collective-permute-done.11.refs_11_
  37.7 0.1 collective-permute-start.13
  37.8 3.1 %collective-permute-done.7.refs_7_ = bf16[320,1152]{1,0:T(8,128)(2,1)S(1)} collective-permute-done((bf16[320,1152]{1,0:T(8,128)(2,1)S(1)}, bf16[320,1152]{1,0:T(8,128)(2,1)S(1)}, u32[]{:S(2)}, u32[]{:S(2)}) %collective-permute-start.7) | collective-permute-done | bytes 737312 | tf_op jit(solution)/shard_map/ppermute | solution.py:57
  40.9 0.4 collective-permute-start.15
  42.6 0.1 pad_maximum_fusion.scale_ref
  42.7 0.0 collective-permute-done.10.refs_10_
  42.7 0.0 collective-permute-done.9.refs_9_
  42.8 0.9 copy-done.20
  43.6 0.9 copy-done.21
  44.6 33.8 %shard_map.60 = (bf16[320,1152]{1,0:T(8,128)(2,1)S(1)}, bf16[320,1152]{1,0:T(8,128)(2,1)S(1)}, bf16[320,1152]{1,0:T(8,128)(2,1)S(1)}, bf16[320,1152]{1,0:T(8,128...) custom-call(f32[2]{0:T(128)S(1)} %pad_maximum_fusion.scale_ref, ...), custom_call_target="tpu_custom_call" | custom-call | flops 22649241600 | bytes 23592960 | tf_op jit(solution)/shard_map/pallas_call | solution.py:185
  78.4 0.5 collective-permute-start.17
  78.9 0.3 collective-permute-start.22
  79.2 0.2 collective-permute-start.19
  79.4 0.3 collective-permute-start.21
  79.7 0.2 collective-permute-start.25
  79.9 1.2 collective-permute-done.17
  81.1 0.2 collective-permute-start.26
  81.3 0.2 add_convert_fusion.8
  81.5 0.7 collective-permute-done.22
  82.2 0.3 copy-done.18
  82.4 0.3 collective-permute-start.28
  82.8 0.2 add_convert_fusion.5
  82.9 4.5 %collective-permute-done.26 = bf16[320,1152]{1,0:T(8,128)(2,1)S(1)} collective-permute-done((bf16[320,1152]{1,0:T(8,128)(2,1)}, bf16[320,1152]{1,0:T(8,128)(2,1)S(1)}, u32[]{:S(2)}, u32[]{:S(2)}) %collective-permute-start.26) | collective-permute-done | bytes 737312 | tf_op jit(solution)/shard_map/ppermute | solution.py:61
  87.5 1.1 collective-permute-start.23
  88.6 0.2 add_convert_fusion.2
  88.8 3.1 %collective-permute-start.27 = (bf16[320,1152]{1,0:T(8,128)(2,1)S(1)}, bf16[320,1152]{1,0:T(8,128)(2,1)S(1)}, u32[]{:S(2)}, u32[]{:S(2)}) collective-permute-start(bf16[320,1152]{1,0:T(8,128)(2,1)S(1)} %add_convert_fusion.2), channel_id=1, source_target_pairs={{0,12},{1,49},{2,14},{3,51},{4,0},{5,53},{6,2},{7,55},{8,4},{9,57}... | collective-permute-start | bytes 2211848 | tf_op jit(solution)/shard_map/ppermute | solution.py:48
  91.9 0.2 add_convert_fusion.1
  92.1 0.1 collective-permute-start.29
  92.2 0.2 add_convert_fusion.7
  92.4 0.9 copy-done.6
  93.3 6.0 %collective-permute-done.23 = bf16[320,1152]{1,0:T(8,128)(2,1)S(1)} collective-permute-done((bf16[320,1152]{1,0:T(8,128)(2,1)S(1)}, bf16[320,1152]{1,0:T(8,128)(2,1)S(1)}, u32[]{:S(2)}, u32[]{:S(2)}) %collective-permute-start.23) | collective-permute-done | bytes 737312 | tf_op jit(solution)/shard_map/ppermute | solution.py:57
  99.3 3.5 %collective-permute-start.18 = (bf16[320,1152]{1,0:T(8,128)(2,1)S(1)}, bf16[320,1152]{1,0:T(8,128)(2,1)S(1)}, u32[]{:S(2)}, u32[]{:S(2)}) collective-permute-start(bf16[320,1152]{1,0:T(8,128)(2,1)S(1)} %add_convert_fusion.8), channel_id=1, source_target_pairs={{0,12},{1,49},{2,14},{3,51},{4,0},{5,53},{6,2},{7,55},{8,4},{9,57}... | collective-permute-start | bytes 2211848 | tf_op jit(solution)/shard_map/ppermute | solution.py:48
  102.8 0.3 add_convert_fusion.4
  103.1 0.1 collective-permute-start.20
  103.2 1.3 %collective-permute-start.24 = (bf16[320,1152]{1,0:T(8,128)(2,1)S(1)}, bf16[320,1152]{1,0:T(8,128)(2,1)S(1)}, u32[]{:S(2)}, u32[]{:S(2)}) collective-permute-start(bf16[320,1152]{1,0:T(8,128)(2,1)S(1)} %add_convert_fusion.4), channel_id=1, source_target_pairs={{0,8},{1,33},{2,10},{3,35},{4,12},{5,37},{6,14},{7,39},{8,0},{9,41... | collective-permute-start | bytes 2211848 | tf_op jit(solution)/shard_map/ppermute | solution.py:48
  104.5 0.4 add_convert_fusion
  104.9 1.3 %collective-permute-start.30 = (bf16[320,1152]{1,0:T(8,128)(2,1)S(1)}, bf16[320,1152]{1,0:T(8,128)(2,1)S(1)}, u32[]{:S(2)}, u32[]{:S(2)}) collective-permute-start(bf16[320,1152]{1,0:T(8,128)(2,1)S(1)} %add_convert_fusion), channel_id=1, source_target_pairs={{0,2},{1,67},{2,0},{3,65},{4,6},{5,71},{6,4},{7,69},{8,10},{9,75},... | collective-permute-start | bytes 2211848 | tf_op jit(solution)/shard_map/ppermute | solution.py:57
  106.2 0.2 add_convert_fusion.9.refs_0_
  106.4 12.7 %collective-permute-done.18.refs_1_ = bf16[320,1152]{1,0:T(8,128)(2,1)S(1)} collective-permute-done((bf16[320,1152]{1,0:T(8,128)(2,1)S(1)}, bf16[320,1152]{1,0:T(8,128)(2,1)S(1)}, u32[]{:S(2)}, u32[]{:S(2)}) %collective-permute-start.18) | collective-permute-done | bytes 737312 | tf_op jit(solution)/shard_map/ppermute | solution.py:48
  119.1 3.5 %collective-permute-done.20.refs_2_ = bf16[320,1152]{1,0:T(8,128)(2,1)S(1)} collective-permute-done((bf16[320,1152]{1,0:T(8,128)(2,1)S(1)}, bf16[320,1152]{1,0:T(8,128)(2,1)S(1)}, u32[]{:S(2)}, u32[]{:S(2)}) %collective-permute-start.20) | collective-permute-done | bytes 737312 | tf_op jit(solution)/shard_map/ppermute | solution.py:48
  122.6 1.0 shard_map.61
  123.6 0.3 collective-permute-start.31
  123.9 1.5 %collective-permute-done.31 = bf16[160,1152]{1,0:T(8,128)(2,1)S(1)} collective-permute-done((bf16[160,1152]{1,0:T(8,128)(2,1)S(1)}, bf16[160,1152]{1,0:T(8,128)(2,1)S(1)}, u32[]{:S(2)}, u32[]{:S(2)}) %collective-permute-start.31) | collective-permute-done | bytes 368672 | tf_op jit(solution)/shard_map/ppermute | solution.py:61
  125.4 0.9 broadcast_select_fusion
  (58 shorter events, 0.1 us)
Async XLA Ops:
  0.6 4.0 %copy-start.1 = (bf16[160,1152]{1,0:T(8,128)(2,1)S(1)}, bf16[160,1152]{1,0:T(8,128)(2,1)}, u32[]{:S(2)}) copy-start(bf16[160,1152]{1,0:T(8,128)(2,1)} %text_ref.1) | copy-start | bytes 1105924
  0.6 3.9 %copy-start = (bf16[160,1152]{1,0:T(8,128)(2,1)S(1)}, bf16[160,1152]{1,0:T(8,128)(2,1)}, u32[]{:S(2)}) copy-start(bf16[160,1152]{1,0:T(8,128)(2,1)} %image_ref.1) | copy-start | bytes 1105924
  1.8 2.8 %collective-permute-start = (bf16[160,1152]{1,0:T(8,128)(2,1)S(1)}, bf16[160,1152]{1,0:T(8,128)(2,1)S(1)}, u32[]{:S(2)}, u32[]{:S(2)}) collective-permute-start(bf16[160,1152]{1,0:T(8,128)(2,1)S(1)} %broadcast_select_fusion.2), channel_id=1, source_target_pairs={{0,1},{1,0},{2,3},{3,2},{4,5},{5,4},{6,7},{7,6},{8,9},{9,8},{10,11... | collective-permute-start | bytes 1105928 | tf_op jit(solution)/shard_map/ppermute | solution.py:61
  5.0 39.5 %copy-start.2 = (bf16[320,1152]{1,0:T(8,128)(2,1)}, bf16[320,1152]{1,0:T(8,128)(2,1)S(1)}, u32[]{:S(2)}) copy-start(bf16[320,1152]{1,0:T(8,128)(2,1)S(1)} %get-tuple-element.23.refs_0_) | copy-start | bytes 2211844
  5.0 12.0 %collective-permute-start.4 = (bf16[320,1152]{1,0:T(8,128)(2,1)S(1)}, bf16[320,1152]{1,0:T(8,128)(2,1)S(1)}, u32[]{:S(2)}, u32[]{:S(2)}) collective-permute-start(bf16[320,1152]{1,0:T(8,128)(2,1)S(1)} %get-tuple-element.23.refs_0_), channel_id=1, source_target_pairs={{0,2},{1,67},{2,0},{3,65},{4,6},{5,71},{6,4},{7,69},{8,10},{9,75},... | collective-permute-start | bytes 2211848 | tf_op jit(solution)/shard_map/ppermute | solution.py:57
  7.9 9.2 %collective-permute-start.8 = (bf16[320,1152]{1,0:T(8,128)(2,1)S(1)}, bf16[320,1152]{1,0:T(8,128)(2,1)S(1)}, u32[]{:S(2)}, u32[]{:S(2)}) collective-permute-start(bf16[320,1152]{1,0:T(8,128)(2,1)S(1)} %get-tuple-element.23.refs_0_), channel_id=1, source_target_pairs={{0,1},{1,0},{2,3},{3,2},{4,5},{5,4},{6,7},{7,6},{8,9},{9,8},{10,11... | collective-permute-start | bytes 2211848 | tf_op jit(solution)/shard_map/ppermute | solution.py:61
  7.9 13.0 %collective-permute-start.3 = (bf16[320,1152]{1,0:T(8,128)(2,1)S(1)}, bf16[320,1152]{1,0:T(8,128)(2,1)S(1)}, u32[]{:S(2)}, u32[]{:S(2)}) collective-permute-start(bf16[320,1152]{1,0:T(8,128)(2,1)S(1)} %get-tuple-element.23.refs_0_), channel_id=1, source_target_pairs={{0,8},{1,33},{2,10},{3,35},{4,12},{5,37},{6,14},{7,39},{8,0},{9,41... | collective-permute-start | bytes 2211848 | tf_op jit(solution)/shard_map/ppermute | solution.py:48
  11.5 17.8 %collective-permute-start.2 = (bf16[320,1152]{1,0:T(8,128)(2,1)S(1)}, bf16[320,1152]{1,0:T(8,128)(2,1)S(1)}, u32[]{:S(2)}, u32[]{:S(2)}) collective-permute-start(bf16[320,1152]{1,0:T(8,128)(2,1)S(1)} %get-tuple-element.23.refs_0_), channel_id=1, source_target_pairs={{0,12},{1,49},{2,14},{3,51},{4,0},{5,53},{6,2},{7,55},{8,4},{9,57}... | collective-permute-start | bytes 2211848 | tf_op jit(solution)/shard_map/ppermute | solution.py:48
  11.9 17.5 %collective-permute-start.1 = (bf16[320,1152]{1,0:T(8,128)(2,1)S(1)}, bf16[320,1152]{1,0:T(8,128)(2,1)S(1)}, u32[]{:S(2)}, u32[]{:S(2)}) collective-permute-start(bf16[320,1152]{1,0:T(8,128)(2,1)S(1)} %get-tuple-element.23.refs_0_), channel_id=1, source_target_pairs={{0,4},{1,17},{2,6},{3,19},{4,8},{5,21},{6,10},{7,23},{8,12},{9,25}... | collective-permute-start | bytes 2211848 | tf_op jit(solution)/shard_map/ppermute | solution.py:48
  17.0 27.5 %copy-start.7 = (bf16[320,1152]{1,0:T(8,128)(2,1)}, bf16[320,1152]{1,0:T(8,128)(2,1)S(1)}, u32[]{:S(2)}) copy-start(bf16[320,1152]{1,0:T(8,128)(2,1)S(1)} %collective-permute-done.4.refs_4_) | copy-start | bytes 2211844
  17.0 13.5 %collective-permute-start.12 = (bf16[320,1152]{1,0:T(8,128)(2,1)S(1)}, bf16[320,1152]{1,0:T(8,128)(2,1)S(1)}, u32[]{:S(2)}, u32[]{:S(2)}) collective-permute-start(bf16[320,1152]{1,0:T(8,128)(2,1)S(1)} %collective-permute-done.4.refs_4_), channel_id=1, source_target_pairs={{0,1},{1,0},{2,3},{3,2},{4,5},{5,4},{6,7},{7,6},{8,9},{9,8},{10,11... | collective-permute-start | bytes 2211848 | tf_op jit(solution)/shard_map/ppermute | solution.py:61
  17.0 27.5 %copy-start.8 = (bf16[320,1152]{1,0:T(8,128)(2,1)}, bf16[320,1152]{1,0:T(8,128)(2,1)S(1)}, u32[]{:S(2)}) copy-start(bf16[320,1152]{1,0:T(8,128)(2,1)S(1)} %collective-permute-done.8.refs_8_) | copy-start | bytes 2211844
  17.0 20.2 %collective-permute-start.6 = (bf16[320,1152]{1,0:T(8,128)(2,1)S(1)}, bf16[320,1152]{1,0:T(8,128)(2,1)S(1)}, u32[]{:S(2)}, u32[]{:S(2)}) collective-permute-start(bf16[320,1152]{1,0:T(8,128)(2,1)S(1)} %collective-permute-done.4.refs_4_), channel_id=1, source_target_pairs={{0,12},{1,49},{2,14},{3,51},{4,0},{5,53},{6,2},{7,55},{8,4},{9,57}... | collective-permute-start | bytes 2211848 | tf_op jit(solution)/shard_map/ppermute | solution.py:48
  20.9 23.7 %copy-start.9 = (bf16[320,1152]{1,0:T(8,128)(2,1)}, bf16[320,1152]{1,0:T(8,128)(2,1)S(1)}, u32[]{:S(2)}) copy-start(bf16[320,1152]{1,0:T(8,128)(2,1)S(1)} %collective-permute-done.3.refs_3_) | copy-start | bytes 2211844
  20.9 16.4 %collective-permute-start.5 = (bf16[320,1152]{1,0:T(8,128)(2,1)S(1)}, bf16[320,1152]{1,0:T(8,128)(2,1)S(1)}, u32[]{:S(2)}, u32[]{:S(2)}) collective-permute-start(bf16[320,1152]{1,0:T(8,128)(2,1)S(1)} %collective-permute-done.4.refs_4_), channel_id=1, source_target_pairs={{0,4},{1,17},{2,6},{3,19},{4,8},{5,21},{6,10},{7,23},{8,12},{9,25}... | collective-permute-start | bytes 2211848 | tf_op jit(solution)/shard_map/ppermute | solution.py:48
  29.3 15.2 %copy-start.10 = (bf16[320,1152]{1,0:T(8,128)(2,1)}, bf16[320,1152]{1,0:T(8,128)(2,1)S(1)}, u32[]{:S(2)}) copy-start(bf16[320,1152]{1,0:T(8,128)(2,1)S(1)} %collective-permute-done.2.refs_2_) | copy-start | bytes 2211844
  29.3 8.4 %collective-permute-start.11 = (bf16[320,1152]{1,0:T(8,128)(2,1)S(1)}, bf16[320,1152]{1,0:T(8,128)(2,1)S(1)}, u32[]{:S(2)}, u32[]{:S(2)}) collective-permute-start(bf16[320,1152]{1,0:T(8,128)(2,1)S(1)} %collective-permute-done.3.refs_3_), channel_id=1, source_target_pairs={{0,1},{1,0},{2,3},{3,2},{4,5},{5,4},{6,7},{7,6},{8,9},{9,8},{10,11... | collective-permute-start | bytes 2211848 | tf_op jit(solution)/shard_map/ppermute | solution.py:61
  29.4 15.2 %copy-start.11 = (bf16[320,1152]{1,0:T(8,128)(2,1)}, bf16[320,1152]{1,0:T(8,128)(2,1)S(1)}, u32[]{:S(2)}) copy-start(bf16[320,1152]{1,0:T(8,128)(2,1)S(1)} %collective-permute-done.1.refs_1_) | copy-start | bytes 2211844
  29.4 11.5 %collective-permute-start.7 = (bf16[320,1152]{1,0:T(8,128)(2,1)S(1)}, bf16[320,1152]{1,0:T(8,128)(2,1)S(1)}, u32[]{:S(2)}, u32[]{:S(2)}) collective-permute-start(bf16[320,1152]{1,0:T(8,128)(2,1)S(1)} %collective-permute-done.3.refs_3_), channel_id=1, source_target_pairs={{0,2},{1,67},{2,0},{3,65},{4,6},{5,71},{6,4},{7,69},{8,10},{9,75},... | collective-permute-start | bytes 2211848 | tf_op jit(solution)/shard_map/ppermute | solution.py:57
  30.5 14.0 %copy-start.12 = (bf16[320,1152]{1,0:T(8,128)(2,1)}, bf16[320,1152]{1,0:T(8,128)(2,1)S(1)}, u32[]{:S(2)}) copy-start(bf16[320,1152]{1,0:T(8,128)(2,1)S(1)} %collective-permute-done.12.refs_12_) | copy-start | bytes 2211844
  30.5 12.2 %collective-permute-start.10 = (bf16[320,1152]{1,0:T(8,128)(2,1)S(1)}, bf16[320,1152]{1,0:T(8,128)(2,1)S(1)}, u32[]{:S(2)}, u32[]{:S(2)}) collective-permute-start(bf16[320,1152]{1,0:T(8,128)(2,1)S(1)} %collective-permute-done.2.refs_2_), channel_id=1, source_target_pairs={{0,1},{1,0},{2,3},{3,2},{4,5},{5,4},{6,7},{7,6},{8,9},{9,8},{10,11... | collective-permute-start | bytes 2211848 | tf_op jit(solution)/shard_map/ppermute | solution.py:61
  37.2 7.4 %copy-start.13 = (bf16[320,1152]{1,0:T(8,128)(2,1)}, bf16[320,1152]{1,0:T(8,128)(2,1)S(1)}, u32[]{:S(2)}) copy-start(bf16[320,1152]{1,0:T(8,128)(2,1)S(1)} %collective-permute-done.6.refs_6_) | copy-start | bytes 2211844
  37.2 5.5 %collective-permute-start.9 = (bf16[320,1152]{1,0:T(8,128)(2,1)S(1)}, bf16[320,1152]{1,0:T(8,128)(2,1)S(1)}, u32[]{:S(2)}, u32[]{:S(2)}) collective-permute-start(bf16[320,1152]{1,0:T(8,128)(2,1)S(1)} %collective-permute-done.1.refs_1_), channel_id=1, source_target_pairs={{0,1},{1,0},{2,3},{3,2},{4,5},{5,4},{6,7},{7,6},{8,9},{9,8},{10,11... | collective-permute-start | bytes 2211848 | tf_op jit(solution)/shard_map/ppermute | solution.py:61
  37.3 7.3 %copy-start.14 = (bf16[320,1152]{1,0:T(8,128)(2,1)}, bf16[320,1152]{1,0:T(8,128)(2,1)S(1)}, u32[]{:S(2)}) copy-start(bf16[320,1152]{1,0:T(8,128)(2,1)S(1)} %collective-permute-done.5.refs_5_) | copy-start | bytes 2211844
  37.3 5.4 %collective-permute-start.14 = (bf16[320,1152]{1,0:T(8,128)(2,1)S(1)}, bf16[320,1152]{1,0:T(8,128)(2,1)S(1)}, u32[]{:S(2)}, u32[]{:S(2)}) collective-permute-start(bf16[320,1152]{1,0:T(8,128)(2,1)S(1)} %collective-permute-done.6.refs_6_), channel_id=1, source_target_pairs={{0,1},{1,0},{2,3},{3,2},{4,5},{5,4},{6,7},{7,6},{8,9},{9,8},{10,11... | collective-permute-start | bytes 2211848 | tf_op jit(solution)/shard_map/ppermute | solution.py:61
  37.7 6.9 %copy-start.15 = (bf16[320,1152]{1,0:T(8,128)(2,1)}, bf16[320,1152]{1,0:T(8,128)(2,1)S(1)}, u32[]{:S(2)}) copy-start(bf16[320,1152]{1,0:T(8,128)(2,1)S(1)} %collective-permute-done.11.refs_11_) | copy-start | bytes 2211844
  37.7 5.0 %collective-permute-start.13 = (bf16[320,1152]{1,0:T(8,128)(2,1)S(1)}, bf16[320,1152]{1,0:T(8,128)(2,1)S(1)}, u32[]{:S(2)}, u32[]{:S(2)}) collective-permute-start(bf16[320,1152]{1,0:T(8,128)(2,1)S(1)} %collective-permute-done.5.refs_5_), channel_id=1, source_target_pairs={{0,1},{1,0},{2,3},{3,2},{4,5},{5,4},{6,7},{7,6},{8,9},{9,8},{10,11... | collective-permute-start | bytes 2211848 | tf_op jit(solution)/shard_map/ppermute | solution.py:61
  40.9 3.7 %copy-start.16 = (bf16[320,1152]{1,0:T(8,128)(2,1)}, bf16[320,1152]{1,0:T(8,128)(2,1)S(1)}, u32[]{:S(2)}) copy-start(bf16[320,1152]{1,0:T(8,128)(2,1)S(1)} %collective-permute-done.7.refs_7_) | copy-start | bytes 2211844
  40.9 3.6 %collective-permute-start.15 = (bf16[320,1152]{1,0:T(8,128)(2,1)S(1)}, bf16[320,1152]{1,0:T(8,128)(2,1)}, u32[]{:S(2)}, u32[]{:S(2)}) collective-permute-start(bf16[320,1152]{1,0:T(8,128)(2,1)S(1)} %collective-permute-done.7.refs_7_), channel_id=1, source_target_pairs={{0,1},{1,0},{2,3},{3,2},{4,5},{5,4},{6,7},{7,6},{8,9},{9,8},{10,11... | collective-permute-start | bytes 2211848 | tf_op jit(solution)/shard_map/ppermute | solution.py:61
  42.7 1.9 %copy-start.17 = (bf16[320,1152]{1,0:T(8,128)(2,1)}, bf16[320,1152]{1,0:T(8,128)(2,1)S(1)}, u32[]{:S(2)}) copy-start(bf16[320,1152]{1,0:T(8,128)(2,1)S(1)} %collective-permute-done.10.refs_10_) | copy-start | bytes 2211844
  42.7 1.9 %copy-start.19 = (bf16[320,1152]{1,0:T(8,128)(2,1)}, bf16[320,1152]{1,0:T(8,128)(2,1)S(1)}, u32[]{:S(2)}) copy-start(bf16[320,1152]{1,0:T(8,128)(2,1)S(1)} %collective-permute-done.9.refs_9_) | copy-start | bytes 2211844
  42.7 0.9 copy-start.20
  43.6 0.9 copy-start.21
  78.4 2.7 %collective-permute-start.17 = (bf16[320,1152]{1,0:T(8,128)(2,1)}, bf16[320,1152]{1,0:T(8,128)(2,1)S(1)}, u32[]{:S(2)}, u32[]{:S(2)}) collective-permute-start(bf16[320,1152]{1,0:T(8,128)(2,1)} %get-tuple-element.27), channel_id=1, source_target_pairs={{0,1},{1,0},{2,3},{3,2},{4,5},{5,4},{6,7},{7,6},{8,9},{9,8},{10,11... | collective-permute-start | bytes 2211848 | tf_op jit(solution)/shard_map/ppermute | solution.py:61
  78.9 3.3 %collective-permute-start.22 = (bf16[320,1152]{1,0:T(8,128)(2,1)}, bf16[320,1152]{1,0:T(8,128)(2,1)S(1)}, u32[]{:S(2)}, u32[]{:S(2)}) collective-permute-start(bf16[320,1152]{1,0:T(8,128)(2,1)} %get-tuple-element.33), channel_id=1, source_target_pairs={{0,1},{1,0},{2,3},{3,2},{4,5},{5,4},{6,7},{7,6},{8,9},{9,8},{10,11... | collective-permute-start | bytes 2211848 | tf_op jit(solution)/shard_map/ppermute | solution.py:61
  79.2 12.8 %collective-permute-start.19 = (bf16[320,1152]{1,0:T(8,128)(2,1)}, bf16[320,1152]{1,0:T(8,128)(2,1)S(1)}, u32[]{:S(2)}, u32[]{:S(2)}) collective-permute-start(bf16[320,1152]{1,0:T(8,128)(2,1)} %get-tuple-element.29), channel_id=1, source_target_pairs={{0,1},{1,0},{2,3},{3,2},{4,5},{5,4},{6,7},{7,6},{8,9},{9,8},{10,11... | collective-permute-start | bytes 2211848 | tf_op jit(solution)/shard_map/ppermute | solution.py:61
  79.4 12.9 %collective-permute-start.21 = (bf16[320,1152]{1,0:T(8,128)(2,1)}, bf16[320,1152]{1,0:T(8,128)(2,1)S(1)}, u32[]{:S(2)}, u32[]{:S(2)}) collective-permute-start(bf16[320,1152]{1,0:T(8,128)(2,1)} %get-tuple-element.31), channel_id=1, source_target_pairs={{0,1},{1,0},{2,3},{3,2},{4,5},{5,4},{6,7},{7,6},{8,9},{9,8},{10,11... | collective-permute-start | bytes 2211848 | tf_op jit(solution)/shard_map/ppermute | solution.py:61
  79.7 23.4 %collective-permute-start.25 = (bf16[320,1152]{1,0:T(8,128)(2,1)}, bf16[320,1152]{1,0:T(8,128)(2,1)S(1)}, u32[]{:S(2)}, u32[]{:S(2)}) collective-permute-start(bf16[320,1152]{1,0:T(8,128)(2,1)} %get-tuple-element.35), channel_id=1, source_target_pairs={{0,1},{1,0},{2,3},{3,2},{4,5},{5,4},{6,7},{7,6},{8,9},{9,8},{10,11... | collective-permute-start | bytes 2211848 | tf_op jit(solution)/shard_map/ppermute | solution.py:61
  81.1 6.3 %collective-permute-start.26 = (bf16[320,1152]{1,0:T(8,128)(2,1)}, bf16[320,1152]{1,0:T(8,128)(2,1)S(1)}, u32[]{:S(2)}, u32[]{:S(2)}) collective-permute-start(bf16[320,1152]{1,0:T(8,128)(2,1)} %get-tuple-element.37), channel_id=1, source_target_pairs={{0,1},{1,0},{2,3},{3,2},{4,5},{5,4},{6,7},{7,6},{8,9},{9,8},{10,11... | collective-permute-start | bytes 2211848 | tf_op jit(solution)/shard_map/ppermute | solution.py:61
  81.3 1.1 copy-start.18
  81.3 1.4 %copy-start.5 = (bf16[320,1152]{1,0:T(8,128)(2,1)S(1)}, bf16[320,1152]{1,0:T(8,128)(2,1)}, u32[]{:S(2)}) copy-start(bf16[320,1152]{1,0:T(8,128)(2,1)} %get-tuple-element.32) | copy-start | bytes 2211844
  82.4 6.3 %collective-permute-start.28 = (bf16[320,1152]{1,0:T(8,128)(2,1)S(1)}, bf16[320,1152]{1,0:T(8,128)(2,1)S(1)}, u32[]{:S(2)}, u32[]{:S(2)}) collective-permute-start(bf16[320,1152]{1,0:T(8,128)(2,1)S(1)} %copy-done.18), channel_id=1, source_target_pairs={{0,1},{1,0},{2,3},{3,2},{4,5},{5,4},{6,7},{7,6},{8,9},{9,8},{10,11... | collective-permute-start | bytes 2211848 | tf_op jit(solution)/shard_map/ppermute | solution.py:61
  82.8 5.8 %copy-start.4 = (bf16[320,1152]{1,0:T(8,128)(2,1)S(1)}, bf16[320,1152]{1,0:T(8,128)(2,1)}, u32[]{:S(2)}) copy-start(bf16[320,1152]{1,0:T(8,128)(2,1)} %get-tuple-element.36) | copy-start | bytes 2211844
  87.5 11.8 %collective-permute-start.23 = (bf16[320,1152]{1,0:T(8,128)(2,1)S(1)}, bf16[320,1152]{1,0:T(8,128)(2,1)S(1)}, u32[]{:S(2)}, u32[]{:S(2)}) collective-permute-start(bf16[320,1152]{1,0:T(8,128)(2,1)S(1)} %add_convert_fusion.5), channel_id=1, source_target_pairs={{0,2},{1,67},{2,0},{3,65},{4,6},{5,71},{6,4},{7,69},{8,10},{9,75},... | collective-permute-start | bytes 2211848 | tf_op jit(solution)/shard_map/ppermute | solution.py:57
  88.6 3.3 %copy-start.3 = (bf16[320,1152]{1,0:T(8,128)(2,1)S(1)}, bf16[320,1152]{1,0:T(8,128)(2,1)}, u32[]{:S(2)}) copy-start(bf16[320,1152]{1,0:T(8,128)(2,1)} %get-tuple-element.38) | copy-start | bytes 2211844
  88.8 14.4 %collective-permute-start.27 = (bf16[320,1152]{1,0:T(8,128)(2,1)S(1)}, bf16[320,1152]{1,0:T(8,128)(2,1)S(1)}, u32[]{:S(2)}, u32[]{:S(2)}) collective-permute-start(bf16[320,1152]{1,0:T(8,128)(2,1)S(1)} %add_convert_fusion.2), channel_id=1, source_target_pairs={{0,12},{1,49},{2,14},{3,51},{4,0},{5,53},{6,2},{7,55},{8,4},{9,57}... | collective-permute-start | bytes 2211848 | tf_op jit(solution)/shard_map/ppermute | solution.py:48
  92.1 12.4 %collective-permute-start.29 = (bf16[320,1152]{1,0:T(8,128)(2,1)S(1)}, bf16[320,1152]{1,0:T(8,128)(2,1)S(1)}, u32[]{:S(2)}, u32[]{:S(2)}) collective-permute-start(bf16[320,1152]{1,0:T(8,128)(2,1)S(1)} %add_convert_fusion.1), channel_id=1, source_target_pairs={{0,4},{1,17},{2,6},{3,19},{4,8},{5,21},{6,10},{7,23},{8,12},{9,25}... | collective-permute-start | bytes 2211848 | tf_op jit(solution)/shard_map/ppermute | solution.py:48
  92.2 1.1 copy-start.6
  93.3 12.9 %collective-permute-start.16 = (bf16[320,1152]{1,0:T(8,128)(2,1)S(1)}, bf16[320,1152]{1,0:T(8,128)(2,1)S(1)}, u32[]{:S(2)}, u32[]{:S(2)}) collective-permute-start(bf16[320,1152]{1,0:T(8,128)(2,1)S(1)} %copy-done.6), channel_id=1, source_target_pairs={{0,1},{1,0},{2,3},{3,2},{4,5},{5,4},{6,7},{7,6},{8,9},{9,8},{10,11... | collective-permute-start | bytes 2211848 | tf_op jit(solution)/shard_map/ppermute | solution.py:61
  99.3 19.8 %collective-permute-start.18 = (bf16[320,1152]{1,0:T(8,128)(2,1)S(1)}, bf16[320,1152]{1,0:T(8,128)(2,1)S(1)}, u32[]{:S(2)}, u32[]{:S(2)}) collective-permute-start(bf16[320,1152]{1,0:T(8,128)(2,1)S(1)} %add_convert_fusion.8), channel_id=1, source_target_pairs={{0,12},{1,49},{2,14},{3,51},{4,0},{5,53},{6,2},{7,55},{8,4},{9,57}... | collective-permute-start | bytes 2211848 | tf_op jit(solution)/shard_map/ppermute | solution.py:48
  103.1 19.5 %collective-permute-start.20 = (bf16[320,1152]{1,0:T(8,128)(2,1)S(1)}, bf16[320,1152]{1,0:T(8,128)(2,1)S(1)}, u32[]{:S(2)}, u32[]{:S(2)}) collective-permute-start(bf16[320,1152]{1,0:T(8,128)(2,1)S(1)} %add_convert_fusion.7), channel_id=1, source_target_pairs={{0,4},{1,17},{2,6},{3,19},{4,8},{5,21},{6,10},{7,23},{8,12},{9,25}... | collective-permute-start | bytes 2211848 | tf_op jit(solution)/shard_map/ppermute | solution.py:48
  103.2 19.4 %collective-permute-start.24 = (bf16[320,1152]{1,0:T(8,128)(2,1)S(1)}, bf16[320,1152]{1,0:T(8,128)(2,1)S(1)}, u32[]{:S(2)}, u32[]{:S(2)}) collective-permute-start(bf16[320,1152]{1,0:T(8,128)(2,1)S(1)} %add_convert_fusion.4), channel_id=1, source_target_pairs={{0,8},{1,33},{2,10},{3,35},{4,12},{5,37},{6,14},{7,39},{8,0},{9,41... | collective-permute-start | bytes 2211848 | tf_op jit(solution)/shard_map/ppermute | solution.py:48
  104.9 17.7 %collective-permute-start.30 = (bf16[320,1152]{1,0:T(8,128)(2,1)S(1)}, bf16[320,1152]{1,0:T(8,128)(2,1)S(1)}, u32[]{:S(2)}, u32[]{:S(2)}) collective-permute-start(bf16[320,1152]{1,0:T(8,128)(2,1)S(1)} %add_convert_fusion), channel_id=1, source_target_pairs={{0,2},{1,67},{2,0},{3,65},{4,6},{5,71},{6,4},{7,69},{8,10},{9,75},... | collective-permute-start | bytes 2211848 | tf_op jit(solution)/shard_map/ppermute | solution.py:57
  123.6 1.8 %collective-permute-start.31 = (bf16[160,1152]{1,0:T(8,128)(2,1)S(1)}, bf16[160,1152]{1,0:T(8,128)(2,1)S(1)}, u32[]{:S(2)}, u32[]{:S(2)}) collective-permute-start(bf16[160,1152]{1,0:T(8,128)(2,1)S(1)} %get-tuple-element.41), channel_id=1, source_target_pairs={{0,1},{1,0},{2,3},{3,2},{4,5},{5,4},{6,7},{7,6},{8,9},{9,8},{10,11... | collective-permute-start | bytes 1105928 | tf_op jit(solution)/shard_map/ppermute | solution.py:61

commit v3 on v2

v3 whole, which is shorter than its diff:
```python
import functools

import jax
import jax.numpy as jnp
from jax import lax
from jax.experimental import pallas as pl
from jax.experimental.pallas import tpu as pltpu
from jax.sharding import Mesh, PartitionSpec as P

norm_eps = 1e-06
log2_e = 1.4426950408889634
axes = ("yh", "z", "x", "yl", "core")
extents = (2, 4, 4, 2, 2)
rows = 160
chip_rows = 2 * rows
chunk = 256


def pairs_of(move):
    pairs = []
    for yh in range(2):
        for z in range(4):
            for x in range(4):
                for yl in range(2):
                    for core in range(2):
                        place = (yh, z, x, yl, core)
                        pairs.append((linear(place), linear(move(*place))))
    return pairs


def linear(place):
    index = 0
    for value, extent in zip(place, extents):
        index = index * extent + value
    return index


def ring_move(steps):
    def move(yh, z, x, yl, core):
        if core == 0:
            return (yh, z, (x + steps) % 4, yl, core)
        return (yh, (z + steps) % 4, x, yl, core)

    return pairs_of(move)


def ring(value, steps):
    return lax.ppermute(value, axes, ring_move(steps))


def pair(value):
    def move(yh, z, x, yl, core):
        if core == 0:
            return (yh, z, x, 1 - yl, core)
        return (1 - yh, z, x, 1 - yl, core)

    return lax.ppermute(value, axes, pairs_of(move))


def swap(value):
    return lax.ppermute(value, "core", [(0, 1), (1, 0)])


def unit_rows(values):
    inverse = lax.rsqrt(jnp.sum(values * values, axis=1, keepdims=True) + norm_eps)
    return values * inverse, inverse


def pack_kernel(core_ref, image_ref, text_ref, got_ref, unit_ref, raw_ref):
    first_core = core_ref[0] == 0
    image = image_ref[...].astype(jnp.float32)
    text = text_ref[...].astype(jnp.float32)
    got = got_ref[...].astype(jnp.float32)
    low = jnp.where(first_core, image, got)
    high = jnp.where(first_core, got, text)
    for half, values in enumerate((low, high)):
        place = pl.ds(half * rows, rows)
        unit_ref[place, :] = unit_rows(values)[0].astype(jnp.bfloat16)
        raw_ref[place, :] = values.astype(jnp.bfloat16)


def stacked(places, begin):
    return jnp.concatenate(
        [ref[pl.ds(first + begin, rows), :] for ref, first in places], axis=0
    )


def places_of(refs):
    return [
        (ref, first) for ref in refs for first in range(0, ref.shape[0], chip_rows)
    ]


def opposite_rows(core, half):
    return pl.multiple_of(jnp.where(core == 0, half, 1 - half) * rows, rows)


def weights_kernel(pieces, scale_ref, core_ref, *refs):
    mine, other = places_of(refs[: pieces[0]]), places_of(refs[pieces[0] : sum(pieces)])
    weights_ref, far_ref = refs[sum(pieces) :]
    count = len(mine) * rows
    core = core_ref[0]
    slope, shift = scale_ref[0], scale_ref[1]
    for half in range(2):
        opposite = opposite_rows(core, half)
        mine_rows = stacked(mine, half * rows)
        other_rows = stacked(other, opposite)
        for begin in range(0, count, chunk):
            dots = lax.dot_general(
                mine_rows,
                other_rows[begin : begin + chunk],
                (((1,), (1,)), ((), ())),
                preferred_element_type=jnp.float32,
            )
            power = jnp.exp2(dots * slope + shift)
            share = pl.reciprocal(1.0 + power, approx=True)
            if begin == 0:
                row = lax.broadcasted_iota(jnp.int32, dots.shape, 0)
                column = lax.broadcasted_iota(jnp.int32, dots.shape, 1)
                matched = (row == column) & (row < rows) & (core == 0)
                share = jnp.where(matched, -power * share, share)
            weights_ref[half, :, pl.ds(begin, chunk)] = share.astype(jnp.bfloat16)
        other_sums(weights_ref, half, opposite, mine_rows, 4, far_ref)


def other_sums(weights_ref, half, opposite, mine_rows, first, sums_ref):
    for chip in range(0, 4, 2):
        total = lax.dot_general(
            weights_ref[half, :, pl.ds((first + chip) * rows, 2 * rows)],
            mine_rows,
            (((0,), (0,)), ((), ())),
            preferred_element_type=jnp.float32,
        ).astype(jnp.bfloat16)
        for step in range(2):
            place = pl.ds((chip + step) * chip_rows + opposite, rows)
            sums_ref[place, :] = total[step * rows : (step + 1) * rows]


def near_kernel(core_ref, weights_ref, *refs):
    mine, sums_ref = places_of(refs[:-1]), refs[-1]
    for half in range(2):
        mine_rows = stacked(mine, half * rows)
        opposite = opposite_rows(core_ref[0], half)
        other_sums(weights_ref, half, opposite, mine_rows, 0, sums_ref)


def sums_kernel(pieces, first, core_ref, weights_ref, *refs):
    other, sums = places_of(refs[:pieces]), refs[-4:]
    core = core_ref[0]
    for half in range(2):
        other_rows = stacked(other, opposite_rows(core, half))
        for chip in range(0, len(sums), 2):
            total = jnp.dot(
                weights_ref[half, pl.ds((first + chip) * rows, 2 * rows), :],
                other_rows,
                preferred_element_type=jnp.float32,
            ).astype(jnp.bfloat16)
            sums[chip][pl.ds(half * rows, rows), :] = total[:rows]
            sums[chip + 1][pl.ds(half * rows, rows), :] = total[rows:]


def final_kernel(scale_ref, core_ref, raw_ref, *refs):
    parts, (keep_ref, give_ref) = refs[:-2], refs[-2:]
    first_core = core_ref[0] == 0
    grads = []
    for half in range(2):
        place = pl.ds(half * rows, rows)
        unit, inverse = unit_rows(raw_ref[place, :].astype(jnp.float32))
        direction = parts[0][place, :].astype(jnp.float32)
        for part in parts[1:]:
            direction = direction + part[place, :].astype(jnp.float32)
        direction = direction * scale_ref[0]
        along = jnp.sum(unit * direction, axis=1, keepdims=True)
        grads.append(inverse * (direction - unit * along))
    low, high = grads
    keep_ref[...] = jnp.where(first_core, low, high).astype(jnp.bfloat16)
    give_ref[...] = jnp.where(first_core, high, low).astype(jnp.bfloat16)


def call(kernel, out_shape, scalars, arrays, flops=0, after=()):
    used = len(scalars) + len(arrays)

    def body(*refs):
        kernel(*refs[:used], *refs[used + len(after) :])

    return pl.pallas_call(
        body,
        in_specs=[pl.BlockSpec(memory_space=pltpu.SMEM)] * len(scalars)
        + [pl.BlockSpec(memory_space=pltpu.VMEM)] * len(arrays)
        + [pl.BlockSpec(memory_space=pl.ANY)] * len(after),
        out_specs=[pl.BlockSpec(memory_space=pltpu.VMEM)] * len(out_shape),
        out_shape=[jax.ShapeDtypeStruct(shape, jnp.bfloat16) for shape in out_shape],
        compiler_params=pltpu.CompilerParams(vmem_limit_bytes=26 * 2**20),
        cost_estimate=pl.CostEstimate(
            flops=flops, bytes_accessed=2**20, transcendentals=0
        ),
    )(*scalars, *arrays, *after)


def add_kernel(groups, *refs):
    count = len(groups)
    inputs, sums = refs[: -count], refs[-count:]
    for sum_ref, group in zip(sums, groups):
        total = None
        for index, first in group:
            part = inputs[index][pl.ds(first, chip_rows), :].astype(jnp.float32)
            total = part if total is None else total + part
        sum_ref[...] = total.astype(jnp.bfloat16)


def add(groups, after):
    arrays = []
    places = []
    for group in groups:
        place = []
        for part in group:
            array, first = part if isinstance(part, tuple) else (part, 0)
            if not any(array is known for known in arrays):
                arrays.append(array)
            index = [array is known for known in arrays].index(True)
            place.append((index, first))
        places.append(place)
    return call(
        functools.partial(add_kernel, places),
        [(chip_rows, arrays[0].shape[1])] * len(groups),
        (),
        arrays,
        after=after,
    )


def on_device(image_embeds, text_embeds, log_scale, logit_bias):
    width = image_embeds.shape[1]
    core = lax.axis_index("core")
    first_core = core == 0
    cores = core.astype(jnp.int32).reshape(1)
    logit_scale = jnp.exp(log_scale)
    factors = jnp.concatenate([-log2_e * logit_scale, -log2_e * logit_bias])
    got = swap(jnp.where(first_core, text_embeds, image_embeds))
    unit, raw = call(
        pack_kernel,
        [(chip_rows, width)] * 2,
        (cores,),
        (image_embeds, text_embeds, got),
    )
    near = [unit, ring(unit, 1), ring(unit, -1), ring(unit, 2)]
    across = pair(unit)
    far = [across, ring(across, 1), ring(across, -1), pair(near[3])]
    mine = near + far
    other = [
        swap(jnp.concatenate([near[0]], axis=0)),
        swap(jnp.concatenate([near[1], near[2]], axis=0)),
        swap(near[3]),
        swap(far[0]),
        swap(jnp.concatenate([far[1], far[2]], axis=0)),
        swap(far[3]),
    ]
    count = len(mine) * rows
    block = (chip_rows, width)
    quarter = count * count * width
    weights, far_other = call(
        functools.partial(weights_kernel, (len(mine), len(other))),
        [(2, count, count), (4 * chip_rows, width)],
        (factors, cores),
        (*mine, *other),
        6 * quarter,
    )
    far_shared = swap(far_other)
    far_own = call(
        functools.partial(sums_kernel, len(other), 4),
        [block] * 4,
        (cores,),
        (weights, *other),
        2 * quarter,
    )
    far_sums = add(
        [(one, (far_shared, k * chip_rows)) for k, one in enumerate(far_own)], ()
    )
    arrived = [ring(far_sums[1], -1), ring(far_sums[2], 1), pair(far_sums[3])]
    (near_other,) = call(
        near_kernel,
        [(4 * chip_rows, width)],
        (cores,),
        (weights, *mine),
        2 * quarter,
        (far_sums[0],),
    )
    near_shared = swap(near_other)
    near_own = call(
        functools.partial(sums_kernel, len(other), 0),
        [block] * 4,
        (cores,),
        (weights, *other),
        2 * quarter,
        (near_other,),
    )
    near = [(one, (near_shared, k * chip_rows)) for k, one in enumerate(near_own)]
    sums = add(
        [
            (far_sums[0], arrived[0], arrived[1]),
            (*near[3], arrived[2]),
            near[1],
            near[2],
            near[0],
        ],
        (),
    )
    parts = [
        sums[4],
        pair(sums[0]),
        ring(sums[1], 2),
        ring(sums[2], -1),
        ring(sums[3], 1),
    ]
    keep, give = call(
        final_kernel, [(rows, width)] * 2, (logit_scale, cores), (raw, *parts)
    )
    given = swap(give)
    image_grad = jnp.where(first_core, keep, given)
    text_grad = jnp.where(first_core, given, keep)
    return (image_grad, text_grad)


def solution(mesh):
    fine = Mesh(mesh.devices.reshape(extents), axes)
    split = P(axes, None)
    return jax.shard_map(
        on_device,
        mesh=fine,
        in_specs=(split, split, P(), P()),
        out_specs=(split, split),
        check_vma=False,
    )
```

time: 127 us -> 114 us (0.90)
  Pallas kernels: 35.2 us -> 31.3 us
  starting transfers between devices: 29.1 us -> 25.5 us
  waiting for transfers between devices: 52.9 us -> 50.4 us
  other arithmetic: 3.86 us -> 2.28 us
    ppermute x18 -> x10, waiting for transfers between devices: 9.22 us -> 4.97 us  [swap(): return lax.ppermute(value, 'core', [(0, 1), (1, 0)])]
    pallas_call x3 -> x8, Pallas kernels: 35.2 us -> 31.3 us  [call(): pl.pallas_call(body, in_specs=[pl.BlockSpec(memory_space=pltpu.SMEM)] * l...]
    ppermute x10, starting transfers between devices: 17.7 us -> 15.1 us  [ring(): return lax.ppermute(value, axes, ring_move(steps))]
    convert_element_type x8 -> x0, other arithmetic: 1.75 us -> none  [add(): return total.astype(jnp.bfloat16)]
    ppermute x18 -> x10, starting transfers between devices: 4.88 us -> 3.32 us  [swap(): return lax.ppermute(value, 'core', [(0, 1), (1, 0)])]
    unnamed x44 -> x4, local copies, waits for them, and re-layouts: 2.99 us -> 1.97 us
  transfers between devices with their start and end apart: 32 -> 24, of which waited for: 12 -> 15; matrix products, arithmetic and copies ran while one was open for 1% -> 0% of each run, Pallas kernels for 0% -> 8%
where the time goes in v3:
time: 114 us; the launch traced here: 113 us
  waiting for transfers between devices  50.4 us (44%)
  Pallas kernels  31.3 us (27%)
  starting transfers between devices  25.5 us (22%)
  other arithmetic  2.28 us (2%)
  between operations  2.08 us (2%)
  local copies, waits for them, and re-layouts  1.97 us (2%)
    ppermute x10, waiting for transfers between devices, ring(): return lax.ppermute(value, axes, ring_move(steps))  31.8 us
    pallas_call x8, Pallas kernels, call(): pl.pallas_call(body, in_specs=[pl.BlockSpec(memory_space=pltpu.SMEM)] * l...  31.3 us
    ppermute x10, starting transfers between devices, ring(): return lax.ppermute(value, axes, ring_move(steps))  15.1 us
    ppermute x4, waiting for transfers between devices, pair(): return lax.ppermute(value, axes, pairs_of(move))  13.7 us
    ppermute x4, starting transfers between devices, pair(): return lax.ppermute(value, axes, pairs_of(move))  7.06 us
    ppermute x10, waiting for transfers between devices, swap(): return lax.ppermute(value, 'core', [(0, 1), (1, 0)])  4.97 us
    ppermute x10, starting transfers between devices, swap(): return lax.ppermute(value, 'core', [(0, 1), (1, 0)])  3.32 us
  transfers between devices with their start and end apart: 24, of which 15 were waited for; matrix products, arithmetic and copies ran while one was open for 0% of the time, Pallas kernels for 8%

profile of v3, /device:TPU:1, one launch (start us, length us, event | category | flops | bytes accessed | tf_op | source)
XLA Modules:
  0.0 113.5 jit_solution(13251946112036725365)
XLA Ops:
  0.6 1.0 broadcast_select_fusion.2
  1.7 1.5 %collective-permute-start = (bf16[160,1152]{1,0:T(8,128)(2,1)S(1)}, bf16[160,1152]{1,0:T(8,128)(2,1)S(1)}, u32[]{:S(2)}, u32[]{:S(2)}) collective-permute-start(bf16[160,1152]{1,0:T(8,128)(2,1)S(1)} %broadcast_select_fusion.2), channel_id=1, source_target_pairs={{0,1},{1,0},{2,3},{3,2},{4,5},{5,4},{6,7},{7,6},{8,9},{9,8},{10,11... | collective-permute-start | bytes 1105928 | tf_op jit(solution)/shard_map/ppermute | solution.py:61
  3.2 1.3 %collective-permute-done.refs_3_ = bf16[160,1152]{1,0:T(8,128)(2,1)S(1)} collective-permute-done((bf16[160,1152]{1,0:T(8,128)(2,1)S(1)}, bf16[160,1152]{1,0:T(8,128)(2,1)S(1)}, u32[]{:S(2)}, u32[]{:S(2)}) %collective-permute-start) | collective-permute-done | bytes 368672 | tf_op jit(solution)/shard_map/ppermute | solution.py:61
  4.5 0.0 copy-start
  4.5 1.0 copy-done
  5.5 1.0 copy-done.1
  6.5 0.4 shard_map.59
  6.8 2.9 %collective-permute-start.4 = (bf16[320,1152]{1,0:T(8,128)(2,1)S(1)}, bf16[320,1152]{1,0:T(8,128)(2,1)S(1)}, u32[]{:S(2)}, u32[]{:S(2)}) collective-permute-start(bf16[320,1152]{1,0:T(8,128)(2,1)S(1)} %get-tuple-element.26.refs_2_), channel_id=1, source_target_pairs={{0,2},{1,67},{2,0},{3,65},{4,6},{5,71},{6,4},{7,69},{8,10},{9,75},... | collective-permute-start | bytes 2211848 | tf_op jit(solution)/shard_map/ppermute | solution.py:57
  9.7 1.6 %collective-permute-start.1 = (bf16[320,1152]{1,0:T(8,128)(2,1)S(1)}, bf16[320,1152]{1,0:T(8,128)(2,1)S(1)}, u32[]{:S(2)}, u32[]{:S(2)}) collective-permute-start(bf16[320,1152]{1,0:T(8,128)(2,1)S(1)} %get-tuple-element.26.refs_2_), channel_id=1, source_target_pairs={{0,4},{1,17},{2,6},{3,19},{4,8},{5,21},{6,10},{7,23},{8,12},{9,25}... | collective-permute-start | bytes 2211848 | tf_op jit(solution)/shard_map/ppermute | solution.py:48
  11.4 2.1 %collective-permute-start.2 = (bf16[320,1152]{1,0:T(8,128)(2,1)S(1)}, bf16[320,1152]{1,0:T(8,128)(2,1)S(1)}, u32[]{:S(2)}, u32[]{:S(2)}) collective-permute-start(bf16[320,1152]{1,0:T(8,128)(2,1)S(1)} %get-tuple-element.26.refs_2_), channel_id=1, source_target_pairs={{0,12},{1,49},{2,14},{3,51},{4,0},{5,53},{6,2},{7,55},{8,4},{9,57}... | collective-permute-start | bytes 2211848 | tf_op jit(solution)/shard_map/ppermute | solution.py:48
  13.5 1.3 %collective-permute-start.3 = (bf16[320,1152]{1,0:T(8,128)(2,1)S(1)}, bf16[320,1152]{1,0:T(8,128)(2,1)S(1)}, u32[]{:S(2)}, u32[]{:S(2)}) collective-permute-start(bf16[320,1152]{1,0:T(8,128)(2,1)S(1)} %get-tuple-element.26.refs_2_), channel_id=1, source_target_pairs={{0,8},{1,33},{2,10},{3,35},{4,12},{5,37},{6,14},{7,39},{8,0},{9,41... | collective-permute-start | bytes 2211848 | tf_op jit(solution)/shard_map/ppermute | solution.py:48
  14.8 4.1 %collective-permute-done.4.refs_6_ = bf16[320,1152]{1,0:T(8,128)(2,1)S(1)} collective-permute-done((bf16[320,1152]{1,0:T(8,128)(2,1)S(1)}, bf16[320,1152]{1,0:T(8,128)(2,1)S(1)}, u32[]{:S(2)}, u32[]{:S(2)}) %collective-permute-start.4) | collective-permute-done | bytes 737312 | tf_op jit(solution)/shard_map/ppermute | solution.py:57
  18.9 1.6 %collective-permute-start.5 = (bf16[320,1152]{1,0:T(8,128)(2,1)S(1)}, bf16[320,1152]{1,0:T(8,128)(2,1)S(1)}, u32[]{:S(2)}, u32[]{:S(2)}) collective-permute-start(bf16[320,1152]{1,0:T(8,128)(2,1)S(1)} %collective-permute-done.4.refs_6_), channel_id=1, source_target_pairs={{0,4},{1,17},{2,6},{3,19},{4,8},{5,21},{6,10},{7,23},{8,12},{9,25}... | collective-permute-start | bytes 2211848 | tf_op jit(solution)/shard_map/ppermute | solution.py:48
  20.5 2.1 %collective-permute-start.6 = (bf16[320,1152]{1,0:T(8,128)(2,1)S(1)}, bf16[320,1152]{1,0:T(8,128)(2,1)S(1)}, u32[]{:S(2)}, u32[]{:S(2)}) collective-permute-start(bf16[320,1152]{1,0:T(8,128)(2,1)S(1)} %collective-permute-done.4.refs_6_), channel_id=1, source_target_pairs={{0,12},{1,49},{2,14},{3,51},{4,0},{5,53},{6,2},{7,55},{8,4},{9,57}... | collective-permute-start | bytes 2211848 | tf_op jit(solution)/shard_map/ppermute | solution.py:48
  22.7 0.0 collective-permute-done.1.refs_3_
  22.7 0.0 collective-permute-start.8
  22.7 7.2 %collective-permute-done.2.refs_4_ = bf16[320,1152]{1,0:T(8,128)(2,1)S(1)} collective-permute-done((bf16[320,1152]{1,0:T(8,128)(2,1)S(1)}, bf16[320,1152]{1,0:T(8,128)(2,1)S(1)}, u32[]{:S(2)}, u32[]{:S(2)}) %collective-permute-start.2) | collective-permute-done | bytes 737312 | tf_op jit(solution)/shard_map/ppermute | solution.py:48
  29.8 0.1 pad_maximum_fusion
  29.9 0.1 collective-permute-start.9
  30.0 1.5 %collective-permute-done.3.refs_5_ = bf16[320,1152]{1,0:T(8,128)(2,1)S(1)} collective-permute-done((bf16[320,1152]{1,0:T(8,128)(2,1)S(1)}, bf16[320,1152]{1,0:T(8,128)(2,1)S(1)}, u32[]{:S(2)}, u32[]{:S(2)}) %collective-permute-start.3) | collective-permute-done | bytes 737312 | tf_op jit(solution)/shard_map/ppermute | solution.py:48
  31.5 0.3 collective-permute-start.7
  31.9 7.5 %collective-permute-done.5.refs_7_ = bf16[320,1152]{1,0:T(8,128)(2,1)S(1)} collective-permute-done((bf16[320,1152]{1,0:T(8,128)(2,1)S(1)}, bf16[320,1152]{1,0:T(8,128)(2,1)S(1)}, u32[]{:S(2)}, u32[]{:S(2)}) %collective-permute-start.5) | collective-permute-done | bytes 737312 | tf_op jit(solution)/shard_map/ppermute | solution.py:48
  39.3 0.0 collective-permute-done.6.refs_8_
  39.3 0.1 pad_maximum_fusion.1
  39.5 0.1 collective-permute-start.12
  39.5 0.5 collective-permute-start.11
  40.0 0.0 collective-permute-done.8.refs_10_.refs_2_
  40.0 0.1 collective-permute-start.10
  40.1 2.9 %collective-permute-done.7.refs_9_ = bf16[320,1152]{1,0:T(8,128)(2,1)S(1)} collective-permute-done((bf16[320,1152]{1,0:T(8,128)(2,1)S(1)}, bf16[320,1152]{1,0:T(8,128)(2,1)S(1)}, u32[]{:S(2)}, u32[]{:S(2)}) %collective-permute-start.7) | collective-permute-done | bytes 737312 | tf_op jit(solution)/shard_map/ppermute | solution.py:57
  43.1 0.0 collective-permute-start.13
  44.4 0.1 pad_maximum_fusion.2.refs_0_
  44.5 0.0 collective-permute-done.11.refs_13_.refs_5_
  44.5 0.4 collective-permute-done.10.refs_12_.refs_4_
  44.9 0.0 collective-permute-done.9.refs_11_.refs_3_
  44.9 1.1 collective-permute-done.13.refs_15_.refs_7_
  46.0 0.0 collective-permute-done.12.refs_14_.refs_6_
  46.0 14.7 %shard_map.60 = (bf16[2,1280,1280]{2,1,0:T(8,128)(2,1)S(1)}, bf16[1280,1152]{1,0:T(8,128)(2,1)S(1)}) custom-call(f32[2]{0:T(128)S(1)} %pad_maximum_fusion.2.refs_0_, s32[1]{0:T(128)} %bitcast.refs_0_.refs_1_, bf16[320,1152]{1,0:T(8,128)(2,1)S(1)} %get-tuple-element.26.refs_2_, bf16[320,1152]{1,0:T(8,128)(2,1)S(1)} %collective-permute-done.1.refs_3_, ...), custom_call_target="tpu_custom_call" | custom-call | flops 11324620800 | bytes 1048576 | tf_op jit(solution)/shard_map/pallas_call | solution.py:186
  60.7 0.4 collective-permute-start.14
  61.1 4.4 %shard_map.61 = (bf16[320,1152]{1,0:T(8,128)(2,1)S(1)}, bf16[320,1152]{1,0:T(8,128)(2,1)S(1)}, bf16[320,1152]{1,0:T(8,128)(2,1)S(1)}, bf16[320,1152]{1,0:T(8,128)(2,1)S(1)}) custom-call(s32[1]{0:T(128)} %bitcast.refs_0_.refs_1_, bf16[2,1280,1280]{2,1,0:T(8,128)(2,1)S(1)} %get-tuple-element.27.refs_1_, ...), custom_call_target="tpu_custom_call" | custom-call | flops 3774873600 | bytes 1048576 | tf_op jit(solution)/shard_map/pallas_call | solution.py:186
  65.6 0.8 collective-permute-done.14.refs_1_
  66.4 0.7 shard_map.62
  67.1 4.5 %shard_map.63.refs_8_ = bf16[1280,1152]{1,0:T(8,128)(2,1)S(1)} custom-call(s32[1]{0:T(128)} %bitcast.refs_0_.refs_1_, bf16[2,1280,1280]{2,1,0:T(8,128)(2,1)S(1)} %get-tuple-element.27.refs_1_, bf16[320,1152]{1,0:T(8,128)(2,1)S(1)} %get-tuple-element.26.refs_2_, bf16[320,1152]{1,0:T(8,128)(2,1)S(1)} %collective-permute-done.1.refs_3_, ...), custom_call_target="tpu_custom_call" | custom-call | flops 3774873600 | bytes 1048576 | tf_op jit(solution)/shard_map/pallas_call | solution.py:186
  71.6 0.2 collective-permute-start.17
  71.8 2.7 %collective-permute-start.15 = (bf16[320,1152]{1,0:T(8,128)(2,1)S(1)}, bf16[320,1152]{1,0:T(8,128)(2,1)S(1)}, u32[]{:S(2)}, u32[]{:S(2)}) collective-permute-start(bf16[320,1152]{1,0:T(8,128)(2,1)S(1)} %get-tuple-element.34), channel_id=1, source_target_pairs={{0,12},{1,49},{2,14},{3,51},{4,0},{5,53},{6,2},{7,55},{8,4},{9,57}... | collective-permute-start | bytes 2211848 | tf_op jit(solution)/shard_map/ppermute | solution.py:48
  74.5 0.0 collective-permute-start.16
  74.5 1.9 %collective-permute-start.18 = (bf16[320,1152]{1,0:T(8,128)(2,1)S(1)}, bf16[320,1152]{1,0:T(8,128)(2,1)S(1)}, u32[]{:S(2)}, u32[]{:S(2)}) collective-permute-start(bf16[320,1152]{1,0:T(8,128)(2,1)S(1)} %get-tuple-element.37), channel_id=1, source_target_pairs={{0,2},{1,67},{2,0},{3,65},{4,6},{5,71},{6,4},{7,69},{8,10},{9,75},... | collective-permute-start | bytes 2211848 | tf_op jit(solution)/shard_map/ppermute | solution.py:57
  76.4 4.4 %shard_map.64 = (bf16[320,1152]{1,0:T(8,128)(2,1)S(1)}, bf16[320,1152]{1,0:T(8,128)(2,1)S(1)}, bf16[320,1152]{1,0:T(8,128)(2,1)S(1)}, bf16[320,1152]{1,0:T(8,128)(2,1)S(1)}) custom-call(s32[1]{0:T(128)} %bitcast.refs_0_.refs_1_, bf16[2,1280,1280]{2,1,0:T(8,128)(2,1)S(1)} %get-tuple-element.27.refs_1_, ...), custom_call_target="tpu_custom_call" | custom-call | flops 3774873600 | bytes 1048576 | tf_op jit(solution)/shard_map/pallas_call | solution.py:186
  80.9 2.1 %collective-permute-done.15.refs_1_ = bf16[320,1152]{1,0:T(8,128)(2,1)S(1)} collective-permute-done((bf16[320,1152]{1,0:T(8,128)(2,1)S(1)}, bf16[320,1152]{1,0:T(8,128)(2,1)S(1)}, u32[]{:S(2)}, u32[]{:S(2)}) %collective-permute-start.15) | collective-permute-done | bytes 737312 | tf_op jit(solution)/shard_map/ppermute | solution.py:48
  82.9 3.4 %collective-permute-done.16.refs_2_ = bf16[320,1152]{1,0:T(8,128)(2,1)S(1)} collective-permute-done((bf16[320,1152]{1,0:T(8,128)(2,1)S(1)}, bf16[320,1152]{1,0:T(8,128)(2,1)S(1)}, u32[]{:S(2)}, u32[]{:S(2)}) %collective-permute-start.16) | collective-permute-done | bytes 737312 | tf_op jit(solution)/shard_map/ppermute | solution.py:48
  86.3 0.0 collective-permute-done.18.refs_5_
  86.3 0.0 collective-permute-done.17.refs_4_
  86.3 1.1 shard_map.65
  87.5 1.9 %collective-permute-start.19 = (bf16[320,1152]{1,0:T(8,128)(2,1)S(1)}, bf16[320,1152]{1,0:T(8,128)(2,1)S(1)}, u32[]{:S(2)}, u32[]{:S(2)}) collective-permute-start(bf16[320,1152]{1,0:T(8,128)(2,1)S(1)} %get-tuple-element.42), channel_id=1, source_target_pairs={{0,2},{1,67},{2,0},{3,65},{4,6},{5,71},{6,4},{7,69},{8,10},{9,75},... | collective-permute-start | bytes 2211848 | tf_op jit(solution)/shard_map/ppermute | solution.py:57
  89.4 1.6 %collective-permute-start.20 = (bf16[320,1152]{1,0:T(8,128)(2,1)S(1)}, bf16[320,1152]{1,0:T(8,128)(2,1)S(1)}, u32[]{:S(2)}, u32[]{:S(2)}) collective-permute-start(bf16[320,1152]{1,0:T(8,128)(2,1)S(1)} %get-tuple-element.43), channel_id=1, source_target_pairs={{0,8},{1,33},{2,10},{3,35},{4,12},{5,37},{6,14},{7,39},{8,0},{9,41... | collective-permute-start | bytes 2211848 | tf_op jit(solution)/shard_map/ppermute | solution.py:48
  91.0 1.4 %collective-permute-start.21 = (bf16[320,1152]{1,0:T(8,128)(2,1)S(1)}, bf16[320,1152]{1,0:T(8,128)(2,1)S(1)}, u32[]{:S(2)}, u32[]{:S(2)}) collective-permute-start(bf16[320,1152]{1,0:T(8,128)(2,1)S(1)} %get-tuple-element.44), channel_id=1, source_target_pairs={{0,12},{1,49},{2,14},{3,51},{4,0},{5,53},{6,2},{7,55},{8,4},{9,57}... | collective-permute-start | bytes 2211848 | tf_op jit(solution)/shard_map/ppermute | solution.py:48
  92.4 0.6 collective-permute-start.22
  93.0 6.7 %collective-permute-done.19.refs_4_ = bf16[320,1152]{1,0:T(8,128)(2,1)S(1)} collective-permute-done((bf16[320,1152]{1,0:T(8,128)(2,1)S(1)}, bf16[320,1152]{1,0:T(8,128)(2,1)S(1)}, u32[]{:S(2)}, u32[]{:S(2)}) %collective-permute-start.19) | collective-permute-done | bytes 737312 | tf_op jit(solution)/shard_map/ppermute | solution.py:57
  99.6 1.9 %collective-permute-done.20.refs_5_ = bf16[320,1152]{1,0:T(8,128)(2,1)S(1)} collective-permute-done((bf16[320,1152]{1,0:T(8,128)(2,1)S(1)}, bf16[320,1152]{1,0:T(8,128)(2,1)S(1)}, u32[]{:S(2)}, u32[]{:S(2)}) %collective-permute-start.20) | collective-permute-done | bytes 737312 | tf_op jit(solution)/shard_map/ppermute | solution.py:48
  101.6 8.2 %collective-permute-done.21.refs_6_ = bf16[320,1152]{1,0:T(8,128)(2,1)S(1)} collective-permute-done((bf16[320,1152]{1,0:T(8,128)(2,1)S(1)}, bf16[320,1152]{1,0:T(8,128)(2,1)S(1)}, u32[]{:S(2)}, u32[]{:S(2)}) %collective-permute-start.21) | collective-permute-done | bytes 737312 | tf_op jit(solution)/shard_map/ppermute | solution.py:48
  109.7 0.0 collective-permute-done.22.refs_7_
  109.7 1.0 shard_map.66
  110.8 0.4 collective-permute-start.23
  111.2 1.4 %collective-permute-done.23 = bf16[160,1152]{1,0:T(8,128)(2,1)S(1)} collective-permute-done((bf16[160,1152]{1,0:T(8,128)(2,1)S(1)}, bf16[160,1152]{1,0:T(8,128)(2,1)S(1)}, u32[]{:S(2)}, u32[]{:S(2)}) %collective-permute-start.23) | collective-permute-done | bytes 368672 | tf_op jit(solution)/shard_map/ppermute | solution.py:61
  112.5 0.9 broadcast_select_fusion
  (1 shorter events, 0.0 us)
Async XLA Ops:
  1.7 2.8 %collective-permute-start = (bf16[160,1152]{1,0:T(8,128)(2,1)S(1)}, bf16[160,1152]{1,0:T(8,128)(2,1)S(1)}, u32[]{:S(2)}, u32[]{:S(2)}) collective-permute-start(bf16[160,1152]{1,0:T(8,128)(2,1)S(1)} %broadcast_select_fusion.2), channel_id=1, source_target_pairs={{0,1},{1,0},{2,3},{3,2},{4,5},{5,4},{6,7},{7,6},{8,9},{9,8},{10,11... | collective-permute-start | bytes 1105928 | tf_op jit(solution)/shard_map/ppermute | solution.py:61
  4.5 1.0 copy-start
  5.5 1.0 copy-start.1
  6.8 12.0 %collective-permute-start.4 = (bf16[320,1152]{1,0:T(8,128)(2,1)S(1)}, bf16[320,1152]{1,0:T(8,128)(2,1)S(1)}, u32[]{:S(2)}, u32[]{:S(2)}) collective-permute-start(bf16[320,1152]{1,0:T(8,128)(2,1)S(1)} %get-tuple-element.26.refs_2_), channel_id=1, source_target_pairs={{0,2},{1,67},{2,0},{3,65},{4,6},{5,71},{6,4},{7,69},{8,10},{9,75},... | collective-permute-start | bytes 2211848 | tf_op jit(solution)/shard_map/ppermute | solution.py:57
  9.7 12.9 %collective-permute-start.1 = (bf16[320,1152]{1,0:T(8,128)(2,1)S(1)}, bf16[320,1152]{1,0:T(8,128)(2,1)S(1)}, u32[]{:S(2)}, u32[]{:S(2)}) collective-permute-start(bf16[320,1152]{1,0:T(8,128)(2,1)S(1)} %get-tuple-element.26.refs_2_), channel_id=1, source_target_pairs={{0,4},{1,17},{2,6},{3,19},{4,8},{5,21},{6,10},{7,23},{8,12},{9,25}... | collective-permute-start | bytes 2211848 | tf_op jit(solution)/shard_map/ppermute | solution.py:48
  11.4 18.4 %collective-permute-start.2 = (bf16[320,1152]{1,0:T(8,128)(2,1)S(1)}, bf16[320,1152]{1,0:T(8,128)(2,1)S(1)}, u32[]{:S(2)}, u32[]{:S(2)}) collective-permute-start(bf16[320,1152]{1,0:T(8,128)(2,1)S(1)} %get-tuple-element.26.refs_2_), channel_id=1, source_target_pairs={{0,12},{1,49},{2,14},{3,51},{4,0},{5,53},{6,2},{7,55},{8,4},{9,57}... | collective-permute-start | bytes 2211848 | tf_op jit(solution)/shard_map/ppermute | solution.py:48
  13.5 18.0 %collective-permute-start.3 = (bf16[320,1152]{1,0:T(8,128)(2,1)S(1)}, bf16[320,1152]{1,0:T(8,128)(2,1)S(1)}, u32[]{:S(2)}, u32[]{:S(2)}) collective-permute-start(bf16[320,1152]{1,0:T(8,128)(2,1)S(1)} %get-tuple-element.26.refs_2_), channel_id=1, source_target_pairs={{0,8},{1,33},{2,10},{3,35},{4,12},{5,37},{6,14},{7,39},{8,0},{9,41... | collective-permute-start | bytes 2211848 | tf_op jit(solution)/shard_map/ppermute | solution.py:48
  18.9 20.4 %collective-permute-start.5 = (bf16[320,1152]{1,0:T(8,128)(2,1)S(1)}, bf16[320,1152]{1,0:T(8,128)(2,1)S(1)}, u32[]{:S(2)}, u32[]{:S(2)}) collective-permute-start(bf16[320,1152]{1,0:T(8,128)(2,1)S(1)} %collective-permute-done.4.refs_6_), channel_id=1, source_target_pairs={{0,4},{1,17},{2,6},{3,19},{4,8},{5,21},{6,10},{7,23},{8,12},{9,25}... | collective-permute-start | bytes 2211848 | tf_op jit(solution)/shard_map/ppermute | solution.py:48
  20.5 18.8 %collective-permute-start.6 = (bf16[320,1152]{1,0:T(8,128)(2,1)S(1)}, bf16[320,1152]{1,0:T(8,128)(2,1)S(1)}, u32[]{:S(2)}, u32[]{:S(2)}) collective-permute-start(bf16[320,1152]{1,0:T(8,128)(2,1)S(1)} %collective-permute-done.4.refs_6_), channel_id=1, source_target_pairs={{0,12},{1,49},{2,14},{3,51},{4,0},{5,53},{6,2},{7,55},{8,4},{9,57}... | collective-permute-start | bytes 2211848 | tf_op jit(solution)/shard_map/ppermute | solution.py:48
  22.7 17.4 %collective-permute-start.8 = (bf16[320,1152]{1,0:T(8,128)(2,1)S(1)}, bf16[320,1152]{1,0:T(8,128)(2,1)S(1)}, u32[]{:S(2)}, u32[]{:S(2)}) collective-permute-start(bf16[320,1152]{1,0:T(8,128)(2,1)S(1)} %get-tuple-element.26.refs_2_), channel_id=1, source_target_pairs={{0,1},{1,0},{2,3},{3,2},{4,5},{5,4},{6,7},{7,6},{8,9},{9,8},{10,11... | collective-permute-start | bytes 2211848 | tf_op jit(solution)/shard_map/ppermute | solution.py:61
  29.9 15.0 %collective-permute-start.9 = (bf16[640,1152]{1,0:T(8,128)(2,1)S(1)}, bf16[640,1152]{1,0:T(8,128)(2,1)S(1)}, u32[]{:S(2)}, u32[]{:S(2)}) collective-permute-start(bf16[640,1152]{1,0:T(8,128)(2,1)S(1)} %pad_maximum_fusion), channel_id=1, source_target_pairs={{0,1},{1,0},{2,3},{3,2},{4,5},{5,4},{6,7},{7,6},{8,9},{9,8},{10,11... | collective-permute-start | bytes 4423688 | tf_op jit(solution)/shard_map/ppermute | solution.py:61
  31.5 11.5 %collective-permute-start.7 = (bf16[320,1152]{1,0:T(8,128)(2,1)S(1)}, bf16[320,1152]{1,0:T(8,128)(2,1)S(1)}, u32[]{:S(2)}, u32[]{:S(2)}) collective-permute-start(bf16[320,1152]{1,0:T(8,128)(2,1)S(1)} %collective-permute-done.3.refs_5_), channel_id=1, source_target_pairs={{0,2},{1,67},{2,0},{3,65},{4,6},{5,71},{6,4},{7,69},{8,10},{9,75},... | collective-permute-start | bytes 2211848 | tf_op jit(solution)/shard_map/ppermute | solution.py:57
  39.5 6.5 %collective-permute-start.12 = (bf16[640,1152]{1,0:T(8,128)(2,1)S(1)}, bf16[640,1152]{1,0:T(8,128)(2,1)S(1)}, u32[]{:S(2)}, u32[]{:S(2)}) collective-permute-start(bf16[640,1152]{1,0:T(8,128)(2,1)S(1)} %pad_maximum_fusion.1), channel_id=1, source_target_pairs={{0,1},{1,0},{2,3},{3,2},{4,5},{5,4},{6,7},{7,6},{8,9},{9,8},{10,11... | collective-permute-start | bytes 4423688 | tf_op jit(solution)/shard_map/ppermute | solution.py:61
  39.5 4.9 %collective-permute-start.11 = (bf16[320,1152]{1,0:T(8,128)(2,1)S(1)}, bf16[320,1152]{1,0:T(8,128)(2,1)S(1)}, u32[]{:S(2)}, u32[]{:S(2)}) collective-permute-start(bf16[320,1152]{1,0:T(8,128)(2,1)S(1)} %collective-permute-done.4.refs_6_), channel_id=1, source_target_pairs={{0,1},{1,0},{2,3},{3,2},{4,5},{5,4},{6,7},{7,6},{8,9},{9,8},{10,11... | collective-permute-start | bytes 2211848 | tf_op jit(solution)/shard_map/ppermute | solution.py:61
  40.0 4.9 %collective-permute-start.10 = (bf16[320,1152]{1,0:T(8,128)(2,1)S(1)}, bf16[320,1152]{1,0:T(8,128)(2,1)S(1)}, u32[]{:S(2)}, u32[]{:S(2)}) collective-permute-start(bf16[320,1152]{1,0:T(8,128)(2,1)S(1)} %collective-permute-done.3.refs_5_), channel_id=1, source_target_pairs={{0,1},{1,0},{2,3},{3,2},{4,5},{5,4},{6,7},{7,6},{8,9},{9,8},{10,11... | collective-permute-start | bytes 2211848 | tf_op jit(solution)/shard_map/ppermute | solution.py:61
  43.1 2.9 %collective-permute-start.13 = (bf16[320,1152]{1,0:T(8,128)(2,1)S(1)}, bf16[320,1152]{1,0:T(8,128)(2,1)S(1)}, u32[]{:S(2)}, u32[]{:S(2)}) collective-permute-start(bf16[320,1152]{1,0:T(8,128)(2,1)S(1)} %collective-permute-done.7.refs_9_), channel_id=1, source_target_pairs={{0,1},{1,0},{2,3},{3,2},{4,5},{5,4},{6,7},{7,6},{8,9},{9,8},{10,11... | collective-permute-start | bytes 2211848 | tf_op jit(solution)/shard_map/ppermute | solution.py:61
  60.7 5.7 %collective-permute-start.14 = (bf16[1280,1152]{1,0:T(8,128)(2,1)S(1)}, bf16[1280,1152]{1,0:T(8,128)(2,1)S(1)}, u32[]{:S(2)}, u32[]{:S(2)}) collective-permute-start(bf16[1280,1152]{1,0:T(8,128)(2,1)S(1)} %get-tuple-element.29), channel_id=1, source_target_pairs={{0,1},{1,0},{2,3},{3,2},{4,5},{5,4},{6,7},{7,6},{8,9},{9,8},{10,11... | collective-permute-start | bytes 8847368 | tf_op jit(solution)/shard_map/ppermute | solution.py:61
  71.6 14.8 %collective-permute-start.17 = (bf16[1280,1152]{1,0:T(8,128)(2,1)S(1)}, bf16[1280,1152]{1,0:T(8,128)(2,1)S(1)}, u32[]{:S(2)}, u32[]{:S(2)}) collective-permute-start(bf16[1280,1152]{1,0:T(8,128)(2,1)S(1)} %shard_map.63.refs_8_), channel_id=1, source_target_pairs={{0,1},{1,0},{2,3},{3,2},{4,5},{5,4},{6,7},{7,6},{8,9},{9,8},{10,11... | collective-permute-start | bytes 8847368 | tf_op jit(solution)/shard_map/ppermute | solution.py:61
  71.8 11.1 %collective-permute-start.15 = (bf16[320,1152]{1,0:T(8,128)(2,1)S(1)}, bf16[320,1152]{1,0:T(8,128)(2,1)S(1)}, u32[]{:S(2)}, u32[]{:S(2)}) collective-permute-start(bf16[320,1152]{1,0:T(8,128)(2,1)S(1)} %get-tuple-element.34), channel_id=1, source_target_pairs={{0,12},{1,49},{2,14},{3,51},{4,0},{5,53},{6,2},{7,55},{8,4},{9,57}... | collective-permute-start | bytes 2211848 | tf_op jit(solution)/shard_map/ppermute | solution.py:48
  74.5 11.8 %collective-permute-start.16 = (bf16[320,1152]{1,0:T(8,128)(2,1)S(1)}, bf16[320,1152]{1,0:T(8,128)(2,1)S(1)}, u32[]{:S(2)}, u32[]{:S(2)}) collective-permute-start(bf16[320,1152]{1,0:T(8,128)(2,1)S(1)} %get-tuple-element.35), channel_id=1, source_target_pairs={{0,4},{1,17},{2,6},{3,19},{4,8},{5,21},{6,10},{7,23},{8,12},{9,25}... | collective-permute-start | bytes 2211848 | tf_op jit(solution)/shard_map/ppermute | solution.py:48
  74.5 11.8 %collective-permute-start.18 = (bf16[320,1152]{1,0:T(8,128)(2,1)S(1)}, bf16[320,1152]{1,0:T(8,128)(2,1)S(1)}, u32[]{:S(2)}, u32[]{:S(2)}) collective-permute-start(bf16[320,1152]{1,0:T(8,128)(2,1)S(1)} %get-tuple-element.37), channel_id=1, source_target_pairs={{0,2},{1,67},{2,0},{3,65},{4,6},{5,71},{6,4},{7,69},{8,10},{9,75},... | collective-permute-start | bytes 2211848 | tf_op jit(solution)/shard_map/ppermute | solution.py:57
  87.5 12.2 %collective-permute-start.19 = (bf16[320,1152]{1,0:T(8,128)(2,1)S(1)}, bf16[320,1152]{1,0:T(8,128)(2,1)S(1)}, u32[]{:S(2)}, u32[]{:S(2)}) collective-permute-start(bf16[320,1152]{1,0:T(8,128)(2,1)S(1)} %get-tuple-element.42), channel_id=1, source_target_pairs={{0,2},{1,67},{2,0},{3,65},{4,6},{5,71},{6,4},{7,69},{8,10},{9,75},... | collective-permute-start | bytes 2211848 | tf_op jit(solution)/shard_map/ppermute | solution.py:57
  89.4 12.2 %collective-permute-start.20 = (bf16[320,1152]{1,0:T(8,128)(2,1)S(1)}, bf16[320,1152]{1,0:T(8,128)(2,1)S(1)}, u32[]{:S(2)}, u32[]{:S(2)}) collective-permute-start(bf16[320,1152]{1,0:T(8,128)(2,1)S(1)} %get-tuple-element.43), channel_id=1, source_target_pairs={{0,8},{1,33},{2,10},{3,35},{4,12},{5,37},{6,14},{7,39},{8,0},{9,41... | collective-permute-start | bytes 2211848 | tf_op jit(solution)/shard_map/ppermute | solution.py:48
  91.0 18.7 %collective-permute-start.21 = (bf16[320,1152]{1,0:T(8,128)(2,1)S(1)}, bf16[320,1152]{1,0:T(8,128)(2,1)S(1)}, u32[]{:S(2)}, u32[]{:S(2)}) collective-permute-start(bf16[320,1152]{1,0:T(8,128)(2,1)S(1)} %get-tuple-element.44), channel_id=1, source_target_pairs={{0,12},{1,49},{2,14},{3,51},{4,0},{5,53},{6,2},{7,55},{8,4},{9,57}... | collective-permute-start | bytes 2211848 | tf_op jit(solution)/shard_map/ppermute | solution.py:48
  92.4 17.4 %collective-permute-start.22 = (bf16[320,1152]{1,0:T(8,128)(2,1)S(1)}, bf16[320,1152]{1,0:T(8,128)(2,1)S(1)}, u32[]{:S(2)}, u32[]{:S(2)}) collective-permute-start(bf16[320,1152]{1,0:T(8,128)(2,1)S(1)} %get-tuple-element.45), channel_id=1, source_target_pairs={{0,4},{1,17},{2,6},{3,19},{4,8},{5,21},{6,10},{7,23},{8,12},{9,25}... | collective-permute-start | bytes 2211848 | tf_op jit(solution)/shard_map/ppermute | solution.py:48
  110.8 1.8 %collective-permute-start.23 = (bf16[160,1152]{1,0:T(8,128)(2,1)S(1)}, bf16[160,1152]{1,0:T(8,128)(2,1)S(1)}, u32[]{:S(2)}, u32[]{:S(2)}) collective-permute-start(bf16[160,1152]{1,0:T(8,128)(2,1)S(1)} %get-tuple-element.47), channel_id=1, source_target_pairs={{0,1},{1,0},{2,3},{3,2},{4,5},{5,4},{6,7},{7,6},{8,9},{9,8},{10,11... | collective-permute-start | bytes 1105928 | tf_op jit(solution)/shard_map/ppermute | solution.py:61

commit v4 on v3

--- a/solution.py
+++ b/solution.py
@@ -66,13 +66,12 @@
     return values * inverse, inverse
 
 
-def pack_kernel(core_ref, image_ref, text_ref, got_ref, unit_ref, raw_ref):
+def pack_kernel(core_ref, keep_ref, got_ref, unit_ref, raw_ref):
     first_core = core_ref[0] == 0
-    image = image_ref[...].astype(jnp.float32)
-    text = text_ref[...].astype(jnp.float32)
+    keep = keep_ref[...].astype(jnp.float32)
     got = got_ref[...].astype(jnp.float32)
-    low = jnp.where(first_core, image, got)
-    high = jnp.where(first_core, got, text)
+    low = jnp.where(first_core, keep, got)
+    high = jnp.where(first_core, got, keep)
     for half, values in enumerate((low, high)):
         place = pl.ds(half * rows, rows)
         unit_ref[place, :] = unit_rows(values)[0].astype(jnp.bfloat16)
@@ -208,7 +207,7 @@
         sum_ref[...] = total.astype(jnp.bfloat16)
 
 
-def add(groups, after):
+def add(groups, after, flops=0):
     arrays = []
     places = []
     for group in groups:
@@ -225,7 +224,8 @@
         [(chip_rows, arrays[0].shape[1])] * len(groups),
         (),
         arrays,
-        after=after,
+        flops,
+        after,
     )
 
 
@@ -236,22 +236,25 @@
     cores = core.astype(jnp.int32).reshape(1)
     logit_scale = jnp.exp(log_scale)
     factors = jnp.concatenate([-log2_e * logit_scale, -log2_e * logit_bias])
-    got = swap(jnp.where(first_core, text_embeds, image_embeds))
+    give = jnp.where(first_core, text_embeds, image_embeds)
+    keep = jnp.where(first_core, image_embeds, text_embeds)
+    got = swap(give)
     unit, raw = call(
         pack_kernel,
         [(chip_rows, width)] * 2,
         (cores,),
-        (image_embeds, text_embeds, got),
-    )
-    near = [unit, ring(unit, 1), ring(unit, -1), ring(unit, 2)]
-    across = pair(unit)
-    far = [across, ring(across, 1), ring(across, -1), pair(near[3])]
+        (keep, got),
+    )
+    left, right, across = ring(unit, 1), ring(unit, -1), pair(unit)
+    distant = jnp.concatenate([ring(left[:rows], 1), ring(right[rows:], -1)], axis=0)
+    near = [unit, left, right, distant]
+    far = [across, ring(across, 1), ring(across, -1), pair(distant)]
     mine = near + far
     other = [
-        swap(jnp.concatenate([near[0]], axis=0)),
-        swap(jnp.concatenate([near[1], near[2]], axis=0)),
-        swap(near[3]),
-        swap(far[0]),
+        swap(unit),
+        swap(jnp.concatenate([left, right], axis=0)),
+        swap(distant),
+        swap(across),
         swap(jnp.concatenate([far[1], far[2]], axis=0)),
         swap(far[3]),
     ]
@@ -294,24 +297,20 @@
         2 * quarter,
         (near_other,),
     )
-    near = [(one, (near_shared, k * chip_rows)) for k, one in enumerate(near_own)]
-    sums = add(
-        [
-            (far_sums[0], arrived[0], arrived[1]),
-            (*near[3], arrived[2]),
-            near[1],
-            near[2],
-            near[0],
-        ],
+    near_sums = add(
+        [(one, (near_shared, k * chip_rows)) for k, one in enumerate(near_own)], ()
+    )
+    far_total, distant_total = add(
+        [(far_sums[0], arrived[0], arrived[1]), (near_sums[3], arrived[2])],
+        (near_sums[0],),
+    )
+    late = [ring(distant_total, 2), pair(far_total)]
+    (near_total,) = add(
+        [(near_sums[0], ring(near_sums[1], -1), ring(near_sums[2], 1))],
         (),
-    )
-    parts = [
-        sums[4],
-        pair(sums[0]),
-        ring(sums[1], 2),
-        ring(sums[2], -1),
-        ring(sums[3], 1),
-    ]
+        16 * quarter,
+    )
+    parts = [near_total, *late]
     keep, give = call(
         final_kernel, [(rows, width)] * 2, (logit_scale, cores), (raw, *parts)
     )

time: 114 us -> 105 us (0.921)
  waiting for transfers between devices: 50.4 us -> 34.3 us
  starting transfers between devices: 25.5 us -> 34.6 us
  local copies, waits for them, and re-layouts: 1.97 us -> 0.12 us
    ppermute x4, waiting for transfers between devices: 13.7 us -> 3.24 us  [pair(): return lax.ppermute(value, axes, pairs_of(move))]
    ppermute x10 -> x11, waiting for transfers between devices: 31.8 us -> 26.3 us  [ring(): return lax.ppermute(value, axes, ring_move(steps))]
    ppermute x4, starting transfers between devices: 7.06 us -> 11 us  [pair(): return lax.ppermute(value, axes, pairs_of(move))]
    ppermute x10 -> x11, starting transfers between devices: 15.1 us -> 18.4 us  [ring(): return lax.ppermute(value, axes, ring_move(steps))]
    unnamed x4 -> x1, local copies, waits for them, and re-layouts: 1.97 us -> 0.03 us
    ppermute x10, starting transfers between devices: 3.32 us -> 5.12 us  [swap(): return lax.ppermute(value, 'core', [(0, 1), (1, 0)])]
    pallas_call x8 -> x10, Pallas kernels: 31.3 us -> 31.4 us  [call(): pl.pallas_call(body, in_specs=[pl.BlockSpec(memory_space=pltpu.SMEM)] * l...]
  transfers between devices with their start and end apart: 24 -> 25, of which waited for: 15 -> 14; matrix products, arithmetic and copies ran while one was open for 0% -> 0% of each run, Pallas kernels for 8% -> 10%
where the time goes in v4:
time: 105 us
  starting transfers between devices  34.6 us (33%)
  waiting for transfers between devices  34.3 us (33%)
  Pallas kernels  31.4 us (30%)
  other arithmetic  2.4 us (2%)
  between operations  2.12 us (2%)
    pallas_call x10, Pallas kernels, call(): pl.pallas_call(body, in_specs=[pl.BlockSpec(memory_space=pltpu.SMEM)] * l...  31.4 us
    ppermute x11, waiting for transfers between devices, ring(): return lax.ppermute(value, axes, ring_move(steps))  26.3 us
    ppermute x11, starting transfers between devices, ring(): return lax.ppermute(value, axes, ring_move(steps))  18.4 us
    ppermute x4, starting transfers between devices, pair(): return lax.ppermute(value, axes, pairs_of(move))  11 us
    ppermute x10, starting transfers between devices, swap(): return lax.ppermute(value, 'core', [(0, 1), (1, 0)])  5.12 us
    ppermute x10, waiting for transfers between devices, swap(): return lax.ppermute(value, 'core', [(0, 1), (1, 0)])  4.76 us
    ppermute x4, waiting for transfers between devices, pair(): return lax.ppermute(value, axes, pairs_of(move))  3.24 us
  transfers between devices with their start and end apart: 25, of which 14 were waited for; matrix products, arithmetic and copies ran while one was open for 0% of the time, Pallas kernels for 10%

profile of v4, /device:TPU:1, one launch (start us, length us, event | category | flops | bytes accessed | tf_op | source)
XLA Modules:
  0.0 105.0 jit_solution(11845694583880182331)
XLA Ops:
  0.6 1.2 %broadcast_select_fusion.2 = (bf16[160,1152]{1,0:T(8,128)(2,1)S(1)}, bf16[160,1152]{1,0:T(8,128)(2,1)S(1)}) fusion(bf16[160,1152]{1,0:T(8,128)(2,1)} %param.5, bf16[160,1152]{1,0:T(8,128)(2,1)} %param.4, pred[]{:T(512)S(6)} %eq.3), kind=kLoop, calls=%fused_computation.4 | loop fusion | flops 368640 | bytes 1474561 | tf_op jit(solution)/shard_map/jit(_where)/select_n | solution.py:239
  1.8 1.5 %collective-permute-start = (bf16[160,1152]{1,0:T(8,128)(2,1)S(1)}, bf16[160,1152]{1,0:T(8,128)(2,1)S(1)}, u32[]{:S(2)}, u32[]{:S(2)}) collective-permute-start(bf16[160,1152]{1,0:T(8,128)(2,1)S(1)} %get-tuple-element.52), channel_id=1, source_target_pairs={{0,1},{1,0},{2,3},{3,2},{4,5},{5,4},{6,7},{7,6},{8,9},{9,8},{10,11... | collective-permute-start | bytes 1105928 | tf_op jit(solution)/shard_map/ppermute | solution.py:61
  3.3 1.3 %collective-permute-done.refs_2_ = bf16[160,1152]{1,0:T(8,128)(2,1)S(1)} collective-permute-done((bf16[160,1152]{1,0:T(8,128)(2,1)S(1)}, bf16[160,1152]{1,0:T(8,128)(2,1)S(1)}, u32[]{:S(2)}, u32[]{:S(2)}) %collective-permute-start) | collective-permute-done | bytes 368672 | tf_op jit(solution)/shard_map/ppermute | solution.py:61
  4.6 0.4 shard_map.59
  5.0 1.8 %collective-permute-start.1 = (bf16[320,1152]{1,0:T(8,128)(2,1)S(1)}, bf16[320,1152]{1,0:T(8,128)(2,1)S(1)}, u32[]{:S(2)}, u32[]{:S(2)}) collective-permute-start(bf16[320,1152]{1,0:T(8,128)(2,1)S(1)} %get-tuple-element.27.refs_2_), channel_id=1, source_target_pairs={{0,4},{1,17},{2,6},{3,19},{4,8},{5,21},{6,10},{7,23},{8,12},{9,25}... | collective-permute-start | bytes 2211848 | tf_op jit(solution)/shard_map/ppermute | solution.py:48
  6.8 2.2 %collective-permute-start.2 = (bf16[320,1152]{1,0:T(8,128)(2,1)S(1)}, bf16[320,1152]{1,0:T(8,128)(2,1)S(1)}, u32[]{:S(2)}, u32[]{:S(2)}) collective-permute-start(bf16[320,1152]{1,0:T(8,128)(2,1)S(1)} %get-tuple-element.27.refs_2_), channel_id=1, source_target_pairs={{0,12},{1,49},{2,14},{3,51},{4,0},{5,53},{6,2},{7,55},{8,4},{9,57}... | collective-permute-start | bytes 2211848 | tf_op jit(solution)/shard_map/ppermute | solution.py:48
  9.0 2.7 %collective-permute-start.5 = (bf16[320,1152]{1,0:T(8,128)(2,1)S(1)}, bf16[320,1152]{1,0:T(8,128)(2,1)S(1)}, u32[]{:S(2)}, u32[]{:S(2)}) collective-permute-start(bf16[320,1152]{1,0:T(8,128)(2,1)S(1)} %get-tuple-element.27.refs_2_), channel_id=1, source_target_pairs={{0,2},{1,67},{2,0},{3,65},{4,6},{5,71},{6,4},{7,69},{8,10},{9,75},... | collective-permute-start | bytes 2211848 | tf_op jit(solution)/shard_map/ppermute | solution.py:57
  11.7 6.0 %collective-permute-done.1.refs_3_ = bf16[320,1152]{1,0:T(8,128)(2,1)S(1)} collective-permute-done((bf16[320,1152]{1,0:T(8,128)(2,1)S(1)}, bf16[320,1152]{1,0:T(8,128)(2,1)S(1)}, u32[]{:S(2)}, u32[]{:S(2)}) %collective-permute-start.1) | collective-permute-done | bytes 737312 | tf_op jit(solution)/shard_map/ppermute | solution.py:48
  17.8 0.1 collective-permute-start.3
  17.9 0.7 collective-permute-start.9
  18.6 0.0 collective-permute-done.2.refs_4_
  18.6 3.8 %collective-permute-start.4 = (bf16[160,1152]{1,0:T(8,128)(2,1)S(1)}, bf16[160,1152]{1,0:T(8,128)(2,1)S(1)}, u32[]{:S(2)}, u32[]{:S(2)}) collective-permute-start(bf16[160,1152]{1,0:T(8,128)(2,1)S(1)} %slice.9), channel_id=1, source_target_pairs={{0,12},{1,49},{2,14},{3,51},{4,0},{5,53},{6,2},{7,55},{8,4},{9,57}... | collective-permute-start | bytes 1105928 | tf_op jit(solution)/shard_map/ppermute | solution.py:48
  22.5 0.0 collective-permute-done.5.refs_6_
  22.5 0.0 collective-permute-start.6
  22.5 2.7 %collective-permute-start.7 = (bf16[320,1152]{1,0:T(8,128)(2,1)S(1)}, bf16[320,1152]{1,0:T(8,128)(2,1)S(1)}, u32[]{:S(2)}, u32[]{:S(2)}) collective-permute-start(bf16[320,1152]{1,0:T(8,128)(2,1)S(1)} %collective-permute-done.5.refs_6_), channel_id=1, source_target_pairs={{0,12},{1,49},{2,14},{3,51},{4,0},{5,53},{6,2},{7,55},{8,4},{9,57}... | collective-permute-start | bytes 2211848 | tf_op jit(solution)/shard_map/ppermute | solution.py:48
  25.1 0.1 pad_maximum_fusion
  25.3 0.5 collective-permute-done.3
  25.7 1.2 %collective-permute-start.10 = (bf16[640,1152]{1,0:T(8,128)(2,1)S(1)}, bf16[640,1152]{1,0:T(8,128)(2,1)S(1)}, u32[]{:S(2)}, u32[]{:S(2)}) collective-permute-start(bf16[640,1152]{1,0:T(8,128)(2,1)S(1)} %pad_maximum_fusion), channel_id=1, source_target_pairs={{0,1},{1,0},{2,3},{3,2},{4,5},{5,4},{6,7},{7,6},{8,9},{9,8},{10,11... | collective-permute-start | bytes 4423688 | tf_op jit(solution)/shard_map/ppermute | solution.py:61
  27.0 0.0 collective-permute-done.4
  27.0 2.9 %collective-permute-start.8 = (bf16[320,1152]{1,0:T(8,128)(2,1)S(1)}, bf16[320,1152]{1,0:T(8,128)(2,1)S(1)}, u32[]{:S(2)}, u32[]{:S(2)}) collective-permute-start(bf16[320,1152]{1,0:T(8,128)(2,1)S(1)} %constant_dynamic-update-slice_fusion.refs_5_), channel_id=1, source_target_pairs={{0,2},{1,67},{2,0},{3,65},{4,6},{5,71},{6,4},{7,69},{8,10},{9,75},... | collective-permute-start | bytes 2211848 | tf_op jit(solution)/shard_map/ppermute | solution.py:57
  29.9 4.3 %collective-permute-done.6.refs_7_ = bf16[320,1152]{1,0:T(8,128)(2,1)S(1)} collective-permute-done((bf16[320,1152]{1,0:T(8,128)(2,1)S(1)}, bf16[320,1152]{1,0:T(8,128)(2,1)S(1)}, u32[]{:S(2)}, u32[]{:S(2)}) %collective-permute-start.6) | collective-permute-done | bytes 737312 | tf_op jit(solution)/shard_map/ppermute | solution.py:48
  34.3 0.5 collective-permute-done.7.refs_8_
  34.8 0.1 pad_maximum_fusion.1
  34.9 0.1 collective-permute-start.13
  35.1 0.5 collective-permute-start.12
  35.5 0.0 collective-permute-done.9.refs_10_.refs_2_
  35.5 0.1 collective-permute-start.11
  35.6 3.2 %collective-permute-done.8.refs_9_ = bf16[320,1152]{1,0:T(8,128)(2,1)S(1)} collective-permute-done((bf16[320,1152]{1,0:T(8,128)(2,1)S(1)}, bf16[320,1152]{1,0:T(8,128)(2,1)S(1)}, u32[]{:S(2)}, u32[]{:S(2)}) %collective-permute-start.8) | collective-permute-done | bytes 737312 | tf_op jit(solution)/shard_map/ppermute | solution.py:57
  38.8 0.0 collective-permute-start.14
  40.1 0.1 pad_maximum_fusion.2.refs_0_
  40.2 0.0 collective-permute-done.12.refs_13_.refs_5_
  40.2 0.2 collective-permute-done.11.refs_12_.refs_4_
  40.4 0.0 collective-permute-done.10.refs_11_.refs_3_
  40.4 1.1 %collective-permute-done.14.refs_15_.refs_7_ = bf16[320,1152]{1,0:T(8,128)(2,1)S(1)} collective-permute-done((bf16[320,1152]{1,0:T(8,128)(2,1)S(1)}, bf16[320,1152]{1,0:T(8,128)(2,1)S(1)}, u32[]{:S(2)}, u32[]{:S(2)}) %collective-permute-start.14) | collective-permute-done | bytes 737312 | tf_op jit(solution)/shard_map/ppermute | solution.py:61
  41.4 0.0 collective-permute-done.13.refs_14_.refs_6_
  41.5 14.8 %shard_map.60 = (bf16[2,1280,1280]{2,1,0:T(8,128)(2,1)S(1)}, bf16[1280,1152]{1,0:T(8,128)(2,1)S(1)}) custom-call(f32[2]{0:T(128)S(1)} %pad_maximum_fusion.2.refs_0_, s32[1]{0:T(128)} %bitcast.refs_0_.refs_1_, bf16[320,1152]{1,0:T(8,128)(2,1)S(1)} %get-tuple-element.27.refs_2_, bf16[320,1152]{1,0:T(8,128)(2,1)S(1)} %collective-permute-done.1.refs_3_, ...), custom_call_target="tpu_custom_call" | custom-call | flops 11324620800 | bytes 1048576 | tf_op jit(solution)/shard_map/pallas_call | solution.py:185
  56.2 0.4 collective-permute-start.15
  56.7 4.4 %shard_map.61 = (bf16[320,1152]{1,0:T(8,128)(2,1)S(1)}, bf16[320,1152]{1,0:T(8,128)(2,1)S(1)}, bf16[320,1152]{1,0:T(8,128)(2,1)S(1)}, bf16[320,1152]{1,0:T(8,128)(2,1)S(1)}) custom-call(s32[1]{0:T(128)} %bitcast.refs_0_.refs_1_, bf16[2,1280,1280]{2,1,0:T(8,128)(2,1)S(1)} %get-tuple-element.28.refs_1_, ...), custom_call_target="tpu_custom_call" | custom-call | flops 3774873600 | bytes 1048576 | tf_op jit(solution)/shard_map/pallas_call | solution.py:185
  61.1 0.8 collective-permute-done.15.refs_1_
  61.9 0.7 shard_map.62
  62.6 4.5 %shard_map.63.refs_8_ = bf16[1280,1152]{1,0:T(8,128)(2,1)S(1)} custom-call(s32[1]{0:T(128)} %bitcast.refs_0_.refs_1_, bf16[2,1280,1280]{2,1,0:T(8,128)(2,1)S(1)} %get-tuple-element.28.refs_1_, bf16[320,1152]{1,0:T(8,128)(2,1)S(1)} %get-tuple-element.27.refs_2_, bf16[320,1152]{1,0:T(8,128)(2,1)S(1)} %collective-permute-done.1.refs_3_, ...), custom_call_target="tpu_custom_call" | custom-call | flops 3774873600 | bytes 1048576 | tf_op jit(solution)/shard_map/pallas_call | solution.py:185
  67.1 0.2 collective-permute-start.16
  67.3 3.7 %collective-permute-start.19 = (bf16[320,1152]{1,0:T(8,128)(2,1)S(1)}, bf16[320,1152]{1,0:T(8,128)(2,1)S(1)}, u32[]{:S(2)}, u32[]{:S(2)}) collective-permute-start(bf16[320,1152]{1,0:T(8,128)(2,1)S(1)} %get-tuple-element.42), channel_id=1, source_target_pairs={{0,12},{1,49},{2,14},{3,51},{4,0},{5,53},{6,2},{7,55},{8,4},{9,57}... | collective-permute-start | bytes 2211848 | tf_op jit(solution)/shard_map/ppermute | solution.py:48
  71.1 0.0 collective-permute-start.20
  71.1 2.7 %collective-permute-start.21 = (bf16[320,1152]{1,0:T(8,128)(2,1)S(1)}, bf16[320,1152]{1,0:T(8,128)(2,1)S(1)}, u32[]{:S(2)}, u32[]{:S(2)}) collective-permute-start(bf16[320,1152]{1,0:T(8,128)(2,1)S(1)} %get-tuple-element.45), channel_id=1, source_target_pairs={{0,2},{1,67},{2,0},{3,65},{4,6},{5,71},{6,4},{7,69},{8,10},{9,75},... | collective-permute-start | bytes 2211848 | tf_op jit(solution)/shard_map/ppermute | solution.py:57
  73.8 4.4 %shard_map.64 = (bf16[320,1152]{1,0:T(8,128)(2,1)S(1)}, bf16[320,1152]{1,0:T(8,128)(2,1)S(1)}, bf16[320,1152]{1,0:T(8,128)(2,1)S(1)}, bf16[320,1152]{1,0:T(8,128)(2,1)S(1)}) custom-call(s32[1]{0:T(128)} %bitcast.refs_0_.refs_1_, bf16[2,1280,1280]{2,1,0:T(8,128)(2,1)S(1)} %get-tuple-element.28.refs_1_, ...), custom_call_target="tpu_custom_call" | custom-call | flops 3774873600 | bytes 1048576 | tf_op jit(solution)/shard_map/pallas_call | solution.py:185
  78.3 0.0 collective-permute-done.16.refs_1_
  78.3 0.7 shard_map.65
  79.0 2.7 %collective-permute-start.17 = (bf16[320,1152]{1,0:T(8,128)(2,1)S(1)}, bf16[320,1152]{1,0:T(8,128)(2,1)S(1)}, u32[]{:S(2)}, u32[]{:S(2)}) collective-permute-start(bf16[320,1152]{1,0:T(8,128)(2,1)S(1)} %get-tuple-element.40), channel_id=1, source_target_pairs={{0,12},{1,49},{2,14},{3,51},{4,0},{5,53},{6,2},{7,55},{8,4},{9,57}... | collective-permute-start | bytes 2211848 | tf_op jit(solution)/shard_map/ppermute | solution.py:48
  81.7 0.0 collective-permute-start.18
  81.7 0.0 collective-permute-done.19.refs_1_
  81.7 1.2 %collective-permute-done.20.refs_2_ = bf16[320,1152]{1,0:T(8,128)(2,1)S(1)} collective-permute-done((bf16[320,1152]{1,0:T(8,128)(2,1)S(1)}, bf16[320,1152]{1,0:T(8,128)(2,1)S(1)}, u32[]{:S(2)}, u32[]{:S(2)}) %collective-permute-start.20) | collective-permute-done | bytes 737312 | tf_op jit(solution)/shard_map/ppermute | solution.py:48
  82.9 0.1 collective-permute-done.21.refs_4_
  83.0 0.4 shard_map.67
  83.4 1.4 %collective-permute-start.22 = (bf16[320,1152]{1,0:T(8,128)(2,1)S(1)}, bf16[320,1152]{1,0:T(8,128)(2,1)S(1)}, u32[]{:S(2)}, u32[]{:S(2)}) collective-permute-start(bf16[320,1152]{1,0:T(8,128)(2,1)S(1)} %get-tuple-element.46), channel_id=1, source_target_pairs={{0,8},{1,33},{2,10},{3,35},{4,12},{5,37},{6,14},{7,39},{8,0},{9,41... | collective-permute-start | bytes 2211848 | tf_op jit(solution)/shard_map/ppermute | solution.py:48
  84.8 2.7 %collective-permute-start.23 = (bf16[320,1152]{1,0:T(8,128)(2,1)S(1)}, bf16[320,1152]{1,0:T(8,128)(2,1)S(1)}, u32[]{:S(2)}, u32[]{:S(2)}) collective-permute-start(bf16[320,1152]{1,0:T(8,128)(2,1)S(1)} %get-tuple-element.47), channel_id=1, source_target_pairs={{0,2},{1,67},{2,0},{3,65},{4,6},{5,71},{6,4},{7,69},{8,10},{9,75},... | collective-permute-start | bytes 2211848 | tf_op jit(solution)/shard_map/ppermute | solution.py:57
  87.5 10.5 %collective-permute-done.17.refs_1_ = bf16[320,1152]{1,0:T(8,128)(2,1)S(1)} collective-permute-done((bf16[320,1152]{1,0:T(8,128)(2,1)S(1)}, bf16[320,1152]{1,0:T(8,128)(2,1)S(1)}, u32[]{:S(2)}, u32[]{:S(2)}) %collective-permute-start.17) | collective-permute-done | bytes 737312 | tf_op jit(solution)/shard_map/ppermute | solution.py:48
  98.0 3.1 %collective-permute-done.18.refs_2_ = bf16[320,1152]{1,0:T(8,128)(2,1)S(1)} collective-permute-done((bf16[320,1152]{1,0:T(8,128)(2,1)S(1)}, bf16[320,1152]{1,0:T(8,128)(2,1)S(1)}, u32[]{:S(2)}, u32[]{:S(2)}) %collective-permute-start.18) | collective-permute-done | bytes 737312 | tf_op jit(solution)/shard_map/ppermute | solution.py:48
  101.1 0.3 shard_map.66.refs_3_
  101.4 0.0 collective-permute-done.23.refs_5_
  101.4 0.8 shard_map.68
  102.3 0.4 collective-permute-start.24
  102.6 1.4 %collective-permute-done.24 = bf16[160,1152]{1,0:T(8,128)(2,1)S(1)} collective-permute-done((bf16[160,1152]{1,0:T(8,128)(2,1)S(1)}, bf16[160,1152]{1,0:T(8,128)(2,1)S(1)}, u32[]{:S(2)}, u32[]{:S(2)}) %collective-permute-start.24) | collective-permute-done | bytes 368672 | tf_op jit(solution)/shard_map/ppermute | solution.py:61
  104.0 0.9 broadcast_select_fusion
  (5 shorter events, 0.1 us)
Async XLA Ops:
  1.8 2.8 %collective-permute-start = (bf16[160,1152]{1,0:T(8,128)(2,1)S(1)}, bf16[160,1152]{1,0:T(8,128)(2,1)S(1)}, u32[]{:S(2)}, u32[]{:S(2)}) collective-permute-start(bf16[160,1152]{1,0:T(8,128)(2,1)S(1)} %get-tuple-element.52), channel_id=1, source_target_pairs={{0,1},{1,0},{2,3},{3,2},{4,5},{5,4},{6,7},{7,6},{8,9},{9,8},{10,11... | collective-permute-start | bytes 1105928 | tf_op jit(solution)/shard_map/ppermute | solution.py:61
  5.0 12.8 %collective-permute-start.1 = (bf16[320,1152]{1,0:T(8,128)(2,1)S(1)}, bf16[320,1152]{1,0:T(8,128)(2,1)S(1)}, u32[]{:S(2)}, u32[]{:S(2)}) collective-permute-start(bf16[320,1152]{1,0:T(8,128)(2,1)S(1)} %get-tuple-element.27.refs_2_), channel_id=1, source_target_pairs={{0,4},{1,17},{2,6},{3,19},{4,8},{5,21},{6,10},{7,23},{8,12},{9,25}... | collective-permute-start | bytes 2211848 | tf_op jit(solution)/shard_map/ppermute | solution.py:48
  6.8 11.8 %collective-permute-start.2 = (bf16[320,1152]{1,0:T(8,128)(2,1)S(1)}, bf16[320,1152]{1,0:T(8,128)(2,1)S(1)}, u32[]{:S(2)}, u32[]{:S(2)}) collective-permute-start(bf16[320,1152]{1,0:T(8,128)(2,1)S(1)} %get-tuple-element.27.refs_2_), channel_id=1, source_target_pairs={{0,12},{1,49},{2,14},{3,51},{4,0},{5,53},{6,2},{7,55},{8,4},{9,57}... | collective-permute-start | bytes 2211848 | tf_op jit(solution)/shard_map/ppermute | solution.py:48
  9.0 13.5 %collective-permute-start.5 = (bf16[320,1152]{1,0:T(8,128)(2,1)S(1)}, bf16[320,1152]{1,0:T(8,128)(2,1)S(1)}, u32[]{:S(2)}, u32[]{:S(2)}) collective-permute-start(bf16[320,1152]{1,0:T(8,128)(2,1)S(1)} %get-tuple-element.27.refs_2_), channel_id=1, source_target_pairs={{0,2},{1,67},{2,0},{3,65},{4,6},{5,71},{6,4},{7,69},{8,10},{9,75},... | collective-permute-start | bytes 2211848 | tf_op jit(solution)/shard_map/ppermute | solution.py:57
  17.8 7.9 %collective-permute-start.3 = (bf16[160,1152]{1,0:T(8,128)(2,1)S(1)}, bf16[160,1152]{1,0:T(8,128)(2,1)S(1)}, u32[]{:S(2)}, u32[]{:S(2)}) collective-permute-start(bf16[160,1152]{1,0:T(8,128)(2,1)S(1)} %slice.8), channel_id=1, source_target_pairs={{0,4},{1,17},{2,6},{3,19},{4,8},{5,21},{6,10},{7,23},{8,12},{9,25}... | collective-permute-start | bytes 1105928 | tf_op jit(solution)/shard_map/ppermute | solution.py:48
  17.9 17.6 %collective-permute-start.9 = (bf16[320,1152]{1,0:T(8,128)(2,1)S(1)}, bf16[320,1152]{1,0:T(8,128)(2,1)S(1)}, u32[]{:S(2)}, u32[]{:S(2)}) collective-permute-start(bf16[320,1152]{1,0:T(8,128)(2,1)S(1)} %get-tuple-element.27.refs_2_), channel_id=1, source_target_pairs={{0,1},{1,0},{2,3},{3,2},{4,5},{5,4},{6,7},{7,6},{8,9},{9,8},{10,11... | collective-permute-start | bytes 2211848 | tf_op jit(solution)/shard_map/ppermute | solution.py:61
  18.6 8.4 %collective-permute-start.4 = (bf16[160,1152]{1,0:T(8,128)(2,1)S(1)}, bf16[160,1152]{1,0:T(8,128)(2,1)S(1)}, u32[]{:S(2)}, u32[]{:S(2)}) collective-permute-start(bf16[160,1152]{1,0:T(8,128)(2,1)S(1)} %slice.9), channel_id=1, source_target_pairs={{0,12},{1,49},{2,14},{3,51},{4,0},{5,53},{6,2},{7,55},{8,4},{9,57}... | collective-permute-start | bytes 1105928 | tf_op jit(solution)/shard_map/ppermute | solution.py:48
  22.5 11.8 %collective-permute-start.6 = (bf16[320,1152]{1,0:T(8,128)(2,1)S(1)}, bf16[320,1152]{1,0:T(8,128)(2,1)S(1)}, u32[]{:S(2)}, u32[]{:S(2)}) collective-permute-start(bf16[320,1152]{1,0:T(8,128)(2,1)S(1)} %collective-permute-done.5.refs_6_), channel_id=1, source_target_pairs={{0,4},{1,17},{2,6},{3,19},{4,8},{5,21},{6,10},{7,23},{8,12},{9,25}... | collective-permute-start | bytes 2211848 | tf_op jit(solution)/shard_map/ppermute | solution.py:48
  22.5 12.4 %collective-permute-start.7 = (bf16[320,1152]{1,0:T(8,128)(2,1)S(1)}, bf16[320,1152]{1,0:T(8,128)(2,1)S(1)}, u32[]{:S(2)}, u32[]{:S(2)}) collective-permute-start(bf16[320,1152]{1,0:T(8,128)(2,1)S(1)} %collective-permute-done.5.refs_6_), channel_id=1, source_target_pairs={{0,12},{1,49},{2,14},{3,51},{4,0},{5,53},{6,2},{7,55},{8,4},{9,57}... | collective-permute-start | bytes 2211848 | tf_op jit(solution)/shard_map/ppermute | solution.py:48
  25.7 14.6 %collective-permute-start.10 = (bf16[640,1152]{1,0:T(8,128)(2,1)S(1)}, bf16[640,1152]{1,0:T(8,128)(2,1)S(1)}, u32[]{:S(2)}, u32[]{:S(2)}) collective-permute-start(bf16[640,1152]{1,0:T(8,128)(2,1)S(1)} %pad_maximum_fusion), channel_id=1, source_target_pairs={{0,1},{1,0},{2,3},{3,2},{4,5},{5,4},{6,7},{7,6},{8,9},{9,8},{10,11... | collective-permute-start | bytes 4423688 | tf_op jit(solution)/shard_map/ppermute | solution.py:61
  27.0 11.8 %collective-permute-start.8 = (bf16[320,1152]{1,0:T(8,128)(2,1)S(1)}, bf16[320,1152]{1,0:T(8,128)(2,1)S(1)}, u32[]{:S(2)}, u32[]{:S(2)}) collective-permute-start(bf16[320,1152]{1,0:T(8,128)(2,1)S(1)} %constant_dynamic-update-slice_fusion.refs_5_), channel_id=1, source_target_pairs={{0,2},{1,67},{2,0},{3,65},{4,6},{5,71},{6,4},{7,69},{8,10},{9,75},... | collective-permute-start | bytes 2211848 | tf_op jit(solution)/shard_map/ppermute | solution.py:57
  34.9 6.5 %collective-permute-start.13 = (bf16[640,1152]{1,0:T(8,128)(2,1)S(1)}, bf16[640,1152]{1,0:T(8,128)(2,1)S(1)}, u32[]{:S(2)}, u32[]{:S(2)}) collective-permute-start(bf16[640,1152]{1,0:T(8,128)(2,1)S(1)} %pad_maximum_fusion.1), channel_id=1, source_target_pairs={{0,1},{1,0},{2,3},{3,2},{4,5},{5,4},{6,7},{7,6},{8,9},{9,8},{10,11... | collective-permute-start | bytes 4423688 | tf_op jit(solution)/shard_map/ppermute | solution.py:61
  35.1 5.2 %collective-permute-start.12 = (bf16[320,1152]{1,0:T(8,128)(2,1)S(1)}, bf16[320,1152]{1,0:T(8,128)(2,1)S(1)}, u32[]{:S(2)}, u32[]{:S(2)}) collective-permute-start(bf16[320,1152]{1,0:T(8,128)(2,1)S(1)} %collective-permute-done.5.refs_6_), channel_id=1, source_target_pairs={{0,1},{1,0},{2,3},{3,2},{4,5},{5,4},{6,7},{7,6},{8,9},{9,8},{10,11... | collective-permute-start | bytes 2211848 | tf_op jit(solution)/shard_map/ppermute | solution.py:61
  35.5 4.9 %collective-permute-start.11 = (bf16[320,1152]{1,0:T(8,128)(2,1)S(1)}, bf16[320,1152]{1,0:T(8,128)(2,1)S(1)}, u32[]{:S(2)}, u32[]{:S(2)}) collective-permute-start(bf16[320,1152]{1,0:T(8,128)(2,1)S(1)} %constant_dynamic-update-slice_fusion.refs_5_), channel_id=1, source_target_pairs={{0,1},{1,0},{2,3},{3,2},{4,5},{5,4},{6,7},{7,6},{8,9},{9,8},{10,11... | collective-permute-start | bytes 2211848 | tf_op jit(solution)/shard_map/ppermute | solution.py:61
  38.8 2.7 %collective-permute-start.14 = (bf16[320,1152]{1,0:T(8,128)(2,1)S(1)}, bf16[320,1152]{1,0:T(8,128)(2,1)S(1)}, u32[]{:S(2)}, u32[]{:S(2)}) collective-permute-start(bf16[320,1152]{1,0:T(8,128)(2,1)S(1)} %collective-permute-done.8.refs_9_), channel_id=1, source_target_pairs={{0,1},{1,0},{2,3},{3,2},{4,5},{5,4},{6,7},{7,6},{8,9},{9,8},{10,11... | collective-permute-start | bytes 2211848 | tf_op jit(solution)/shard_map/ppermute | solution.py:61
  56.2 5.7 %collective-permute-start.15 = (bf16[1280,1152]{1,0:T(8,128)(2,1)S(1)}, bf16[1280,1152]{1,0:T(8,128)(2,1)S(1)}, u32[]{:S(2)}, u32[]{:S(2)}) collective-permute-start(bf16[1280,1152]{1,0:T(8,128)(2,1)S(1)} %get-tuple-element.30), channel_id=1, source_target_pairs={{0,1},{1,0},{2,3},{3,2},{4,5},{5,4},{6,7},{7,6},{8,9},{9,8},{10,11... | collective-permute-start | bytes 8847368 | tf_op jit(solution)/shard_map/ppermute | solution.py:61
  67.1 11.1 %collective-permute-start.16 = (bf16[1280,1152]{1,0:T(8,128)(2,1)S(1)}, bf16[1280,1152]{1,0:T(8,128)(2,1)S(1)}, u32[]{:S(2)}, u32[]{:S(2)}) collective-permute-start(bf16[1280,1152]{1,0:T(8,128)(2,1)S(1)} %shard_map.63.refs_8_), channel_id=1, source_target_pairs={{0,1},{1,0},{2,3},{3,2},{4,5},{5,4},{6,7},{7,6},{8,9},{9,8},{10,11... | collective-permute-start | bytes 8847368 | tf_op jit(solution)/shard_map/ppermute | solution.py:61
  67.3 14.4 %collective-permute-start.19 = (bf16[320,1152]{1,0:T(8,128)(2,1)S(1)}, bf16[320,1152]{1,0:T(8,128)(2,1)S(1)}, u32[]{:S(2)}, u32[]{:S(2)}) collective-permute-start(bf16[320,1152]{1,0:T(8,128)(2,1)S(1)} %get-tuple-element.42), channel_id=1, source_target_pairs={{0,12},{1,49},{2,14},{3,51},{4,0},{5,53},{6,2},{7,55},{8,4},{9,57}... | collective-permute-start | bytes 2211848 | tf_op jit(solution)/shard_map/ppermute | solution.py:48
  71.1 11.8 %collective-permute-start.20 = (bf16[320,1152]{1,0:T(8,128)(2,1)S(1)}, bf16[320,1152]{1,0:T(8,128)(2,1)S(1)}, u32[]{:S(2)}, u32[]{:S(2)}) collective-permute-start(bf16[320,1152]{1,0:T(8,128)(2,1)S(1)} %get-tuple-element.43), channel_id=1, source_target_pairs={{0,4},{1,17},{2,6},{3,19},{4,8},{5,21},{6,10},{7,23},{8,12},{9,25}... | collective-permute-start | bytes 2211848 | tf_op jit(solution)/shard_map/ppermute | solution.py:48
  71.1 11.9 %collective-permute-start.21 = (bf16[320,1152]{1,0:T(8,128)(2,1)S(1)}, bf16[320,1152]{1,0:T(8,128)(2,1)S(1)}, u32[]{:S(2)}, u32[]{:S(2)}) collective-permute-start(bf16[320,1152]{1,0:T(8,128)(2,1)S(1)} %get-tuple-element.45), channel_id=1, source_target_pairs={{0,2},{1,67},{2,0},{3,65},{4,6},{5,71},{6,4},{7,69},{8,10},{9,75},... | collective-permute-start | bytes 2211848 | tf_op jit(solution)/shard_map/ppermute | solution.py:57
  79.0 19.1 %collective-permute-start.17 = (bf16[320,1152]{1,0:T(8,128)(2,1)S(1)}, bf16[320,1152]{1,0:T(8,128)(2,1)S(1)}, u32[]{:S(2)}, u32[]{:S(2)}) collective-permute-start(bf16[320,1152]{1,0:T(8,128)(2,1)S(1)} %get-tuple-element.40), channel_id=1, source_target_pairs={{0,12},{1,49},{2,14},{3,51},{4,0},{5,53},{6,2},{7,55},{8,4},{9,57}... | collective-permute-start | bytes 2211848 | tf_op jit(solution)/shard_map/ppermute | solution.py:48
  81.7 19.4 %collective-permute-start.18 = (bf16[320,1152]{1,0:T(8,128)(2,1)S(1)}, bf16[320,1152]{1,0:T(8,128)(2,1)S(1)}, u32[]{:S(2)}, u32[]{:S(2)}) collective-permute-start(bf16[320,1152]{1,0:T(8,128)(2,1)S(1)} %get-tuple-element.41), channel_id=1, source_target_pairs={{0,4},{1,17},{2,6},{3,19},{4,8},{5,21},{6,10},{7,23},{8,12},{9,25}... | collective-permute-start | bytes 2211848 | tf_op jit(solution)/shard_map/ppermute | solution.py:48
  83.4 18.0 %collective-permute-start.22 = (bf16[320,1152]{1,0:T(8,128)(2,1)S(1)}, bf16[320,1152]{1,0:T(8,128)(2,1)S(1)}, u32[]{:S(2)}, u32[]{:S(2)}) collective-permute-start(bf16[320,1152]{1,0:T(8,128)(2,1)S(1)} %get-tuple-element.46), channel_id=1, source_target_pairs={{0,8},{1,33},{2,10},{3,35},{4,12},{5,37},{6,14},{7,39},{8,0},{9,41... | collective-permute-start | bytes 2211848 | tf_op jit(solution)/shard_map/ppermute | solution.py:48
  84.8 16.6 %collective-permute-start.23 = (bf16[320,1152]{1,0:T(8,128)(2,1)S(1)}, bf16[320,1152]{1,0:T(8,128)(2,1)S(1)}, u32[]{:S(2)}, u32[]{:S(2)}) collective-permute-start(bf16[320,1152]{1,0:T(8,128)(2,1)S(1)} %get-tuple-element.47), channel_id=1, source_target_pairs={{0,2},{1,67},{2,0},{3,65},{4,6},{5,71},{6,4},{7,69},{8,10},{9,75},... | collective-permute-start | bytes 2211848 | tf_op jit(solution)/shard_map/ppermute | solution.py:57
  102.3 1.8 %collective-permute-start.24 = (bf16[160,1152]{1,0:T(8,128)(2,1)S(1)}, bf16[160,1152]{1,0:T(8,128)(2,1)S(1)}, u32[]{:S(2)}, u32[]{:S(2)}) collective-permute-start(bf16[160,1152]{1,0:T(8,128)(2,1)S(1)} %get-tuple-element.49), channel_id=1, source_target_pairs={{0,1},{1,0},{2,3},{3,2},{4,5},{5,4},{6,7},{7,6},{8,9},{9,8},{10,11... | collective-permute-start | bytes 1105928 | tf_op jit(solution)/shard_map/ppermute | solution.py:61

commit v5 on v4

--- a/solution.py
+++ b/solution.py
@@ -94,68 +94,144 @@
     return pl.multiple_of(jnp.where(core == 0, half, 1 - half) * rows, rows)
 
 
-def weights_kernel(pieces, scale_ref, core_ref, *refs):
+def spans(count):
+    return [(begin, min(chunk, count - begin)) for begin in range(0, count, chunk)]
+
+
+def weights_of(scale_ref, mine_rows, other_rows, matched=None):
+    dots = lax.dot_general(
+        mine_rows,
+        other_rows,
+        (((1,), (1,)), ((), ())),
+        preferred_element_type=jnp.float32,
+    )
+    power = jnp.exp2(dots * scale_ref[0] + scale_ref[1])
+    share = pl.reciprocal(1.0 + power, approx=True)
+    if matched is not None:
+        row = lax.broadcasted_iota(jnp.int32, dots.shape, 0)
+        column = lax.broadcasted_iota(jnp.int32, dots.shape, 1)
+        share = jnp.where((row == column) & (row < rows) & matched, -power * share, share)
+    return share.astype(jnp.bfloat16)
+
+
+def transposed_dot(weights, values):
+    return lax.dot_general(
+        weights, values, (((0,), (0,)), ((), ())), preferred_element_type=jnp.float32
+    )
+
+
+def early_kernel(half, pieces, scale_ref, core_ref, *refs):
     mine, other = places_of(refs[: pieces[0]]), places_of(refs[pieces[0] : sum(pieces)])
-    weights_ref, far_ref = refs[sum(pieces) :]
+    mine_sum, other_sum, weights_ref = refs[sum(pieces) :]
+    core = core_ref[0]
+    mine_rows = stacked(mine, half * rows)
+    other_rows = stacked(other, opposite_rows(core, half))
     count = len(mine) * rows
+    for begin, size in spans(count):
+        weights_ref[:, pl.ds(begin, size)] = weights_of(
+            scale_ref,
+            mine_rows,
+            other_rows[begin : begin + size],
+            core == 0 if begin == 0 else None,
+        )
+    for begin, size in spans(count):
+        other_sum[pl.ds(begin, size), :] = transposed_dot(
+            weights_ref[:, pl.ds(begin, size)], mine_rows
+        )
+    mine_sum[...] = jnp.dot(
+        weights_ref[...], other_rows, preferred_element_type=jnp.float32
+    )
+
+
+def main_kernel(pieces, scale_ref, core_ref, *refs):
+    mine, other = places_of(refs[: pieces[0]]), places_of(refs[pieces[0] : sum(pieces)])
+    upper_ref, lower_ref, far_ref = refs[sum(pieces) :]
     core = core_ref[0]
-    slope, shift = scale_ref[0], scale_ref[1]
+    near = 4 * rows
     for half in range(2):
         opposite = opposite_rows(core, half)
         mine_rows = stacked(mine, half * rows)
         other_rows = stacked(other, opposite)
-        for begin in range(0, count, chunk):
-            dots = lax.dot_general(
-                mine_rows,
-                other_rows[begin : begin + chunk],
-                (((1,), (1,)), ((), ())),
+        for begin, size in spans(near):
+            upper_ref[half, :, pl.ds(begin, size)] = weights_of(
+                scale_ref,
+                mine_rows[:near],
+                other_rows[near + begin : near + begin + size],
+            )
+        for begin, size in spans(2 * near):
+            lower_ref[half, :, pl.ds(begin, size)] = weights_of(
+                scale_ref, mine_rows[near:], other_rows[begin : begin + size]
+            )
+        for chip in range(0, 4, 2):
+            place = pl.ds(chip * rows, 2 * rows)
+            right = pl.ds(near + chip * rows, 2 * rows)
+            weights = jnp.concatenate(
+                [upper_ref[half, :, place], lower_ref[half, :, right]], axis=0
+            )
+            total = transposed_dot(weights, mine_rows).astype(jnp.bfloat16)
+            for step in range(2):
+                far_ref[pl.ds((chip + step) * chip_rows + opposite, rows), :] = total[
+                    step * rows : (step + 1) * rows
+                ]
+
+
+def far_kernel(pieces, core_ref, lower_ref, *refs):
+    other, sums = places_of(refs[:pieces]), refs[-4:]
+    for half in range(2):
+        other_rows = stacked(other, opposite_rows(core_ref[0], half))
+        for chip in range(0, 4, 2):
+            total = jnp.dot(
+                lower_ref[half, pl.ds(chip * rows, 2 * rows), :],
+                other_rows,
                 preferred_element_type=jnp.float32,
-            )
-            power = jnp.exp2(dots * slope + shift)
-            share = pl.reciprocal(1.0 + power, approx=True)
-            if begin == 0:
-                row = lax.broadcasted_iota(jnp.int32, dots.shape, 0)
-                column = lax.broadcasted_iota(jnp.int32, dots.shape, 1)
-                matched = (row == column) & (row < rows) & (core == 0)
-                share = jnp.where(matched, -power * share, share)
-            weights_ref[half, :, pl.ds(begin, chunk)] = share.astype(jnp.bfloat16)
-        other_sums(weights_ref, half, opposite, mine_rows, 4, far_ref)
-
-
-def other_sums(weights_ref, half, opposite, mine_rows, first, sums_ref):
-    for chip in range(0, 4, 2):
-        total = lax.dot_general(
-            weights_ref[half, :, pl.ds((first + chip) * rows, 2 * rows)],
-            mine_rows,
-            (((0,), (0,)), ((), ())),
-            preferred_element_type=jnp.float32,
-        ).astype(jnp.bfloat16)
-        for step in range(2):
-            place = pl.ds((chip + step) * chip_rows + opposite, rows)
-            sums_ref[place, :] = total[step * rows : (step + 1) * rows]
-
-
-def near_kernel(core_ref, weights_ref, *refs):
-    mine, sums_ref = places_of(refs[:-1]), refs[-1]
+            ).astype(jnp.bfloat16)
+            for step in range(2):
+                sums[chip + step][pl.ds(half * rows, rows), :] = total[
+                    step * rows : (step + 1) * rows
+                ]
+
+
+def near_other_kernel(core_ref, lower_ref, *refs):
+    mine, parts, sums_ref = places_of(refs[:4]), refs[4:6], refs[-1]
     for half in range(2):
         mine_rows = stacked(mine, half * rows)
         opposite = opposite_rows(core_ref[0], half)
-        other_sums(weights_ref, half, opposite, mine_rows, 0, sums_ref)
-
-
-def sums_kernel(pieces, first, core_ref, weights_ref, *refs):
-    other, sums = places_of(refs[:pieces]), refs[-4:]
-    core = core_ref[0]
+        for chip in range(0, 4, 2):
+            place = pl.ds(chip * rows, 2 * rows)
+            total = transposed_dot(lower_ref[half, :, place], mine_rows)
+            total = (total + parts[half][place, :]).astype(jnp.bfloat16)
+            for step in range(2):
+                sums_ref[pl.ds((chip + step) * chip_rows + opposite, rows), :] = total[
+                    step * rows : (step + 1) * rows
+                ]
+
+
+def near_own_kernel(pieces, core_ref, upper_ref, *refs):
+    other, parts, sums = places_of(refs[:pieces]), refs[pieces : pieces + 2], refs[-4:]
     for half in range(2):
-        other_rows = stacked(other, opposite_rows(core, half))
-        for chip in range(0, len(sums), 2):
+        other_rows = stacked(other, opposite_rows(core_ref[0], half))
+        for chip in range(0, 4, 2):
+            place = pl.ds(chip * rows, 2 * rows)
             total = jnp.dot(
-                weights_ref[half, pl.ds((first + chip) * rows, 2 * rows), :],
-                other_rows,
-                preferred_element_type=jnp.float32,
-            ).astype(jnp.bfloat16)
-            sums[chip][pl.ds(half * rows, rows), :] = total[:rows]
-            sums[chip + 1][pl.ds(half * rows, rows), :] = total[rows:]
+                upper_ref[half, place, :], other_rows, preferred_element_type=jnp.float32
+            )
+            total = (total + parts[half][place, :]).astype(jnp.bfloat16)
+            for step in range(2):
+                sums[chip + step][pl.ds(half * rows, rows), :] = total[
+                    step * rows : (step + 1) * rows
+                ]
+
+
+def joined_kernel(*refs):
+    first = 0
+    for ref in refs[:-1]:
+        refs[-1][pl.ds(first, ref.shape[0]), :] = ref[...]
+        first += ref.shape[0]
+
+
+def joined(arrays, after=()):
+    shape = (sum(array.shape[0] for array in arrays), arrays[0].shape[1])
+    return call(joined_kernel, [shape], (), arrays, after=after)[0]
 
 
 def final_kernel(scale_ref, core_ref, raw_ref, *refs):
@@ -176,7 +252,7 @@
     give_ref[...] = jnp.where(first_core, high, low).astype(jnp.bfloat16)
 
 
-def call(kernel, out_shape, scalars, arrays, flops=0, after=()):
+def call(kernel, out_shape, scalars, arrays, flops=0, after=(), scratch=(), kind=jnp.bfloat16):
     used = len(scalars) + len(arrays)
 
     def body(*refs):
@@ -188,8 +264,9 @@
         + [pl.BlockSpec(memory_space=pltpu.VMEM)] * len(arrays)
         + [pl.BlockSpec(memory_space=pl.ANY)] * len(after),
         out_specs=[pl.BlockSpec(memory_space=pltpu.VMEM)] * len(out_shape),
-        out_shape=[jax.ShapeDtypeStruct(shape, jnp.bfloat16) for shape in out_shape],
-        compiler_params=pltpu.CompilerParams(vmem_limit_bytes=26 * 2**20),
+        out_shape=[jax.ShapeDtypeStruct(shape, kind) for shape in out_shape],
+        scratch_shapes=list(scratch),
+        compiler_params=pltpu.CompilerParams(vmem_limit_bytes=8 * 2**20),
         cost_estimate=pl.CostEstimate(
             flops=flops, bytes_accessed=2**20, transcendentals=0
         ),
@@ -204,10 +281,10 @@
         for index, first in group:
             part = inputs[index][pl.ds(first, chip_rows), :].astype(jnp.float32)
             total = part if total is None else total + part
-        sum_ref[...] = total.astype(jnp.bfloat16)
-
-
-def add(groups, after, flops=0):
+        sum_ref[...] = total.astype(sum_ref.dtype)
+
+
+def add(groups, after=(), flops=0, kind=jnp.bfloat16):
     arrays = []
     places = []
     for group in groups:
@@ -226,6 +303,19 @@
         arrays,
         flops,
         after,
+        kind=kind,
+    )
+
+
+def call_main(factors, cores, mine, other, after, quarter):
+    near, width = 4 * rows, mine[0].shape[1]
+    return call(
+        functools.partial(main_kernel, (len(mine), len(other))),
+        [(2, near, near), (2, near, 2 * near), (4 * chip_rows, width)],
+        (factors, cores),
+        (*mine, *other),
+        5 * quarter,
+        (after,),
     )
 
 
@@ -246,69 +336,81 @@
         (keep, got),
     )
     left, right, across = ring(unit, 1), ring(unit, -1), pair(unit)
-    distant = jnp.concatenate([ring(left[:rows], 1), ring(right[rows:], -1)], axis=0)
-    near = [unit, left, right, distant]
-    far = [across, ring(across, 1), ring(across, -1), pair(distant)]
-    mine = near + far
-    other = [
-        swap(unit),
-        swap(jnp.concatenate([left, right], axis=0)),
+    near = [unit, left, right, across]
+    near_other = [swap(joined(near))]
+    halves = [ring(left[:rows], 1), ring(right[rows:], -1)]
+    far_left, far_right = ring(across, 1), ring(across, -1)
+    block = (chip_rows, width)
+    near_block = (4 * rows, width)
+    quarter = 64 * rows * rows * width
+
+    def early(half, after):
+        return call(
+            functools.partial(early_kernel, half, (len(near), len(near_other))),
+            [near_block] * 2,
+            (factors, cores),
+            (*near, *near_other),
+            3 * quarter // 2,
+            after,
+            [pltpu.VMEM((4 * rows, 4 * rows), jnp.bfloat16)],
+            jnp.float32,
+        )
+
+    distant = joined(halves)
+    far_distant = pair(distant)
+    early_low = early(0, (distant,))
+    early_high = early(1, early_low[:1])
+    own_parts, other_parts = zip(early_low, early_high)
+    far = [distant, far_left, far_right, far_distant]
+    far_other = [
         swap(distant),
-        swap(across),
-        swap(jnp.concatenate([far[1], far[2]], axis=0)),
-        swap(far[3]),
+        swap(joined(far[1:3], early_high[:1])),
+        swap(far_distant),
     ]
-    count = len(mine) * rows
-    block = (chip_rows, width)
-    quarter = count * count * width
-    weights, far_other = call(
-        functools.partial(weights_kernel, (len(mine), len(other))),
-        [(2, count, count), (4 * chip_rows, width)],
-        (factors, cores),
-        (*mine, *other),
-        6 * quarter,
-    )
-    far_shared = swap(far_other)
+    mine, other = near + far, near_other + far_other
+    upper, lower, far_back = call_main(factors, cores, mine, other, early_high[0], quarter)
+    far_shared = swap(far_back)
     far_own = call(
-        functools.partial(sums_kernel, len(other), 4),
+        functools.partial(far_kernel, len(other)),
         [block] * 4,
         (cores,),
-        (weights, *other),
+        (lower, *other),
         2 * quarter,
     )
     far_sums = add(
-        [(one, (far_shared, k * chip_rows)) for k, one in enumerate(far_own)], ()
+        [(one, (far_shared, k * chip_rows)) for k, one in enumerate(far_own)]
     )
     arrived = [ring(far_sums[1], -1), ring(far_sums[2], 1), pair(far_sums[3])]
-    (near_other,) = call(
-        near_kernel,
+    (near_back,) = call(
+        near_other_kernel,
         [(4 * chip_rows, width)],
         (cores,),
-        (weights, *mine),
-        2 * quarter,
+        (lower, *far, *other_parts),
+        quarter,
         (far_sums[0],),
     )
-    near_shared = swap(near_other)
+    near_shared = swap(near_back)
     near_own = call(
-        functools.partial(sums_kernel, len(other), 0),
+        functools.partial(near_own_kernel, len(far_other)),
         [block] * 4,
         (cores,),
-        (weights, *other),
-        2 * quarter,
-        (near_other,),
+        (upper, *far_other, *own_parts),
+        quarter,
+        (near_back,),
     )
     near_sums = add(
-        [(one, (near_shared, k * chip_rows)) for k, one in enumerate(near_own)], ()
-    )
-    far_total, distant_total = add(
-        [(far_sums[0], arrived[0], arrived[1]), (near_sums[3], arrived[2])],
+        [(one, (near_shared, k * chip_rows)) for k, one in enumerate(near_own)]
+    )
+    across_total, distant_total = add(
+        [(near_sums[3], arrived[0], arrived[1]), (far_sums[0], arrived[2])],
         (near_sums[0],),
     )
-    late = [ring(distant_total, 2), pair(far_total)]
+    late = [ring(distant_total, 2), pair(across_total)]
     (near_total,) = add(
         [(near_sums[0], ring(near_sums[1], -1), ring(near_sums[2], 1))],
         (),
         16 * quarter,
+        jnp.float32,
     )
     parts = [near_total, *late]
     keep, give = call(

time: 105 us -> 106 us (level)
  starting transfers between devices: 34.6 us -> 25.4 us
  waiting for transfers between devices: 34.3 us -> 40.7 us
  Pallas kernels: 31.4 us -> 35.1 us
    ppermute x11, starting transfers between devices: 18.4 us -> 13.5 us  [ring(): return lax.ppermute(value, axes, ring_move(steps))]
    pallas_call x10 -> x15, Pallas kernels: 31.4 us -> 35.1 us  [call(): pl.pallas_call(body, in_specs=[pl.BlockSpec(memory_space=pltpu.SMEM)] * l...]
    ppermute x4, waiting for transfers between devices: 3.24 us -> 6.83 us  [pair(): return lax.ppermute(value, axes, pairs_of(move))]
    ppermute x4, starting transfers between devices: 11 us -> 7.5 us  [pair(): return lax.ppermute(value, axes, pairs_of(move))]
    ppermute x10 -> x8, waiting for transfers between devices: 4.76 us -> 8.1 us  [swap(): return lax.ppermute(value, 'core', [(0, 1), (1, 0)])]
    ppermute x10 -> x8, starting transfers between devices: 5.12 us -> 4.4 us  [swap(): return lax.ppermute(value, 'core', [(0, 1), (1, 0)])]
  transfers between devices with their start and end apart: 25 -> 23, of which waited for: 14 -> 16; matrix products, arithmetic and copies ran while one was open for 0% -> 0% of each run, Pallas kernels for 10% -> 17%
where the time goes in v5:
time: 106 us
  waiting for transfers between devices  40.7 us (38%)
  Pallas kernels  35.1 us (33%)
  starting transfers between devices  25.4 us (24%)
  other arithmetic  2.18 us (2%)
  between operations  2.14 us (2%)
    pallas_call x15, Pallas kernels, call(): pl.pallas_call(body, in_specs=[pl.BlockSpec(memory_space=pltpu.SMEM)] * l...  35.1 us
    ppermute x11, waiting for transfers between devices, ring(): return lax.ppermute(value, axes, ring_move(steps))  25.8 us
    ppermute x11, starting transfers between devices, ring(): return lax.ppermute(value, axes, ring_move(steps))  13.5 us
    ppermute x8, waiting for transfers between devices, swap(): return lax.ppermute(value, 'core', [(0, 1), (1, 0)])  8.1 us
    ppermute x4, starting transfers between devices, pair(): return lax.ppermute(value, axes, pairs_of(move))  7.5 us
    ppermute x4, waiting for transfers between devices, pair(): return lax.ppermute(value, axes, pairs_of(move))  6.83 us
    ppermute x8, starting transfers between devices, swap(): return lax.ppermute(value, 'core', [(0, 1), (1, 0)])  4.4 us
  transfers between devices with their start and end apart: 23, of which 16 were waited for; matrix products, arithmetic and copies ran while one was open for 0% of the time, Pallas kernels for 17%

profile of v5, /device:TPU:1, one launch (start us, length us, event | category | flops | bytes accessed | tf_op | source)
XLA Modules:
  0.0 105.5 jit_solution(16518042444192109)
XLA Ops:
  0.6 1.2 %broadcast_select_fusion.2 = (bf16[160,1152]{1,0:T(8,128)(2,1)S(1)}, bf16[160,1152]{1,0:T(8,128)(2,1)S(1)}) fusion(bf16[160,1152]{1,0:T(8,128)(2,1)} %param.5, bf16[160,1152]{1,0:T(8,128)(2,1)} %param.4, pred[]{:T(512)S(6)} %eq.3), kind=kLoop, calls=%fused_computation.2 | loop fusion | flops 368640 | bytes 1474561 | tf_op jit(solution)/shard_map/jit(_where)/select_n | solution.py:329
  1.8 1.5 %collective-permute-start = (bf16[160,1152]{1,0:T(8,128)(2,1)S(1)}, bf16[160,1152]{1,0:T(8,128)(2,1)S(1)}, u32[]{:S(2)}, u32[]{:S(2)}) collective-permute-start(bf16[160,1152]{1,0:T(8,128)(2,1)S(1)} %get-tuple-element.62), channel_id=1, source_target_pairs={{0,1},{1,0},{2,3},{3,2},{4,5},{5,4},{6,7},{7,6},{8,9},{9,8},{10,11... | collective-permute-start | bytes 1105928 | tf_op jit(solution)/shard_map/ppermute | solution.py:61
  3.3 1.3 %collective-permute-done.refs_2_ = bf16[160,1152]{1,0:T(8,128)(2,1)S(1)} collective-permute-done((bf16[160,1152]{1,0:T(8,128)(2,1)S(1)}, bf16[160,1152]{1,0:T(8,128)(2,1)S(1)}, u32[]{:S(2)}, u32[]{:S(2)}) %collective-permute-start) | collective-permute-done | bytes 368672 | tf_op jit(solution)/shard_map/ppermute | solution.py:61
  4.6 0.4 shard_map.59
  5.0 2.9 %collective-permute-start.3 = (bf16[320,1152]{1,0:T(8,128)(2,1)S(1)}, bf16[320,1152]{1,0:T(8,128)(2,1)S(1)}, u32[]{:S(2)}, u32[]{:S(2)}) collective-permute-start(bf16[320,1152]{1,0:T(8,128)(2,1)S(1)} %get-tuple-element.32.refs_0_.refs_2_), channel_id=1, source_target_pairs={{0,2},{1,67},{2,0},{3,65},{4,6},{5,71},{6,4},{7,69},{8,10},{9,75},... | collective-permute-start | bytes 2211848 | tf_op jit(solution)/shard_map/ppermute | solution.py:57
  7.9 3.8 %collective-permute-start.2 = (bf16[320,1152]{1,0:T(8,128)(2,1)S(1)}, bf16[320,1152]{1,0:T(8,128)(2,1)S(1)}, u32[]{:S(2)}, u32[]{:S(2)}) collective-permute-start(bf16[320,1152]{1,0:T(8,128)(2,1)S(1)} %get-tuple-element.32.refs_0_.refs_2_), channel_id=1, source_target_pairs={{0,12},{1,49},{2,14},{3,51},{4,0},{5,53},{6,2},{7,55},{8,4},{9,57}... | collective-permute-start | bytes 2211848 | tf_op jit(solution)/shard_map/ppermute | solution.py:48
  11.7 0.0 collective-permute-start.1
  11.7 5.4 %collective-permute-done.3.refs_3_.refs_5_ = bf16[320,1152]{1,0:T(8,128)(2,1)S(1)} collective-permute-done((bf16[320,1152]{1,0:T(8,128)(2,1)S(1)}, bf16[320,1152]{1,0:T(8,128)(2,1)S(1)}, u32[]{:S(2)}, u32[]{:S(2)}) %collective-permute-start.3) | collective-permute-done | bytes 737312 | tf_op jit(solution)/shard_map/ppermute | solution.py:57
  17.1 3.0 %collective-permute-done.2.refs_2_.refs_4_ = bf16[320,1152]{1,0:T(8,128)(2,1)S(1)} collective-permute-done((bf16[320,1152]{1,0:T(8,128)(2,1)S(1)}, bf16[320,1152]{1,0:T(8,128)(2,1)S(1)}, u32[]{:S(2)}, u32[]{:S(2)}) %collective-permute-start.2) | collective-permute-done | bytes 737312 | tf_op jit(solution)/shard_map/ppermute | solution.py:48
  20.1 3.1 %collective-permute-done.1.refs_1_.refs_3_ = bf16[320,1152]{1,0:T(8,128)(2,1)S(1)} collective-permute-done((bf16[320,1152]{1,0:T(8,128)(2,1)S(1)}, bf16[320,1152]{1,0:T(8,128)(2,1)S(1)}, u32[]{:S(2)}, u32[]{:S(2)}) %collective-permute-start.1) | collective-permute-done | bytes 737312 | tf_op jit(solution)/shard_map/ppermute | solution.py:48
  23.2 0.2 shard_map.61
  23.4 0.1 collective-permute-start.9
  23.5 3.2 %collective-permute-start.5 = (bf16[160,1152]{1,0:T(8,128)(2,1)S(1)}, bf16[160,1152]{1,0:T(8,128)(2,1)S(1)}, u32[]{:S(2)}, u32[]{:S(2)}) collective-permute-start(bf16[160,1152]{1,0:T(8,128)(2,1)S(1)} %slice.9), channel_id=1, source_target_pairs={{0,12},{1,49},{2,14},{3,51},{4,0},{5,53},{6,2},{7,55},{8,4},{9,57}... | collective-permute-start | bytes 1105928 | tf_op jit(solution)/shard_map/ppermute | solution.py:48
  26.7 0.1 collective-permute-start.4
  26.8 2.7 %collective-permute-start.7 = (bf16[320,1152]{1,0:T(8,128)(2,1)S(1)}, bf16[320,1152]{1,0:T(8,128)(2,1)S(1)}, u32[]{:S(2)}, u32[]{:S(2)}) collective-permute-start(bf16[320,1152]{1,0:T(8,128)(2,1)S(1)} %collective-permute-done.3.refs_3_.refs_5_), channel_id=1, source_target_pairs={{0,12},{1,49},{2,14},{3,51},{4,0},{5,53},{6,2},{7,55},{8,4},{9,57}... | collective-permute-start | bytes 2211848 | tf_op jit(solution)/shard_map/ppermute | solution.py:48
  29.5 0.0 collective-permute-start.6
  30.8 0.1 pad_maximum_fusion.refs_0_
  30.9 0.3 collective-permute-done.5.refs_1_
  31.2 3.5 %collective-permute-done.4.refs_0_ = bf16[160,1152]{1,0:T(8,128)(2,1)S(1)} collective-permute-done((bf16[160,1152]{1,0:T(8,128)(2,1)S(1)}, bf16[160,1152]{1,0:T(8,128)(2,1)S(1)}, u32[]{:S(2)}, u32[]{:S(2)}) %collective-permute-start.4) | collective-permute-done | bytes 368672 | tf_op jit(solution)/shard_map/ppermute | solution.py:48
  34.7 0.1 shard_map.60.refs_7_.refs_6_.refs_2_
  34.7 2.0 %collective-permute-start.8 = (bf16[320,1152]{1,0:T(8,128)(2,1)S(1)}, bf16[320,1152]{1,0:T(8,128)(2,1)S(1)}, u32[]{:S(2)}, u32[]{:S(2)}) collective-permute-start(bf16[320,1152]{1,0:T(8,128)(2,1)S(1)} %shard_map.60.refs_7_.refs_6_.refs_2_), channel_id=1, source_target_pairs={{0,2},{1,67},{2,0},{3,65},{4,6},{5,71},{6,4},{7,69},{8,10},{9,75},... | collective-permute-start | bytes 2211848 | tf_op jit(solution)/shard_map/ppermute | solution.py:57
  36.7 0.0 collective-permute-done.9.refs_6_.refs_10_.refs_2_
  36.7 4.6 %shard_map.62 = (f32[640,1152]{1,0:T(8,128)S(1)}, f32[640,1152]{1,0:T(8,128)S(1)}) custom-call(f32[2]{0:T(128)S(1)} %pad_maximum_fusion.refs_0_, s32[1]{0:T(128)} %bitcast.refs_0_.refs_1_, bf16[320,1152]{1,0:T(8,128)(2,1)S(1)} %get-tuple-element.32.refs_0_.refs_2_, bf16[320,1152]{1,0:T(8,128)(2,1)S(1)} %collective-permute-done.1.refs_1_.refs_3_, ...), custom_call_target="tpu_custom_call" | custom-call | flops 2831155200 | bytes 1048576 | tf_op jit(solution)/shard_map/pallas_call | solution.py:261
  41.4 4.6 %shard_map.63 = (f32[640,1152]{1,0:T(8,128)S(1)}, f32[640,1152]{1,0:T(8,128)S(1)}) custom-call(f32[2]{0:T(128)S(1)} %pad_maximum_fusion.refs_0_, s32[1]{0:T(128)} %bitcast.refs_0_.refs_1_, bf16[320,1152]{1,0:T(8,128)(2,1)S(1)} %get-tuple-element.32.refs_0_.refs_2_, bf16[320,1152]{1,0:T(8,128)(2,1)S(1)} %collective-permute-done.1.refs_1_.refs_3_, ...), custom_call_target="tpu_custom_call" | custom-call | flops 2831155200 | bytes 1048576 | tf_op jit(solution)/shard_map/pallas_call | solution.py:261
  46.0 0.0 collective-permute-done.7.refs_1_.refs_8_.refs_4_
  46.0 0.0 collective-permute-done.6.refs_0_.refs_7_.refs_3_
  46.0 0.1 shard_map.64
  46.2 0.1 collective-permute-start.11
  46.3 0.5 collective-permute-start.10
  46.8 0.0 collective-permute-done.8.refs_9_.refs_5_
  46.8 0.5 collective-permute-start.12
  47.3 3.3 %collective-permute-done.10.refs_11_.refs_3_.refs_2_ = bf16[320,1152]{1,0:T(8,128)(2,1)S(1)} collective-permute-done((bf16[320,1152]{1,0:T(8,128)(2,1)S(1)}, bf16[320,1152]{1,0:T(8,128)(2,1)S(1)}, u32[]{:S(2)}, u32[]{:S(2)}) %collective-permute-start.10) | collective-permute-done | bytes 737312 | tf_op jit(solution)/shard_map/ppermute | solution.py:61
  50.6 1.1 collective-permute-done.12.refs_13_.refs_5_.refs_4_
  51.6 0.0 collective-permute-done.11.refs_12_.refs_4_.refs_3_
  51.6 12.2 %shard_map.65 = (bf16[2,640,640]{2,1,0:T(8,128)(2,1)S(1)}, bf16[2,640,1280]{2,1,0:T(8,128)(2,1)S(1)}, bf16[1280,1152]{1,0:T(8,128)(2,1)S(1)}) custom-call(f32[2]{0:T(128)S(1)} %pad_maximum_fusion.refs_0_, s32[1]{0:T(128)} %bitcast.refs_0_.refs_1_, bf16[320,1152]{1,0:T(8,128)(2,1)S(1)} %get-tuple-element.32.refs_0_.refs_2_, ...), custom_call_target="tpu_custom_call" | custom-call | flops 9437184000 | bytes 1048576 | tf_op jit(solution)/shard_map/pallas_call | solution.py:261
  63.9 0.4 collective-permute-start.13
  64.3 4.4 %shard_map.66 = (bf16[320,1152]{1,0:T(8,128)(2,1)S(1)}, bf16[320,1152]{1,0:T(8,128)(2,1)S(1)}, bf16[320,1152]{1,0:T(8,128)(2,1)S(1)}, bf16[320,1152]{1,0:T(8,128)(2,1)S(1)}) custom-call(s32[1]{0:T(128)} %bitcast.refs_0_.refs_1_, bf16[2,640,1280]{2,1,0:T(8,128)(2,1)S(1)} %get-tuple-element.36.refs_1_, ...), custom_call_target="tpu_custom_call" | custom-call | flops 3774873600 | bytes 1048576 | tf_op jit(solution)/shard_map/pallas_call | solution.py:261
  68.7 0.8 collective-permute-done.13.refs_1_
  69.5 0.8 shard_map.67
  70.3 2.7 %shard_map.68.refs_7_ = bf16[1280,1152]{1,0:T(8,128)(2,1)S(1)} custom-call(s32[1]{0:T(128)} %bitcast.refs_0_.refs_1_, bf16[2,640,1280]{2,1,0:T(8,128)(2,1)S(1)} %get-tuple-element.36.refs_1_, bf16[320,1152]{1,0:T(8,128)(2,1)S(1)} %shard_map.60.refs_7_.refs_6_.refs_2_, bf16[320,1152]{1,0:T(8,128)(2,1)S(1)} %collective-permute-done.6.refs_0_.refs_7_.refs_3_, ...), custom_call_target="tpu_custom_call" | custom-call | flops 1887436800 | bytes 1048576 | tf_op jit(solution)/shard_map/pallas_call | solution.py:261
  73.0 0.2 collective-permute-start.14
  73.3 0.0 collective-permute-start.17
  73.3 1.5 %collective-permute-start.18 = (bf16[320,1152]{1,0:T(8,128)(2,1)S(1)}, bf16[320,1152]{1,0:T(8,128)(2,1)S(1)}, u32[]{:S(2)}, u32[]{:S(2)}) collective-permute-start(bf16[320,1152]{1,0:T(8,128)(2,1)S(1)} %get-tuple-element.54), channel_id=1, source_target_pairs={{0,4},{1,17},{2,6},{3,19},{4,8},{5,21},{6,10},{7,23},{8,12},{9,25}... | collective-permute-start | bytes 2211848 | tf_op jit(solution)/shard_map/ppermute | solution.py:48
  74.7 0.8 collective-permute-start.19
  75.5 2.7 %shard_map.69 = (bf16[320,1152]{1,0:T(8,128)(2,1)S(1)}, bf16[320,1152]{1,0:T(8,128)(2,1)S(1)}, bf16[320,1152]{1,0:T(8,128)(2,1)S(1)}, bf16[320,1152]{1,0:T(8,128)(2,1)S(1)}) custom-call(s32[1]{0:T(128)} %bitcast.refs_0_.refs_1_, bf16[2,640,640]{2,1,0:T(8,128)(2,1)S(1)} %get-tuple-element.35.refs_1_, ...), custom_call_target="tpu_custom_call" | custom-call | flops 1887436800 | bytes 1048576 | tf_op jit(solution)/shard_map/pallas_call | solution.py:261
  78.2 0.3 collective-permute-done.14.refs_1_
  78.5 0.7 shard_map.70
  79.2 2.2 %collective-permute-start.15 = (bf16[320,1152]{1,0:T(8,128)(2,1)S(1)}, bf16[320,1152]{1,0:T(8,128)(2,1)S(1)}, u32[]{:S(2)}, u32[]{:S(2)}) collective-permute-start(bf16[320,1152]{1,0:T(8,128)(2,1)S(1)} %get-tuple-element.50), channel_id=1, source_target_pairs={{0,12},{1,49},{2,14},{3,51},{4,0},{5,53},{6,2},{7,55},{8,4},{9,57}... | collective-permute-start | bytes 2211848 | tf_op jit(solution)/shard_map/ppermute | solution.py:48
  81.4 0.0 collective-permute-start.16
  81.4 2.5 %collective-permute-done.17.refs_1_ = bf16[320,1152]{1,0:T(8,128)(2,1)S(1)} collective-permute-done((bf16[320,1152]{1,0:T(8,128)(2,1)S(1)}, bf16[320,1152]{1,0:T(8,128)(2,1)S(1)}, u32[]{:S(2)}, u32[]{:S(2)}) %collective-permute-start.17) | collective-permute-done | bytes 737312 | tf_op jit(solution)/shard_map/ppermute | solution.py:48
  83.9 1.2 %collective-permute-done.18.refs_2_ = bf16[320,1152]{1,0:T(8,128)(2,1)S(1)} collective-permute-done((bf16[320,1152]{1,0:T(8,128)(2,1)S(1)}, bf16[320,1152]{1,0:T(8,128)(2,1)S(1)}, u32[]{:S(2)}, u32[]{:S(2)}) %collective-permute-start.18) | collective-permute-done | bytes 737312 | tf_op jit(solution)/shard_map/ppermute | solution.py:48
  85.1 1.4 %collective-permute-done.19.refs_4_ = bf16[320,1152]{1,0:T(8,128)(2,1)S(1)} collective-permute-done((bf16[320,1152]{1,0:T(8,128)(2,1)S(1)}, bf16[320,1152]{1,0:T(8,128)(2,1)S(1)}, u32[]{:S(2)}, u32[]{:S(2)}) %collective-permute-start.19) | collective-permute-done | bytes 737312 | tf_op jit(solution)/shard_map/ppermute | solution.py:57
  86.5 0.5 shard_map.72
  87.0 0.1 collective-permute-start.20
  87.1 1.9 %collective-permute-start.21 = (bf16[320,1152]{1,0:T(8,128)(2,1)S(1)}, bf16[320,1152]{1,0:T(8,128)(2,1)S(1)}, u32[]{:S(2)}, u32[]{:S(2)}) collective-permute-start(bf16[320,1152]{1,0:T(8,128)(2,1)S(1)} %get-tuple-element.57), channel_id=1, source_target_pairs={{0,2},{1,67},{2,0},{3,65},{4,6},{5,71},{6,4},{7,69},{8,10},{9,75},... | collective-permute-start | bytes 2211848 | tf_op jit(solution)/shard_map/ppermute | solution.py:57
  89.0 2.8 %collective-permute-done.15.refs_1_ = bf16[320,1152]{1,0:T(8,128)(2,1)S(1)} collective-permute-done((bf16[320,1152]{1,0:T(8,128)(2,1)S(1)}, bf16[320,1152]{1,0:T(8,128)(2,1)S(1)}, u32[]{:S(2)}, u32[]{:S(2)}) %collective-permute-start.15) | collective-permute-done | bytes 737312 | tf_op jit(solution)/shard_map/ppermute | solution.py:48
  91.8 9.4 %collective-permute-done.16.refs_2_ = bf16[320,1152]{1,0:T(8,128)(2,1)S(1)} collective-permute-done((bf16[320,1152]{1,0:T(8,128)(2,1)S(1)}, bf16[320,1152]{1,0:T(8,128)(2,1)S(1)}, u32[]{:S(2)}, u32[]{:S(2)}) %collective-permute-start.16) | collective-permute-done | bytes 737312 | tf_op jit(solution)/shard_map/ppermute | solution.py:48
  101.1 0.3 shard_map.71.refs_3_
  101.4 0.0 collective-permute-done.20.refs_4_
  101.4 0.0 collective-permute-done.21.refs_5_
  101.4 0.8 shard_map.73
  102.2 1.1 %collective-permute-start.22 = (bf16[160,1152]{1,0:T(8,128)(2,1)S(1)}, bf16[160,1152]{1,0:T(8,128)(2,1)S(1)}, u32[]{:S(2)}, u32[]{:S(2)}) collective-permute-start(bf16[160,1152]{1,0:T(8,128)(2,1)S(1)} %get-tuple-element.59), channel_id=1, source_target_pairs={{0,1},{1,0},{2,3},{3,2},{4,5},{5,4},{6,7},{7,6},{8,9},{9,8},{10,11... | collective-permute-start | bytes 1105928 | tf_op jit(solution)/shard_map/ppermute | solution.py:61
  103.3 1.3 %collective-permute-done.22 = bf16[160,1152]{1,0:T(8,128)(2,1)S(1)} collective-permute-done((bf16[160,1152]{1,0:T(8,128)(2,1)S(1)}, bf16[160,1152]{1,0:T(8,128)(2,1)S(1)}, u32[]{:S(2)}, u32[]{:S(2)}) %collective-permute-start.22) | collective-permute-done | bytes 368672 | tf_op jit(solution)/shard_map/ppermute | solution.py:61
  104.6 0.9 broadcast_select_fusion
  (2 shorter events, 0.1 us)
Async XLA Ops:
  1.8 2.8 %collective-permute-start = (bf16[160,1152]{1,0:T(8,128)(2,1)S(1)}, bf16[160,1152]{1,0:T(8,128)(2,1)S(1)}, u32[]{:S(2)}, u32[]{:S(2)}) collective-permute-start(bf16[160,1152]{1,0:T(8,128)(2,1)S(1)} %get-tuple-element.62), channel_id=1, source_target_pairs={{0,1},{1,0},{2,3},{3,2},{4,5},{5,4},{6,7},{7,6},{8,9},{9,8},{10,11... | collective-permute-start | bytes 1105928 | tf_op jit(solution)/shard_map/ppermute | solution.py:61
  5.0 12.0 %collective-permute-start.3 = (bf16[320,1152]{1,0:T(8,128)(2,1)S(1)}, bf16[320,1152]{1,0:T(8,128)(2,1)S(1)}, u32[]{:S(2)}, u32[]{:S(2)}) collective-permute-start(bf16[320,1152]{1,0:T(8,128)(2,1)S(1)} %get-tuple-element.32.refs_0_.refs_2_), channel_id=1, source_target_pairs={{0,2},{1,67},{2,0},{3,65},{4,6},{5,71},{6,4},{7,69},{8,10},{9,75},... | collective-permute-start | bytes 2211848 | tf_op jit(solution)/shard_map/ppermute | solution.py:57
  7.9 12.2 %collective-permute-start.2 = (bf16[320,1152]{1,0:T(8,128)(2,1)S(1)}, bf16[320,1152]{1,0:T(8,128)(2,1)S(1)}, u32[]{:S(2)}, u32[]{:S(2)}) collective-permute-start(bf16[320,1152]{1,0:T(8,128)(2,1)S(1)} %get-tuple-element.32.refs_0_.refs_2_), channel_id=1, source_target_pairs={{0,12},{1,49},{2,14},{3,51},{4,0},{5,53},{6,2},{7,55},{8,4},{9,57}... | collective-permute-start | bytes 2211848 | tf_op jit(solution)/shard_map/ppermute | solution.py:48
  11.7 11.5 %collective-permute-start.1 = (bf16[320,1152]{1,0:T(8,128)(2,1)S(1)}, bf16[320,1152]{1,0:T(8,128)(2,1)S(1)}, u32[]{:S(2)}, u32[]{:S(2)}) collective-permute-start(bf16[320,1152]{1,0:T(8,128)(2,1)S(1)} %get-tuple-element.32.refs_0_.refs_2_), channel_id=1, source_target_pairs={{0,4},{1,17},{2,6},{3,19},{4,8},{5,21},{6,10},{7,23},{8,12},{9,25}... | collective-permute-start | bytes 2211848 | tf_op jit(solution)/shard_map/ppermute | solution.py:48
  23.4 13.3 %collective-permute-start.9 = (bf16[1280,1152]{1,0:T(8,128)(2,1)S(1)}, bf16[1280,1152]{1,0:T(8,128)(2,1)S(1)}, u32[]{:S(2)}, u32[]{:S(2)}) collective-permute-start(bf16[1280,1152]{1,0:T(8,128)(2,1)S(1)} %shard_map.61), channel_id=1, source_target_pairs={{0,1},{1,0},{2,3},{3,2},{4,5},{5,4},{6,7},{7,6},{8,9},{9,8},{10,11... | collective-permute-start | bytes 8847368 | tf_op jit(solution)/shard_map/ppermute | solution.py:61
  23.5 7.6 %collective-permute-start.5 = (bf16[160,1152]{1,0:T(8,128)(2,1)S(1)}, bf16[160,1152]{1,0:T(8,128)(2,1)S(1)}, u32[]{:S(2)}, u32[]{:S(2)}) collective-permute-start(bf16[160,1152]{1,0:T(8,128)(2,1)S(1)} %slice.9), channel_id=1, source_target_pairs={{0,12},{1,49},{2,14},{3,51},{4,0},{5,53},{6,2},{7,55},{8,4},{9,57}... | collective-permute-start | bytes 1105928 | tf_op jit(solution)/shard_map/ppermute | solution.py:48
  26.7 7.9 %collective-permute-start.4 = (bf16[160,1152]{1,0:T(8,128)(2,1)S(1)}, bf16[160,1152]{1,0:T(8,128)(2,1)S(1)}, u32[]{:S(2)}, u32[]{:S(2)}) collective-permute-start(bf16[160,1152]{1,0:T(8,128)(2,1)S(1)} %slice.8), channel_id=1, source_target_pairs={{0,4},{1,17},{2,6},{3,19},{4,8},{5,21},{6,10},{7,23},{8,12},{9,25}... | collective-permute-start | bytes 1105928 | tf_op jit(solution)/shard_map/ppermute | solution.py:48
  26.8 19.2 %collective-permute-start.7 = (bf16[320,1152]{1,0:T(8,128)(2,1)S(1)}, bf16[320,1152]{1,0:T(8,128)(2,1)S(1)}, u32[]{:S(2)}, u32[]{:S(2)}) collective-permute-start(bf16[320,1152]{1,0:T(8,128)(2,1)S(1)} %collective-permute-done.3.refs_3_.refs_5_), channel_id=1, source_target_pairs={{0,12},{1,49},{2,14},{3,51},{4,0},{5,53},{6,2},{7,55},{8,4},{9,57}... | collective-permute-start | bytes 2211848 | tf_op jit(solution)/shard_map/ppermute | solution.py:48
  29.5 16.5 %collective-permute-start.6 = (bf16[320,1152]{1,0:T(8,128)(2,1)S(1)}, bf16[320,1152]{1,0:T(8,128)(2,1)S(1)}, u32[]{:S(2)}, u32[]{:S(2)}) collective-permute-start(bf16[320,1152]{1,0:T(8,128)(2,1)S(1)} %collective-permute-done.3.refs_3_.refs_5_), channel_id=1, source_target_pairs={{0,4},{1,17},{2,6},{3,19},{4,8},{5,21},{6,10},{7,23},{8,12},{9,25}... | collective-permute-start | bytes 2211848 | tf_op jit(solution)/shard_map/ppermute | solution.py:48
  34.7 12.0 %collective-permute-start.8 = (bf16[320,1152]{1,0:T(8,128)(2,1)S(1)}, bf16[320,1152]{1,0:T(8,128)(2,1)S(1)}, u32[]{:S(2)}, u32[]{:S(2)}) collective-permute-start(bf16[320,1152]{1,0:T(8,128)(2,1)S(1)} %shard_map.60.refs_7_.refs_6_.refs_2_), channel_id=1, source_target_pairs={{0,2},{1,67},{2,0},{3,65},{4,6},{5,71},{6,4},{7,69},{8,10},{9,75},... | collective-permute-start | bytes 2211848 | tf_op jit(solution)/shard_map/ppermute | solution.py:57
  46.2 5.5 %collective-permute-start.11 = (bf16[640,1152]{1,0:T(8,128)(2,1)S(1)}, bf16[640,1152]{1,0:T(8,128)(2,1)S(1)}, u32[]{:S(2)}, u32[]{:S(2)}) collective-permute-start(bf16[640,1152]{1,0:T(8,128)(2,1)S(1)} %shard_map.64), channel_id=1, source_target_pairs={{0,1},{1,0},{2,3},{3,2},{4,5},{5,4},{6,7},{7,6},{8,9},{9,8},{10,11... | collective-permute-start | bytes 4423688 | tf_op jit(solution)/shard_map/ppermute | solution.py:61
  46.3 4.3 %collective-permute-start.10 = (bf16[320,1152]{1,0:T(8,128)(2,1)S(1)}, bf16[320,1152]{1,0:T(8,128)(2,1)S(1)}, u32[]{:S(2)}, u32[]{:S(2)}) collective-permute-start(bf16[320,1152]{1,0:T(8,128)(2,1)S(1)} %shard_map.60.refs_7_.refs_6_.refs_2_), channel_id=1, source_target_pairs={{0,1},{1,0},{2,3},{3,2},{4,5},{5,4},{6,7},{7,6},{8,9},{9,8},{10,11... | collective-permute-start | bytes 2211848 | tf_op jit(solution)/shard_map/ppermute | solution.py:61
  46.8 4.9 %collective-permute-start.12 = (bf16[320,1152]{1,0:T(8,128)(2,1)S(1)}, bf16[320,1152]{1,0:T(8,128)(2,1)S(1)}, u32[]{:S(2)}, u32[]{:S(2)}) collective-permute-start(bf16[320,1152]{1,0:T(8,128)(2,1)S(1)} %collective-permute-done.8.refs_9_.refs_5_), channel_id=1, source_target_pairs={{0,1},{1,0},{2,3},{3,2},{4,5},{5,4},{6,7},{7,6},{8,9},{9,8},{10,11... | collective-permute-start | bytes 2211848 | tf_op jit(solution)/shard_map/ppermute | solution.py:61
  63.9 5.7 %collective-permute-start.13 = (bf16[1280,1152]{1,0:T(8,128)(2,1)S(1)}, bf16[1280,1152]{1,0:T(8,128)(2,1)S(1)}, u32[]{:S(2)}, u32[]{:S(2)}) collective-permute-start(bf16[1280,1152]{1,0:T(8,128)(2,1)S(1)} %get-tuple-element.40), channel_id=1, source_target_pairs={{0,1},{1,0},{2,3},{3,2},{4,5},{5,4},{6,7},{7,6},{8,9},{9,8},{10,11... | collective-permute-start | bytes 8847368 | tf_op jit(solution)/shard_map/ppermute | solution.py:61
  73.0 5.5 %collective-permute-start.14 = (bf16[1280,1152]{1,0:T(8,128)(2,1)S(1)}, bf16[1280,1152]{1,0:T(8,128)(2,1)S(1)}, u32[]{:S(2)}, u32[]{:S(2)}) collective-permute-start(bf16[1280,1152]{1,0:T(8,128)(2,1)S(1)} %shard_map.68.refs_7_), channel_id=1, source_target_pairs={{0,1},{1,0},{2,3},{3,2},{4,5},{5,4},{6,7},{7,6},{8,9},{9,8},{10,11... | collective-permute-start | bytes 8847368 | tf_op jit(solution)/shard_map/ppermute | solution.py:61
  73.3 10.6 %collective-permute-start.17 = (bf16[320,1152]{1,0:T(8,128)(2,1)S(1)}, bf16[320,1152]{1,0:T(8,128)(2,1)S(1)}, u32[]{:S(2)}, u32[]{:S(2)}) collective-permute-start(bf16[320,1152]{1,0:T(8,128)(2,1)S(1)} %get-tuple-element.53), channel_id=1, source_target_pairs={{0,12},{1,49},{2,14},{3,51},{4,0},{5,53},{6,2},{7,55},{8,4},{9,57}... | collective-permute-start | bytes 2211848 | tf_op jit(solution)/shard_map/ppermute | solution.py:48
  73.3 11.8 %collective-permute-start.18 = (bf16[320,1152]{1,0:T(8,128)(2,1)S(1)}, bf16[320,1152]{1,0:T(8,128)(2,1)S(1)}, u32[]{:S(2)}, u32[]{:S(2)}) collective-permute-start(bf16[320,1152]{1,0:T(8,128)(2,1)S(1)} %get-tuple-element.54), channel_id=1, source_target_pairs={{0,4},{1,17},{2,6},{3,19},{4,8},{5,21},{6,10},{7,23},{8,12},{9,25}... | collective-permute-start | bytes 2211848 | tf_op jit(solution)/shard_map/ppermute | solution.py:48
  74.7 11.8 %collective-permute-start.19 = (bf16[320,1152]{1,0:T(8,128)(2,1)S(1)}, bf16[320,1152]{1,0:T(8,128)(2,1)S(1)}, u32[]{:S(2)}, u32[]{:S(2)}) collective-permute-start(bf16[320,1152]{1,0:T(8,128)(2,1)S(1)} %get-tuple-element.55), channel_id=1, source_target_pairs={{0,2},{1,67},{2,0},{3,65},{4,6},{5,71},{6,4},{7,69},{8,10},{9,75},... | collective-permute-start | bytes 2211848 | tf_op jit(solution)/shard_map/ppermute | solution.py:57
  79.2 12.6 %collective-permute-start.15 = (bf16[320,1152]{1,0:T(8,128)(2,1)S(1)}, bf16[320,1152]{1,0:T(8,128)(2,1)S(1)}, u32[]{:S(2)}, u32[]{:S(2)}) collective-permute-start(bf16[320,1152]{1,0:T(8,128)(2,1)S(1)} %get-tuple-element.50), channel_id=1, source_target_pairs={{0,12},{1,49},{2,14},{3,51},{4,0},{5,53},{6,2},{7,55},{8,4},{9,57}... | collective-permute-start | bytes 2211848 | tf_op jit(solution)/shard_map/ppermute | solution.py:48
  81.4 19.7 %collective-permute-start.16 = (bf16[320,1152]{1,0:T(8,128)(2,1)S(1)}, bf16[320,1152]{1,0:T(8,128)(2,1)S(1)}, u32[]{:S(2)}, u32[]{:S(2)}) collective-permute-start(bf16[320,1152]{1,0:T(8,128)(2,1)S(1)} %get-tuple-element.51), channel_id=1, source_target_pairs={{0,4},{1,17},{2,6},{3,19},{4,8},{5,21},{6,10},{7,23},{8,12},{9,25}... | collective-permute-start | bytes 2211848 | tf_op jit(solution)/shard_map/ppermute | solution.py:48
  87.0 14.4 %collective-permute-start.20 = (bf16[320,1152]{1,0:T(8,128)(2,1)S(1)}, bf16[320,1152]{1,0:T(8,128)(2,1)S(1)}, u32[]{:S(2)}, u32[]{:S(2)}) collective-permute-start(bf16[320,1152]{1,0:T(8,128)(2,1)S(1)} %get-tuple-element.56), channel_id=1, source_target_pairs={{0,8},{1,33},{2,10},{3,35},{4,12},{5,37},{6,14},{7,39},{8,0},{9,41... | collective-permute-start | bytes 2211848 | tf_op jit(solution)/shard_map/ppermute | solution.py:48
  87.1 14.3 %collective-permute-start.21 = (bf16[320,1152]{1,0:T(8,128)(2,1)S(1)}, bf16[320,1152]{1,0:T(8,128)(2,1)S(1)}, u32[]{:S(2)}, u32[]{:S(2)}) collective-permute-start(bf16[320,1152]{1,0:T(8,128)(2,1)S(1)} %get-tuple-element.57), channel_id=1, source_target_pairs={{0,2},{1,67},{2,0},{3,65},{4,6},{5,71},{6,4},{7,69},{8,10},{9,75},... | collective-permute-start | bytes 2211848 | tf_op jit(solution)/shard_map/ppermute | solution.py:57
  102.2 2.4 %collective-permute-start.22 = (bf16[160,1152]{1,0:T(8,128)(2,1)S(1)}, bf16[160,1152]{1,0:T(8,128)(2,1)S(1)}, u32[]{:S(2)}, u32[]{:S(2)}) collective-permute-start(bf16[160,1152]{1,0:T(8,128)(2,1)S(1)} %get-tuple-element.59), channel_id=1, source_target_pairs={{0,1},{1,0},{2,3},{3,2},{4,5},{5,4},{6,7},{7,6},{8,9},{9,8},{10,11... | collective-permute-start | bytes 1105928 | tf_op jit(solution)/shard_map/ppermute | solution.py:61

commit v6 on v4

--- a/solution.py
+++ b/solution.py
@@ -94,68 +94,112 @@
     return pl.multiple_of(jnp.where(core == 0, half, 1 - half) * rows, rows)
 
 
-def weights_kernel(pieces, scale_ref, core_ref, *refs):
+def spans(count):
+    return [(begin, min(chunk, count - begin)) for begin in range(0, count, chunk)]
+
+
+def weights_of(scale_ref, mine_rows, other_rows, matched=None):
+    dots = lax.dot_general(
+        mine_rows,
+        other_rows,
+        (((1,), (1,)), ((), ())),
+        preferred_element_type=jnp.float32,
+    )
+    power = jnp.exp2(dots * scale_ref[0] + scale_ref[1])
+    share = pl.reciprocal(1.0 + power, approx=True)
+    if matched is not None:
+        row = lax.broadcasted_iota(jnp.int32, dots.shape, 0)
+        column = lax.broadcasted_iota(jnp.int32, dots.shape, 1)
+        share = jnp.where((row == column) & (row < rows) & matched, -power * share, share)
+    return share.astype(jnp.bfloat16)
+
+
+def transposed_dot(weights, values):
+    return lax.dot_general(
+        weights, values, (((0,), (0,)), ((), ())), preferred_element_type=jnp.float32
+    )
+
+
+def store_chips(refs, first, begin, total):
+    done = 0
+    while done < total.shape[0]:
+        chip, offset = divmod(begin + done, rows)
+        size = min(rows - offset, total.shape[0] - done)
+        ref, base = refs[chip]
+        ref[pl.ds(base + first + offset, size), :] = total[done : done + size].astype(
+            ref.dtype
+        )
+        done += size
+
+
+def main_kernel(pieces, scale_ref, core_ref, *refs):
     mine, other = places_of(refs[: pieces[0]]), places_of(refs[pieces[0] : sum(pieces)])
-    weights_ref, far_ref = refs[sum(pieces) :]
+    weights_ref, sums = refs[sum(pieces)], places_of(refs[sum(pieces) + 1 :])
+    core = core_ref[0]
     count = len(mine) * rows
-    core = core_ref[0]
-    slope, shift = scale_ref[0], scale_ref[1]
+    near = count - len(sums) * rows
     for half in range(2):
         opposite = opposite_rows(core, half)
         mine_rows = stacked(mine, half * rows)
         other_rows = stacked(other, opposite)
-        for begin in range(0, count, chunk):
-            dots = lax.dot_general(
+        for begin, size in spans(count):
+            weights_ref[half, :, pl.ds(begin, size)] = weights_of(
+                scale_ref,
                 mine_rows,
-                other_rows[begin : begin + chunk],
-                (((1,), (1,)), ((), ())),
-                preferred_element_type=jnp.float32,
+                other_rows[begin : begin + size],
+                core == 0 if begin == 0 else None,
             )
-            power = jnp.exp2(dots * slope + shift)
-            share = pl.reciprocal(1.0 + power, approx=True)
-            if begin == 0:
-                row = lax.broadcasted_iota(jnp.int32, dots.shape, 0)
-                column = lax.broadcasted_iota(jnp.int32, dots.shape, 1)
-                matched = (row == column) & (row < rows) & (core == 0)
-                share = jnp.where(matched, -power * share, share)
-            weights_ref[half, :, pl.ds(begin, chunk)] = share.astype(jnp.bfloat16)
-        other_sums(weights_ref, half, opposite, mine_rows, 4, far_ref)
-
-
-def other_sums(weights_ref, half, opposite, mine_rows, first, sums_ref):
-    for chip in range(0, 4, 2):
-        total = lax.dot_general(
-            weights_ref[half, :, pl.ds((first + chip) * rows, 2 * rows)],
-            mine_rows,
-            (((0,), (0,)), ((), ())),
+        for begin, size in spans(count - near):
+            total = transposed_dot(
+                weights_ref[half, :, pl.ds(near + begin, size)], mine_rows
+            )
+            store_chips(sums, opposite, begin, total)
+
+
+def far_kernel(pieces, core_ref, weights_ref, *refs):
+    other, sums = places_of(refs[:pieces]), places_of(refs[pieces:])
+    count = len(other) * rows
+    near = count - len(sums) * rows
+    for half in range(2):
+        other_rows = stacked(other, opposite_rows(core_ref[0], half))
+        total = jnp.dot(
+            weights_ref[half, pl.ds(near, count - near), :],
+            other_rows,
             preferred_element_type=jnp.float32,
-        ).astype(jnp.bfloat16)
-        for step in range(2):
-            place = pl.ds((chip + step) * chip_rows + opposite, rows)
-            sums_ref[place, :] = total[step * rows : (step + 1) * rows]
-
-
-def near_kernel(core_ref, weights_ref, *refs):
-    mine, sums_ref = places_of(refs[:-1]), refs[-1]
+        )
+        store_chips(sums, half * rows, 0, total)
+
+
+def near_kernel(pieces, core_ref, weights_ref, *refs):
+    mine, other = places_of(refs[: pieces[0]]), places_of(refs[pieces[0] : sum(pieces)])
+    sums = places_of(refs[sum(pieces) :])
+    near = len(sums) // 2
     for half in range(2):
+        opposite = opposite_rows(core_ref[0], half)
         mine_rows = stacked(mine, half * rows)
-        opposite = opposite_rows(core_ref[0], half)
-        other_sums(weights_ref, half, opposite, mine_rows, 0, sums_ref)
-
-
-def sums_kernel(pieces, first, core_ref, weights_ref, *refs):
-    other, sums = places_of(refs[:pieces]), refs[-4:]
-    core = core_ref[0]
-    for half in range(2):
-        other_rows = stacked(other, opposite_rows(core, half))
-        for chip in range(0, len(sums), 2):
-            total = jnp.dot(
-                weights_ref[half, pl.ds((first + chip) * rows, 2 * rows), :],
-                other_rows,
-                preferred_element_type=jnp.float32,
-            ).astype(jnp.bfloat16)
-            sums[chip][pl.ds(half * rows, rows), :] = total[:rows]
-            sums[chip + 1][pl.ds(half * rows, rows), :] = total[rows:]
+        other_rows = stacked(other, opposite)
+        for begin, size in spans(near * rows):
+            place = pl.ds(begin, size)
+            total = transposed_dot(weights_ref[half, :, place], mine_rows)
+            store_chips(sums[:near], opposite, begin, total)
+        total = jnp.dot(
+            weights_ref[half, pl.ds(0, near * rows), :],
+            other_rows,
+            preferred_element_type=jnp.float32,
+        )
+        store_chips(sums[near:], half * rows, 0, total)
+
+
+def joined_kernel(*refs):
+    first = 0
+    for ref in refs[:-1]:
+        refs[-1][pl.ds(first, ref.shape[0]), :] = ref[...]
+        first += ref.shape[0]
+
+
+def joined(arrays, after=()):
+    shape = (sum(array.shape[0] for array in arrays), arrays[0].shape[1])
+    return call(joined_kernel, [shape], (), arrays, after=after)[0]
 
 
 def final_kernel(scale_ref, core_ref, raw_ref, *refs):
@@ -176,7 +220,7 @@
     give_ref[...] = jnp.where(first_core, high, low).astype(jnp.bfloat16)
 
 
-def call(kernel, out_shape, scalars, arrays, flops=0, after=()):
+def call(kernel, out_shape, scalars, arrays, flops=0, after=(), kind=jnp.bfloat16):
     used = len(scalars) + len(arrays)
 
     def body(*refs):
@@ -188,8 +232,8 @@
         + [pl.BlockSpec(memory_space=pltpu.VMEM)] * len(arrays)
         + [pl.BlockSpec(memory_space=pl.ANY)] * len(after),
         out_specs=[pl.BlockSpec(memory_space=pltpu.VMEM)] * len(out_shape),
-        out_shape=[jax.ShapeDtypeStruct(shape, jnp.bfloat16) for shape in out_shape],
-        compiler_params=pltpu.CompilerParams(vmem_limit_bytes=26 * 2**20),
+        out_shape=[jax.ShapeDtypeStruct(shape, kind) for shape in out_shape],
+        compiler_params=pltpu.CompilerParams(vmem_limit_bytes=16 * 2**20),
         cost_estimate=pl.CostEstimate(
             flops=flops, bytes_accessed=2**20, transcendentals=0
         ),
@@ -204,10 +248,10 @@
         for index, first in group:
             part = inputs[index][pl.ds(first, chip_rows), :].astype(jnp.float32)
             total = part if total is None else total + part
-        sum_ref[...] = total.astype(jnp.bfloat16)
-
-
-def add(groups, after, flops=0):
+        sum_ref[...] = total.astype(sum_ref.dtype)
+
+
+def add(groups, after=(), flops=0, kind=jnp.bfloat16):
     arrays = []
     places = []
     for group in groups:
@@ -226,6 +270,7 @@
         arrays,
         flops,
         after,
+        kind,
     )
 
 
@@ -247,70 +292,65 @@
     )
     left, right, across = ring(unit, 1), ring(unit, -1), pair(unit)
     distant = jnp.concatenate([ring(left[:rows], 1), ring(right[rows:], -1)], axis=0)
-    near = [unit, left, right, distant]
-    far = [across, ring(across, 1), ring(across, -1), pair(distant)]
+    near = [unit, left, right, across]
+    far = [distant, ring(across, 1), ring(across, -1), pair(distant)]
     mine = near + far
     other = [
         swap(unit),
         swap(jnp.concatenate([left, right], axis=0)),
+        swap(across),
         swap(distant),
-        swap(across),
-        swap(jnp.concatenate([far[1], far[2]], axis=0)),
+        swap(jnp.concatenate(far[1:3], axis=0)),
         swap(far[3]),
     ]
     count = len(mine) * rows
     block = (chip_rows, width)
+    four_blocks = (4 * chip_rows, width)
     quarter = count * count * width
-    weights, far_other = call(
-        functools.partial(weights_kernel, (len(mine), len(other))),
-        [(2, count, count), (4 * chip_rows, width)],
+    weights, far_back = call(
+        functools.partial(main_kernel, (len(mine), len(other))),
+        [(2, count, count), four_blocks],
         (factors, cores),
         (*mine, *other),
         6 * quarter,
     )
-    far_shared = swap(far_other)
+    far_shared = swap(far_back)
     far_own = call(
-        functools.partial(sums_kernel, len(other), 4),
+        functools.partial(far_kernel, len(other)),
         [block] * 4,
         (cores,),
         (weights, *other),
         2 * quarter,
     )
     far_sums = add(
-        [(one, (far_shared, k * chip_rows)) for k, one in enumerate(far_own)], ()
+        [(one, (far_shared, k * chip_rows)) for k, one in enumerate(far_own)]
     )
     arrived = [ring(far_sums[1], -1), ring(far_sums[2], 1), pair(far_sums[3])]
-    (near_other,) = call(
-        near_kernel,
-        [(4 * chip_rows, width)],
+    near_back, *near_own = call(
+        functools.partial(near_kernel, (len(mine), len(other))),
+        [four_blocks] + [block] * 4,
         (cores,),
-        (weights, *mine),
-        2 * quarter,
+        (weights, *mine, *other),
+        4 * quarter,
         (far_sums[0],),
     )
-    near_shared = swap(near_other)
-    near_own = call(
-        functools.partial(sums_kernel, len(other), 0),
-        [block] * 4,
-        (cores,),
-        (weights, *other),
-        2 * quarter,
-        (near_other,),
-    )
-    near_sums = add(
-        [(one, (near_shared, k * chip_rows)) for k, one in enumerate(near_own)], ()
-    )
-    far_total, distant_total = add(
-        [(far_sums[0], arrived[0], arrived[1]), (near_sums[3], arrived[2])],
-        (near_sums[0],),
-    )
-    late = [ring(distant_total, 2), pair(far_total)]
-    (near_total,) = add(
-        [(near_sums[0], ring(near_sums[1], -1), ring(near_sums[2], 1))],
-        (),
-        16 * quarter,
-    )
-    parts = [near_total, *late]
+    distant_total, across_part = add(
+        [(far_sums[0], arrived[2]), (near_own[3], arrived[0], arrived[1])], (near_back,)
+    )
+    near_shared = swap(joined([near_back], (distant_total,)))
+    (near_part,) = add([(near_own[0], ring(distant_total, 2))], (), 0, jnp.float32)
+    left_total, right_total, across_total = add(
+        [(near_own[k], (near_shared, k * chip_rows)) for k in (1, 2)]
+        + [(across_part, (near_shared, 3 * chip_rows))],
+        (distant_total,),
+    )
+    parts = [
+        near_part,
+        near_shared[:chip_rows],
+        ring(left_total, -1),
+        ring(right_total, 1),
+        pair(across_total),
+    ]
     keep, give = call(
         final_kernel, [(rows, width)] * 2, (logit_scale, cores), (raw, *parts)
     )

time: 105 us -> 107 us (1.019)
  starting transfers between devices: 34.6 us -> 36.8 us
    ppermute x11, starting transfers between devices: 18.4 us -> 21 us  [ring(): return lax.ppermute(value, axes, ring_move(steps))]
    ppermute x11, waiting for transfers between devices: 26.3 us -> 24 us  [ring(): return lax.ppermute(value, axes, ring_move(steps))]
    ppermute x10, waiting for transfers between devices: 4.76 us -> 6.52 us  [swap(): return lax.ppermute(value, 'core', [(0, 1), (1, 0)])]
  transfers between devices with their start and end apart: 25 -> 25, of which waited for: 14 -> 14; matrix products, arithmetic and copies ran while one was open for 0% -> 0% of each run, Pallas kernels for 10% -> 13%
where the time goes in v6:
time: 107 us
  starting transfers between devices  36.8 us (34%)
  waiting for transfers between devices  33.7 us (31%)
  Pallas kernels  31.3 us (29%)
  other arithmetic  2.41 us (2%)
  between operations  2.12 us (2%)
    pallas_call x10, Pallas kernels, call(): pl.pallas_call(body, in_specs=[pl.BlockSpec(memory_space=pltpu.SMEM)] * l...  31.3 us
    ppermute x11, waiting for transfers between devices, ring(): return lax.ppermute(value, axes, ring_move(steps))  24 us
    ppermute x11, starting transfers between devices, ring(): return lax.ppermute(value, axes, ring_move(steps))  21 us
    ppermute x4, starting transfers between devices, pair(): return lax.ppermute(value, axes, pairs_of(move))  10.4 us
    ppermute x10, waiting for transfers between devices, swap(): return lax.ppermute(value, 'core', [(0, 1), (1, 0)])  6.52 us
    ppermute x10, starting transfers between devices, swap(): return lax.ppermute(value, 'core', [(0, 1), (1, 0)])  5.45 us
    ppermute x4, waiting for transfers between devices, pair(): return lax.ppermute(value, axes, pairs_of(move))  3.18 us
  transfers between devices with their start and end apart: 25, of which 14 were waited for; matrix products, arithmetic and copies ran while one was open for 0% of the time, Pallas kernels for 13%

profile of v6, /device:TPU:1, one launch (start us, length us, event | category | flops | bytes accessed | tf_op | source)
XLA Modules:
  0.0 106.6 jit_solution(4869768097610728354)
XLA Ops:
  0.6 1.2 %broadcast_select_fusion.2 = (bf16[160,1152]{1,0:T(8,128)(2,1)S(1)}, bf16[160,1152]{1,0:T(8,128)(2,1)S(1)}) fusion(bf16[160,1152]{1,0:T(8,128)(2,1)} %param.5, bf16[160,1152]{1,0:T(8,128)(2,1)} %param.4, pred[]{:T(512)S(6)} %eq.3), kind=kLoop, calls=%fused_computation.4 | loop fusion | flops 368640 | bytes 1474561 | tf_op jit(solution)/shard_map/jit(_where)/select_n | solution.py:284
  1.8 1.5 %collective-permute-start = (bf16[160,1152]{1,0:T(8,128)(2,1)S(1)}, bf16[160,1152]{1,0:T(8,128)(2,1)S(1)}, u32[]{:S(2)}, u32[]{:S(2)}) collective-permute-start(bf16[160,1152]{1,0:T(8,128)(2,1)S(1)} %get-tuple-element.52), channel_id=1, source_target_pairs={{0,1},{1,0},{2,3},{3,2},{4,5},{5,4},{6,7},{7,6},{8,9},{9,8},{10,11... | collective-permute-start | bytes 1105928 | tf_op jit(solution)/shard_map/ppermute | solution.py:61
  3.3 1.3 %collective-permute-done.refs_2_ = bf16[160,1152]{1,0:T(8,128)(2,1)S(1)} collective-permute-done((bf16[160,1152]{1,0:T(8,128)(2,1)S(1)}, bf16[160,1152]{1,0:T(8,128)(2,1)S(1)}, u32[]{:S(2)}, u32[]{:S(2)}) %collective-permute-start) | collective-permute-done | bytes 368672 | tf_op jit(solution)/shard_map/ppermute | solution.py:61
  4.6 0.4 shard_map.59
  5.0 1.8 %collective-permute-start.1 = (bf16[320,1152]{1,0:T(8,128)(2,1)S(1)}, bf16[320,1152]{1,0:T(8,128)(2,1)S(1)}, u32[]{:S(2)}, u32[]{:S(2)}) collective-permute-start(bf16[320,1152]{1,0:T(8,128)(2,1)S(1)} %get-tuple-element.27.refs_2_), channel_id=1, source_target_pairs={{0,4},{1,17},{2,6},{3,19},{4,8},{5,21},{6,10},{7,23},{8,12},{9,25}... | collective-permute-start | bytes 2211848 | tf_op jit(solution)/shard_map/ppermute | solution.py:48
  6.8 2.2 %collective-permute-start.2 = (bf16[320,1152]{1,0:T(8,128)(2,1)S(1)}, bf16[320,1152]{1,0:T(8,128)(2,1)S(1)}, u32[]{:S(2)}, u32[]{:S(2)}) collective-permute-start(bf16[320,1152]{1,0:T(8,128)(2,1)S(1)} %get-tuple-element.27.refs_2_), channel_id=1, source_target_pairs={{0,12},{1,49},{2,14},{3,51},{4,0},{5,53},{6,2},{7,55},{8,4},{9,57}... | collective-permute-start | bytes 2211848 | tf_op jit(solution)/shard_map/ppermute | solution.py:48
  9.0 2.7 %collective-permute-start.3 = (bf16[320,1152]{1,0:T(8,128)(2,1)S(1)}, bf16[320,1152]{1,0:T(8,128)(2,1)S(1)}, u32[]{:S(2)}, u32[]{:S(2)}) collective-permute-start(bf16[320,1152]{1,0:T(8,128)(2,1)S(1)} %get-tuple-element.27.refs_2_), channel_id=1, source_target_pairs={{0,2},{1,67},{2,0},{3,65},{4,6},{5,71},{6,4},{7,69},{8,10},{9,75},... | collective-permute-start | bytes 2211848 | tf_op jit(solution)/shard_map/ppermute | solution.py:57
  11.7 6.0 %collective-permute-done.1.refs_3_ = bf16[320,1152]{1,0:T(8,128)(2,1)S(1)} collective-permute-done((bf16[320,1152]{1,0:T(8,128)(2,1)S(1)}, bf16[320,1152]{1,0:T(8,128)(2,1)S(1)}, u32[]{:S(2)}, u32[]{:S(2)}) %collective-permute-start.1) | collective-permute-done | bytes 737312 | tf_op jit(solution)/shard_map/ppermute | solution.py:48
  17.8 0.1 collective-permute-start.4
  17.9 0.7 collective-permute-start.9
  18.6 0.0 collective-permute-done.2.refs_4_
  18.6 3.8 %collective-permute-start.5 = (bf16[160,1152]{1,0:T(8,128)(2,1)S(1)}, bf16[160,1152]{1,0:T(8,128)(2,1)S(1)}, u32[]{:S(2)}, u32[]{:S(2)}) collective-permute-start(bf16[160,1152]{1,0:T(8,128)(2,1)S(1)} %slice.13), channel_id=1, source_target_pairs={{0,12},{1,49},{2,14},{3,51},{4,0},{5,53},{6,2},{7,55},{8,4},{9,57}... | collective-permute-start | bytes 1105928 | tf_op jit(solution)/shard_map/ppermute | solution.py:48
  22.5 0.0 collective-permute-done.3.refs_5_
  22.5 0.0 collective-permute-start.6
  22.5 2.7 %collective-permute-start.7 = (bf16[320,1152]{1,0:T(8,128)(2,1)S(1)}, bf16[320,1152]{1,0:T(8,128)(2,1)S(1)}, u32[]{:S(2)}, u32[]{:S(2)}) collective-permute-start(bf16[320,1152]{1,0:T(8,128)(2,1)S(1)} %collective-permute-done.3.refs_5_), channel_id=1, source_target_pairs={{0,12},{1,49},{2,14},{3,51},{4,0},{5,53},{6,2},{7,55},{8,4},{9,57}... | collective-permute-start | bytes 2211848 | tf_op jit(solution)/shard_map/ppermute | solution.py:48
  25.1 0.1 pad_maximum_fusion
  25.3 0.5 collective-permute-done.4
  25.7 1.2 %collective-permute-start.10 = (bf16[640,1152]{1,0:T(8,128)(2,1)S(1)}, bf16[640,1152]{1,0:T(8,128)(2,1)S(1)}, u32[]{:S(2)}, u32[]{:S(2)}) collective-permute-start(bf16[640,1152]{1,0:T(8,128)(2,1)S(1)} %pad_maximum_fusion), channel_id=1, source_target_pairs={{0,1},{1,0},{2,3},{3,2},{4,5},{5,4},{6,7},{7,6},{8,9},{9,8},{10,11... | collective-permute-start | bytes 4423688 | tf_op jit(solution)/shard_map/ppermute | solution.py:61
  27.0 0.0 collective-permute-done.5
  27.0 2.9 %collective-permute-start.8 = (bf16[320,1152]{1,0:T(8,128)(2,1)S(1)}, bf16[320,1152]{1,0:T(8,128)(2,1)S(1)}, u32[]{:S(2)}, u32[]{:S(2)}) collective-permute-start(bf16[320,1152]{1,0:T(8,128)(2,1)S(1)} %constant_dynamic-update-slice_fusion.refs_6_), channel_id=1, source_target_pairs={{0,2},{1,67},{2,0},{3,65},{4,6},{5,71},{6,4},{7,69},{8,10},{9,75},... | collective-permute-start | bytes 2211848 | tf_op jit(solution)/shard_map/ppermute | solution.py:57
  29.9 4.3 %collective-permute-done.6.refs_7_ = bf16[320,1152]{1,0:T(8,128)(2,1)S(1)} collective-permute-done((bf16[320,1152]{1,0:T(8,128)(2,1)S(1)}, bf16[320,1152]{1,0:T(8,128)(2,1)S(1)}, u32[]{:S(2)}, u32[]{:S(2)}) %collective-permute-start.6) | collective-permute-done | bytes 737312 | tf_op jit(solution)/shard_map/ppermute | solution.py:48
  34.3 0.5 collective-permute-done.7.refs_8_
  34.8 0.1 pad_maximum_fusion.1
  34.9 0.1 collective-permute-start.13
  35.1 0.5 collective-permute-start.11
  35.5 0.0 collective-permute-done.9.refs_10_.refs_2_
  35.5 0.1 collective-permute-start.12
  35.6 3.2 %collective-permute-done.8.refs_9_ = bf16[320,1152]{1,0:T(8,128)(2,1)S(1)} collective-permute-done((bf16[320,1152]{1,0:T(8,128)(2,1)S(1)}, bf16[320,1152]{1,0:T(8,128)(2,1)S(1)}, u32[]{:S(2)}, u32[]{:S(2)}) %collective-permute-start.8) | collective-permute-done | bytes 737312 | tf_op jit(solution)/shard_map/ppermute | solution.py:57
  38.8 0.0 collective-permute-start.14
  40.1 0.1 pad_maximum_fusion.2.refs_0_
  40.2 0.0 collective-permute-done.11.refs_12_.refs_4_
  40.2 0.2 collective-permute-done.12.refs_13_.refs_5_
  40.4 0.0 collective-permute-done.10.refs_11_.refs_3_
  40.4 1.1 collective-permute-done.14.refs_15_.refs_7_
  41.4 0.0 collective-permute-done.13.refs_14_.refs_6_
  41.5 14.7 %shard_map.60 = (bf16[2,1280,1280]{2,1,0:T(8,128)(2,1)S(1)}, bf16[1280,1152]{1,0:T(8,128)(2,1)S(1)}) custom-call(f32[2]{0:T(128)S(1)} %pad_maximum_fusion.2.refs_0_, s32[1]{0:T(128)} %bitcast.refs_0_.refs_1_, bf16[320,1152]{1,0:T(8,128)(2,1)S(1)} %get-tuple-element.27.refs_2_, bf16[320,1152]{1,0:T(8,128)(2,1)S(1)} %collective-permute-done.1.refs_3_, ...), custom_call_target="tpu_custom_call" | custom-call | flops 11324620800 | bytes 1048576 | tf_op jit(solution)/shard_map/pallas_call | solution.py:229
  56.2 0.4 collective-permute-start.15
  56.6 4.4 %shard_map.61 = (bf16[320,1152]{1,0:T(8,128)(2,1)S(1)}, bf16[320,1152]{1,0:T(8,128)(2,1)S(1)}, bf16[320,1152]{1,0:T(8,128)(2,1)S(1)}, bf16[320,1152]{1,0:T(8,128)(2,1)S(1)}) custom-call(s32[1]{0:T(128)} %bitcast.refs_0_.refs_1_, bf16[2,1280,1280]{2,1,0:T(8,128)(2,1)S(1)} %get-tuple-element.28.refs_1_, ...), custom_call_target="tpu_custom_call" | custom-call | flops 3774873600 | bytes 1048576 | tf_op jit(solution)/shard_map/pallas_call | solution.py:229
  61.0 0.8 collective-permute-done.15.refs_1_
  61.8 0.7 shard_map.62
  62.5 2.9 %collective-permute-start.16 = (bf16[320,1152]{1,0:T(8,128)(2,1)S(1)}, bf16[320,1152]{1,0:T(8,128)(2,1)S(1)}, u32[]{:S(2)}, u32[]{:S(2)}) collective-permute-start(bf16[320,1152]{1,0:T(8,128)(2,1)S(1)} %get-tuple-element.36), channel_id=1, source_target_pairs={{0,2},{1,67},{2,0},{3,65},{4,6},{5,71},{6,4},{7,69},{8,10},{9,75},... | collective-permute-start | bytes 2211848 | tf_op jit(solution)/shard_map/ppermute | solution.py:57
  65.4 3.5 %collective-permute-start.17 = (bf16[320,1152]{1,0:T(8,128)(2,1)S(1)}, bf16[320,1152]{1,0:T(8,128)(2,1)S(1)}, u32[]{:S(2)}, u32[]{:S(2)}) collective-permute-start(bf16[320,1152]{1,0:T(8,128)(2,1)S(1)} %get-tuple-element.38), channel_id=1, source_target_pairs={{0,12},{1,49},{2,14},{3,51},{4,0},{5,53},{6,2},{7,55},{8,4},{9,57}... | collective-permute-start | bytes 2211848 | tf_op jit(solution)/shard_map/ppermute | solution.py:48
  68.9 0.0 collective-permute-start.18
  68.9 8.8 %shard_map.63 = (bf16[1280,1152]{1,0:T(8,128)(2,1)S(1)}, bf16[320,1152]{1,0:T(8,128)(2,1)S(1)}, bf16[320,1152]{1,0:T(8,128)(2,1)S(1)}, bf16[320,1152]{1,0:T(8,128)(2,1)S(1)}, bf16[320,1152]{1,0:T(8,128)(2,1)S(1)}) custom-call(s32[1]{0:T(128)} %bitcast.refs_0_.refs_1_, bf16[2,1280,1280]{2,1,0:T(8,128)(2,1)S(1)} %get-tuple-element.28.refs_1_, ...), custom_call_target="tpu_custom_call" | custom-call | flops 7549747200 | bytes 1048576 | tf_op jit(solution)/shard_map/pallas_call | solution.py:229
  77.7 0.0 collective-permute-done.16.refs_1_
  77.7 0.0 collective-permute-done.17.refs_3_
  77.7 2.7 %collective-permute-done.18.refs_4_ = bf16[320,1152]{1,0:T(8,128)(2,1)S(1)} collective-permute-done((bf16[320,1152]{1,0:T(8,128)(2,1)S(1)}, bf16[320,1152]{1,0:T(8,128)(2,1)S(1)}, u32[]{:S(2)}, u32[]{:S(2)}) %collective-permute-start.18) | collective-permute-done | bytes 737312 | tf_op jit(solution)/shard_map/ppermute | solution.py:48
  80.4 0.4 shard_map.64
  80.8 0.2 shard_map.66
  81.0 0.1 collective-permute-start.20
  81.1 3.5 %collective-permute-start.19 = (bf16[320,1152]{1,0:T(8,128)(2,1)S(1)}, bf16[320,1152]{1,0:T(8,128)(2,1)S(1)}, u32[]{:S(2)}, u32[]{:S(2)}) collective-permute-start(bf16[320,1152]{1,0:T(8,128)(2,1)S(1)} %get-tuple-element.41.refs_1_.refs_4_), channel_id=1, source_target_pairs={{0,8},{1,33},{2,10},{3,35},{4,12},{5,37},{6,14},{7,39},{8,0},{9,41... | collective-permute-start | bytes 2211848 | tf_op jit(solution)/shard_map/ppermute | solution.py:48
  84.7 1.8 %collective-permute-done.20.refs_1_ = bf16[1280,1152]{1,0:T(8,128)(2,1)S(1)} collective-permute-done((bf16[1280,1152]{1,0:T(8,128)(2,1)S(1)}, bf16[1280,1152]{1,0:T(8,128)(2,1)S(1)}, u32[]{:S(2)}, u32[]{:S(2)}) %collective-permute-start.20) | collective-permute-done | bytes 2949152 | tf_op jit(solution)/shard_map/ppermute | solution.py:61
  86.5 0.5 shard_map.67
  87.0 3.4 %collective-permute-start.21 = (bf16[320,1152]{1,0:T(8,128)(2,1)S(1)}, bf16[320,1152]{1,0:T(8,128)(2,1)S(1)}, u32[]{:S(2)}, u32[]{:S(2)}) collective-permute-start(bf16[320,1152]{1,0:T(8,128)(2,1)S(1)} %get-tuple-element.45), channel_id=1, source_target_pairs={{0,12},{1,49},{2,14},{3,51},{4,0},{5,53},{6,2},{7,55},{8,4},{9,57}... | collective-permute-start | bytes 2211848 | tf_op jit(solution)/shard_map/ppermute | solution.py:48
  90.4 0.0 collective-permute-start.22
  90.4 1.9 %collective-permute-start.23 = (bf16[320,1152]{1,0:T(8,128)(2,1)S(1)}, bf16[320,1152]{1,0:T(8,128)(2,1)S(1)}, u32[]{:S(2)}, u32[]{:S(2)}) collective-permute-start(bf16[320,1152]{1,0:T(8,128)(2,1)S(1)} %get-tuple-element.47), channel_id=1, source_target_pairs={{0,2},{1,67},{2,0},{3,65},{4,6},{5,71},{6,4},{7,69},{8,10},{9,75},... | collective-permute-start | bytes 2211848 | tf_op jit(solution)/shard_map/ppermute | solution.py:57
  92.3 1.5 %collective-permute-done.19.refs_1_ = bf16[320,1152]{1,0:T(8,128)(2,1)S(1)} collective-permute-done((bf16[320,1152]{1,0:T(8,128)(2,1)S(1)}, bf16[320,1152]{1,0:T(8,128)(2,1)S(1)}, u32[]{:S(2)}, u32[]{:S(2)}) %collective-permute-start.19) | collective-permute-done | bytes 737312 | tf_op jit(solution)/shard_map/ppermute | solution.py:48
  93.8 0.1 shard_map.65.refs_3_
  94.0 0.1 slice.14.refs_4_
  94.0 8.5 %collective-permute-done.21.refs_5_ = bf16[320,1152]{1,0:T(8,128)(2,1)S(1)} collective-permute-done((bf16[320,1152]{1,0:T(8,128)(2,1)S(1)}, bf16[320,1152]{1,0:T(8,128)(2,1)S(1)}, u32[]{:S(2)}, u32[]{:S(2)}) %collective-permute-start.21) | collective-permute-done | bytes 737312 | tf_op jit(solution)/shard_map/ppermute | solution.py:48
  102.5 1.0 shard_map.68
  103.5 0.8 collective-permute-start.24
  104.3 1.3 %collective-permute-done.24 = bf16[160,1152]{1,0:T(8,128)(2,1)S(1)} collective-permute-done((bf16[160,1152]{1,0:T(8,128)(2,1)S(1)}, bf16[160,1152]{1,0:T(8,128)(2,1)S(1)}, u32[]{:S(2)}, u32[]{:S(2)}) %collective-permute-start.24) | collective-permute-done | bytes 368672 | tf_op jit(solution)/shard_map/ppermute | solution.py:61
  105.7 0.9 broadcast_select_fusion
  (6 shorter events, 0.1 us)
Async XLA Ops:
  1.8 2.8 %collective-permute-start = (bf16[160,1152]{1,0:T(8,128)(2,1)S(1)}, bf16[160,1152]{1,0:T(8,128)(2,1)S(1)}, u32[]{:S(2)}, u32[]{:S(2)}) collective-permute-start(bf16[160,1152]{1,0:T(8,128)(2,1)S(1)} %get-tuple-element.52), channel_id=1, source_target_pairs={{0,1},{1,0},{2,3},{3,2},{4,5},{5,4},{6,7},{7,6},{8,9},{9,8},{10,11... | collective-permute-start | bytes 1105928 | tf_op jit(solution)/shard_map/ppermute | solution.py:61
  5.0 12.8 %collective-permute-start.1 = (bf16[320,1152]{1,0:T(8,128)(2,1)S(1)}, bf16[320,1152]{1,0:T(8,128)(2,1)S(1)}, u32[]{:S(2)}, u32[]{:S(2)}) collective-permute-start(bf16[320,1152]{1,0:T(8,128)(2,1)S(1)} %get-tuple-element.27.refs_2_), channel_id=1, source_target_pairs={{0,4},{1,17},{2,6},{3,19},{4,8},{5,21},{6,10},{7,23},{8,12},{9,25}... | collective-permute-start | bytes 2211848 | tf_op jit(solution)/shard_map/ppermute | solution.py:48
  6.8 11.8 %collective-permute-start.2 = (bf16[320,1152]{1,0:T(8,128)(2,1)S(1)}, bf16[320,1152]{1,0:T(8,128)(2,1)S(1)}, u32[]{:S(2)}, u32[]{:S(2)}) collective-permute-start(bf16[320,1152]{1,0:T(8,128)(2,1)S(1)} %get-tuple-element.27.refs_2_), channel_id=1, source_target_pairs={{0,12},{1,49},{2,14},{3,51},{4,0},{5,53},{6,2},{7,55},{8,4},{9,57}... | collective-permute-start | bytes 2211848 | tf_op jit(solution)/shard_map/ppermute | solution.py:48
  9.0 13.5 %collective-permute-start.3 = (bf16[320,1152]{1,0:T(8,128)(2,1)S(1)}, bf16[320,1152]{1,0:T(8,128)(2,1)S(1)}, u32[]{:S(2)}, u32[]{:S(2)}) collective-permute-start(bf16[320,1152]{1,0:T(8,128)(2,1)S(1)} %get-tuple-element.27.refs_2_), channel_id=1, source_target_pairs={{0,2},{1,67},{2,0},{3,65},{4,6},{5,71},{6,4},{7,69},{8,10},{9,75},... | collective-permute-start | bytes 2211848 | tf_op jit(solution)/shard_map/ppermute | solution.py:57
  17.8 7.9 %collective-permute-start.4 = (bf16[160,1152]{1,0:T(8,128)(2,1)S(1)}, bf16[160,1152]{1,0:T(8,128)(2,1)S(1)}, u32[]{:S(2)}, u32[]{:S(2)}) collective-permute-start(bf16[160,1152]{1,0:T(8,128)(2,1)S(1)} %slice.12), channel_id=1, source_target_pairs={{0,4},{1,17},{2,6},{3,19},{4,8},{5,21},{6,10},{7,23},{8,12},{9,25}... | collective-permute-start | bytes 1105928 | tf_op jit(solution)/shard_map/ppermute | solution.py:48
  17.9 17.6 %collective-permute-start.9 = (bf16[320,1152]{1,0:T(8,128)(2,1)S(1)}, bf16[320,1152]{1,0:T(8,128)(2,1)S(1)}, u32[]{:S(2)}, u32[]{:S(2)}) collective-permute-start(bf16[320,1152]{1,0:T(8,128)(2,1)S(1)} %get-tuple-element.27.refs_2_), channel_id=1, source_target_pairs={{0,1},{1,0},{2,3},{3,2},{4,5},{5,4},{6,7},{7,6},{8,9},{9,8},{10,11... | collective-permute-start | bytes 2211848 | tf_op jit(solution)/shard_map/ppermute | solution.py:61
  18.6 8.4 %collective-permute-start.5 = (bf16[160,1152]{1,0:T(8,128)(2,1)S(1)}, bf16[160,1152]{1,0:T(8,128)(2,1)S(1)}, u32[]{:S(2)}, u32[]{:S(2)}) collective-permute-start(bf16[160,1152]{1,0:T(8,128)(2,1)S(1)} %slice.13), channel_id=1, source_target_pairs={{0,12},{1,49},{2,14},{3,51},{4,0},{5,53},{6,2},{7,55},{8,4},{9,57}... | collective-permute-start | bytes 1105928 | tf_op jit(solution)/shard_map/ppermute | solution.py:48
  22.5 11.8 %collective-permute-start.6 = (bf16[320,1152]{1,0:T(8,128)(2,1)S(1)}, bf16[320,1152]{1,0:T(8,128)(2,1)S(1)}, u32[]{:S(2)}, u32[]{:S(2)}) collective-permute-start(bf16[320,1152]{1,0:T(8,128)(2,1)S(1)} %collective-permute-done.3.refs_5_), channel_id=1, source_target_pairs={{0,4},{1,17},{2,6},{3,19},{4,8},{5,21},{6,10},{7,23},{8,12},{9,25}... | collective-permute-start | bytes 2211848 | tf_op jit(solution)/shard_map/ppermute | solution.py:48
  22.5 12.4 %collective-permute-start.7 = (bf16[320,1152]{1,0:T(8,128)(2,1)S(1)}, bf16[320,1152]{1,0:T(8,128)(2,1)S(1)}, u32[]{:S(2)}, u32[]{:S(2)}) collective-permute-start(bf16[320,1152]{1,0:T(8,128)(2,1)S(1)} %collective-permute-done.3.refs_5_), channel_id=1, source_target_pairs={{0,12},{1,49},{2,14},{3,51},{4,0},{5,53},{6,2},{7,55},{8,4},{9,57}... | collective-permute-start | bytes 2211848 | tf_op jit(solution)/shard_map/ppermute | solution.py:48
  25.7 14.6 %collective-permute-start.10 = (bf16[640,1152]{1,0:T(8,128)(2,1)S(1)}, bf16[640,1152]{1,0:T(8,128)(2,1)S(1)}, u32[]{:S(2)}, u32[]{:S(2)}) collective-permute-start(bf16[640,1152]{1,0:T(8,128)(2,1)S(1)} %pad_maximum_fusion), channel_id=1, source_target_pairs={{0,1},{1,0},{2,3},{3,2},{4,5},{5,4},{6,7},{7,6},{8,9},{9,8},{10,11... | collective-permute-start | bytes 4423688 | tf_op jit(solution)/shard_map/ppermute | solution.py:61
  27.0 11.8 %collective-permute-start.8 = (bf16[320,1152]{1,0:T(8,128)(2,1)S(1)}, bf16[320,1152]{1,0:T(8,128)(2,1)S(1)}, u32[]{:S(2)}, u32[]{:S(2)}) collective-permute-start(bf16[320,1152]{1,0:T(8,128)(2,1)S(1)} %constant_dynamic-update-slice_fusion.refs_6_), channel_id=1, source_target_pairs={{0,2},{1,67},{2,0},{3,65},{4,6},{5,71},{6,4},{7,69},{8,10},{9,75},... | collective-permute-start | bytes 2211848 | tf_op jit(solution)/shard_map/ppermute | solution.py:57
  34.9 6.5 %collective-permute-start.13 = (bf16[640,1152]{1,0:T(8,128)(2,1)S(1)}, bf16[640,1152]{1,0:T(8,128)(2,1)S(1)}, u32[]{:S(2)}, u32[]{:S(2)}) collective-permute-start(bf16[640,1152]{1,0:T(8,128)(2,1)S(1)} %pad_maximum_fusion.1), channel_id=1, source_target_pairs={{0,1},{1,0},{2,3},{3,2},{4,5},{5,4},{6,7},{7,6},{8,9},{9,8},{10,11... | collective-permute-start | bytes 4423688 | tf_op jit(solution)/shard_map/ppermute | solution.py:61
  35.1 5.2 %collective-permute-start.11 = (bf16[320,1152]{1,0:T(8,128)(2,1)S(1)}, bf16[320,1152]{1,0:T(8,128)(2,1)S(1)}, u32[]{:S(2)}, u32[]{:S(2)}) collective-permute-start(bf16[320,1152]{1,0:T(8,128)(2,1)S(1)} %collective-permute-done.3.refs_5_), channel_id=1, source_target_pairs={{0,1},{1,0},{2,3},{3,2},{4,5},{5,4},{6,7},{7,6},{8,9},{9,8},{10,11... | collective-permute-start | bytes 2211848 | tf_op jit(solution)/shard_map/ppermute | solution.py:61
  35.5 4.9 %collective-permute-start.12 = (bf16[320,1152]{1,0:T(8,128)(2,1)S(1)}, bf16[320,1152]{1,0:T(8,128)(2,1)S(1)}, u32[]{:S(2)}, u32[]{:S(2)}) collective-permute-start(bf16[320,1152]{1,0:T(8,128)(2,1)S(1)} %constant_dynamic-update-slice_fusion.refs_6_), channel_id=1, source_target_pairs={{0,1},{1,0},{2,3},{3,2},{4,5},{5,4},{6,7},{7,6},{8,9},{9,8},{10,11... | collective-permute-start | bytes 2211848 | tf_op jit(solution)/shard_map/ppermute | solution.py:61
  38.8 2.7 %collective-permute-start.14 = (bf16[320,1152]{1,0:T(8,128)(2,1)S(1)}, bf16[320,1152]{1,0:T(8,128)(2,1)S(1)}, u32[]{:S(2)}, u32[]{:S(2)}) collective-permute-start(bf16[320,1152]{1,0:T(8,128)(2,1)S(1)} %collective-permute-done.8.refs_9_), channel_id=1, source_target_pairs={{0,1},{1,0},{2,3},{3,2},{4,5},{5,4},{6,7},{7,6},{8,9},{9,8},{10,11... | collective-permute-start | bytes 2211848 | tf_op jit(solution)/shard_map/ppermute | solution.py:61
  56.2 5.7 %collective-permute-start.15 = (bf16[1280,1152]{1,0:T(8,128)(2,1)S(1)}, bf16[1280,1152]{1,0:T(8,128)(2,1)S(1)}, u32[]{:S(2)}, u32[]{:S(2)}) collective-permute-start(bf16[1280,1152]{1,0:T(8,128)(2,1)S(1)} %get-tuple-element.30), channel_id=1, source_target_pairs={{0,1},{1,0},{2,3},{3,2},{4,5},{5,4},{6,7},{7,6},{8,9},{9,8},{10,11... | collective-permute-start | bytes 8847368 | tf_op jit(solution)/shard_map/ppermute | solution.py:61
  62.5 15.2 %collective-permute-start.16 = (bf16[320,1152]{1,0:T(8,128)(2,1)S(1)}, bf16[320,1152]{1,0:T(8,128)(2,1)S(1)}, u32[]{:S(2)}, u32[]{:S(2)}) collective-permute-start(bf16[320,1152]{1,0:T(8,128)(2,1)S(1)} %get-tuple-element.36), channel_id=1, source_target_pairs={{0,2},{1,67},{2,0},{3,65},{4,6},{5,71},{6,4},{7,69},{8,10},{9,75},... | collective-permute-start | bytes 2211848 | tf_op jit(solution)/shard_map/ppermute | solution.py:57
  65.4 12.3 %collective-permute-start.17 = (bf16[320,1152]{1,0:T(8,128)(2,1)S(1)}, bf16[320,1152]{1,0:T(8,128)(2,1)S(1)}, u32[]{:S(2)}, u32[]{:S(2)}) collective-permute-start(bf16[320,1152]{1,0:T(8,128)(2,1)S(1)} %get-tuple-element.38), channel_id=1, source_target_pairs={{0,12},{1,49},{2,14},{3,51},{4,0},{5,53},{6,2},{7,55},{8,4},{9,57}... | collective-permute-start | bytes 2211848 | tf_op jit(solution)/shard_map/ppermute | solution.py:48
  68.9 11.5 %collective-permute-start.18 = (bf16[320,1152]{1,0:T(8,128)(2,1)S(1)}, bf16[320,1152]{1,0:T(8,128)(2,1)S(1)}, u32[]{:S(2)}, u32[]{:S(2)}) collective-permute-start(bf16[320,1152]{1,0:T(8,128)(2,1)S(1)} %get-tuple-element.39), channel_id=1, source_target_pairs={{0,4},{1,17},{2,6},{3,19},{4,8},{5,21},{6,10},{7,23},{8,12},{9,25}... | collective-permute-start | bytes 2211848 | tf_op jit(solution)/shard_map/ppermute | solution.py:48
  81.0 5.5 %collective-permute-start.20 = (bf16[1280,1152]{1,0:T(8,128)(2,1)S(1)}, bf16[1280,1152]{1,0:T(8,128)(2,1)S(1)}, u32[]{:S(2)}, u32[]{:S(2)}) collective-permute-start(bf16[1280,1152]{1,0:T(8,128)(2,1)S(1)} %shard_map.66), channel_id=1, source_target_pairs={{0,1},{1,0},{2,3},{3,2},{4,5},{5,4},{6,7},{7,6},{8,9},{9,8},{10,11... | collective-permute-start | bytes 8847368 | tf_op jit(solution)/shard_map/ppermute | solution.py:61
  81.1 12.7 %collective-permute-start.19 = (bf16[320,1152]{1,0:T(8,128)(2,1)S(1)}, bf16[320,1152]{1,0:T(8,128)(2,1)S(1)}, u32[]{:S(2)}, u32[]{:S(2)}) collective-permute-start(bf16[320,1152]{1,0:T(8,128)(2,1)S(1)} %get-tuple-element.41.refs_1_.refs_4_), channel_id=1, source_target_pairs={{0,8},{1,33},{2,10},{3,35},{4,12},{5,37},{6,14},{7,39},{8,0},{9,41... | collective-permute-start | bytes 2211848 | tf_op jit(solution)/shard_map/ppermute | solution.py:48
  87.0 15.5 %collective-permute-start.21 = (bf16[320,1152]{1,0:T(8,128)(2,1)S(1)}, bf16[320,1152]{1,0:T(8,128)(2,1)S(1)}, u32[]{:S(2)}, u32[]{:S(2)}) collective-permute-start(bf16[320,1152]{1,0:T(8,128)(2,1)S(1)} %get-tuple-element.45), channel_id=1, source_target_pairs={{0,12},{1,49},{2,14},{3,51},{4,0},{5,53},{6,2},{7,55},{8,4},{9,57}... | collective-permute-start | bytes 2211848 | tf_op jit(solution)/shard_map/ppermute | solution.py:48
  90.4 12.1 %collective-permute-start.22 = (bf16[320,1152]{1,0:T(8,128)(2,1)S(1)}, bf16[320,1152]{1,0:T(8,128)(2,1)S(1)}, u32[]{:S(2)}, u32[]{:S(2)}) collective-permute-start(bf16[320,1152]{1,0:T(8,128)(2,1)S(1)} %get-tuple-element.46), channel_id=1, source_target_pairs={{0,4},{1,17},{2,6},{3,19},{4,8},{5,21},{6,10},{7,23},{8,12},{9,25}... | collective-permute-start | bytes 2211848 | tf_op jit(solution)/shard_map/ppermute | solution.py:48
  90.4 12.1 %collective-permute-start.23 = (bf16[320,1152]{1,0:T(8,128)(2,1)S(1)}, bf16[320,1152]{1,0:T(8,128)(2,1)S(1)}, u32[]{:S(2)}, u32[]{:S(2)}) collective-permute-start(bf16[320,1152]{1,0:T(8,128)(2,1)S(1)} %get-tuple-element.47), channel_id=1, source_target_pairs={{0,2},{1,67},{2,0},{3,65},{4,6},{5,71},{6,4},{7,69},{8,10},{9,75},... | collective-permute-start | bytes 2211848 | tf_op jit(solution)/shard_map/ppermute | solution.py:57
  103.5 2.1 %collective-permute-start.24 = (bf16[160,1152]{1,0:T(8,128)(2,1)S(1)}, bf16[160,1152]{1,0:T(8,128)(2,1)S(1)}, u32[]{:S(2)}, u32[]{:S(2)}) collective-permute-start(bf16[160,1152]{1,0:T(8,128)(2,1)S(1)} %get-tuple-element.49), channel_id=1, source_target_pairs={{0,1},{1,0},{2,3},{3,2},{4,5},{5,4},{6,7},{7,6},{8,9},{9,8},{10,11... | collective-permute-start | bytes 1105928 | tf_op jit(solution)/shard_map/ppermute | solution.py:61

commit v7 on v6

--- a/solution.py
+++ b/solution.py
@@ -132,74 +132,73 @@
         done += size
 
 
-def main_kernel(pieces, scale_ref, core_ref, *refs):
+def first_kernel(pieces, scale_ref, core_ref, *refs):
     mine, other = places_of(refs[: pieces[0]]), places_of(refs[pieces[0] : sum(pieces)])
-    weights_ref, sums = refs[sum(pieces)], places_of(refs[sum(pieces) + 1 :])
+    far_ref, near_ref = refs[sum(pieces) :]
+    for half in range(2):
+        mine_rows = stacked(mine, half * rows)
+        other_rows = stacked(other, opposite_rows(core_ref[0], half))
+        edge = 4 * rows - near_ref.shape[2]
+        near_ref[half] = weights_of(scale_ref, mine_rows, other_rows[edge : 4 * rows])
+        for begin, size in spans(4 * rows):
+            place = pl.ds(begin, size)
+            far_ref[half, :, place] = weights_of(
+                scale_ref,
+                mine_rows,
+                other_rows[4 * rows + begin : 4 * rows + begin + size],
+            )
+
+
+def second_kernel(pieces, scale_ref, core_ref, far_ref, edge_ref, *refs):
+    mine, other = places_of(refs[: pieces[0]]), places_of(refs[pieces[0] : sum(pieces)])
+    near_ref, part_ref = refs[sum(pieces) :]
     core = core_ref[0]
-    count = len(mine) * rows
-    near = count - len(sums) * rows
-    for half in range(2):
-        opposite = opposite_rows(core, half)
+    edge = 4 * rows - edge_ref.shape[2]
+    for half in range(2):
         mine_rows = stacked(mine, half * rows)
-        other_rows = stacked(other, opposite)
-        for begin, size in spans(count):
-            weights_ref[half, :, pl.ds(begin, size)] = weights_of(
+        other_rows = stacked(other, opposite_rows(core, half))
+        for begin, size in spans(edge):
+            near_ref[half, :, pl.ds(begin, size)] = weights_of(
                 scale_ref,
                 mine_rows,
                 other_rows[begin : begin + size],
                 core == 0 if begin == 0 else None,
             )
-        for begin, size in spans(count - near):
-            total = transposed_dot(
-                weights_ref[half, :, pl.ds(near + begin, size)], mine_rows
-            )
-            store_chips(sums, opposite, begin, total)
-
-
-def far_kernel(pieces, core_ref, weights_ref, *refs):
+        near_ref[half, :, pl.ds(edge, edge_ref.shape[2])] = edge_ref[half]
+        place = pl.ds(4 * rows, 4 * rows)
+        weights = jnp.concatenate(
+            [near_ref[half, place, :], far_ref[half, place, :]], axis=1
+        )
+        part_ref[half] = jnp.dot(
+            weights, other_rows, preferred_element_type=jnp.float32
+        )
+
+
+def received(core, half, weights_ref, other):
+    its_half = jnp.where(core == 0, 1 - half, half)
+    other_rows = stacked(other, pl.multiple_of(its_half * rows, rows))
+    return transposed_dot(weights_ref[its_half], other_rows)
+
+
+def far_kernel(pieces, core_ref, weights_ref, part_ref, *refs):
     other, sums = places_of(refs[:pieces]), places_of(refs[pieces:])
-    count = len(other) * rows
-    near = count - len(sums) * rows
-    for half in range(2):
-        other_rows = stacked(other, opposite_rows(core_ref[0], half))
-        total = jnp.dot(
-            weights_ref[half, pl.ds(near, count - near), :],
-            other_rows,
-            preferred_element_type=jnp.float32,
+    for half in range(2):
+        total = part_ref[half] + received(core_ref[0], half, weights_ref, other)
+        store_chips(sums, half * rows, 0, total)
+
+
+def near_kernel(pieces, core_ref, far_ref, near_ref, weights_ref, *refs):
+    other, sums = places_of(refs[:pieces]), places_of(refs[pieces:])
+    core = core_ref[0]
+    for half in range(2):
+        place = pl.ds(0, 4 * rows)
+        weights = jnp.concatenate(
+            [near_ref[half, place, :], far_ref[half, place, :]], axis=1
         )
+        other_rows = stacked(other, opposite_rows(core, half))
+        total = jnp.dot(weights, other_rows, preferred_element_type=jnp.float32)
+        total = total + received(core, half, weights_ref, other)
         store_chips(sums, half * rows, 0, total)
-
-
-def near_kernel(pieces, core_ref, weights_ref, *refs):
-    mine, other = places_of(refs[: pieces[0]]), places_of(refs[pieces[0] : sum(pieces)])
-    sums = places_of(refs[sum(pieces) :])
-    near = len(sums) // 2
-    for half in range(2):
-        opposite = opposite_rows(core_ref[0], half)
-        mine_rows = stacked(mine, half * rows)
-        other_rows = stacked(other, opposite)
-        for begin, size in spans(near * rows):
-            place = pl.ds(begin, size)
-            total = transposed_dot(weights_ref[half, :, place], mine_rows)
-            store_chips(sums[:near], opposite, begin, total)
-        total = jnp.dot(
-            weights_ref[half, pl.ds(0, near * rows), :],
-            other_rows,
-            preferred_element_type=jnp.float32,
-        )
-        store_chips(sums[near:], half * rows, 0, total)
-
-
-def joined_kernel(*refs):
-    first = 0
-    for ref in refs[:-1]:
-        refs[-1][pl.ds(first, ref.shape[0]), :] = ref[...]
-        first += ref.shape[0]
-
-
-def joined(arrays, after=()):
-    shape = (sum(array.shape[0] for array in arrays), arrays[0].shape[1])
-    return call(joined_kernel, [shape], (), arrays, after=after)[0]
 
 
 def final_kernel(scale_ref, core_ref, raw_ref, *refs):
@@ -220,7 +219,8 @@
     give_ref[...] = jnp.where(first_core, high, low).astype(jnp.bfloat16)
 
 
-def call(kernel, out_shape, scalars, arrays, flops=0, after=(), kind=jnp.bfloat16):
+def call(kernel, out_shape, scalars, arrays, flops=0, after=(), kinds=None):
+    kinds = kinds or [jnp.bfloat16] * len(out_shape)
     used = len(scalars) + len(arrays)
 
     def body(*refs):
@@ -232,7 +232,10 @@
         + [pl.BlockSpec(memory_space=pltpu.VMEM)] * len(arrays)
         + [pl.BlockSpec(memory_space=pl.ANY)] * len(after),
         out_specs=[pl.BlockSpec(memory_space=pltpu.VMEM)] * len(out_shape),
-        out_shape=[jax.ShapeDtypeStruct(shape, kind) for shape in out_shape],
+        out_shape=[
+            jax.ShapeDtypeStruct(shape, kind_of)
+            for shape, kind_of in zip(out_shape, kinds)
+        ],
         compiler_params=pltpu.CompilerParams(vmem_limit_bytes=16 * 2**20),
         cost_estimate=pl.CostEstimate(
             flops=flops, bytes_accessed=2**20, transcendentals=0
@@ -251,7 +254,7 @@
         sum_ref[...] = total.astype(sum_ref.dtype)
 
 
-def add(groups, after=(), flops=0, kind=jnp.bfloat16):
+def add(groups, after=()):
     arrays = []
     places = []
     for group in groups:
@@ -268,9 +271,7 @@
         [(chip_rows, arrays[0].shape[1])] * len(groups),
         (),
         arrays,
-        flops,
-        after,
-        kind,
+        after=after,
     )
 
 
@@ -303,52 +304,52 @@
         swap(jnp.concatenate(far[1:3], axis=0)),
         swap(far[3]),
     ]
-    count = len(mine) * rows
+    near_rows, all_rows = 4 * rows, 8 * rows
+    edge = near_rows % chunk
     block = (chip_rows, width)
-    four_blocks = (4 * chip_rows, width)
-    quarter = count * count * width
-    weights, far_back = call(
-        functools.partial(main_kernel, (len(mine), len(other))),
-        [(2, count, count), four_blocks],
+    share = all_rows * all_rows * width
+    sizes = (len(mine), len(other))
+    far_weights, edge_weights = call(
+        functools.partial(first_kernel, sizes),
+        [(2, all_rows, near_rows), (2, all_rows, edge)],
         (factors, cores),
         (*mine, *other),
-        6 * quarter,
-    )
-    far_shared = swap(far_back)
-    far_own = call(
+        2 * share,
+    )
+    far_received = swap(far_weights)
+    near_weights, far_part = call(
+        functools.partial(second_kernel, sizes),
+        [(2, all_rows, near_rows), (2, near_rows, width)],
+        (factors, cores),
+        (far_weights, edge_weights, *mine, *other),
+        4 * share,
+        kinds=(jnp.bfloat16, jnp.float32),
+    )
+    near_received = swap(near_weights)
+    far_sums = call(
         functools.partial(far_kernel, len(other)),
         [block] * 4,
         (cores,),
-        (weights, *other),
-        2 * quarter,
-    )
-    far_sums = add(
-        [(one, (far_shared, k * chip_rows)) for k, one in enumerate(far_own)]
+        (far_received, far_part, *other),
+        2 * share,
     )
     arrived = [ring(far_sums[1], -1), ring(far_sums[2], 1), pair(far_sums[3])]
-    near_back, *near_own = call(
-        functools.partial(near_kernel, (len(mine), len(other))),
-        [four_blocks] + [block] * 4,
+    near_sums = call(
+        functools.partial(near_kernel, len(other)),
+        [block] * 4,
         (cores,),
-        (weights, *mine, *other),
-        4 * quarter,
-        (far_sums[0],),
-    )
-    distant_total, across_part = add(
-        [(far_sums[0], arrived[2]), (near_own[3], arrived[0], arrived[1])], (near_back,)
-    )
-    near_shared = swap(joined([near_back], (distant_total,)))
-    (near_part,) = add([(near_own[0], ring(distant_total, 2))], (), 0, jnp.float32)
-    left_total, right_total, across_total = add(
-        [(near_own[k], (near_shared, k * chip_rows)) for k in (1, 2)]
-        + [(across_part, (near_shared, 3 * chip_rows))],
-        (distant_total,),
+        (far_weights, near_weights, near_received, *other),
+        4 * share,
+    )
+    distant_total, across_total = add(
+        [(far_sums[0], arrived[2]), (near_sums[3], arrived[0], arrived[1])],
+        (near_sums[0],),
     )
     parts = [
-        near_part,
-        near_shared[:chip_rows],
-        ring(left_total, -1),
-        ring(right_total, 1),
+        near_sums[0],
+        ring(near_sums[1], -1),
+        ring(near_sums[2], 1),
+        ring(distant_total, 2),
         pair(across_total),
     ]
     keep, give = call(

time: 107 us -> 105 us (0.981)
  starting transfers between devices: 36.8 us -> 30.8 us
  waiting for transfers between devices: 33.7 us -> 37.4 us
    ppermute x11, waiting for transfers between devices: 24 us -> 30.3 us  [ring(): return lax.ppermute(value, axes, ring_move(steps))]
    ppermute x11, starting transfers between devices: 21 us -> 16.9 us  [ring(): return lax.ppermute(value, axes, ring_move(steps))]
    ppermute x10, waiting for transfers between devices: 6.52 us -> 3.87 us  [swap(): return lax.ppermute(value, 'core', [(0, 1), (1, 0)])]
    ppermute x4, starting transfers between devices: 10.4 us -> 8.52 us  [pair(): return lax.ppermute(value, axes, pairs_of(move))]
    pallas_call x10 -> x7, Pallas kernels: 31.3 us -> 31.9 us  [call(): pl.pallas_call(body, in_specs=[pl.BlockSpec(memory_space=pltpu.SMEM)] * l...]
  transfers between devices with their start and end apart: 25 -> 25, of which waited for: 14 -> 11; matrix products, arithmetic and copies ran while one was open for 0% -> 0% of each run, Pallas kernels for 13% -> 22%
where the time goes in v7:
time: 105 us
  waiting for transfers between devices  37.4 us (36%)
  Pallas kernels  31.9 us (30%)
  starting transfers between devices  30.8 us (29%)
  other arithmetic  2.41 us (2%)
  between operations  2.09 us (2%)
    pallas_call x7, Pallas kernels, call(): pl.pallas_call(body, in_specs=[pl.BlockSpec(memory_space=pltpu.SMEM)] * l...  31.9 us
    ppermute x11, waiting for transfers between devices, ring(): return lax.ppermute(value, axes, ring_move(steps))  30.3 us
    ppermute x11, starting transfers between devices, ring(): return lax.ppermute(value, axes, ring_move(steps))  16.9 us
    ppermute x4, starting transfers between devices, pair(): return lax.ppermute(value, axes, pairs_of(move))  8.52 us
    ppermute x10, starting transfers between devices, swap(): return lax.ppermute(value, 'core', [(0, 1), (1, 0)])  5.42 us
    ppermute x10, waiting for transfers between devices, swap(): return lax.ppermute(value, 'core', [(0, 1), (1, 0)])  3.87 us
    ppermute x4, waiting for transfers between devices, pair(): return lax.ppermute(value, axes, pairs_of(move))  3.18 us
  transfers between devices with their start and end apart: 25, of which 11 were waited for; matrix products, arithmetic and copies ran while one was open for 0% of the time, Pallas kernels for 22%

profile of v7, /device:TPU:1, one launch (start us, length us, event | category | flops | bytes accessed | tf_op | source)
XLA Modules:
  0.0 104.7 jit_solution(18023673035020348740)
XLA Ops:
  0.6 1.2 %broadcast_select_fusion.2 = (bf16[160,1152]{1,0:T(8,128)(2,1)S(1)}, bf16[160,1152]{1,0:T(8,128)(2,1)S(1)}) fusion(bf16[160,1152]{1,0:T(8,128)(2,1)} %param.5, bf16[160,1152]{1,0:T(8,128)(2,1)} %param.4, pred[]{:T(512)S(6)} %eq.3), kind=kLoop, calls=%fused_computation.4 | loop fusion | flops 368640 | bytes 1474561 | tf_op jit(solution)/shard_map/jit(_where)/select_n | solution.py:285
  1.8 1.5 %collective-permute-start = (bf16[160,1152]{1,0:T(8,128)(2,1)S(1)}, bf16[160,1152]{1,0:T(8,128)(2,1)S(1)}, u32[]{:S(2)}, u32[]{:S(2)}) collective-permute-start(bf16[160,1152]{1,0:T(8,128)(2,1)S(1)} %get-tuple-element.40), channel_id=1, source_target_pairs={{0,1},{1,0},{2,3},{3,2},{4,5},{5,4},{6,7},{7,6},{8,9},{9,8},{10,11... | collective-permute-start | bytes 1105928 | tf_op jit(solution)/shard_map/ppermute | solution.py:61
  3.3 1.3 %collective-permute-done.refs_2_ = bf16[160,1152]{1,0:T(8,128)(2,1)S(1)} collective-permute-done((bf16[160,1152]{1,0:T(8,128)(2,1)S(1)}, bf16[160,1152]{1,0:T(8,128)(2,1)S(1)}, u32[]{:S(2)}, u32[]{:S(2)}) %collective-permute-start) | collective-permute-done | bytes 368672 | tf_op jit(solution)/shard_map/ppermute | solution.py:61
  4.6 0.4 shard_map.59
  5.0 1.8 %collective-permute-start.1 = (bf16[320,1152]{1,0:T(8,128)(2,1)S(1)}, bf16[320,1152]{1,0:T(8,128)(2,1)S(1)}, u32[]{:S(2)}, u32[]{:S(2)}) collective-permute-start(bf16[320,1152]{1,0:T(8,128)(2,1)S(1)} %get-tuple-element.21.refs_2_.refs_4_), channel_id=1, source_target_pairs={{0,4},{1,17},{2,6},{3,19},{4,8},{5,21},{6,10},{7,23},{8,12},{9,25}... | collective-permute-start | bytes 2211848 | tf_op jit(solution)/shard_map/ppermute | solution.py:48
  6.8 2.2 %collective-permute-start.2 = (bf16[320,1152]{1,0:T(8,128)(2,1)S(1)}, bf16[320,1152]{1,0:T(8,128)(2,1)S(1)}, u32[]{:S(2)}, u32[]{:S(2)}) collective-permute-start(bf16[320,1152]{1,0:T(8,128)(2,1)S(1)} %get-tuple-element.21.refs_2_.refs_4_), channel_id=1, source_target_pairs={{0,12},{1,49},{2,14},{3,51},{4,0},{5,53},{6,2},{7,55},{8,4},{9,57}... | collective-permute-start | bytes 2211848 | tf_op jit(solution)/shard_map/ppermute | solution.py:48
  9.0 2.7 %collective-permute-start.3 = (bf16[320,1152]{1,0:T(8,128)(2,1)S(1)}, bf16[320,1152]{1,0:T(8,128)(2,1)S(1)}, u32[]{:S(2)}, u32[]{:S(2)}) collective-permute-start(bf16[320,1152]{1,0:T(8,128)(2,1)S(1)} %get-tuple-element.21.refs_2_.refs_4_), channel_id=1, source_target_pairs={{0,2},{1,67},{2,0},{3,65},{4,6},{5,71},{6,4},{7,69},{8,10},{9,75},... | collective-permute-start | bytes 2211848 | tf_op jit(solution)/shard_map/ppermute | solution.py:57
  11.7 6.0 %collective-permute-done.1.refs_3_.refs_5_ = bf16[320,1152]{1,0:T(8,128)(2,1)S(1)} collective-permute-done((bf16[320,1152]{1,0:T(8,128)(2,1)S(1)}, bf16[320,1152]{1,0:T(8,128)(2,1)S(1)}, u32[]{:S(2)}, u32[]{:S(2)}) %collective-permute-start.1) | collective-permute-done | bytes 737312 | tf_op jit(solution)/shard_map/ppermute | solution.py:48
  17.8 0.1 collective-permute-start.4
  17.9 0.7 collective-permute-start.9
  18.6 0.0 collective-permute-done.2.refs_4_.refs_6_
  18.6 3.8 %collective-permute-start.5 = (bf16[160,1152]{1,0:T(8,128)(2,1)S(1)}, bf16[160,1152]{1,0:T(8,128)(2,1)S(1)}, u32[]{:S(2)}, u32[]{:S(2)}) collective-permute-start(bf16[160,1152]{1,0:T(8,128)(2,1)S(1)} %slice.9), channel_id=1, source_target_pairs={{0,12},{1,49},{2,14},{3,51},{4,0},{5,53},{6,2},{7,55},{8,4},{9,57}... | collective-permute-start | bytes 1105928 | tf_op jit(solution)/shard_map/ppermute | solution.py:48
  22.5 0.0 collective-permute-done.3.refs_5_.refs_7_
  22.5 0.1 collective-permute-start.7
  22.6 1.3 %collective-permute-start.6 = (bf16[320,1152]{1,0:T(8,128)(2,1)S(1)}, bf16[320,1152]{1,0:T(8,128)(2,1)S(1)}, u32[]{:S(2)}, u32[]{:S(2)}) collective-permute-start(bf16[320,1152]{1,0:T(8,128)(2,1)S(1)} %collective-permute-done.3.refs_5_.refs_7_), channel_id=1, source_target_pairs={{0,4},{1,17},{2,6},{3,19},{4,8},{5,21},{6,10},{7,23},{8,12},{9,25}... | collective-permute-start | bytes 2211848 | tf_op jit(solution)/shard_map/ppermute | solution.py:48
  23.9 0.1 pad_maximum_fusion
  24.0 1.7 %collective-permute-done.4 = bf16[160,1152]{1,0:T(8,128)(2,1)S(1)} collective-permute-done((bf16[160,1152]{1,0:T(8,128)(2,1)S(1)}, bf16[160,1152]{1,0:T(8,128)(2,1)S(1)}, u32[]{:S(2)}, u32[]{:S(2)}) %collective-permute-start.4) | collective-permute-done | bytes 368672 | tf_op jit(solution)/shard_map/ppermute | solution.py:48
  25.7 1.2 %collective-permute-start.10 = (bf16[640,1152]{1,0:T(8,128)(2,1)S(1)}, bf16[640,1152]{1,0:T(8,128)(2,1)S(1)}, u32[]{:S(2)}, u32[]{:S(2)}) collective-permute-start(bf16[640,1152]{1,0:T(8,128)(2,1)S(1)} %pad_maximum_fusion), channel_id=1, source_target_pairs={{0,1},{1,0},{2,3},{3,2},{4,5},{5,4},{6,7},{7,6},{8,9},{9,8},{10,11... | collective-permute-start | bytes 4423688 | tf_op jit(solution)/shard_map/ppermute | solution.py:61
  27.0 0.0 collective-permute-done.5
  27.0 2.9 %collective-permute-start.8 = (bf16[320,1152]{1,0:T(8,128)(2,1)S(1)}, bf16[320,1152]{1,0:T(8,128)(2,1)S(1)}, u32[]{:S(2)}, u32[]{:S(2)}) collective-permute-start(bf16[320,1152]{1,0:T(8,128)(2,1)S(1)} %constant_dynamic-update-slice_fusion.refs_6_.refs_8_), channel_id=1, source_target_pairs={{0,2},{1,67},{2,0},{3,65},{4,6},{5,71},{6,4},{7,69},{8,10},{9,75},... | collective-permute-start | bytes 2211848 | tf_op jit(solution)/shard_map/ppermute | solution.py:57
  29.9 4.9 %collective-permute-done.7.refs_8_.refs_10_ = bf16[320,1152]{1,0:T(8,128)(2,1)S(1)} collective-permute-done((bf16[320,1152]{1,0:T(8,128)(2,1)S(1)}, bf16[320,1152]{1,0:T(8,128)(2,1)S(1)}, u32[]{:S(2)}, u32[]{:S(2)}) %collective-permute-start.7) | collective-permute-done | bytes 737312 | tf_op jit(solution)/shard_map/ppermute | solution.py:48
  34.8 0.0 collective-permute-done.6.refs_7_.refs_9_
  34.8 0.1 pad_maximum_fusion.1
  34.9 0.1 collective-permute-start.13
  35.1 0.5 collective-permute-start.11
  35.5 0.0 collective-permute-done.9.refs_10_.refs_12_.refs_4_.refs_3_
  35.5 0.1 collective-permute-start.12
  35.6 3.2 %collective-permute-done.8.refs_9_.refs_11_ = bf16[320,1152]{1,0:T(8,128)(2,1)S(1)} collective-permute-done((bf16[320,1152]{1,0:T(8,128)(2,1)S(1)}, bf16[320,1152]{1,0:T(8,128)(2,1)S(1)}, u32[]{:S(2)}, u32[]{:S(2)}) %collective-permute-start.8) | collective-permute-done | bytes 737312 | tf_op jit(solution)/shard_map/ppermute | solution.py:57
  38.8 0.0 collective-permute-start.14
  40.1 0.1 pad_maximum_fusion.2.refs_0_
  40.2 0.0 collective-permute-done.11.refs_12_.refs_14_.refs_6_.refs_5_
  40.2 0.2 collective-permute-done.12.refs_13_.refs_15_.refs_7_.refs_6_
  40.4 0.0 collective-permute-done.10.refs_11_.refs_13_.refs_5_.refs_4_
  40.4 1.1 %collective-permute-done.14.refs_15_.refs_17_.refs_9_.refs_8_ = bf16[320,1152]{1,0:T(8,128)(2,1)S(1)} collective-permute-done((bf16[320,1152]{1,0:T(8,128)(2,1)S(1)}, bf16[320,1152]{1,0:T(8,128)(2,1)S(1)}, u32[]{:S(2)}, u32[]{:S(2)}) %collective-permute-start.14) | collective-permute-done | bytes 737312 | tf_op jit(solution)/shard_map/ppermute | solution.py:61
  41.5 0.0 collective-permute-done.13.refs_14_.refs_16_.refs_8_.refs_7_
  41.5 7.3 %shard_map.60 = (bf16[2,1280,640]{2,1,0:T(8,128)(2,1)S(1)}, bf16[2,1280,128]{2,1,0:T(8,128)(2,1)S(1)}) custom-call(f32[2]{0:T(128)S(1)} %pad_maximum_fusion.2.refs_0_, s32[1]{0:T(128)} %bitcast.refs_0_.refs_1_, bf16[320,1152]{1,0:T(8,128)(2,1)S(1)} %get-tuple-element.21.refs_2_.refs_4_, bf16[320,1152]{1,0:T(8,128)(2,1)S(1)} %collective-permute-done.1.refs_3_.refs_5_, ...), custom_call_target="tpu_custom_call" | custom-call | flops 3774873600 | bytes 1048576 | tf_op jit(solution)/shard_map/pallas_call | solution.py:229
  48.8 0.4 collective-permute-start.18
  49.2 9.5 %shard_map.61 = (bf16[2,1280,640]{2,1,0:T(8,128)(2,1)S(1)}, f32[2,640,1152]{2,1,0:T(8,128)S(1)}) custom-call(f32[2]{0:T(128)S(1)} %pad_maximum_fusion.2.refs_0_, s32[1]{0:T(128)} %bitcast.refs_0_.refs_1_, bf16[2,1280,640]{2,1,0:T(8,128)(2,1)S(1)} %get-tuple-element.22.refs_2_.refs_1_, bf16[2,1280,128]{2,1,0:T(8,128)(2,1)S(1)} %get-tuple-element.23.refs_3_, ...), custom_call_target="tpu_custom_call" | custom-call | flops 7549747200 | bytes 1048576 | tf_op jit(solution)/shard_map/pallas_call | solution.py:229
  58.7 0.5 collective-permute-start.15
  59.1 0.0 collective-permute-done.18.refs_1_
  59.1 4.5 %shard_map.63 = (bf16[320,1152]{1,0:T(8,128)(2,1)S(1)}, bf16[320,1152]{1,0:T(8,128)(2,1)S(1)}, bf16[320,1152]{1,0:T(8,128)(2,1)S(1)}, bf16[320,1152]{1,0:T(8,128)(2,1)S(1)}) custom-call(s32[1]{0:T(128)} %bitcast.refs_0_.refs_1_, bf16[2,1280,640]{2,1,0:T(8,128)(2,1)S(1)} %collective-permute-done.18.refs_1_, f32[2,640,1152]{2,1,0:T(8,128)S(1)} %get-tuple-element.28.refs_2_, ...), custom_call_target="tpu_custom_call" | custom-call | flops 3774873600 | bytes 1048576 | tf_op jit(solution)/shard_map/pallas_call | solution.py:229
  63.6 2.8 %collective-permute-start.19 = (bf16[320,1152]{1,0:T(8,128)(2,1)S(1)}, bf16[320,1152]{1,0:T(8,128)(2,1)S(1)}, u32[]{:S(2)}, u32[]{:S(2)}) collective-permute-start(bf16[320,1152]{1,0:T(8,128)(2,1)S(1)} %get-tuple-element.30), channel_id=1, source_target_pairs={{0,2},{1,67},{2,0},{3,65},{4,6},{5,71},{6,4},{7,69},{8,10},{9,75},... | collective-permute-start | bytes 2211848 | tf_op jit(solution)/shard_map/ppermute | solution.py:57
  66.4 3.5 %collective-permute-start.20 = (bf16[320,1152]{1,0:T(8,128)(2,1)S(1)}, bf16[320,1152]{1,0:T(8,128)(2,1)S(1)}, u32[]{:S(2)}, u32[]{:S(2)}) collective-permute-start(bf16[320,1152]{1,0:T(8,128)(2,1)S(1)} %get-tuple-element.32), channel_id=1, source_target_pairs={{0,12},{1,49},{2,14},{3,51},{4,0},{5,53},{6,2},{7,55},{8,4},{9,57}... | collective-permute-start | bytes 2211848 | tf_op jit(solution)/shard_map/ppermute | solution.py:48
  69.9 0.0 collective-permute-start.21
  70.0 0.0 collective-permute-done.15.refs_3_
  70.0 8.7 %shard_map.62 = (bf16[320,1152]{1,0:T(8,128)(2,1)S(1)}, bf16[320,1152]{1,0:T(8,128)(2,1)S(1)}, bf16[320,1152]{1,0:T(8,128)(2,1)S(1)}, bf16[320,1152]{1,0:T(8,128)(2,1)S(1)}) custom-call(s32[1]{0:T(128)} %bitcast.refs_0_.refs_1_, bf16[2,1280,640]{2,1,0:T(8,128)(2,1)S(1)} %get-tuple-element.22.refs_2_.refs_1_, ...), custom_call_target="tpu_custom_call" | custom-call | flops 7549747200 | bytes 1048576 | tf_op jit(solution)/shard_map/pallas_call | solution.py:229
  78.7 2.7 %collective-permute-start.16 = (bf16[320,1152]{1,0:T(8,128)(2,1)S(1)}, bf16[320,1152]{1,0:T(8,128)(2,1)S(1)}, u32[]{:S(2)}, u32[]{:S(2)}) collective-permute-start(bf16[320,1152]{1,0:T(8,128)(2,1)S(1)} %get-tuple-element.26), channel_id=1, source_target_pairs={{0,12},{1,49},{2,14},{3,51},{4,0},{5,53},{6,2},{7,55},{8,4},{9,57}... | collective-permute-start | bytes 2211848 | tf_op jit(solution)/shard_map/ppermute | solution.py:48
  81.4 0.0 collective-permute-start.17
  81.4 0.0 collective-permute-done.19.refs_1_
  81.4 0.0 collective-permute-done.20.refs_3_
  81.4 0.1 collective-permute-done.21.refs_4_
  81.5 0.5 shard_map.64
  81.9 1.3 %collective-permute-start.22 = (bf16[320,1152]{1,0:T(8,128)(2,1)S(1)}, bf16[320,1152]{1,0:T(8,128)(2,1)S(1)}, u32[]{:S(2)}, u32[]{:S(2)}) collective-permute-start(bf16[320,1152]{1,0:T(8,128)(2,1)S(1)} %get-tuple-element.34), channel_id=1, source_target_pairs={{0,8},{1,33},{2,10},{3,35},{4,12},{5,37},{6,14},{7,39},{8,0},{9,41... | collective-permute-start | bytes 2211848 | tf_op jit(solution)/shard_map/ppermute | solution.py:48
  83.2 0.1 collective-permute-start.23
  83.3 14.4 %collective-permute-done.16.refs_4_ = bf16[320,1152]{1,0:T(8,128)(2,1)S(1)} collective-permute-done((bf16[320,1152]{1,0:T(8,128)(2,1)S(1)}, bf16[320,1152]{1,0:T(8,128)(2,1)S(1)}, u32[]{:S(2)}, u32[]{:S(2)}) %collective-permute-start.16) | collective-permute-done | bytes 737312 | tf_op jit(solution)/shard_map/ppermute | solution.py:48
  97.7 3.2 %collective-permute-done.17.refs_5_ = bf16[320,1152]{1,0:T(8,128)(2,1)S(1)} collective-permute-done((bf16[320,1152]{1,0:T(8,128)(2,1)S(1)}, bf16[320,1152]{1,0:T(8,128)(2,1)S(1)}, u32[]{:S(2)}, u32[]{:S(2)}) %collective-permute-start.17) | collective-permute-done | bytes 737312 | tf_op jit(solution)/shard_map/ppermute | solution.py:48
  101.0 0.0 collective-permute-done.22.refs_6_
  101.0 0.0 collective-permute-done.23.refs_7_
  101.0 1.0 shard_map.65
  102.0 0.5 collective-permute-start.24
  102.5 1.3 %collective-permute-done.24 = bf16[160,1152]{1,0:T(8,128)(2,1)S(1)} collective-permute-done((bf16[160,1152]{1,0:T(8,128)(2,1)S(1)}, bf16[160,1152]{1,0:T(8,128)(2,1)S(1)}, u32[]{:S(2)}, u32[]{:S(2)}) %collective-permute-start.24) | collective-permute-done | bytes 368672 | tf_op jit(solution)/shard_map/ppermute | solution.py:61
  103.8 0.9 broadcast_select_fusion
  (4 shorter events, 0.1 us)
Async XLA Ops:
  1.8 2.8 %collective-permute-start = (bf16[160,1152]{1,0:T(8,128)(2,1)S(1)}, bf16[160,1152]{1,0:T(8,128)(2,1)S(1)}, u32[]{:S(2)}, u32[]{:S(2)}) collective-permute-start(bf16[160,1152]{1,0:T(8,128)(2,1)S(1)} %get-tuple-element.40), channel_id=1, source_target_pairs={{0,1},{1,0},{2,3},{3,2},{4,5},{5,4},{6,7},{7,6},{8,9},{9,8},{10,11... | collective-permute-start | bytes 1105928 | tf_op jit(solution)/shard_map/ppermute | solution.py:61
  5.0 12.8 %collective-permute-start.1 = (bf16[320,1152]{1,0:T(8,128)(2,1)S(1)}, bf16[320,1152]{1,0:T(8,128)(2,1)S(1)}, u32[]{:S(2)}, u32[]{:S(2)}) collective-permute-start(bf16[320,1152]{1,0:T(8,128)(2,1)S(1)} %get-tuple-element.21.refs_2_.refs_4_), channel_id=1, source_target_pairs={{0,4},{1,17},{2,6},{3,19},{4,8},{5,21},{6,10},{7,23},{8,12},{9,25}... | collective-permute-start | bytes 2211848 | tf_op jit(solution)/shard_map/ppermute | solution.py:48
  6.8 11.8 %collective-permute-start.2 = (bf16[320,1152]{1,0:T(8,128)(2,1)S(1)}, bf16[320,1152]{1,0:T(8,128)(2,1)S(1)}, u32[]{:S(2)}, u32[]{:S(2)}) collective-permute-start(bf16[320,1152]{1,0:T(8,128)(2,1)S(1)} %get-tuple-element.21.refs_2_.refs_4_), channel_id=1, source_target_pairs={{0,12},{1,49},{2,14},{3,51},{4,0},{5,53},{6,2},{7,55},{8,4},{9,57}... | collective-permute-start | bytes 2211848 | tf_op jit(solution)/shard_map/ppermute | solution.py:48
  9.0 13.5 %collective-permute-start.3 = (bf16[320,1152]{1,0:T(8,128)(2,1)S(1)}, bf16[320,1152]{1,0:T(8,128)(2,1)S(1)}, u32[]{:S(2)}, u32[]{:S(2)}) collective-permute-start(bf16[320,1152]{1,0:T(8,128)(2,1)S(1)} %get-tuple-element.21.refs_2_.refs_4_), channel_id=1, source_target_pairs={{0,2},{1,67},{2,0},{3,65},{4,6},{5,71},{6,4},{7,69},{8,10},{9,75},... | collective-permute-start | bytes 2211848 | tf_op jit(solution)/shard_map/ppermute | solution.py:57
  17.8 7.9 %collective-permute-start.4 = (bf16[160,1152]{1,0:T(8,128)(2,1)S(1)}, bf16[160,1152]{1,0:T(8,128)(2,1)S(1)}, u32[]{:S(2)}, u32[]{:S(2)}) collective-permute-start(bf16[160,1152]{1,0:T(8,128)(2,1)S(1)} %slice.8), channel_id=1, source_target_pairs={{0,4},{1,17},{2,6},{3,19},{4,8},{5,21},{6,10},{7,23},{8,12},{9,25}... | collective-permute-start | bytes 1105928 | tf_op jit(solution)/shard_map/ppermute | solution.py:48
  17.9 17.6 %collective-permute-start.9 = (bf16[320,1152]{1,0:T(8,128)(2,1)S(1)}, bf16[320,1152]{1,0:T(8,128)(2,1)S(1)}, u32[]{:S(2)}, u32[]{:S(2)}) collective-permute-start(bf16[320,1152]{1,0:T(8,128)(2,1)S(1)} %get-tuple-element.21.refs_2_.refs_4_), channel_id=1, source_target_pairs={{0,1},{1,0},{2,3},{3,2},{4,5},{5,4},{6,7},{7,6},{8,9},{9,8},{10,11... | collective-permute-start | bytes 2211848 | tf_op jit(solution)/shard_map/ppermute | solution.py:61
  18.6 8.4 %collective-permute-start.5 = (bf16[160,1152]{1,0:T(8,128)(2,1)S(1)}, bf16[160,1152]{1,0:T(8,128)(2,1)S(1)}, u32[]{:S(2)}, u32[]{:S(2)}) collective-permute-start(bf16[160,1152]{1,0:T(8,128)(2,1)S(1)} %slice.9), channel_id=1, source_target_pairs={{0,12},{1,49},{2,14},{3,51},{4,0},{5,53},{6,2},{7,55},{8,4},{9,57}... | collective-permute-start | bytes 1105928 | tf_op jit(solution)/shard_map/ppermute | solution.py:48
  22.5 12.4 %collective-permute-start.7 = (bf16[320,1152]{1,0:T(8,128)(2,1)S(1)}, bf16[320,1152]{1,0:T(8,128)(2,1)S(1)}, u32[]{:S(2)}, u32[]{:S(2)}) collective-permute-start(bf16[320,1152]{1,0:T(8,128)(2,1)S(1)} %collective-permute-done.3.refs_5_.refs_7_), channel_id=1, source_target_pairs={{0,12},{1,49},{2,14},{3,51},{4,0},{5,53},{6,2},{7,55},{8,4},{9,57}... | collective-permute-start | bytes 2211848 | tf_op jit(solution)/shard_map/ppermute | solution.py:48
  22.6 12.2 %collective-permute-start.6 = (bf16[320,1152]{1,0:T(8,128)(2,1)S(1)}, bf16[320,1152]{1,0:T(8,128)(2,1)S(1)}, u32[]{:S(2)}, u32[]{:S(2)}) collective-permute-start(bf16[320,1152]{1,0:T(8,128)(2,1)S(1)} %collective-permute-done.3.refs_5_.refs_7_), channel_id=1, source_target_pairs={{0,4},{1,17},{2,6},{3,19},{4,8},{5,21},{6,10},{7,23},{8,12},{9,25}... | collective-permute-start | bytes 2211848 | tf_op jit(solution)/shard_map/ppermute | solution.py:48
  25.7 14.7 %collective-permute-start.10 = (bf16[640,1152]{1,0:T(8,128)(2,1)S(1)}, bf16[640,1152]{1,0:T(8,128)(2,1)S(1)}, u32[]{:S(2)}, u32[]{:S(2)}) collective-permute-start(bf16[640,1152]{1,0:T(8,128)(2,1)S(1)} %pad_maximum_fusion), channel_id=1, source_target_pairs={{0,1},{1,0},{2,3},{3,2},{4,5},{5,4},{6,7},{7,6},{8,9},{9,8},{10,11... | collective-permute-start | bytes 4423688 | tf_op jit(solution)/shard_map/ppermute | solution.py:61
  27.0 11.8 %collective-permute-start.8 = (bf16[320,1152]{1,0:T(8,128)(2,1)S(1)}, bf16[320,1152]{1,0:T(8,128)(2,1)S(1)}, u32[]{:S(2)}, u32[]{:S(2)}) collective-permute-start(bf16[320,1152]{1,0:T(8,128)(2,1)S(1)} %constant_dynamic-update-slice_fusion.refs_6_.refs_8_), channel_id=1, source_target_pairs={{0,2},{1,67},{2,0},{3,65},{4,6},{5,71},{6,4},{7,69},{8,10},{9,75},... | collective-permute-start | bytes 2211848 | tf_op jit(solution)/shard_map/ppermute | solution.py:57
  34.9 6.5 %collective-permute-start.13 = (bf16[640,1152]{1,0:T(8,128)(2,1)S(1)}, bf16[640,1152]{1,0:T(8,128)(2,1)S(1)}, u32[]{:S(2)}, u32[]{:S(2)}) collective-permute-start(bf16[640,1152]{1,0:T(8,128)(2,1)S(1)} %pad_maximum_fusion.1), channel_id=1, source_target_pairs={{0,1},{1,0},{2,3},{3,2},{4,5},{5,4},{6,7},{7,6},{8,9},{9,8},{10,11... | collective-permute-start | bytes 4423688 | tf_op jit(solution)/shard_map/ppermute | solution.py:61
  35.1 5.2 %collective-permute-start.11 = (bf16[320,1152]{1,0:T(8,128)(2,1)S(1)}, bf16[320,1152]{1,0:T(8,128)(2,1)S(1)}, u32[]{:S(2)}, u32[]{:S(2)}) collective-permute-start(bf16[320,1152]{1,0:T(8,128)(2,1)S(1)} %collective-permute-done.3.refs_5_.refs_7_), channel_id=1, source_target_pairs={{0,1},{1,0},{2,3},{3,2},{4,5},{5,4},{6,7},{7,6},{8,9},{9,8},{10,11... | collective-permute-start | bytes 2211848 | tf_op jit(solution)/shard_map/ppermute | solution.py:61
  35.5 4.9 %collective-permute-start.12 = (bf16[320,1152]{1,0:T(8,128)(2,1)S(1)}, bf16[320,1152]{1,0:T(8,128)(2,1)S(1)}, u32[]{:S(2)}, u32[]{:S(2)}) collective-permute-start(bf16[320,1152]{1,0:T(8,128)(2,1)S(1)} %constant_dynamic-update-slice_fusion.refs_6_.refs_8_), channel_id=1, source_target_pairs={{0,1},{1,0},{2,3},{3,2},{4,5},{5,4},{6,7},{7,6},{8,9},{9,8},{10,11... | collective-permute-start | bytes 2211848 | tf_op jit(solution)/shard_map/ppermute | solution.py:61
  38.8 2.7 %collective-permute-start.14 = (bf16[320,1152]{1,0:T(8,128)(2,1)S(1)}, bf16[320,1152]{1,0:T(8,128)(2,1)S(1)}, u32[]{:S(2)}, u32[]{:S(2)}) collective-permute-start(bf16[320,1152]{1,0:T(8,128)(2,1)S(1)} %collective-permute-done.8.refs_9_.refs_11_), channel_id=1, source_target_pairs={{0,1},{1,0},{2,3},{3,2},{4,5},{5,4},{6,7},{7,6},{8,9},{9,8},{10,11... | collective-permute-start | bytes 2211848 | tf_op jit(solution)/shard_map/ppermute | solution.py:61
  48.8 10.3 %collective-permute-start.18 = (bf16[2,1280,640]{2,1,0:T(8,128)(2,1)S(1)}, bf16[2,1280,640]{2,1,0:T(8,128)(2,1)S(1)}, u32[]{:S(2)}, u32[]{:S(2)}) collective-permute-start(bf16[2,1280,640]{2,1,0:T(8,128)(2,1)S(1)} %get-tuple-element.22.refs_2_.refs_1_), channel_id=1, source_target_pairs={{0,1},{1,0},{2,3},{3,2},{4,5},{5,4},{6,7},{7,6},{8,9},{9,8},{10,11... | collective-permute-start | bytes 9830408 | tf_op jit(solution)/shard_map/ppermute | solution.py:61
  58.7 11.3 %collective-permute-start.15 = (bf16[2,1280,640]{2,1,0:T(8,128)(2,1)S(1)}, bf16[2,1280,640]{2,1,0:T(8,128)(2,1)S(1)}, u32[]{:S(2)}, u32[]{:S(2)}) collective-permute-start(bf16[2,1280,640]{2,1,0:T(8,128)(2,1)S(1)} %get-tuple-element.24.refs_2_), channel_id=1, source_target_pairs={{0,1},{1,0},{2,3},{3,2},{4,5},{5,4},{6,7},{7,6},{8,9},{9,8},{10,11... | collective-permute-start | bytes 9830408 | tf_op jit(solution)/shard_map/ppermute | solution.py:61
  63.6 17.8 %collective-permute-start.19 = (bf16[320,1152]{1,0:T(8,128)(2,1)S(1)}, bf16[320,1152]{1,0:T(8,128)(2,1)S(1)}, u32[]{:S(2)}, u32[]{:S(2)}) collective-permute-start(bf16[320,1152]{1,0:T(8,128)(2,1)S(1)} %get-tuple-element.30), channel_id=1, source_target_pairs={{0,2},{1,67},{2,0},{3,65},{4,6},{5,71},{6,4},{7,69},{8,10},{9,75},... | collective-permute-start | bytes 2211848 | tf_op jit(solution)/shard_map/ppermute | solution.py:57
  66.4 15.0 %collective-permute-start.20 = (bf16[320,1152]{1,0:T(8,128)(2,1)S(1)}, bf16[320,1152]{1,0:T(8,128)(2,1)S(1)}, u32[]{:S(2)}, u32[]{:S(2)}) collective-permute-start(bf16[320,1152]{1,0:T(8,128)(2,1)S(1)} %get-tuple-element.32), channel_id=1, source_target_pairs={{0,12},{1,49},{2,14},{3,51},{4,0},{5,53},{6,2},{7,55},{8,4},{9,57}... | collective-permute-start | bytes 2211848 | tf_op jit(solution)/shard_map/ppermute | solution.py:48
  69.9 11.5 %collective-permute-start.21 = (bf16[320,1152]{1,0:T(8,128)(2,1)S(1)}, bf16[320,1152]{1,0:T(8,128)(2,1)S(1)}, u32[]{:S(2)}, u32[]{:S(2)}) collective-permute-start(bf16[320,1152]{1,0:T(8,128)(2,1)S(1)} %get-tuple-element.33), channel_id=1, source_target_pairs={{0,4},{1,17},{2,6},{3,19},{4,8},{5,21},{6,10},{7,23},{8,12},{9,25}... | collective-permute-start | bytes 2211848 | tf_op jit(solution)/shard_map/ppermute | solution.py:48
  78.7 19.1 %collective-permute-start.16 = (bf16[320,1152]{1,0:T(8,128)(2,1)S(1)}, bf16[320,1152]{1,0:T(8,128)(2,1)S(1)}, u32[]{:S(2)}, u32[]{:S(2)}) collective-permute-start(bf16[320,1152]{1,0:T(8,128)(2,1)S(1)} %get-tuple-element.26), channel_id=1, source_target_pairs={{0,12},{1,49},{2,14},{3,51},{4,0},{5,53},{6,2},{7,55},{8,4},{9,57}... | collective-permute-start | bytes 2211848 | tf_op jit(solution)/shard_map/ppermute | solution.py:48
  81.4 19.6 %collective-permute-start.17 = (bf16[320,1152]{1,0:T(8,128)(2,1)S(1)}, bf16[320,1152]{1,0:T(8,128)(2,1)S(1)}, u32[]{:S(2)}, u32[]{:S(2)}) collective-permute-start(bf16[320,1152]{1,0:T(8,128)(2,1)S(1)} %get-tuple-element.27), channel_id=1, source_target_pairs={{0,4},{1,17},{2,6},{3,19},{4,8},{5,21},{6,10},{7,23},{8,12},{9,25}... | collective-permute-start | bytes 2211848 | tf_op jit(solution)/shard_map/ppermute | solution.py:48
  81.9 19.0 %collective-permute-start.22 = (bf16[320,1152]{1,0:T(8,128)(2,1)S(1)}, bf16[320,1152]{1,0:T(8,128)(2,1)S(1)}, u32[]{:S(2)}, u32[]{:S(2)}) collective-permute-start(bf16[320,1152]{1,0:T(8,128)(2,1)S(1)} %get-tuple-element.34), channel_id=1, source_target_pairs={{0,8},{1,33},{2,10},{3,35},{4,12},{5,37},{6,14},{7,39},{8,0},{9,41... | collective-permute-start | bytes 2211848 | tf_op jit(solution)/shard_map/ppermute | solution.py:48
  83.2 17.7 %collective-permute-start.23 = (bf16[320,1152]{1,0:T(8,128)(2,1)S(1)}, bf16[320,1152]{1,0:T(8,128)(2,1)S(1)}, u32[]{:S(2)}, u32[]{:S(2)}) collective-permute-start(bf16[320,1152]{1,0:T(8,128)(2,1)S(1)} %get-tuple-element.35), channel_id=1, source_target_pairs={{0,2},{1,67},{2,0},{3,65},{4,6},{5,71},{6,4},{7,69},{8,10},{9,75},... | collective-permute-start | bytes 2211848 | tf_op jit(solution)/shard_map/ppermute | solution.py:57
  102.0 1.8 %collective-permute-start.24 = (bf16[160,1152]{1,0:T(8,128)(2,1)S(1)}, bf16[160,1152]{1,0:T(8,128)(2,1)S(1)}, u32[]{:S(2)}, u32[]{:S(2)}) collective-permute-start(bf16[160,1152]{1,0:T(8,128)(2,1)S(1)} %get-tuple-element.37), channel_id=1, source_target_pairs={{0,1},{1,0},{2,3},{3,2},{4,5},{5,4},{6,7},{7,6},{8,9},{9,8},{10,11... | collective-permute-start | bytes 1105928 | tf_op jit(solution)/shard_map/ppermute | solution.py:61

commit v8 on v7

--- a/solution.py
+++ b/solution.py
@@ -99,19 +99,23 @@
 
 
 def weights_of(scale_ref, mine_rows, other_rows, matched=None):
-    dots = lax.dot_general(
-        mine_rows,
-        other_rows,
-        (((1,), (1,)), ((), ())),
-        preferred_element_type=jnp.float32,
-    )
-    power = jnp.exp2(dots * scale_ref[0] + scale_ref[1])
-    share = pl.reciprocal(1.0 + power, approx=True)
-    if matched is not None:
-        row = lax.broadcasted_iota(jnp.int32, dots.shape, 0)
-        column = lax.broadcasted_iota(jnp.int32, dots.shape, 1)
-        share = jnp.where((row == column) & (row < rows) & matched, -power * share, share)
-    return share.astype(jnp.bfloat16)
+    blocks = []
+    for begin in range(0, mine_rows.shape[0], 2 * rows):
+        dots = lax.dot_general(
+            mine_rows[begin : begin + 2 * rows],
+            other_rows,
+            (((1,), (1,)), ((), ())),
+            preferred_element_type=jnp.float32,
+        )
+        power = jnp.exp2(dots * scale_ref[0] + scale_ref[1])
+        share = pl.reciprocal(1.0 + power, approx=True)
+        if matched is not None and begin == 0:
+            row = lax.broadcasted_iota(jnp.int32, dots.shape, 0)
+            column = lax.broadcasted_iota(jnp.int32, dots.shape, 1)
+            own = (row == column) & (row < rows) & matched
+            share = jnp.where(own, -power * share, share)
+        blocks.append(share.astype(jnp.bfloat16))
+    return jnp.concatenate(blocks, axis=0)
 
 
 def transposed_dot(weights, values):
@@ -132,73 +136,99 @@
         done += size
 
 
-def first_kernel(pieces, scale_ref, core_ref, *refs):
+def near_weights_kernel(pieces, scale_ref, core_ref, *refs):
     mine, other = places_of(refs[: pieces[0]]), places_of(refs[pieces[0] : sum(pieces)])
-    far_ref, near_ref = refs[sum(pieces) :]
-    for half in range(2):
-        mine_rows = stacked(mine, half * rows)
-        other_rows = stacked(other, opposite_rows(core_ref[0], half))
-        edge = 4 * rows - near_ref.shape[2]
-        near_ref[half] = weights_of(scale_ref, mine_rows, other_rows[edge : 4 * rows])
-        for begin, size in spans(4 * rows):
-            place = pl.ds(begin, size)
-            far_ref[half, :, place] = weights_of(
-                scale_ref,
-                mine_rows,
-                other_rows[4 * rows + begin : 4 * rows + begin + size],
-            )
-
-
-def second_kernel(pieces, scale_ref, core_ref, far_ref, edge_ref, *refs):
-    mine, other = places_of(refs[: pieces[0]]), places_of(refs[pieces[0] : sum(pieces)])
-    near_ref, part_ref = refs[sum(pieces) :]
+    (near_ref,) = refs[sum(pieces) :]
     core = core_ref[0]
-    edge = 4 * rows - edge_ref.shape[2]
     for half in range(2):
         mine_rows = stacked(mine, half * rows)
         other_rows = stacked(other, opposite_rows(core, half))
-        for begin, size in spans(edge):
+        for begin, size in spans(near_ref.shape[2]):
             near_ref[half, :, pl.ds(begin, size)] = weights_of(
                 scale_ref,
                 mine_rows,
                 other_rows[begin : begin + size],
                 core == 0 if begin == 0 else None,
             )
-        near_ref[half, :, pl.ds(edge, edge_ref.shape[2])] = edge_ref[half]
-        place = pl.ds(4 * rows, 4 * rows)
-        weights = jnp.concatenate(
-            [near_ref[half, place, :], far_ref[half, place, :]], axis=1
+
+
+def far_weights_kernel(pieces, scale_ref, core_ref, *refs):
+    mine, other = places_of(refs[: pieces[0]]), places_of(refs[pieces[0] : sum(pieces)])
+    edge_ref, far_ref = refs[sum(pieces) :]
+    edge = edge_ref.shape[2]
+    first = 4 * rows - edge
+    for half in range(2):
+        mine_rows = stacked(mine, half * rows)
+        other_rows = stacked(other, opposite_rows(core_ref[0], half))
+        for begin, size in spans(edge + far_ref.shape[2]):
+            start = first + begin
+            weights = weights_of(
+                scale_ref, mine_rows, other_rows[start : start + size]
+            )
+            if begin == 0:
+                edge_ref[half] = weights[:, :edge]
+                far_ref[half, :, pl.ds(0, size - edge)] = weights[:, edge:]
+            else:
+                far_ref[half, :, pl.ds(begin - edge, size)] = weights
+
+
+def own_product(half, first, count, weights_refs, other_rows):
+    weights = jnp.concatenate(
+        [ref[half, pl.ds(first, count), :] for ref in weights_refs], axis=1
+    )
+    return jnp.dot(weights, other_rows, preferred_element_type=jnp.float32)
+
+
+def own_kernel(pieces, core_ref, *refs):
+    weights_refs, other = refs[:3], places_of(refs[3 : 3 + pieces])
+    near_ref, far_ref, joined_ref = refs[3 + pieces :]
+    edge = 4 * rows - weights_refs[1].shape[2]
+    for half in range(2):
+        other_rows = stacked(other, opposite_rows(core_ref[0], half))
+        joined_ref[half, :, pl.ds(0, edge)] = weights_refs[0][half]
+        joined_ref[half, :, pl.ds(edge, 4 * rows - edge)] = weights_refs[1][half]
+        far_ref[half] = own_product(
+            half, 4 * rows, 4 * rows, weights_refs, other_rows
         )
-        part_ref[half] = jnp.dot(
-            weights, other_rows, preferred_element_type=jnp.float32
-        )
-
-
-def received(core, half, weights_ref, other):
+        near_ref[half] = own_product(half, rows, 3 * rows, weights_refs, other_rows)
+
+
+def received(core, half, columns, other):
     its_half = jnp.where(core == 0, 1 - half, half)
     other_rows = stacked(other, pl.multiple_of(its_half * rows, rows))
-    return transposed_dot(weights_ref[its_half], other_rows)
+    weights = jnp.concatenate(
+        [ref[its_half, :, pl.ds(first, size)] for ref, first, size in columns], axis=1
+    )
+    return transposed_dot(weights, other_rows)
 
 
 def far_kernel(pieces, core_ref, weights_ref, part_ref, *refs):
     other, sums = places_of(refs[:pieces]), places_of(refs[pieces:])
     for half in range(2):
-        total = part_ref[half] + received(core_ref[0], half, weights_ref, other)
+        columns = [(weights_ref, 0, 4 * rows)]
+        total = part_ref[half] + received(core_ref[0], half, columns, other)
         store_chips(sums, half * rows, 0, total)
 
 
-def near_kernel(pieces, core_ref, far_ref, near_ref, weights_ref, *refs):
+def near_kernel(pieces, core_ref, weights_ref, part_ref, *refs):
     other, sums = places_of(refs[:pieces]), places_of(refs[pieces:])
+    first = rows // 128 * 128
+    columns = [(weights_ref, first, 4 * rows - first)]
+    for half in range(2):
+        total = received(core_ref[0], half, columns, other)
+        total = total[rows - first :] + part_ref[half]
+        store_chips(sums, half * rows, 0, total)
+
+
+def self_kernel(pieces, core_ref, received_ref, *refs):
+    weights_refs, other = refs[:3], places_of(refs[3 : 3 + pieces])
+    sum_ref = refs[3 + pieces]
     core = core_ref[0]
     for half in range(2):
-        place = pl.ds(0, 4 * rows)
-        weights = jnp.concatenate(
-            [near_ref[half, place, :], far_ref[half, place, :]], axis=1
-        )
         other_rows = stacked(other, opposite_rows(core, half))
-        total = jnp.dot(weights, other_rows, preferred_element_type=jnp.float32)
-        total = total + received(core, half, weights_ref, other)
-        store_chips(sums, half * rows, 0, total)
+        total = own_product(half, 0, rows, weights_refs, other_rows)
+        total = total + received(core, half, [(received_ref, 0, chunk)], other)[:rows]
+        sum_ref[pl.ds(half * rows, rows), :] = total
 
 
 def final_kernel(scale_ref, core_ref, raw_ref, *refs):
@@ -307,48 +337,66 @@
     near_rows, all_rows = 4 * rows, 8 * rows
     edge = near_rows % chunk
     block = (chip_rows, width)
-    share = all_rows * all_rows * width
-    sizes = (len(mine), len(other))
-    far_weights, edge_weights = call(
-        functools.partial(first_kernel, sizes),
-        [(2, all_rows, near_rows), (2, all_rows, edge)],
+    share = all_rows * all_rows * width // 5
+    (near_weights,) = call(
+        functools.partial(near_weights_kernel, (len(mine), 3)),
+        [(2, all_rows, near_rows - edge)],
+        (factors, cores),
+        (*mine, *other[:3]),
+        8 * share,
+        (),
+    )
+    edge_weights, far_weights = call(
+        functools.partial(far_weights_kernel, (len(mine), len(other))),
+        [(2, all_rows, edge), (2, all_rows, near_rows)],
         (factors, cores),
         (*mine, *other),
-        2 * share,
+        12 * share,
+        (near_weights,),
     )
     far_received = swap(far_weights)
-    near_weights, far_part = call(
-        functools.partial(second_kernel, sizes),
-        [(2, all_rows, near_rows), (2, near_rows, width)],
-        (factors, cores),
-        (far_weights, edge_weights, *mine, *other),
-        4 * share,
-        kinds=(jnp.bfloat16, jnp.float32),
-    )
-    near_received = swap(near_weights)
+    weights = (near_weights, edge_weights, far_weights)
+    near_part, far_part, near_joined = call(
+        functools.partial(own_kernel, len(other)),
+        [(2, 3 * rows, width), (2, 4 * rows, width), (2, all_rows, near_rows)],
+        (cores,),
+        (*weights, *other),
+        18 * share,
+        kinds=(jnp.float32, jnp.float32, jnp.bfloat16),
+    )
+    near_received = swap(near_joined)
     far_sums = call(
         functools.partial(far_kernel, len(other)),
         [block] * 4,
         (cores,),
         (far_received, far_part, *other),
-        2 * share,
+        10 * share,
     )
     arrived = [ring(far_sums[1], -1), ring(far_sums[2], 1), pair(far_sums[3])]
     near_sums = call(
         functools.partial(near_kernel, len(other)),
-        [block] * 4,
+        [block] * 3,
         (cores,),
-        (far_weights, near_weights, near_received, *other),
-        4 * share,
+        (near_received, near_part, *other),
+        8 * share,
     )
     distant_total, across_total = add(
-        [(far_sums[0], arrived[2]), (near_sums[3], arrived[0], arrived[1])],
+        [(far_sums[0], arrived[2]), (near_sums[2], arrived[0], arrived[1])],
         (near_sums[0],),
     )
+    (own_sum,) = call(
+        functools.partial(self_kernel, len(other)),
+        [block],
+        (cores,),
+        (near_received, *weights, *other),
+        5 * share,
+        (distant_total,),
+        (jnp.float32,),
+    )
     parts = [
-        near_sums[0],
-        ring(near_sums[1], -1),
-        ring(near_sums[2], 1),
+        own_sum,
+        ring(near_sums[0], -1),
+        ring(near_sums[1], 1),
         ring(distant_total, 2),
         pair(across_total),
     ]

time: 105 us -> 102 us (0.971)
  waiting for transfers between devices: 37.4 us -> 34.8 us
    ppermute x11, waiting for transfers between devices: 30.3 us -> 28.6 us  [ring(): return lax.ppermute(value, axes, ring_move(steps))]
    pallas_call x7 -> x9, Pallas kernels: 31.9 us -> 31.4 us  [call(): pl.pallas_call(body, in_specs=[pl.BlockSpec(memory_space=pltpu.SMEM)] * l...]
  transfers between devices with their start and end apart: 25 -> 25, of which waited for: 11 -> 11; matrix products, arithmetic and copies ran while one was open for 0% -> 0% of each run, Pallas kernels for 22% -> 23%
where the time goes in v8:
time: 102 us
  waiting for transfers between devices  34.8 us (34%)
  Pallas kernels  31.4 us (31%)
  starting transfers between devices  30.8 us (30%)
  other arithmetic  2.41 us (2%)
  between operations  2.14 us (2%)
    pallas_call x9, Pallas kernels, call(): pl.pallas_call(body, in_specs=[pl.BlockSpec(memory_space=pltpu.SMEM)] * l...  31.4 us
    ppermute x11, waiting for transfers between devices, ring(): return lax.ppermute(value, axes, ring_move(steps))  28.6 us
    ppermute x11, starting transfers between devices, ring(): return lax.ppermute(value, axes, ring_move(steps))  17.2 us
    ppermute x4, starting transfers between devices, pair(): return lax.ppermute(value, axes, pairs_of(move))  8.54 us
    ppermute x10, starting transfers between devices, swap(): return lax.ppermute(value, 'core', [(0, 1), (1, 0)])  5.12 us
    ppermute x4, waiting for transfers between devices, pair(): return lax.ppermute(value, axes, pairs_of(move))  3.18 us
    ppermute x10, waiting for transfers between devices, swap(): return lax.ppermute(value, 'core', [(0, 1), (1, 0)])  3.01 us
  transfers between devices with their start and end apart: 25, of which 11 were waited for; matrix products, arithmetic and copies ran while one was open for 0% of the time, Pallas kernels for 23%

profile of v8, /device:TPU:1, one launch (start us, length us, event | category | flops | bytes accessed | tf_op | source)
XLA Modules:
  0.0 101.7 jit_solution(16619335383753067113)
XLA Ops:
  0.6 1.2 %broadcast_select_fusion.2 = (bf16[160,1152]{1,0:T(8,128)(2,1)S(1)}, bf16[160,1152]{1,0:T(8,128)(2,1)S(1)}) fusion(bf16[160,1152]{1,0:T(8,128)(2,1)} %param.5, bf16[160,1152]{1,0:T(8,128)(2,1)} %param.4, pred[]{:T(512)S(6)} %eq.3), kind=kLoop, calls=%fused_computation.4 | loop fusion | flops 368640 | bytes 1474561 | tf_op jit(solution)/shard_map/jit(_where)/select_n | solution.py:315
  1.8 1.5 %collective-permute-start = (bf16[160,1152]{1,0:T(8,128)(2,1)S(1)}, bf16[160,1152]{1,0:T(8,128)(2,1)S(1)}, u32[]{:S(2)}, u32[]{:S(2)}) collective-permute-start(bf16[160,1152]{1,0:T(8,128)(2,1)S(1)} %get-tuple-element.40), channel_id=1, source_target_pairs={{0,1},{1,0},{2,3},{3,2},{4,5},{5,4},{6,7},{7,6},{8,9},{9,8},{10,11... | collective-permute-start | bytes 1105928 | tf_op jit(solution)/shard_map/ppermute | solution.py:61
  3.3 1.3 %collective-permute-done.refs_2_ = bf16[160,1152]{1,0:T(8,128)(2,1)S(1)} collective-permute-done((bf16[160,1152]{1,0:T(8,128)(2,1)S(1)}, bf16[160,1152]{1,0:T(8,128)(2,1)S(1)}, u32[]{:S(2)}, u32[]{:S(2)}) %collective-permute-start) | collective-permute-done | bytes 368672 | tf_op jit(solution)/shard_map/ppermute | solution.py:61
  4.6 0.4 shard_map.59
  5.0 1.8 %collective-permute-start.1 = (bf16[320,1152]{1,0:T(8,128)(2,1)S(1)}, bf16[320,1152]{1,0:T(8,128)(2,1)S(1)}, u32[]{:S(2)}, u32[]{:S(2)}) collective-permute-start(bf16[320,1152]{1,0:T(8,128)(2,1)S(1)} %get-tuple-element.21.refs_2_), channel_id=1, source_target_pairs={{0,4},{1,17},{2,6},{3,19},{4,8},{5,21},{6,10},{7,23},{8,12},{9,25}... | collective-permute-start | bytes 2211848 | tf_op jit(solution)/shard_map/ppermute | solution.py:48
  6.8 2.2 %collective-permute-start.2 = (bf16[320,1152]{1,0:T(8,128)(2,1)S(1)}, bf16[320,1152]{1,0:T(8,128)(2,1)S(1)}, u32[]{:S(2)}, u32[]{:S(2)}) collective-permute-start(bf16[320,1152]{1,0:T(8,128)(2,1)S(1)} %get-tuple-element.21.refs_2_), channel_id=1, source_target_pairs={{0,12},{1,49},{2,14},{3,51},{4,0},{5,53},{6,2},{7,55},{8,4},{9,57}... | collective-permute-start | bytes 2211848 | tf_op jit(solution)/shard_map/ppermute | solution.py:48
  9.0 2.7 %collective-permute-start.3 = (bf16[320,1152]{1,0:T(8,128)(2,1)S(1)}, bf16[320,1152]{1,0:T(8,128)(2,1)S(1)}, u32[]{:S(2)}, u32[]{:S(2)}) collective-permute-start(bf16[320,1152]{1,0:T(8,128)(2,1)S(1)} %get-tuple-element.21.refs_2_), channel_id=1, source_target_pairs={{0,2},{1,67},{2,0},{3,65},{4,6},{5,71},{6,4},{7,69},{8,10},{9,75},... | collective-permute-start | bytes 2211848 | tf_op jit(solution)/shard_map/ppermute | solution.py:57
  11.7 6.0 %collective-permute-done.1.refs_3_ = bf16[320,1152]{1,0:T(8,128)(2,1)S(1)} collective-permute-done((bf16[320,1152]{1,0:T(8,128)(2,1)S(1)}, bf16[320,1152]{1,0:T(8,128)(2,1)S(1)}, u32[]{:S(2)}, u32[]{:S(2)}) %collective-permute-start.1) | collective-permute-done | bytes 737312 | tf_op jit(solution)/shard_map/ppermute | solution.py:48
  17.8 0.1 collective-permute-start.4
  17.9 0.7 collective-permute-start.9
  18.6 0.0 collective-permute-done.2.refs_4_
  18.6 3.8 %collective-permute-start.5 = (bf16[160,1152]{1,0:T(8,128)(2,1)S(1)}, bf16[160,1152]{1,0:T(8,128)(2,1)S(1)}, u32[]{:S(2)}, u32[]{:S(2)}) collective-permute-start(bf16[160,1152]{1,0:T(8,128)(2,1)S(1)} %slice.9), channel_id=1, source_target_pairs={{0,12},{1,49},{2,14},{3,51},{4,0},{5,53},{6,2},{7,55},{8,4},{9,57}... | collective-permute-start | bytes 1105928 | tf_op jit(solution)/shard_map/ppermute | solution.py:48
  22.5 0.0 collective-permute-done.3.refs_5_
  22.5 0.0 collective-permute-start.6
  22.5 2.7 %collective-permute-start.7 = (bf16[320,1152]{1,0:T(8,128)(2,1)S(1)}, bf16[320,1152]{1,0:T(8,128)(2,1)S(1)}, u32[]{:S(2)}, u32[]{:S(2)}) collective-permute-start(bf16[320,1152]{1,0:T(8,128)(2,1)S(1)} %collective-permute-done.3.refs_5_), channel_id=1, source_target_pairs={{0,12},{1,49},{2,14},{3,51},{4,0},{5,53},{6,2},{7,55},{8,4},{9,57}... | collective-permute-start | bytes 2211848 | tf_op jit(solution)/shard_map/ppermute | solution.py:48
  25.1 0.1 pad_maximum_fusion
  25.3 0.5 collective-permute-done.4
  25.8 1.2 %collective-permute-start.10 = (bf16[640,1152]{1,0:T(8,128)(2,1)S(1)}, bf16[640,1152]{1,0:T(8,128)(2,1)S(1)}, u32[]{:S(2)}, u32[]{:S(2)}) collective-permute-start(bf16[640,1152]{1,0:T(8,128)(2,1)S(1)} %pad_maximum_fusion), channel_id=1, source_target_pairs={{0,1},{1,0},{2,3},{3,2},{4,5},{5,4},{6,7},{7,6},{8,9},{9,8},{10,11... | collective-permute-start | bytes 4423688 | tf_op jit(solution)/shard_map/ppermute | solution.py:61
  27.0 0.0 collective-permute-done.5
  27.0 2.9 %collective-permute-start.8 = (bf16[320,1152]{1,0:T(8,128)(2,1)S(1)}, bf16[320,1152]{1,0:T(8,128)(2,1)S(1)}, u32[]{:S(2)}, u32[]{:S(2)}) collective-permute-start(bf16[320,1152]{1,0:T(8,128)(2,1)S(1)} %constant_dynamic-update-slice_fusion.refs_6_), channel_id=1, source_target_pairs={{0,2},{1,67},{2,0},{3,65},{4,6},{5,71},{6,4},{7,69},{8,10},{9,75},... | collective-permute-start | bytes 2211848 | tf_op jit(solution)/shard_map/ppermute | solution.py:57
  29.9 4.3 %collective-permute-done.6.refs_7_ = bf16[320,1152]{1,0:T(8,128)(2,1)S(1)} collective-permute-done((bf16[320,1152]{1,0:T(8,128)(2,1)S(1)}, bf16[320,1152]{1,0:T(8,128)(2,1)S(1)}, u32[]{:S(2)}, u32[]{:S(2)}) %collective-permute-start.6) | collective-permute-done | bytes 737312 | tf_op jit(solution)/shard_map/ppermute | solution.py:48
  34.3 0.5 collective-permute-done.7.refs_8_
  34.8 0.1 pad_maximum_fusion.1
  34.9 0.1 collective-permute-start.13
  35.1 0.5 collective-permute-start.11
  35.5 0.0 collective-permute-done.9.refs_10_.refs_4_.refs_3_.refs_5_
  35.5 0.1 collective-permute-start.12
  35.6 3.2 %collective-permute-done.8.refs_9_ = bf16[320,1152]{1,0:T(8,128)(2,1)S(1)} collective-permute-done((bf16[320,1152]{1,0:T(8,128)(2,1)S(1)}, bf16[320,1152]{1,0:T(8,128)(2,1)S(1)}, u32[]{:S(2)}, u32[]{:S(2)}) %collective-permute-start.8) | collective-permute-done | bytes 737312 | tf_op jit(solution)/shard_map/ppermute | solution.py:57
  38.8 0.0 collective-permute-start.14
  40.1 0.1 pad_maximum_fusion.2.refs_0_
  40.2 0.0 collective-permute-done.11.refs_12_.refs_6_.refs_5_.refs_7_
  40.2 0.0 collective-permute-done.10.refs_11_.refs_5_.refs_4_.refs_6_
  40.2 4.4 %shard_map.60.refs_16_.refs_1_.refs_2_ = bf16[2,1280,512]{2,1,0:T(8,128)(2,1)S(1)} custom-call(f32[2]{0:T(128)S(1)} %pad_maximum_fusion.2.refs_0_, s32[1]{0:T(128)} %bitcast.refs_0_.refs_1_, bf16[320,1152]{1,0:T(8,128)(2,1)S(1)} %get-tuple-element.21.refs_2_, bf16[320,1152]{1,0:T(8,128)(2,1)S(1)} %collective-permute-done.1.refs_3_, ...), custom_call_target="tpu_custom_call" | custom-call | flops 3019898880 | bytes 1048576 | tf_op jit(solution)/shard_map/pallas_call | solution.py:259
  44.7 0.0 collective-permute-done.12.refs_13_.refs_7_.refs_6_.refs_8_
  44.7 0.0 collective-permute-done.14.refs_15_.refs_9_.refs_8_.refs_10_
  44.7 0.0 collective-permute-done.13.refs_14_.refs_8_.refs_7_.refs_9_
  44.7 6.2 %shard_map.61 = (bf16[2,1280,128]{2,1,0:T(8,128)(2,1)S(1)}, bf16[2,1280,640]{2,1,0:T(8,128)(2,1)S(1)}) custom-call(f32[2]{0:T(128)S(1)} %pad_maximum_fusion.2.refs_0_, s32[1]{0:T(128)} %bitcast.refs_0_.refs_1_, bf16[320,1152]{1,0:T(8,128)(2,1)S(1)} %get-tuple-element.21.refs_2_, bf16[320,1152]{1,0:T(8,128)(2,1)S(1)} %collective-permute-done.1.refs_3_, ...), custom_call_target="tpu_custom_call" | custom-call | flops 4529848320 | bytes 1048576 | tf_op jit(solution)/shard_map/pallas_call | solution.py:259
  50.9 0.8 collective-permute-start.16
  51.8 7.7 %shard_map.62 = (f32[2,480,1152]{2,1,0:T(8,128)S(1)}, f32[2,640,1152]{2,1,0:T(8,128)S(1)}, bf16[2,1280,640]{2,1,0:T(8,128)(2,1)S(1)}) custom-call(s32[1]{0:T(128)} %bitcast.refs_0_.refs_1_, bf16[2,1280,512]{2,1,0:T(8,128)(2,1)S(1)} %shard_map.60.refs_16_.refs_1_.refs_2_, bf16[2,1280,128]{2,1,0:T(8,128)(2,1)S(1)} %get-tuple-element.22.refs_2_.refs_3_, ...), custom_call_target="tpu_custom_call" | custom-call | flops 6794772480 | bytes 1048576 | tf_op jit(solution)/shard_map/pallas_call | solution.py:259
  59.5 0.1 collective-permute-start.15
  59.6 0.0 collective-permute-done.16.refs_1_
  59.6 4.5 %shard_map.63 = (bf16[320,1152]{1,0:T(8,128)(2,1)S(1)}, bf16[320,1152]{1,0:T(8,128)(2,1)S(1)}, bf16[320,1152]{1,0:T(8,128)(2,1)S(1)}, bf16[320,1152]{1,0:T(8,128)(2,1)S(1)}) custom-call(s32[1]{0:T(128)} %bitcast.refs_0_.refs_1_, bf16[2,1280,640]{2,1,0:T(8,128)(2,1)S(1)} %collective-permute-done.16.refs_1_, f32[2,640,1152]{2,1,0:T(8,128)S(1)} %get-tuple-element.25.refs_2_, ...), custom_call_target="tpu_custom_call" | custom-call | flops 3774873600 | bytes 1048576 | tf_op jit(solution)/shard_map/pallas_call | solution.py:259
  64.1 2.8 %collective-permute-start.17 = (bf16[320,1152]{1,0:T(8,128)(2,1)S(1)}, bf16[320,1152]{1,0:T(8,128)(2,1)S(1)}, u32[]{:S(2)}, u32[]{:S(2)}) collective-permute-start(bf16[320,1152]{1,0:T(8,128)(2,1)S(1)} %get-tuple-element.27), channel_id=1, source_target_pairs={{0,2},{1,67},{2,0},{3,65},{4,6},{5,71},{6,4},{7,69},{8,10},{9,75},... | collective-permute-start | bytes 2211848 | tf_op jit(solution)/shard_map/ppermute | solution.py:57
  66.9 3.8 %collective-permute-start.18 = (bf16[320,1152]{1,0:T(8,128)(2,1)S(1)}, bf16[320,1152]{1,0:T(8,128)(2,1)S(1)}, u32[]{:S(2)}, u32[]{:S(2)}) collective-permute-start(bf16[320,1152]{1,0:T(8,128)(2,1)S(1)} %get-tuple-element.30), channel_id=1, source_target_pairs={{0,12},{1,49},{2,14},{3,51},{4,0},{5,53},{6,2},{7,55},{8,4},{9,57}... | collective-permute-start | bytes 2211848 | tf_op jit(solution)/shard_map/ppermute | solution.py:48
  70.6 0.0 collective-permute-start.19
  70.6 0.0 collective-permute-done.15.refs_1_
  70.6 3.7 %shard_map.64 = (bf16[320,1152]{1,0:T(8,128)(2,1)S(1)}, bf16[320,1152]{1,0:T(8,128)(2,1)S(1)}, bf16[320,1152]{1,0:T(8,128)(2,1)S(1)}) custom-call(s32[1]{0:T(128)} %bitcast.refs_0_.refs_1_, bf16[2,1280,640]{2,1,0:T(8,128)(2,1)S(1)} %collective-permute-done.15.refs_1_, f32[2,480,1152]{2,1,0:T(8,128)S(1)} %get-tuple-element.28.refs_2_, ...), custom_call_target="tpu_custom_call" | custom-call | flops 3019898880 | bytes 1048576 | tf_op jit(solution)/shard_map/pallas_call | solution.py:259
  74.3 2.7 %collective-permute-start.20 = (bf16[320,1152]{1,0:T(8,128)(2,1)S(1)}, bf16[320,1152]{1,0:T(8,128)(2,1)S(1)}, u32[]{:S(2)}, u32[]{:S(2)}) collective-permute-start(bf16[320,1152]{1,0:T(8,128)(2,1)S(1)} %get-tuple-element.32.refs_5_), channel_id=1, source_target_pairs={{0,12},{1,49},{2,14},{3,51},{4,0},{5,53},{6,2},{7,55},{8,4},{9,57}... | collective-permute-start | bytes 2211848 | tf_op jit(solution)/shard_map/ppermute | solution.py:48
  77.0 0.0 collective-permute-start.21
  77.0 0.0 collective-permute-done.17.refs_1_
  77.0 2.0 %collective-permute-done.18.refs_3_ = bf16[320,1152]{1,0:T(8,128)(2,1)S(1)} collective-permute-done((bf16[320,1152]{1,0:T(8,128)(2,1)S(1)}, bf16[320,1152]{1,0:T(8,128)(2,1)S(1)}, u32[]{:S(2)}, u32[]{:S(2)}) %collective-permute-start.18) | collective-permute-done | bytes 737312 | tf_op jit(solution)/shard_map/ppermute | solution.py:48
  79.0 3.4 %collective-permute-done.19.refs_4_ = bf16[320,1152]{1,0:T(8,128)(2,1)S(1)} collective-permute-done((bf16[320,1152]{1,0:T(8,128)(2,1)S(1)}, bf16[320,1152]{1,0:T(8,128)(2,1)S(1)}, u32[]{:S(2)}, u32[]{:S(2)}) %collective-permute-start.19) | collective-permute-done | bytes 737312 | tf_op jit(solution)/shard_map/ppermute | solution.py:48
  82.4 0.4 shard_map.65
  82.9 0.1 collective-permute-start.22
  83.0 0.2 collective-permute-start.23
  83.1 3.0 %shard_map.66.refs_3_ = f32[320,1152]{1,0:T(8,128)S(1)} custom-call(s32[1]{0:T(128)} %bitcast.refs_0_.refs_1_, bf16[2,1280,640]{2,1,0:T(8,128)(2,1)S(1)} %collective-permute-done.15.refs_1_, bf16[2,1280,512]{2,1,0:T(8,128)(2,1)S(1)} %shard_map.60.refs_16_.refs_1_.refs_2_, bf16[2,1280,128]{2,1,0:T(8,128)(2,1)S(1)} %get-tuple-element.22.refs_2_.refs_3_, ...), custom_call_target="tpu_custom_call" | custom-call | flops 1887436800 | bytes 1048576 | tf_op jit(solution)/shard_map/pallas_call | solution.py:259
  86.1 8.7 %collective-permute-done.20.refs_4_ = bf16[320,1152]{1,0:T(8,128)(2,1)S(1)} collective-permute-done((bf16[320,1152]{1,0:T(8,128)(2,1)S(1)}, bf16[320,1152]{1,0:T(8,128)(2,1)S(1)}, u32[]{:S(2)}, u32[]{:S(2)}) %collective-permute-start.20) | collective-permute-done | bytes 737312 | tf_op jit(solution)/shard_map/ppermute | solution.py:48
  94.8 3.1 %collective-permute-done.21.refs_5_ = bf16[320,1152]{1,0:T(8,128)(2,1)S(1)} collective-permute-done((bf16[320,1152]{1,0:T(8,128)(2,1)S(1)}, bf16[320,1152]{1,0:T(8,128)(2,1)S(1)}, u32[]{:S(2)}, u32[]{:S(2)}) %collective-permute-start.21) | collective-permute-done | bytes 737312 | tf_op jit(solution)/shard_map/ppermute | solution.py:48
  97.9 0.0 collective-permute-done.22.refs_6_
  97.9 0.0 collective-permute-done.23.refs_7_
  97.9 1.0 shard_map.67
  99.0 0.1 collective-permute-start.24
  99.0 1.7 %collective-permute-done.24 = bf16[160,1152]{1,0:T(8,128)(2,1)S(1)} collective-permute-done((bf16[160,1152]{1,0:T(8,128)(2,1)S(1)}, bf16[160,1152]{1,0:T(8,128)(2,1)S(1)}, u32[]{:S(2)}, u32[]{:S(2)}) %collective-permute-start.24) | collective-permute-done | bytes 368672 | tf_op jit(solution)/shard_map/ppermute | solution.py:61
  100.7 0.9 broadcast_select_fusion
  (4 shorter events, 0.1 us)
Async XLA Ops:
  1.8 2.8 %collective-permute-start = (bf16[160,1152]{1,0:T(8,128)(2,1)S(1)}, bf16[160,1152]{1,0:T(8,128)(2,1)S(1)}, u32[]{:S(2)}, u32[]{:S(2)}) collective-permute-start(bf16[160,1152]{1,0:T(8,128)(2,1)S(1)} %get-tuple-element.40), channel_id=1, source_target_pairs={{0,1},{1,0},{2,3},{3,2},{4,5},{5,4},{6,7},{7,6},{8,9},{9,8},{10,11... | collective-permute-start | bytes 1105928 | tf_op jit(solution)/shard_map/ppermute | solution.py:61
  5.0 12.8 %collective-permute-start.1 = (bf16[320,1152]{1,0:T(8,128)(2,1)S(1)}, bf16[320,1152]{1,0:T(8,128)(2,1)S(1)}, u32[]{:S(2)}, u32[]{:S(2)}) collective-permute-start(bf16[320,1152]{1,0:T(8,128)(2,1)S(1)} %get-tuple-element.21.refs_2_), channel_id=1, source_target_pairs={{0,4},{1,17},{2,6},{3,19},{4,8},{5,21},{6,10},{7,23},{8,12},{9,25}... | collective-permute-start | bytes 2211848 | tf_op jit(solution)/shard_map/ppermute | solution.py:48
  6.8 11.8 %collective-permute-start.2 = (bf16[320,1152]{1,0:T(8,128)(2,1)S(1)}, bf16[320,1152]{1,0:T(8,128)(2,1)S(1)}, u32[]{:S(2)}, u32[]{:S(2)}) collective-permute-start(bf16[320,1152]{1,0:T(8,128)(2,1)S(1)} %get-tuple-element.21.refs_2_), channel_id=1, source_target_pairs={{0,12},{1,49},{2,14},{3,51},{4,0},{5,53},{6,2},{7,55},{8,4},{9,57}... | collective-permute-start | bytes 2211848 | tf_op jit(solution)/shard_map/ppermute | solution.py:48
  9.0 13.5 %collective-permute-start.3 = (bf16[320,1152]{1,0:T(8,128)(2,1)S(1)}, bf16[320,1152]{1,0:T(8,128)(2,1)S(1)}, u32[]{:S(2)}, u32[]{:S(2)}) collective-permute-start(bf16[320,1152]{1,0:T(8,128)(2,1)S(1)} %get-tuple-element.21.refs_2_), channel_id=1, source_target_pairs={{0,2},{1,67},{2,0},{3,65},{4,6},{5,71},{6,4},{7,69},{8,10},{9,75},... | collective-permute-start | bytes 2211848 | tf_op jit(solution)/shard_map/ppermute | solution.py:57
  17.8 7.9 %collective-permute-start.4 = (bf16[160,1152]{1,0:T(8,128)(2,1)S(1)}, bf16[160,1152]{1,0:T(8,128)(2,1)S(1)}, u32[]{:S(2)}, u32[]{:S(2)}) collective-permute-start(bf16[160,1152]{1,0:T(8,128)(2,1)S(1)} %slice.8), channel_id=1, source_target_pairs={{0,4},{1,17},{2,6},{3,19},{4,8},{5,21},{6,10},{7,23},{8,12},{9,25}... | collective-permute-start | bytes 1105928 | tf_op jit(solution)/shard_map/ppermute | solution.py:48
  17.9 17.6 %collective-permute-start.9 = (bf16[320,1152]{1,0:T(8,128)(2,1)S(1)}, bf16[320,1152]{1,0:T(8,128)(2,1)S(1)}, u32[]{:S(2)}, u32[]{:S(2)}) collective-permute-start(bf16[320,1152]{1,0:T(8,128)(2,1)S(1)} %get-tuple-element.21.refs_2_), channel_id=1, source_target_pairs={{0,1},{1,0},{2,3},{3,2},{4,5},{5,4},{6,7},{7,6},{8,9},{9,8},{10,11... | collective-permute-start | bytes 2211848 | tf_op jit(solution)/shard_map/ppermute | solution.py:61
  18.6 8.4 %collective-permute-start.5 = (bf16[160,1152]{1,0:T(8,128)(2,1)S(1)}, bf16[160,1152]{1,0:T(8,128)(2,1)S(1)}, u32[]{:S(2)}, u32[]{:S(2)}) collective-permute-start(bf16[160,1152]{1,0:T(8,128)(2,1)S(1)} %slice.9), channel_id=1, source_target_pairs={{0,12},{1,49},{2,14},{3,51},{4,0},{5,53},{6,2},{7,55},{8,4},{9,57}... | collective-permute-start | bytes 1105928 | tf_op jit(solution)/shard_map/ppermute | solution.py:48
  22.5 11.8 %collective-permute-start.6 = (bf16[320,1152]{1,0:T(8,128)(2,1)S(1)}, bf16[320,1152]{1,0:T(8,128)(2,1)S(1)}, u32[]{:S(2)}, u32[]{:S(2)}) collective-permute-start(bf16[320,1152]{1,0:T(8,128)(2,1)S(1)} %collective-permute-done.3.refs_5_), channel_id=1, source_target_pairs={{0,4},{1,17},{2,6},{3,19},{4,8},{5,21},{6,10},{7,23},{8,12},{9,25}... | collective-permute-start | bytes 2211848 | tf_op jit(solution)/shard_map/ppermute | solution.py:48
  22.5 12.4 %collective-permute-start.7 = (bf16[320,1152]{1,0:T(8,128)(2,1)S(1)}, bf16[320,1152]{1,0:T(8,128)(2,1)S(1)}, u32[]{:S(2)}, u32[]{:S(2)}) collective-permute-start(bf16[320,1152]{1,0:T(8,128)(2,1)S(1)} %collective-permute-done.3.refs_5_), channel_id=1, source_target_pairs={{0,12},{1,49},{2,14},{3,51},{4,0},{5,53},{6,2},{7,55},{8,4},{9,57}... | collective-permute-start | bytes 2211848 | tf_op jit(solution)/shard_map/ppermute | solution.py:48
  25.8 14.5 %collective-permute-start.10 = (bf16[640,1152]{1,0:T(8,128)(2,1)S(1)}, bf16[640,1152]{1,0:T(8,128)(2,1)S(1)}, u32[]{:S(2)}, u32[]{:S(2)}) collective-permute-start(bf16[640,1152]{1,0:T(8,128)(2,1)S(1)} %pad_maximum_fusion), channel_id=1, source_target_pairs={{0,1},{1,0},{2,3},{3,2},{4,5},{5,4},{6,7},{7,6},{8,9},{9,8},{10,11... | collective-permute-start | bytes 4423688 | tf_op jit(solution)/shard_map/ppermute | solution.py:61
  27.0 11.8 %collective-permute-start.8 = (bf16[320,1152]{1,0:T(8,128)(2,1)S(1)}, bf16[320,1152]{1,0:T(8,128)(2,1)S(1)}, u32[]{:S(2)}, u32[]{:S(2)}) collective-permute-start(bf16[320,1152]{1,0:T(8,128)(2,1)S(1)} %constant_dynamic-update-slice_fusion.refs_6_), channel_id=1, source_target_pairs={{0,2},{1,67},{2,0},{3,65},{4,6},{5,71},{6,4},{7,69},{8,10},{9,75},... | collective-permute-start | bytes 2211848 | tf_op jit(solution)/shard_map/ppermute | solution.py:57
  34.9 9.7 %collective-permute-start.13 = (bf16[640,1152]{1,0:T(8,128)(2,1)S(1)}, bf16[640,1152]{1,0:T(8,128)(2,1)S(1)}, u32[]{:S(2)}, u32[]{:S(2)}) collective-permute-start(bf16[640,1152]{1,0:T(8,128)(2,1)S(1)} %pad_maximum_fusion.1), channel_id=1, source_target_pairs={{0,1},{1,0},{2,3},{3,2},{4,5},{5,4},{6,7},{7,6},{8,9},{9,8},{10,11... | collective-permute-start | bytes 4423688 | tf_op jit(solution)/shard_map/ppermute | solution.py:61
  35.1 5.2 %collective-permute-start.11 = (bf16[320,1152]{1,0:T(8,128)(2,1)S(1)}, bf16[320,1152]{1,0:T(8,128)(2,1)S(1)}, u32[]{:S(2)}, u32[]{:S(2)}) collective-permute-start(bf16[320,1152]{1,0:T(8,128)(2,1)S(1)} %collective-permute-done.3.refs_5_), channel_id=1, source_target_pairs={{0,1},{1,0},{2,3},{3,2},{4,5},{5,4},{6,7},{7,6},{8,9},{9,8},{10,11... | collective-permute-start | bytes 2211848 | tf_op jit(solution)/shard_map/ppermute | solution.py:61
  35.5 9.1 %collective-permute-start.12 = (bf16[320,1152]{1,0:T(8,128)(2,1)S(1)}, bf16[320,1152]{1,0:T(8,128)(2,1)S(1)}, u32[]{:S(2)}, u32[]{:S(2)}) collective-permute-start(bf16[320,1152]{1,0:T(8,128)(2,1)S(1)} %constant_dynamic-update-slice_fusion.refs_6_), channel_id=1, source_target_pairs={{0,1},{1,0},{2,3},{3,2},{4,5},{5,4},{6,7},{7,6},{8,9},{9,8},{10,11... | collective-permute-start | bytes 2211848 | tf_op jit(solution)/shard_map/ppermute | solution.py:61
  38.8 5.9 %collective-permute-start.14 = (bf16[320,1152]{1,0:T(8,128)(2,1)S(1)}, bf16[320,1152]{1,0:T(8,128)(2,1)S(1)}, u32[]{:S(2)}, u32[]{:S(2)}) collective-permute-start(bf16[320,1152]{1,0:T(8,128)(2,1)S(1)} %collective-permute-done.8.refs_9_), channel_id=1, source_target_pairs={{0,1},{1,0},{2,3},{3,2},{4,5},{5,4},{6,7},{7,6},{8,9},{9,8},{10,11... | collective-permute-start | bytes 2211848 | tf_op jit(solution)/shard_map/ppermute | solution.py:61
  50.9 8.7 %collective-permute-start.16 = (bf16[2,1280,640]{2,1,0:T(8,128)(2,1)S(1)}, bf16[2,1280,640]{2,1,0:T(8,128)(2,1)S(1)}, u32[]{:S(2)}, u32[]{:S(2)}) collective-permute-start(bf16[2,1280,640]{2,1,0:T(8,128)(2,1)S(1)} %get-tuple-element.23.refs_3_.refs_4_), channel_id=1, source_target_pairs={{0,1},{1,0},{2,3},{3,2},{4,5},{5,4},{6,7},{7,6},{8,9},{9,8},{10,11... | collective-permute-start | bytes 9830408 | tf_op jit(solution)/shard_map/ppermute | solution.py:61
  59.5 11.1 %collective-permute-start.15 = (bf16[2,1280,640]{2,1,0:T(8,128)(2,1)S(1)}, bf16[2,1280,640]{2,1,0:T(8,128)(2,1)S(1)}, u32[]{:S(2)}, u32[]{:S(2)}) collective-permute-start(bf16[2,1280,640]{2,1,0:T(8,128)(2,1)S(1)} %get-tuple-element.24), channel_id=1, source_target_pairs={{0,1},{1,0},{2,3},{3,2},{4,5},{5,4},{6,7},{7,6},{8,9},{9,8},{10,11... | collective-permute-start | bytes 9830408 | tf_op jit(solution)/shard_map/ppermute | solution.py:61
  64.1 12.9 %collective-permute-start.17 = (bf16[320,1152]{1,0:T(8,128)(2,1)S(1)}, bf16[320,1152]{1,0:T(8,128)(2,1)S(1)}, u32[]{:S(2)}, u32[]{:S(2)}) collective-permute-start(bf16[320,1152]{1,0:T(8,128)(2,1)S(1)} %get-tuple-element.27), channel_id=1, source_target_pairs={{0,2},{1,67},{2,0},{3,65},{4,6},{5,71},{6,4},{7,69},{8,10},{9,75},... | collective-permute-start | bytes 2211848 | tf_op jit(solution)/shard_map/ppermute | solution.py:57
  66.9 12.2 %collective-permute-start.18 = (bf16[320,1152]{1,0:T(8,128)(2,1)S(1)}, bf16[320,1152]{1,0:T(8,128)(2,1)S(1)}, u32[]{:S(2)}, u32[]{:S(2)}) collective-permute-start(bf16[320,1152]{1,0:T(8,128)(2,1)S(1)} %get-tuple-element.30), channel_id=1, source_target_pairs={{0,12},{1,49},{2,14},{3,51},{4,0},{5,53},{6,2},{7,55},{8,4},{9,57}... | collective-permute-start | bytes 2211848 | tf_op jit(solution)/shard_map/ppermute | solution.py:48
  70.6 11.8 %collective-permute-start.19 = (bf16[320,1152]{1,0:T(8,128)(2,1)S(1)}, bf16[320,1152]{1,0:T(8,128)(2,1)S(1)}, u32[]{:S(2)}, u32[]{:S(2)}) collective-permute-start(bf16[320,1152]{1,0:T(8,128)(2,1)S(1)} %get-tuple-element.31), channel_id=1, source_target_pairs={{0,4},{1,17},{2,6},{3,19},{4,8},{5,21},{6,10},{7,23},{8,12},{9,25}... | collective-permute-start | bytes 2211848 | tf_op jit(solution)/shard_map/ppermute | solution.py:48
  74.3 20.5 %collective-permute-start.20 = (bf16[320,1152]{1,0:T(8,128)(2,1)S(1)}, bf16[320,1152]{1,0:T(8,128)(2,1)S(1)}, u32[]{:S(2)}, u32[]{:S(2)}) collective-permute-start(bf16[320,1152]{1,0:T(8,128)(2,1)S(1)} %get-tuple-element.32.refs_5_), channel_id=1, source_target_pairs={{0,12},{1,49},{2,14},{3,51},{4,0},{5,53},{6,2},{7,55},{8,4},{9,57}... | collective-permute-start | bytes 2211848 | tf_op jit(solution)/shard_map/ppermute | solution.py:48
  77.0 20.9 %collective-permute-start.21 = (bf16[320,1152]{1,0:T(8,128)(2,1)S(1)}, bf16[320,1152]{1,0:T(8,128)(2,1)S(1)}, u32[]{:S(2)}, u32[]{:S(2)}) collective-permute-start(bf16[320,1152]{1,0:T(8,128)(2,1)S(1)} %get-tuple-element.34), channel_id=1, source_target_pairs={{0,4},{1,17},{2,6},{3,19},{4,8},{5,21},{6,10},{7,23},{8,12},{9,25}... | collective-permute-start | bytes 2211848 | tf_op jit(solution)/shard_map/ppermute | solution.py:48
  82.9 15.1 %collective-permute-start.22 = (bf16[320,1152]{1,0:T(8,128)(2,1)S(1)}, bf16[320,1152]{1,0:T(8,128)(2,1)S(1)}, u32[]{:S(2)}, u32[]{:S(2)}) collective-permute-start(bf16[320,1152]{1,0:T(8,128)(2,1)S(1)} %get-tuple-element.33.refs_11_), channel_id=1, source_target_pairs={{0,8},{1,33},{2,10},{3,35},{4,12},{5,37},{6,14},{7,39},{8,0},{9,41... | collective-permute-start | bytes 2211848 | tf_op jit(solution)/shard_map/ppermute | solution.py:48
  83.0 15.0 %collective-permute-start.23 = (bf16[320,1152]{1,0:T(8,128)(2,1)S(1)}, bf16[320,1152]{1,0:T(8,128)(2,1)S(1)}, u32[]{:S(2)}, u32[]{:S(2)}) collective-permute-start(bf16[320,1152]{1,0:T(8,128)(2,1)S(1)} %get-tuple-element.35), channel_id=1, source_target_pairs={{0,2},{1,67},{2,0},{3,65},{4,6},{5,71},{6,4},{7,69},{8,10},{9,75},... | collective-permute-start | bytes 2211848 | tf_op jit(solution)/shard_map/ppermute | solution.py:57
  99.0 1.8 %collective-permute-start.24 = (bf16[160,1152]{1,0:T(8,128)(2,1)S(1)}, bf16[160,1152]{1,0:T(8,128)(2,1)S(1)}, u32[]{:S(2)}, u32[]{:S(2)}) collective-permute-start(bf16[160,1152]{1,0:T(8,128)(2,1)S(1)} %get-tuple-element.37), channel_id=1, source_target_pairs={{0,1},{1,0},{2,3},{3,2},{4,5},{5,4},{6,7},{7,6},{8,9},{9,8},{10,11... | collective-permute-start | bytes 1105928 | tf_op jit(solution)/shard_map/ppermute | solution.py:61

commit v9 on v8

--- a/solution.py
+++ b/solution.py
@@ -66,15 +66,22 @@
     return values * inverse, inverse
 
 
-def pack_kernel(core_ref, keep_ref, got_ref, unit_ref, raw_ref):
+def pack_kernel(scale_ref, bias_ref, core_ref, keep_ref, got_ref, *refs):
+    unit_ref, low_ref, high_ref, raw_ref, factors_ref = refs
     first_core = core_ref[0] == 0
+    scale = jnp.exp(jnp.full((1, 128), scale_ref[0], jnp.float32))
+    factors_ref[0:1, :] = -log2_e * scale
+    factors_ref[1:2, :] = jnp.full((1, 128), -log2_e * bias_ref[0], jnp.float32)
+    factors_ref[2:3, :] = scale
     keep = keep_ref[...].astype(jnp.float32)
     got = got_ref[...].astype(jnp.float32)
     low = jnp.where(first_core, keep, got)
     high = jnp.where(first_core, got, keep)
     for half, values in enumerate((low, high)):
         place = pl.ds(half * rows, rows)
-        unit_ref[place, :] = unit_rows(values)[0].astype(jnp.bfloat16)
+        unit = unit_rows(values)[0].astype(jnp.bfloat16)
+        unit_ref[place, :] = unit
+        (low_ref, high_ref)[half][...] = unit
         raw_ref[place, :] = values.astype(jnp.bfloat16)
 
 
@@ -98,7 +105,7 @@
     return [(begin, min(chunk, count - begin)) for begin in range(0, count, chunk)]
 
 
-def weights_of(scale_ref, mine_rows, other_rows, matched=None):
+def weights_of(factors_ref, mine_rows, other_rows, matched=None):
     blocks = []
     for begin in range(0, mine_rows.shape[0], 2 * rows):
         dots = lax.dot_general(
@@ -107,7 +114,7 @@
             (((1,), (1,)), ((), ())),
             preferred_element_type=jnp.float32,
         )
-        power = jnp.exp2(dots * scale_ref[0] + scale_ref[1])
+        power = jnp.exp2(dots * factors_ref[0:1, 0:1] + factors_ref[1:2, 0:1])
         share = pl.reciprocal(1.0 + power, approx=True)
         if matched is not None and begin == 0:
             row = lax.broadcasted_iota(jnp.int32, dots.shape, 0)
@@ -136,7 +143,7 @@
         done += size
 
 
-def near_weights_kernel(pieces, scale_ref, core_ref, *refs):
+def near_weights_kernel(pieces, core_ref, factors_ref, *refs):
     mine, other = places_of(refs[: pieces[0]]), places_of(refs[pieces[0] : sum(pieces)])
     (near_ref,) = refs[sum(pieces) :]
     core = core_ref[0]
@@ -145,14 +152,14 @@
         other_rows = stacked(other, opposite_rows(core, half))
         for begin, size in spans(near_ref.shape[2]):
             near_ref[half, :, pl.ds(begin, size)] = weights_of(
-                scale_ref,
+                factors_ref,
                 mine_rows,
                 other_rows[begin : begin + size],
                 core == 0 if begin == 0 else None,
             )
 
 
-def far_weights_kernel(pieces, scale_ref, core_ref, *refs):
+def far_weights_kernel(pieces, core_ref, factors_ref, *refs):
     mine, other = places_of(refs[: pieces[0]]), places_of(refs[pieces[0] : sum(pieces)])
     edge_ref, far_ref = refs[sum(pieces) :]
     edge = edge_ref.shape[2]
@@ -163,7 +170,7 @@
         for begin, size in spans(edge + far_ref.shape[2]):
             start = first + begin
             weights = weights_of(
-                scale_ref, mine_rows, other_rows[start : start + size]
+                factors_ref, mine_rows, other_rows[start : start + size]
             )
             if begin == 0:
                 edge_ref[half] = weights[:, :edge]
@@ -231,22 +238,17 @@
         sum_ref[pl.ds(half * rows, rows), :] = total
 
 
-def final_kernel(scale_ref, core_ref, raw_ref, *refs):
-    parts, (keep_ref, give_ref) = refs[:-2], refs[-2:]
-    first_core = core_ref[0] == 0
-    grads = []
-    for half in range(2):
-        place = pl.ds(half * rows, rows)
-        unit, inverse = unit_rows(raw_ref[place, :].astype(jnp.float32))
-        direction = parts[0][place, :].astype(jnp.float32)
-        for part in parts[1:]:
-            direction = direction + part[place, :].astype(jnp.float32)
-        direction = direction * scale_ref[0]
-        along = jnp.sum(unit * direction, axis=1, keepdims=True)
-        grads.append(inverse * (direction - unit * along))
-    low, high = grads
-    keep_ref[...] = jnp.where(first_core, low, high).astype(jnp.bfloat16)
-    give_ref[...] = jnp.where(first_core, high, low).astype(jnp.bfloat16)
+def final_kernel(kept, core_ref, factors_ref, raw_ref, *refs):
+    parts, grad_ref = refs[:-1], refs[-1]
+    half = jnp.where(core_ref[0] == 0, 1 - kept, kept)
+    place = pl.ds(pl.multiple_of(half * rows, rows), rows)
+    unit, inverse = unit_rows(raw_ref[place, :].astype(jnp.float32))
+    direction = parts[0][place, :].astype(jnp.float32)
+    for part in parts[1:]:
+        direction = direction + part[place, :].astype(jnp.float32)
+    direction = direction * factors_ref[2:3, 0:1]
+    along = jnp.sum(unit * direction, axis=1, keepdims=True)
+    grad_ref[...] = (inverse * (direction - unit * along)).astype(jnp.bfloat16)
 
 
 def call(kernel, out_shape, scalars, arrays, flops=0, after=(), kinds=None):
@@ -284,7 +286,7 @@
         sum_ref[...] = total.astype(sum_ref.dtype)
 
 
-def add(groups, after=()):
+def add(groups, after=(), kind=jnp.bfloat16):
     arrays = []
     places = []
     for group in groups:
@@ -302,6 +304,7 @@
         (),
         arrays,
         after=after,
+        kinds=[kind] * len(groups),
     )
 
 
@@ -310,19 +313,21 @@
     core = lax.axis_index("core")
     first_core = core == 0
     cores = core.astype(jnp.int32).reshape(1)
-    logit_scale = jnp.exp(log_scale)
-    factors = jnp.concatenate([-log2_e * logit_scale, -log2_e * logit_bias])
     give = jnp.where(first_core, text_embeds, image_embeds)
     keep = jnp.where(first_core, image_embeds, text_embeds)
     got = swap(give)
-    unit, raw = call(
+    unit, low, high, raw, factors = call(
         pack_kernel,
-        [(chip_rows, width)] * 2,
-        (cores,),
+        [(chip_rows, width)] + [(rows, width)] * 2 + [(chip_rows, width), (8, 128)],
+        (log_scale, logit_bias, cores),
         (keep, got),
-    )
-    left, right, across = ring(unit, 1), ring(unit, -1), pair(unit)
-    distant = jnp.concatenate([ring(left[:rows], 1), ring(right[rows:], -1)], axis=0)
+        kinds=(jnp.bfloat16,) * 4 + (jnp.float32,),
+    )
+    left_low, right_high = ring(low, 1), ring(high, -1)
+    left = jnp.concatenate([left_low, ring(high, 1)], axis=0)
+    right = jnp.concatenate([ring(low, -1), right_high], axis=0)
+    across = pair(unit)
+    distant = jnp.concatenate([ring(left_low, 1), ring(right_high, -1)], axis=0)
     near = [unit, left, right, across]
     far = [distant, ring(across, 1), ring(across, -1), pair(distant)]
     mine = near + far
@@ -341,16 +346,16 @@
     (near_weights,) = call(
         functools.partial(near_weights_kernel, (len(mine), 3)),
         [(2, all_rows, near_rows - edge)],
-        (factors, cores),
-        (*mine, *other[:3]),
+        (cores,),
+        (factors, *mine, *other[:3]),
         8 * share,
         (),
     )
     edge_weights, far_weights = call(
         functools.partial(far_weights_kernel, (len(mine), len(other))),
         [(2, all_rows, edge), (2, all_rows, near_rows)],
-        (factors, cores),
-        (*mine, *other),
+        (cores,),
+        (factors, *mine, *other),
         12 * share,
         (near_weights,),
     )
@@ -380,10 +385,7 @@
         (near_received, near_part, *other),
         8 * share,
     )
-    distant_total, across_total = add(
-        [(far_sums[0], arrived[2]), (near_sums[2], arrived[0], arrived[1])],
-        (near_sums[0],),
-    )
+    (distant_total,) = add([(far_sums[0], arrived[2])], (near_sums[0],))
     (own_sum,) = call(
         functools.partial(self_kernel, len(other)),
         [block],
@@ -393,17 +395,28 @@
         (distant_total,),
         (jnp.float32,),
     )
+    (across_total,) = add([(near_sums[2], arrived[0], arrived[1])], (own_sum,))
+    (own_part,) = add([(own_sum, ring(distant_total, 2))], kind=jnp.float32)
     parts = [
-        own_sum,
+        own_part,
         ring(near_sums[0], -1),
         ring(near_sums[1], 1),
-        ring(distant_total, 2),
         pair(across_total),
     ]
-    keep, give = call(
-        final_kernel, [(rows, width)] * 2, (logit_scale, cores), (raw, *parts)
+    (give,) = call(
+        functools.partial(final_kernel, 0),
+        [(rows, width)],
+        (cores,),
+        (factors, raw, *parts),
     )
     given = swap(give)
+    (keep,) = call(
+        functools.partial(final_kernel, 1),
+        [(rows, width)],
+        (cores,),
+        (factors, raw, *parts),
+        after=(give,),
+    )
     image_grad = jnp.where(first_core, keep, given)
     text_grad = jnp.where(first_core, given, keep)
     return (image_grad, text_grad)

time: 102 us -> 98.5 us (0.966)
  waiting for transfers between devices: 34.8 us -> 33.3 us
    ppermute x11 -> x13, starting transfers between devices: 17.2 us -> 20.2 us  [ring(): return lax.ppermute(value, axes, ring_move(steps))]
    ppermute x4, starting transfers between devices: 8.54 us -> 6.49 us  [pair(): return lax.ppermute(value, axes, pairs_of(move))]
    ppermute x10, starting transfers between devices: 5.12 us -> 3.33 us  [swap(): return lax.ppermute(value, 'core', [(0, 1), (1, 0)])]
    ppermute x10, waiting for transfers between devices: 3.01 us -> 1.95 us  [swap(): return lax.ppermute(value, 'core', [(0, 1), (1, 0)])]
    pallas_call x9 -> x12, Pallas kernels: 31.4 us -> 30.4 us  [call(): pl.pallas_call(body, in_specs=[pl.BlockSpec(memory_space=pltpu.SMEM)] * l...]
    ppermute x11 -> x13, waiting for transfers between devices: 28.6 us -> 28.3 us  [ring(): return lax.ppermute(value, axes, ring_move(steps))]
  transfers between devices with their start and end apart: 25 -> 27, of which waited for: 11 -> 11; matrix products, arithmetic and copies ran while one was open for 0% -> 0% of each run, Pallas kernels for 23% -> 24%
where the time goes in v9:
time: 98.5 us; the launch traced here: 98.4 us
  waiting for transfers between devices  33.3 us (34%)
  Pallas kernels  30.4 us (31%)
  starting transfers between devices  30 us (30%)
  other arithmetic  2.33 us (2%)
  between operations  2.16 us (2%)
    pallas_call x12, Pallas kernels, call(): pl.pallas_call(body, in_specs=[pl.BlockSpec(memory_space=pltpu.SMEM)] * l...  30.4 us
    ppermute x13, waiting for transfers between devices, ring(): return lax.ppermute(value, axes, ring_move(steps))  28.3 us
    ppermute x13, starting transfers between devices, ring(): return lax.ppermute(value, axes, ring_move(steps))  20.2 us
    ppermute x4, starting transfers between devices, pair(): return lax.ppermute(value, axes, pairs_of(move))  6.49 us
    ppermute x10, starting transfers between devices, swap(): return lax.ppermute(value, 'core', [(0, 1), (1, 0)])  3.33 us
    ppermute x4, waiting for transfers between devices, pair(): return lax.ppermute(value, axes, pairs_of(move))  3.06 us
  transfers between devices with their start and end apart: 27, of which 11 were waited for; matrix products, arithmetic and copies ran while one was open for 0% of the time, Pallas kernels for 24%

profile of v9, /device:TPU:1, one launch (start us, length us, event | category | flops | bytes accessed | tf_op | source)
XLA Modules:
  0.0 98.4 jit_solution(5234347626538039696)
XLA Ops:
  0.6 1.2 %broadcast_select_fusion.2 = (bf16[160,1152]{1,0:T(8,128)(2,1)S(1)}, bf16[160,1152]{1,0:T(8,128)(2,1)S(1)}) fusion(bf16[160,1152]{1,0:T(8,128)(2,1)} %param.5, bf16[160,1152]{1,0:T(8,128)(2,1)} %param.4, pred[]{:T(512)S(6)} %eq.3), kind=kLoop, calls=%fused_computation.4 | loop fusion | flops 368640 | bytes 1474561 | tf_op jit(solution)/shard_map/jit(_where)/select_n | solution.py:316
  1.8 1.5 %collective-permute-start = (bf16[160,1152]{1,0:T(8,128)(2,1)S(1)}, bf16[160,1152]{1,0:T(8,128)(2,1)S(1)}, u32[]{:S(2)}, u32[]{:S(2)}) collective-permute-start(bf16[160,1152]{1,0:T(8,128)(2,1)S(1)} %get-tuple-element.38), channel_id=1, source_target_pairs={{0,1},{1,0},{2,3},{3,2},{4,5},{5,4},{6,7},{7,6},{8,9},{9,8},{10,11... | collective-permute-start | bytes 1105928 | tf_op jit(solution)/shard_map/ppermute | solution.py:61
  4.6 0.0 collective-permute-done.refs_4_
  4.6 0.4 shard_map.59
  5.0 2.9 %collective-permute-start.5 = (bf16[320,1152]{1,0:T(8,128)(2,1)S(1)}, bf16[320,1152]{1,0:T(8,128)(2,1)S(1)}, u32[]{:S(2)}, u32[]{:S(2)}) collective-permute-start(bf16[320,1152]{1,0:T(8,128)(2,1)S(1)} %get-tuple-element.21.refs_2_), channel_id=1, source_target_pairs={{0,2},{1,67},{2,0},{3,65},{4,6},{5,71},{6,4},{7,69},{8,10},{9,75},... | collective-permute-start | bytes 2211848 | tf_op jit(solution)/shard_map/ppermute | solution.py:57
  7.9 1.6 %collective-permute-start.1 = (bf16[160,1152]{1,0:T(8,128)(2,1)S(1)}, bf16[160,1152]{1,0:T(8,128)(2,1)S(1)}, u32[]{:S(2)}, u32[]{:S(2)}) collective-permute-start(bf16[160,1152]{1,0:T(8,128)(2,1)S(1)} %get-tuple-element.22), channel_id=1, source_target_pairs={{0,4},{1,17},{2,6},{3,19},{4,8},{5,21},{6,10},{7,23},{8,12},{9,25}... | collective-permute-start | bytes 1105928 | tf_op jit(solution)/shard_map/ppermute | solution.py:48
  9.6 2.1 %collective-permute-start.4 = (bf16[160,1152]{1,0:T(8,128)(2,1)S(1)}, bf16[160,1152]{1,0:T(8,128)(2,1)S(1)}, u32[]{:S(2)}, u32[]{:S(2)}) collective-permute-start(bf16[160,1152]{1,0:T(8,128)(2,1)S(1)} %get-tuple-element.23), channel_id=1, source_target_pairs={{0,12},{1,49},{2,14},{3,51},{4,0},{5,53},{6,2},{7,55},{8,4},{9,57}... | collective-permute-start | bytes 1105928 | tf_op jit(solution)/shard_map/ppermute | solution.py:48
  11.7 0.0 collective-permute-start.2
  11.7 2.7 %collective-permute-start.3 = (bf16[160,1152]{1,0:T(8,128)(2,1)S(1)}, bf16[160,1152]{1,0:T(8,128)(2,1)S(1)}, u32[]{:S(2)}, u32[]{:S(2)}) collective-permute-start(bf16[160,1152]{1,0:T(8,128)(2,1)S(1)} %get-tuple-element.22), channel_id=1, source_target_pairs={{0,12},{1,49},{2,14},{3,51},{4,0},{5,53},{6,2},{7,55},{8,4},{9,57}... | collective-permute-start | bytes 1105928 | tf_op jit(solution)/shard_map/ppermute | solution.py:48
  14.4 2.5 %collective-permute-done.1 = bf16[160,1152]{1,0:T(8,128)(2,1)S(1)} collective-permute-done((bf16[160,1152]{1,0:T(8,128)(2,1)S(1)}, bf16[160,1152]{1,0:T(8,128)(2,1)S(1)}, u32[]{:S(2)}, u32[]{:S(2)}) %collective-permute-start.1) | collective-permute-done | bytes 368672 | tf_op jit(solution)/shard_map/ppermute | solution.py:48
  16.9 0.0 collective-permute-start.6
  16.9 0.0 collective-permute-done.4
  16.9 0.0 collective-permute-start.11
  16.9 3.9 %collective-permute-done.2 = bf16[160,1152]{1,0:T(8,128)(2,1)S(1)} collective-permute-done((bf16[160,1152]{1,0:T(8,128)(2,1)S(1)}, bf16[160,1152]{1,0:T(8,128)(2,1)S(1)}, u32[]{:S(2)}, u32[]{:S(2)}) %collective-permute-start.2) | collective-permute-done | bytes 368672 | tf_op jit(solution)/shard_map/ppermute | solution.py:48
  20.8 1.5 %collective-permute-start.7 = (bf16[160,1152]{1,0:T(8,128)(2,1)S(1)}, bf16[160,1152]{1,0:T(8,128)(2,1)S(1)}, u32[]{:S(2)}, u32[]{:S(2)}) collective-permute-start(bf16[160,1152]{1,0:T(8,128)(2,1)S(1)} %collective-permute-done.4), channel_id=1, source_target_pairs={{0,12},{1,49},{2,14},{3,51},{4,0},{5,53},{6,2},{7,55},{8,4},{9,57}... | collective-permute-start | bytes 1105928 | tf_op jit(solution)/shard_map/ppermute | solution.py:48
  22.3 0.0 collective-permute-start.8
  22.3 0.0 collective-permute-done.3
  22.3 2.7 %collective-permute-start.9 = (bf16[320,1152]{1,0:T(8,128)(2,1)S(1)}, bf16[320,1152]{1,0:T(8,128)(2,1)S(1)}, u32[]{:S(2)}, u32[]{:S(2)}) collective-permute-start(bf16[320,1152]{1,0:T(8,128)(2,1)S(1)} %collective-permute-done.5.refs_5_), channel_id=1, source_target_pairs={{0,12},{1,49},{2,14},{3,51},{4,0},{5,53},{6,2},{7,55},{8,4},{9,57}... | collective-permute-start | bytes 2211848 | tf_op jit(solution)/shard_map/ppermute | solution.py:48
  25.0 0.1 pad_maximum_fusion
  25.1 0.0 collective-permute-done.6
  25.1 0.1 collective-permute-start.12
  25.2 2.3 %collective-permute-done.7 = bf16[160,1152]{1,0:T(8,128)(2,1)S(1)} collective-permute-done((bf16[160,1152]{1,0:T(8,128)(2,1)S(1)}, bf16[160,1152]{1,0:T(8,128)(2,1)S(1)}, u32[]{:S(2)}, u32[]{:S(2)}) %collective-permute-start.7) | collective-permute-done | bytes 368672 | tf_op jit(solution)/shard_map/ppermute | solution.py:48
  27.5 0.2 collective-permute-start.10
  27.7 6.1 %collective-permute-done.8.refs_7_ = bf16[320,1152]{1,0:T(8,128)(2,1)S(1)} collective-permute-done((bf16[320,1152]{1,0:T(8,128)(2,1)S(1)}, bf16[320,1152]{1,0:T(8,128)(2,1)S(1)}, u32[]{:S(2)}, u32[]{:S(2)}) %collective-permute-start.8) | collective-permute-done | bytes 737312 | tf_op jit(solution)/shard_map/ppermute | solution.py:48
  33.8 1.6 %collective-permute-done.9.refs_8_ = bf16[320,1152]{1,0:T(8,128)(2,1)S(1)} collective-permute-done((bf16[320,1152]{1,0:T(8,128)(2,1)S(1)}, bf16[320,1152]{1,0:T(8,128)(2,1)S(1)}, u32[]{:S(2)}, u32[]{:S(2)}) %collective-permute-start.9) | collective-permute-done | bytes 737312 | tf_op jit(solution)/shard_map/ppermute | solution.py:48
  35.4 0.1 pad_maximum_fusion.1
  35.5 0.1 collective-permute-start.15
  35.6 0.5 collective-permute-start.13
  36.2 0.0 collective-permute-done.11.refs_10_.refs_4_.refs_3_.refs_5_
  36.2 0.2 collective-permute-start.14
  36.4 2.8 %collective-permute-done.10.refs_9_ = bf16[320,1152]{1,0:T(8,128)(2,1)S(1)} collective-permute-done((bf16[320,1152]{1,0:T(8,128)(2,1)S(1)}, bf16[320,1152]{1,0:T(8,128)(2,1)S(1)}, u32[]{:S(2)}, u32[]{:S(2)}) %collective-permute-start.10) | collective-permute-done | bytes 737312 | tf_op jit(solution)/shard_map/ppermute | solution.py:57
  39.1 0.0 collective-permute-start.16
  39.2 0.7 collective-permute-done.13.refs_12_.refs_6_.refs_5_.refs_7_
  39.9 3.9 %shard_map.60.refs_16_.refs_1_.refs_2_ = bf16[2,1280,512]{2,1,0:T(8,128)(2,1)S(1)} custom-call(s32[1]{0:T(128)} %bitcast.refs_2_.refs_0_, f32[8,128]{1,0:T(8,128)S(1)} %get-tuple-element.19.refs_1_, bf16[320,1152]{1,0:T(8,128)(2,1)S(1)} %get-tuple-element.21.refs_2_, bf16[320,1152]{1,0:T(8,128)(2,1)S(1)} %constant_dynamic-update-slice_fusion.refs_3_, ...), custom_call_target="tpu_custom_call" | custom-call | flops 3019898880 | bytes 1048576 | tf_op jit(solution)/shard_map/pallas_call | solution.py:261
  43.9 0.0 collective-permute-done.16.refs_15_.refs_9_.refs_8_.refs_10_
  43.9 0.0 collective-permute-done.15.refs_14_.refs_8_.refs_7_.refs_9_
  43.9 5.7 %shard_map.61 = (bf16[2,1280,128]{2,1,0:T(8,128)(2,1)S(1)}, bf16[2,1280,640]{2,1,0:T(8,128)(2,1)S(1)}) custom-call(s32[1]{0:T(128)} %bitcast.refs_2_.refs_0_, f32[8,128]{1,0:T(8,128)S(1)} %get-tuple-element.19.refs_1_, bf16[320,1152]{1,0:T(8,128)(2,1)S(1)} %get-tuple-element.21.refs_2_, bf16[320,1152]{1,0:T(8,128)(2,1)S(1)} %constant_dynamic-update-slice_fusion.refs_3_, ...), custom_call_target="tpu_custom_call" | custom-call | flops 4529848320 | bytes 1048576 | tf_op jit(solution)/shard_map/pallas_call | solution.py:261
  49.6 0.5 collective-permute-start.18
  50.1 7.7 %shard_map.62 = (f32[2,480,1152]{2,1,0:T(8,128)S(1)}, f32[2,640,1152]{2,1,0:T(8,128)S(1)}, bf16[2,1280,640]{2,1,0:T(8,128)(2,1)S(1)}) custom-call(s32[1]{0:T(128)} %bitcast.refs_2_.refs_0_, bf16[2,1280,512]{2,1,0:T(8,128)(2,1)S(1)} %shard_map.60.refs_16_.refs_1_.refs_2_, bf16[2,1280,128]{2,1,0:T(8,128)(2,1)S(1)} %get-tuple-element.24.refs_2_.refs_3_, ...), custom_call_target="tpu_custom_call" | custom-call | flops 6794772480 | bytes 1048576 | tf_op jit(solution)/shard_map/pallas_call | solution.py:261
  57.8 0.4 collective-permute-start.17
  58.2 4.5 %shard_map.63 = (bf16[320,1152]{1,0:T(8,128)(2,1)S(1)}, bf16[320,1152]{1,0:T(8,128)(2,1)S(1)}, bf16[320,1152]{1,0:T(8,128)(2,1)S(1)}, bf16[320,1152]{1,0:T(8,128)(2,1)S(1)}) custom-call(s32[1]{0:T(128)} %bitcast.refs_2_.refs_0_, bf16[2,1280,640]{2,1,0:T(8,128)(2,1)S(1)} %collective-permute-done.18.refs_1_, f32[2,640,1152]{2,1,0:T(8,128)S(1)} %get-tuple-element.27.refs_2_, ...), custom_call_target="tpu_custom_call" | custom-call | flops 3774873600 | bytes 1048576 | tf_op jit(solution)/shard_map/pallas_call | solution.py:261
  62.7 1.5 %collective-permute-start.19 = (bf16[320,1152]{1,0:T(8,128)(2,1)S(1)}, bf16[320,1152]{1,0:T(8,128)(2,1)S(1)}, u32[]{:S(2)}, u32[]{:S(2)}) collective-permute-start(bf16[320,1152]{1,0:T(8,128)(2,1)S(1)} %get-tuple-element.29), channel_id=1, source_target_pairs={{0,2},{1,67},{2,0},{3,65},{4,6},{5,71},{6,4},{7,69},{8,10},{9,75},... | collective-permute-start | bytes 2211848 | tf_op jit(solution)/shard_map/ppermute | solution.py:57
  64.2 3.7 %collective-permute-start.23 = (bf16[320,1152]{1,0:T(8,128)(2,1)S(1)}, bf16[320,1152]{1,0:T(8,128)(2,1)S(1)}, u32[]{:S(2)}, u32[]{:S(2)}) collective-permute-start(bf16[320,1152]{1,0:T(8,128)(2,1)S(1)} %get-tuple-element.34), channel_id=1, source_target_pairs={{0,12},{1,49},{2,14},{3,51},{4,0},{5,53},{6,2},{7,55},{8,4},{9,57}... | collective-permute-start | bytes 2211848 | tf_op jit(solution)/shard_map/ppermute | solution.py:48
  67.9 0.0 collective-permute-start.24
  67.9 0.0 collective-permute-done.17.refs_1_
  67.9 3.7 %shard_map.64 = (bf16[320,1152]{1,0:T(8,128)(2,1)S(1)}, bf16[320,1152]{1,0:T(8,128)(2,1)S(1)}, bf16[320,1152]{1,0:T(8,128)(2,1)S(1)}) custom-call(s32[1]{0:T(128)} %bitcast.refs_2_.refs_0_, bf16[2,1280,640]{2,1,0:T(8,128)(2,1)S(1)} %collective-permute-done.17.refs_1_, f32[2,480,1152]{2,1,0:T(8,128)S(1)} %get-tuple-element.30.refs_2_, ...), custom_call_target="tpu_custom_call" | custom-call | flops 3019898880 | bytes 1048576 | tf_op jit(solution)/shard_map/pallas_call | solution.py:261
  71.6 2.7 %collective-permute-start.21 = (bf16[320,1152]{1,0:T(8,128)(2,1)S(1)}, bf16[320,1152]{1,0:T(8,128)(2,1)S(1)}, u32[]{:S(2)}, u32[]{:S(2)}) collective-permute-start(bf16[320,1152]{1,0:T(8,128)(2,1)S(1)} %get-tuple-element.31.refs_2_), channel_id=1, source_target_pairs={{0,12},{1,49},{2,14},{3,51},{4,0},{5,53},{6,2},{7,55},{8,4},{9,57}... | collective-permute-start | bytes 2211848 | tf_op jit(solution)/shard_map/ppermute | solution.py:48
  74.4 0.3 collective-permute-done.19.refs_1_
  74.6 0.2 shard_map.65.refs_11_
  74.8 3.1 %collective-permute-start.20 = (bf16[320,1152]{1,0:T(8,128)(2,1)S(1)}, bf16[320,1152]{1,0:T(8,128)(2,1)S(1)}, u32[]{:S(2)}, u32[]{:S(2)}) collective-permute-start(bf16[320,1152]{1,0:T(8,128)(2,1)S(1)} %shard_map.65.refs_11_), channel_id=1, source_target_pairs={{0,8},{1,33},{2,10},{3,35},{4,12},{5,37},{6,14},{7,39},{8,0},{9,41... | collective-permute-start | bytes 2211848 | tf_op jit(solution)/shard_map/ppermute | solution.py:48
  77.9 3.0 %shard_map.66.refs_0_.refs_3_ = f32[320,1152]{1,0:T(8,128)S(1)} custom-call(s32[1]{0:T(128)} %bitcast.refs_2_.refs_0_, bf16[2,1280,640]{2,1,0:T(8,128)(2,1)S(1)} %collective-permute-done.17.refs_1_, bf16[2,1280,512]{2,1,0:T(8,128)(2,1)S(1)} %shard_map.60.refs_16_.refs_1_.refs_2_, bf16[2,1280,128]{2,1,0:T(8,128)(2,1)S(1)} %get-tuple-element.24.refs_2_.refs_3_, ...), custom_call_target="tpu_custom_call" | custom-call | flops 1887436800 | bytes 1048576 | tf_op jit(solution)/shard_map/pallas_call | solution.py:261
  80.9 0.0 collective-permute-done.23.refs_1_
  81.0 0.3 shard_map.68
  81.2 2.0 %collective-permute-start.25 = (bf16[320,1152]{1,0:T(8,128)(2,1)S(1)}, bf16[320,1152]{1,0:T(8,128)(2,1)S(1)}, u32[]{:S(2)}, u32[]{:S(2)}) collective-permute-start(bf16[320,1152]{1,0:T(8,128)(2,1)S(1)} %shard_map.68), channel_id=1, source_target_pairs={{0,2},{1,67},{2,0},{3,65},{4,6},{5,71},{6,4},{7,69},{8,10},{9,75},... | collective-permute-start | bytes 2211848 | tf_op jit(solution)/shard_map/ppermute | solution.py:57
  83.2 10.8 %collective-permute-done.20.refs_1_ = bf16[320,1152]{1,0:T(8,128)(2,1)S(1)} collective-permute-done((bf16[320,1152]{1,0:T(8,128)(2,1)S(1)}, bf16[320,1152]{1,0:T(8,128)(2,1)S(1)}, u32[]{:S(2)}, u32[]{:S(2)}) %collective-permute-start.20) | collective-permute-done | bytes 737312 | tf_op jit(solution)/shard_map/ppermute | solution.py:48
  94.0 0.2 shard_map.67.refs_3_
  94.2 0.0 collective-permute-done.21.refs_4_
  94.2 1.1 %collective-permute-done.22.refs_5_ = bf16[320,1152]{1,0:T(8,128)(2,1)S(1)} collective-permute-done((bf16[320,1152]{1,0:T(8,128)(2,1)S(1)}, bf16[320,1152]{1,0:T(8,128)(2,1)S(1)}, u32[]{:S(2)}, u32[]{:S(2)}) %collective-permute-start.22) | collective-permute-done | bytes 737312 | tf_op jit(solution)/shard_map/ppermute | solution.py:48
  95.3 0.0 collective-permute-done.25.refs_6_
  95.3 0.4 shard_map.69.refs_7_
  95.7 0.1 collective-permute-start.26
  95.8 0.4 shard_map.70
  96.2 1.2 %collective-permute-done.26 = bf16[160,1152]{1,0:T(8,128)(2,1)S(1)} collective-permute-done((bf16[160,1152]{1,0:T(8,128)(2,1)S(1)}, bf16[160,1152]{1,0:T(8,128)(2,1)S(1)}, u32[]{:S(2)}, u32[]{:S(2)}) %collective-permute-start.26) | collective-permute-done | bytes 368672 | tf_op jit(solution)/shard_map/ppermute | solution.py:61
  97.5 0.9 broadcast_select_fusion
  (12 shorter events, 0.2 us)
Async XLA Ops:
  1.8 2.8 %collective-permute-start = (bf16[160,1152]{1,0:T(8,128)(2,1)S(1)}, bf16[160,1152]{1,0:T(8,128)(2,1)S(1)}, u32[]{:S(2)}, u32[]{:S(2)}) collective-permute-start(bf16[160,1152]{1,0:T(8,128)(2,1)S(1)} %get-tuple-element.38), channel_id=1, source_target_pairs={{0,1},{1,0},{2,3},{3,2},{4,5},{5,4},{6,7},{7,6},{8,9},{9,8},{10,11... | collective-permute-start | bytes 1105928 | tf_op jit(solution)/shard_map/ppermute | solution.py:61
  5.0 17.3 %collective-permute-start.5 = (bf16[320,1152]{1,0:T(8,128)(2,1)S(1)}, bf16[320,1152]{1,0:T(8,128)(2,1)S(1)}, u32[]{:S(2)}, u32[]{:S(2)}) collective-permute-start(bf16[320,1152]{1,0:T(8,128)(2,1)S(1)} %get-tuple-element.21.refs_2_), channel_id=1, source_target_pairs={{0,2},{1,67},{2,0},{3,65},{4,6},{5,71},{6,4},{7,69},{8,10},{9,75},... | collective-permute-start | bytes 2211848 | tf_op jit(solution)/shard_map/ppermute | solution.py:57
  7.9 9.0 %collective-permute-start.1 = (bf16[160,1152]{1,0:T(8,128)(2,1)S(1)}, bf16[160,1152]{1,0:T(8,128)(2,1)S(1)}, u32[]{:S(2)}, u32[]{:S(2)}) collective-permute-start(bf16[160,1152]{1,0:T(8,128)(2,1)S(1)} %get-tuple-element.22), channel_id=1, source_target_pairs={{0,4},{1,17},{2,6},{3,19},{4,8},{5,21},{6,10},{7,23},{8,12},{9,25}... | collective-permute-start | bytes 1105928 | tf_op jit(solution)/shard_map/ppermute | solution.py:48
  9.6 7.3 %collective-permute-start.4 = (bf16[160,1152]{1,0:T(8,128)(2,1)S(1)}, bf16[160,1152]{1,0:T(8,128)(2,1)S(1)}, u32[]{:S(2)}, u32[]{:S(2)}) collective-permute-start(bf16[160,1152]{1,0:T(8,128)(2,1)S(1)} %get-tuple-element.23), channel_id=1, source_target_pairs={{0,12},{1,49},{2,14},{3,51},{4,0},{5,53},{6,2},{7,55},{8,4},{9,57}... | collective-permute-start | bytes 1105928 | tf_op jit(solution)/shard_map/ppermute | solution.py:48
  11.7 9.1 %collective-permute-start.2 = (bf16[160,1152]{1,0:T(8,128)(2,1)S(1)}, bf16[160,1152]{1,0:T(8,128)(2,1)S(1)}, u32[]{:S(2)}, u32[]{:S(2)}) collective-permute-start(bf16[160,1152]{1,0:T(8,128)(2,1)S(1)} %get-tuple-element.23), channel_id=1, source_target_pairs={{0,4},{1,17},{2,6},{3,19},{4,8},{5,21},{6,10},{7,23},{8,12},{9,25}... | collective-permute-start | bytes 1105928 | tf_op jit(solution)/shard_map/ppermute | solution.py:48
  11.7 10.6 %collective-permute-start.3 = (bf16[160,1152]{1,0:T(8,128)(2,1)S(1)}, bf16[160,1152]{1,0:T(8,128)(2,1)S(1)}, u32[]{:S(2)}, u32[]{:S(2)}) collective-permute-start(bf16[160,1152]{1,0:T(8,128)(2,1)S(1)} %get-tuple-element.22), channel_id=1, source_target_pairs={{0,12},{1,49},{2,14},{3,51},{4,0},{5,53},{6,2},{7,55},{8,4},{9,57}... | collective-permute-start | bytes 1105928 | tf_op jit(solution)/shard_map/ppermute | solution.py:48
  16.9 8.2 %collective-permute-start.6 = (bf16[160,1152]{1,0:T(8,128)(2,1)S(1)}, bf16[160,1152]{1,0:T(8,128)(2,1)S(1)}, u32[]{:S(2)}, u32[]{:S(2)}) collective-permute-start(bf16[160,1152]{1,0:T(8,128)(2,1)S(1)} %collective-permute-done.1), channel_id=1, source_target_pairs={{0,4},{1,17},{2,6},{3,19},{4,8},{5,21},{6,10},{7,23},{8,12},{9,25}... | collective-permute-start | bytes 1105928 | tf_op jit(solution)/shard_map/ppermute | solution.py:48
  16.9 19.3 %collective-permute-start.11 = (bf16[320,1152]{1,0:T(8,128)(2,1)S(1)}, bf16[320,1152]{1,0:T(8,128)(2,1)S(1)}, u32[]{:S(2)}, u32[]{:S(2)}) collective-permute-start(bf16[320,1152]{1,0:T(8,128)(2,1)S(1)} %get-tuple-element.21.refs_2_), channel_id=1, source_target_pairs={{0,1},{1,0},{2,3},{3,2},{4,5},{5,4},{6,7},{7,6},{8,9},{9,8},{10,11... | collective-permute-start | bytes 2211848 | tf_op jit(solution)/shard_map/ppermute | solution.py:61
  20.8 6.7 %collective-permute-start.7 = (bf16[160,1152]{1,0:T(8,128)(2,1)S(1)}, bf16[160,1152]{1,0:T(8,128)(2,1)S(1)}, u32[]{:S(2)}, u32[]{:S(2)}) collective-permute-start(bf16[160,1152]{1,0:T(8,128)(2,1)S(1)} %collective-permute-done.4), channel_id=1, source_target_pairs={{0,12},{1,49},{2,14},{3,51},{4,0},{5,53},{6,2},{7,55},{8,4},{9,57}... | collective-permute-start | bytes 1105928 | tf_op jit(solution)/shard_map/ppermute | solution.py:48
  22.3 11.5 %collective-permute-start.8 = (bf16[320,1152]{1,0:T(8,128)(2,1)S(1)}, bf16[320,1152]{1,0:T(8,128)(2,1)S(1)}, u32[]{:S(2)}, u32[]{:S(2)}) collective-permute-start(bf16[320,1152]{1,0:T(8,128)(2,1)S(1)} %collective-permute-done.5.refs_5_), channel_id=1, source_target_pairs={{0,4},{1,17},{2,6},{3,19},{4,8},{5,21},{6,10},{7,23},{8,12},{9,25}... | collective-permute-start | bytes 2211848 | tf_op jit(solution)/shard_map/ppermute | solution.py:48
  22.3 13.1 %collective-permute-start.9 = (bf16[320,1152]{1,0:T(8,128)(2,1)S(1)}, bf16[320,1152]{1,0:T(8,128)(2,1)S(1)}, u32[]{:S(2)}, u32[]{:S(2)}) collective-permute-start(bf16[320,1152]{1,0:T(8,128)(2,1)S(1)} %collective-permute-done.5.refs_5_), channel_id=1, source_target_pairs={{0,12},{1,49},{2,14},{3,51},{4,0},{5,53},{6,2},{7,55},{8,4},{9,57}... | collective-permute-start | bytes 2211848 | tf_op jit(solution)/shard_map/ppermute | solution.py:48
  25.1 14.8 %collective-permute-start.12 = (bf16[640,1152]{1,0:T(8,128)(2,1)S(1)}, bf16[640,1152]{1,0:T(8,128)(2,1)S(1)}, u32[]{:S(2)}, u32[]{:S(2)}) collective-permute-start(bf16[640,1152]{1,0:T(8,128)(2,1)S(1)} %pad_maximum_fusion), channel_id=1, source_target_pairs={{0,1},{1,0},{2,3},{3,2},{4,5},{5,4},{6,7},{7,6},{8,9},{9,8},{10,11... | collective-permute-start | bytes 4423688 | tf_op jit(solution)/shard_map/ppermute | solution.py:61
  27.5 11.6 %collective-permute-start.10 = (bf16[320,1152]{1,0:T(8,128)(2,1)S(1)}, bf16[320,1152]{1,0:T(8,128)(2,1)S(1)}, u32[]{:S(2)}, u32[]{:S(2)}) collective-permute-start(bf16[320,1152]{1,0:T(8,128)(2,1)S(1)} %constant_dynamic-update-slice_fusion.4.refs_6_), channel_id=1, source_target_pairs={{0,2},{1,67},{2,0},{3,65},{4,6},{5,71},{6,4},{7,69},{8,10},{9,75},... | collective-permute-start | bytes 2211848 | tf_op jit(solution)/shard_map/ppermute | solution.py:57
  35.5 8.4 %collective-permute-start.15 = (bf16[640,1152]{1,0:T(8,128)(2,1)S(1)}, bf16[640,1152]{1,0:T(8,128)(2,1)S(1)}, u32[]{:S(2)}, u32[]{:S(2)}) collective-permute-start(bf16[640,1152]{1,0:T(8,128)(2,1)S(1)} %pad_maximum_fusion.1), channel_id=1, source_target_pairs={{0,1},{1,0},{2,3},{3,2},{4,5},{5,4},{6,7},{7,6},{8,9},{9,8},{10,11... | collective-permute-start | bytes 4423688 | tf_op jit(solution)/shard_map/ppermute | solution.py:61
  35.6 4.3 %collective-permute-start.13 = (bf16[320,1152]{1,0:T(8,128)(2,1)S(1)}, bf16[320,1152]{1,0:T(8,128)(2,1)S(1)}, u32[]{:S(2)}, u32[]{:S(2)}) collective-permute-start(bf16[320,1152]{1,0:T(8,128)(2,1)S(1)} %collective-permute-done.5.refs_5_), channel_id=1, source_target_pairs={{0,1},{1,0},{2,3},{3,2},{4,5},{5,4},{6,7},{7,6},{8,9},{9,8},{10,11... | collective-permute-start | bytes 2211848 | tf_op jit(solution)/shard_map/ppermute | solution.py:61
  36.2 7.7 %collective-permute-start.14 = (bf16[320,1152]{1,0:T(8,128)(2,1)S(1)}, bf16[320,1152]{1,0:T(8,128)(2,1)S(1)}, u32[]{:S(2)}, u32[]{:S(2)}) collective-permute-start(bf16[320,1152]{1,0:T(8,128)(2,1)S(1)} %constant_dynamic-update-slice_fusion.4.refs_6_), channel_id=1, source_target_pairs={{0,1},{1,0},{2,3},{3,2},{4,5},{5,4},{6,7},{7,6},{8,9},{9,8},{10,11... | collective-permute-start | bytes 2211848 | tf_op jit(solution)/shard_map/ppermute | solution.py:61
  39.1 4.7 %collective-permute-start.16 = (bf16[320,1152]{1,0:T(8,128)(2,1)S(1)}, bf16[320,1152]{1,0:T(8,128)(2,1)S(1)}, u32[]{:S(2)}, u32[]{:S(2)}) collective-permute-start(bf16[320,1152]{1,0:T(8,128)(2,1)S(1)} %collective-permute-done.10.refs_9_), channel_id=1, source_target_pairs={{0,1},{1,0},{2,3},{3,2},{4,5},{5,4},{6,7},{7,6},{8,9},{9,8},{10,11... | collective-permute-start | bytes 2211848 | tf_op jit(solution)/shard_map/ppermute | solution.py:61
  49.6 8.6 %collective-permute-start.18 = (bf16[2,1280,640]{2,1,0:T(8,128)(2,1)S(1)}, bf16[2,1280,640]{2,1,0:T(8,128)(2,1)S(1)}, u32[]{:S(2)}, u32[]{:S(2)}) collective-permute-start(bf16[2,1280,640]{2,1,0:T(8,128)(2,1)S(1)} %get-tuple-element.25.refs_3_.refs_4_), channel_id=1, source_target_pairs={{0,1},{1,0},{2,3},{3,2},{4,5},{5,4},{6,7},{7,6},{8,9},{9,8},{10,11... | collective-permute-start | bytes 9830408 | tf_op jit(solution)/shard_map/ppermute | solution.py:61
  57.8 10.1 %collective-permute-start.17 = (bf16[2,1280,640]{2,1,0:T(8,128)(2,1)S(1)}, bf16[2,1280,640]{2,1,0:T(8,128)(2,1)S(1)}, u32[]{:S(2)}, u32[]{:S(2)}) collective-permute-start(bf16[2,1280,640]{2,1,0:T(8,128)(2,1)S(1)} %get-tuple-element.26), channel_id=1, source_target_pairs={{0,1},{1,0},{2,3},{3,2},{4,5},{5,4},{6,7},{7,6},{8,9},{9,8},{10,11... | collective-permute-start | bytes 9830408 | tf_op jit(solution)/shard_map/ppermute | solution.py:61
  62.7 11.9 %collective-permute-start.19 = (bf16[320,1152]{1,0:T(8,128)(2,1)S(1)}, bf16[320,1152]{1,0:T(8,128)(2,1)S(1)}, u32[]{:S(2)}, u32[]{:S(2)}) collective-permute-start(bf16[320,1152]{1,0:T(8,128)(2,1)S(1)} %get-tuple-element.29), channel_id=1, source_target_pairs={{0,2},{1,67},{2,0},{3,65},{4,6},{5,71},{6,4},{7,69},{8,10},{9,75},... | collective-permute-start | bytes 2211848 | tf_op jit(solution)/shard_map/ppermute | solution.py:57
  64.2 16.8 %collective-permute-start.23 = (bf16[320,1152]{1,0:T(8,128)(2,1)S(1)}, bf16[320,1152]{1,0:T(8,128)(2,1)S(1)}, u32[]{:S(2)}, u32[]{:S(2)}) collective-permute-start(bf16[320,1152]{1,0:T(8,128)(2,1)S(1)} %get-tuple-element.34), channel_id=1, source_target_pairs={{0,12},{1,49},{2,14},{3,51},{4,0},{5,53},{6,2},{7,55},{8,4},{9,57}... | collective-permute-start | bytes 2211848 | tf_op jit(solution)/shard_map/ppermute | solution.py:48
  67.9 13.0 %collective-permute-start.24 = (bf16[320,1152]{1,0:T(8,128)(2,1)S(1)}, bf16[320,1152]{1,0:T(8,128)(2,1)S(1)}, u32[]{:S(2)}, u32[]{:S(2)}) collective-permute-start(bf16[320,1152]{1,0:T(8,128)(2,1)S(1)} %get-tuple-element.35), channel_id=1, source_target_pairs={{0,4},{1,17},{2,6},{3,19},{4,8},{5,21},{6,10},{7,23},{8,12},{9,25}... | collective-permute-start | bytes 2211848 | tf_op jit(solution)/shard_map/ppermute | solution.py:48
  71.6 22.6 %collective-permute-start.21 = (bf16[320,1152]{1,0:T(8,128)(2,1)S(1)}, bf16[320,1152]{1,0:T(8,128)(2,1)S(1)}, u32[]{:S(2)}, u32[]{:S(2)}) collective-permute-start(bf16[320,1152]{1,0:T(8,128)(2,1)S(1)} %get-tuple-element.31.refs_2_), channel_id=1, source_target_pairs={{0,12},{1,49},{2,14},{3,51},{4,0},{5,53},{6,2},{7,55},{8,4},{9,57}... | collective-permute-start | bytes 2211848 | tf_op jit(solution)/shard_map/ppermute | solution.py:48
  74.3 20.9 %collective-permute-start.22 = (bf16[320,1152]{1,0:T(8,128)(2,1)S(1)}, bf16[320,1152]{1,0:T(8,128)(2,1)S(1)}, u32[]{:S(2)}, u32[]{:S(2)}) collective-permute-start(bf16[320,1152]{1,0:T(8,128)(2,1)S(1)} %get-tuple-element.32), channel_id=1, source_target_pairs={{0,4},{1,17},{2,6},{3,19},{4,8},{5,21},{6,10},{7,23},{8,12},{9,25}... | collective-permute-start | bytes 2211848 | tf_op jit(solution)/shard_map/ppermute | solution.py:48
  74.8 19.2 %collective-permute-start.20 = (bf16[320,1152]{1,0:T(8,128)(2,1)S(1)}, bf16[320,1152]{1,0:T(8,128)(2,1)S(1)}, u32[]{:S(2)}, u32[]{:S(2)}) collective-permute-start(bf16[320,1152]{1,0:T(8,128)(2,1)S(1)} %shard_map.65.refs_11_), channel_id=1, source_target_pairs={{0,8},{1,33},{2,10},{3,35},{4,12},{5,37},{6,14},{7,39},{8,0},{9,41... | collective-permute-start | bytes 2211848 | tf_op jit(solution)/shard_map/ppermute | solution.py:48
  81.2 14.0 %collective-permute-start.25 = (bf16[320,1152]{1,0:T(8,128)(2,1)S(1)}, bf16[320,1152]{1,0:T(8,128)(2,1)S(1)}, u32[]{:S(2)}, u32[]{:S(2)}) collective-permute-start(bf16[320,1152]{1,0:T(8,128)(2,1)S(1)} %shard_map.68), channel_id=1, source_target_pairs={{0,2},{1,67},{2,0},{3,65},{4,6},{5,71},{6,4},{7,69},{8,10},{9,75},... | collective-permute-start | bytes 2211848 | tf_op jit(solution)/shard_map/ppermute | solution.py:57
  95.7 1.8 %collective-permute-start.26 = (bf16[160,1152]{1,0:T(8,128)(2,1)S(1)}, bf16[160,1152]{1,0:T(8,128)(2,1)S(1)}, u32[]{:S(2)}, u32[]{:S(2)}) collective-permute-start(bf16[160,1152]{1,0:T(8,128)(2,1)S(1)} %shard_map.69.refs_7_), channel_id=1, source_target_pairs={{0,1},{1,0},{2,3},{3,2},{4,5},{5,4},{6,7},{7,6},{8,9},{9,8},{10,11... | collective-permute-start | bytes 1105928 | tf_op jit(solution)/shard_map/ppermute | solution.py:61

commit v10 on v9

--- a/solution.py
+++ b/solution.py
@@ -145,18 +145,24 @@
 
 def near_weights_kernel(pieces, core_ref, factors_ref, *refs):
     mine, other = places_of(refs[: pieces[0]]), places_of(refs[pieces[0] : sum(pieces)])
-    (near_ref,) = refs[sum(pieces) :]
+    near_ref, begun_ref = refs[sum(pieces) :]
     core = core_ref[0]
+    count = near_ref.shape[2]
     for half in range(2):
         mine_rows = stacked(mine, half * rows)
         other_rows = stacked(other, opposite_rows(core, half))
-        for begin, size in spans(near_ref.shape[2]):
+        for begin, size in spans(count):
             near_ref[half, :, pl.ds(begin, size)] = weights_of(
                 factors_ref,
                 mine_rows,
                 other_rows[begin : begin + size],
                 core == 0 if begin == 0 else None,
             )
+        begun_ref[half] = jnp.dot(
+            near_ref[half, pl.ds(4 * rows, 4 * rows), :],
+            other_rows[:count],
+            preferred_element_type=jnp.float32,
+        )
 
 
 def far_weights_kernel(pieces, core_ref, factors_ref, *refs):
@@ -187,15 +193,16 @@
 
 
 def own_kernel(pieces, core_ref, *refs):
-    weights_refs, other = refs[:3], places_of(refs[3 : 3 + pieces])
-    near_ref, far_ref, joined_ref = refs[3 + pieces :]
+    weights_refs, begun_ref, other = refs[:3], refs[3], places_of(refs[4 : 4 + pieces])
+    near_ref, far_ref, joined_ref = refs[4 + pieces :]
+    count = weights_refs[0].shape[2]
     edge = 4 * rows - weights_refs[1].shape[2]
     for half in range(2):
         other_rows = stacked(other, opposite_rows(core_ref[0], half))
         joined_ref[half, :, pl.ds(0, edge)] = weights_refs[0][half]
         joined_ref[half, :, pl.ds(edge, 4 * rows - edge)] = weights_refs[1][half]
-        far_ref[half] = own_product(
-            half, 4 * rows, 4 * rows, weights_refs, other_rows
+        far_ref[half] = begun_ref[half] + own_product(
+            half, 4 * rows, 4 * rows, weights_refs[1:], other_rows[count:]
         )
         near_ref[half] = own_product(half, rows, 3 * rows, weights_refs, other_rows)
 
@@ -268,7 +275,7 @@
             jax.ShapeDtypeStruct(shape, kind_of)
             for shape, kind_of in zip(out_shape, kinds)
         ],
-        compiler_params=pltpu.CompilerParams(vmem_limit_bytes=16 * 2**20),
+        compiler_params=pltpu.CompilerParams(vmem_limit_bytes=8 * 2**20),
         cost_estimate=pl.CostEstimate(
             flops=flops, bytes_accessed=2**20, transcendentals=0
         ),
@@ -327,29 +334,27 @@
     left = jnp.concatenate([left_low, ring(high, 1)], axis=0)
     right = jnp.concatenate([ring(low, -1), right_high], axis=0)
     across = pair(unit)
-    distant = jnp.concatenate([ring(left_low, 1), ring(right_high, -1)], axis=0)
+    distant_low, distant_high = ring(left_low, 1), ring(right_high, -1)
+    distant = jnp.concatenate([distant_low, distant_high], axis=0)
+    far_distant = jnp.concatenate([pair(distant_low), pair(distant_high)], axis=0)
     near = [unit, left, right, across]
-    far = [distant, ring(across, 1), ring(across, -1), pair(distant)]
+    far = [distant, ring(across, 1), ring(across, -1), far_distant]
     mine = near + far
     other = [
-        swap(unit),
-        swap(jnp.concatenate([left, right], axis=0)),
-        swap(across),
-        swap(distant),
-        swap(jnp.concatenate(far[1:3], axis=0)),
-        swap(far[3]),
+        swap(jnp.concatenate(near, axis=0)),
+        swap(jnp.concatenate(far, axis=0)),
     ]
     near_rows, all_rows = 4 * rows, 8 * rows
     edge = near_rows % chunk
     block = (chip_rows, width)
     share = all_rows * all_rows * width // 5
-    (near_weights,) = call(
-        functools.partial(near_weights_kernel, (len(mine), 3)),
-        [(2, all_rows, near_rows - edge)],
-        (cores,),
-        (factors, *mine, *other[:3]),
-        8 * share,
-        (),
+    near_weights, far_begun = call(
+        functools.partial(near_weights_kernel, (len(mine), 1)),
+        [(2, all_rows, near_rows - edge), (2, near_rows, width)],
+        (cores,),
+        (factors, *mine, other[0]),
+        12 * share,
+        kinds=(jnp.bfloat16, jnp.float32),
     )
     edge_weights, far_weights = call(
         functools.partial(far_weights_kernel, (len(mine), len(other))),
@@ -365,8 +370,8 @@
         functools.partial(own_kernel, len(other)),
         [(2, 3 * rows, width), (2, 4 * rows, width), (2, all_rows, near_rows)],
         (cores,),
-        (*weights, *other),
-        18 * share,
+        (*weights, far_begun, *other),
+        14 * share,
         kinds=(jnp.float32, jnp.float32, jnp.bfloat16),
     )
     near_received = swap(near_joined)

time: 98.5 us -> 96.1 us (0.976)
  waiting for transfers between devices: 33.3 us -> 25.4 us
  starting transfers between devices: 30 us -> 34.7 us
    ppermute x13, waiting for transfers between devices: 28.3 us -> 18.3 us  [ring(): return lax.ppermute(value, axes, ring_move(steps))]
    ppermute x4 -> x5, starting transfers between devices: 6.49 us -> 11.1 us  [pair(): return lax.ppermute(value, axes, pairs_of(move))]
    ppermute x4 -> x5, waiting for transfers between devices: 3.06 us -> 5.81 us  [pair(): return lax.ppermute(value, axes, pairs_of(move))]
    ppermute x10 -> x6, starting transfers between devices: 3.33 us -> 3.07 us  [swap(): return lax.ppermute(value, 'core', [(0, 1), (1, 0)])]
  transfers between devices with their start and end apart: 27 -> 24, of which waited for: 11 -> 10; matrix products, arithmetic and copies ran while one was open for 0% -> 1% of each run, Pallas kernels for 24% -> 25%
where the time goes in v10:
time: 96.1 us; the launch traced here: 96 us
  starting transfers between devices  34.7 us (36%)
  Pallas kernels  30.7 us (32%)
  waiting for transfers between devices  25.4 us (26%)
  between operations  2.13 us (2%)
  other arithmetic  2.1 us (2%)
    pallas_call x12, Pallas kernels, call(): pl.pallas_call(body, in_specs=[pl.BlockSpec(memory_space=pltpu.SMEM)] * l...  30.7 us
    ppermute x13, starting transfers between devices, ring(): return lax.ppermute(value, axes, ring_move(steps))  20.6 us
    ppermute x13, waiting for transfers between devices, ring(): return lax.ppermute(value, axes, ring_move(steps))  18.3 us
    ppermute x5, starting transfers between devices, pair(): return lax.ppermute(value, axes, pairs_of(move))  11.1 us
    ppermute x5, waiting for transfers between devices, pair(): return lax.ppermute(value, axes, pairs_of(move))  5.81 us
    ppermute x6, starting transfers between devices, swap(): return lax.ppermute(value, 'core', [(0, 1), (1, 0)])  3.07 us
  transfers between devices with their start and end apart: 24, of which 10 were waited for; matrix products, arithmetic and copies ran while one was open for 1% of the time, Pallas kernels for 25%

profile of v10, /device:TPU:1, one launch (start us, length us, event | category | flops | bytes accessed | tf_op | source)
XLA Modules:
  0.0 96.0 jit_solution(14329612310908611695)
XLA Ops:
  0.6 1.2 %broadcast_select_fusion.2 = (bf16[160,1152]{1,0:T(8,128)(2,1)S(1)}, bf16[160,1152]{1,0:T(8,128)(2,1)S(1)}) fusion(bf16[160,1152]{1,0:T(8,128)(2,1)} %param.5, bf16[160,1152]{1,0:T(8,128)(2,1)} %param.4, pred[]{:T(512)S(6)} %eq.3), kind=kLoop, calls=%fused_computation.2 | loop fusion | flops 368640 | bytes 1474561 | tf_op jit(solution)/shard_map/jit(_where)/select_n | solution.py:323
  1.8 1.5 %collective-permute-start = (bf16[160,1152]{1,0:T(8,128)(2,1)S(1)}, bf16[160,1152]{1,0:T(8,128)(2,1)S(1)}, u32[]{:S(2)}, u32[]{:S(2)}) collective-permute-start(bf16[160,1152]{1,0:T(8,128)(2,1)S(1)} %get-tuple-element.42), channel_id=1, source_target_pairs={{0,1},{1,0},{2,3},{3,2},{4,5},{5,4},{6,7},{7,6},{8,9},{9,8},{10,11... | collective-permute-start | bytes 1105928 | tf_op jit(solution)/shard_map/ppermute | solution.py:61
  4.6 0.0 collective-permute-done.refs_4_
  4.6 0.4 shard_map.59
  5.0 1.8 %collective-permute-start.1 = (bf16[160,1152]{1,0:T(8,128)(2,1)S(1)}, bf16[160,1152]{1,0:T(8,128)(2,1)S(1)}, u32[]{:S(2)}, u32[]{:S(2)}) collective-permute-start(bf16[160,1152]{1,0:T(8,128)(2,1)S(1)} %get-tuple-element.24), channel_id=1, source_target_pairs={{0,4},{1,17},{2,6},{3,19},{4,8},{5,21},{6,10},{7,23},{8,12},{9,25}... | collective-permute-start | bytes 1105928 | tf_op jit(solution)/shard_map/ppermute | solution.py:48
  6.8 2.2 %collective-permute-start.4 = (bf16[160,1152]{1,0:T(8,128)(2,1)S(1)}, bf16[160,1152]{1,0:T(8,128)(2,1)S(1)}, u32[]{:S(2)}, u32[]{:S(2)}) collective-permute-start(bf16[160,1152]{1,0:T(8,128)(2,1)S(1)} %get-tuple-element.25), channel_id=1, source_target_pairs={{0,12},{1,49},{2,14},{3,51},{4,0},{5,53},{6,2},{7,55},{8,4},{9,57}... | collective-permute-start | bytes 1105928 | tf_op jit(solution)/shard_map/ppermute | solution.py:48
  9.0 2.7 %collective-permute-start.5 = (bf16[320,1152]{1,0:T(8,128)(2,1)S(1)}, bf16[320,1152]{1,0:T(8,128)(2,1)S(1)}, u32[]{:S(2)}, u32[]{:S(2)}) collective-permute-start(bf16[320,1152]{1,0:T(8,128)(2,1)S(1)} %get-tuple-element.23.refs_2_), channel_id=1, source_target_pairs={{0,2},{1,67},{2,0},{3,65},{4,6},{5,71},{6,4},{7,69},{8,10},{9,75},... | collective-permute-start | bytes 2211848 | tf_op jit(solution)/shard_map/ppermute | solution.py:57
  11.8 0.1 constant_dynamic-update-slice_fusion.13
  11.8 2.7 %collective-permute-start.3 = (bf16[160,1152]{1,0:T(8,128)(2,1)S(1)}, bf16[160,1152]{1,0:T(8,128)(2,1)S(1)}, u32[]{:S(2)}, u32[]{:S(2)}) collective-permute-start(bf16[160,1152]{1,0:T(8,128)(2,1)S(1)} %get-tuple-element.24), channel_id=1, source_target_pairs={{0,12},{1,49},{2,14},{3,51},{4,0},{5,53},{6,2},{7,55},{8,4},{9,57}... | collective-permute-start | bytes 1105928 | tf_op jit(solution)/shard_map/ppermute | solution.py:48
  14.6 2.7 %collective-permute-start.7 = (bf16[160,1152]{1,0:T(8,128)(2,1)S(1)}, bf16[160,1152]{1,0:T(8,128)(2,1)S(1)}, u32[]{:S(2)}, u32[]{:S(2)}) collective-permute-start(bf16[160,1152]{1,0:T(8,128)(2,1)S(1)} %collective-permute-done.4), channel_id=1, source_target_pairs={{0,12},{1,49},{2,14},{3,51},{4,0},{5,53},{6,2},{7,55},{8,4},{9,57}... | collective-permute-start | bytes 1105928 | tf_op jit(solution)/shard_map/ppermute | solution.py:48
  17.2 0.1 constant_dynamic-update-slice_fusion.12
  17.3 0.5 collective-permute-done.2
  17.8 0.1 constant_dynamic-update-slice_fusion.11
  17.9 1.1 %collective-permute-done.3 = bf16[160,1152]{1,0:T(8,128)(2,1)S(1)} collective-permute-done((bf16[160,1152]{1,0:T(8,128)(2,1)S(1)}, bf16[160,1152]{1,0:T(8,128)(2,1)S(1)}, u32[]{:S(2)}, u32[]{:S(2)}) %collective-permute-start.3) | collective-permute-done | bytes 368672 | tf_op jit(solution)/shard_map/ppermute | solution.py:48
  19.0 0.1 constant_dynamic-update-slice_fusion.10
  19.1 0.1 constant_dynamic-update-slice_fusion.9
  19.2 1.7 %collective-permute-done.5.refs_5_ = bf16[320,1152]{1,0:T(8,128)(2,1)S(1)} collective-permute-done((bf16[320,1152]{1,0:T(8,128)(2,1)S(1)}, bf16[320,1152]{1,0:T(8,128)(2,1)S(1)}, u32[]{:S(2)}, u32[]{:S(2)}) %collective-permute-start.5) | collective-permute-done | bytes 737312 | tf_op jit(solution)/shard_map/ppermute | solution.py:57
  20.9 0.9 collective-permute-start.8
  21.8 0.1 constant_dynamic-update-slice_fusion.8
  21.9 0.3 collective-permute-start.12
  22.2 3.8 %collective-permute-start.9 = (bf16[320,1152]{1,0:T(8,128)(2,1)S(1)}, bf16[320,1152]{1,0:T(8,128)(2,1)S(1)}, u32[]{:S(2)}, u32[]{:S(2)}) collective-permute-start(bf16[320,1152]{1,0:T(8,128)(2,1)S(1)} %collective-permute-done.5.refs_5_), channel_id=1, source_target_pairs={{0,12},{1,49},{2,14},{3,51},{4,0},{5,53},{6,2},{7,55},{8,4},{9,57}... | collective-permute-start | bytes 2211848 | tf_op jit(solution)/shard_map/ppermute | solution.py:48
  26.0 0.0 collective-permute-done.6
  26.0 2.7 %collective-permute-start.10 = (bf16[160,1152]{1,0:T(8,128)(2,1)S(1)}, bf16[160,1152]{1,0:T(8,128)(2,1)S(1)}, u32[]{:S(2)}, u32[]{:S(2)}) collective-permute-start(bf16[160,1152]{1,0:T(8,128)(2,1)S(1)} %collective-permute-done.6), channel_id=1, source_target_pairs={{0,2},{1,67},{2,0},{3,65},{4,6},{5,71},{6,4},{7,69},{8,10},{9,75},... | collective-permute-start | bytes 1105928 | tf_op jit(solution)/shard_map/ppermute | solution.py:57
  28.7 0.1 collective-permute-start.11
  28.8 0.1 constant_dynamic-update-slice_fusion.19
  28.9 0.1 constant_dynamic-update-slice_fusion.18
  28.9 3.8 %collective-permute-done.8.refs_7_ = bf16[320,1152]{1,0:T(8,128)(2,1)S(1)} collective-permute-done((bf16[320,1152]{1,0:T(8,128)(2,1)S(1)}, bf16[320,1152]{1,0:T(8,128)(2,1)S(1)}, u32[]{:S(2)}, u32[]{:S(2)}) %collective-permute-start.8) | collective-permute-done | bytes 737312 | tf_op jit(solution)/shard_map/ppermute | solution.py:48
  32.7 0.1 constant_dynamic-update-slice_fusion.17
  32.8 1.6 %collective-permute-done.9.refs_8_ = bf16[320,1152]{1,0:T(8,128)(2,1)S(1)} collective-permute-done((bf16[320,1152]{1,0:T(8,128)(2,1)S(1)}, bf16[320,1152]{1,0:T(8,128)(2,1)S(1)}, u32[]{:S(2)}, u32[]{:S(2)}) %collective-permute-start.9) | collective-permute-done | bytes 737312 | tf_op jit(solution)/shard_map/ppermute | solution.py:48
  34.4 0.1 constant_dynamic-update-slice_fusion.16
  34.5 0.1 constant_dynamic-update-slice_fusion.15
  34.6 3.0 %collective-permute-done.11 = bf16[160,1152]{1,0:T(8,128)(2,1)S(1)} collective-permute-done((bf16[160,1152]{1,0:T(8,128)(2,1)S(1)}, bf16[160,1152]{1,0:T(8,128)(2,1)S(1)}, u32[]{:S(2)}, u32[]{:S(2)}) %collective-permute-start.11) | collective-permute-done | bytes 368672 | tf_op jit(solution)/shard_map/ppermute | solution.py:57
  37.6 0.1 constant_dynamic-update-slice_fusion.14
  37.6 0.3 collective-permute-start.13
  37.9 0.0 collective-permute-done.12.refs_10_.refs_5_.refs_3_
  37.9 5.6 %shard_map.60 = (bf16[2,1280,512]{2,1,0:T(8,128)(2,1)S(1)}, f32[2,640,1152]{2,1,0:T(8,128)S(1)}) custom-call(s32[1]{0:T(128)} %bitcast.refs_2_.refs_0_, f32[8,128]{1,0:T(8,128)S(1)} %get-tuple-element.21.refs_1_, bf16[320,1152]{1,0:T(8,128)(2,1)S(1)} %get-tuple-element.23.refs_2_, bf16[320,1152]{1,0:T(8,128)(2,1)S(1)} %get-tuple-element.57.refs_3_, ...), custom_call_target="tpu_custom_call" | custom-call | flops 4529848320 | bytes 1048576 | tf_op jit(solution)/shard_map/pallas_call | solution.py:268
  43.6 5.8 %shard_map.61 = (bf16[2,1280,128]{2,1,0:T(8,128)(2,1)S(1)}, bf16[2,1280,640]{2,1,0:T(8,128)(2,1)S(1)}) custom-call(s32[1]{0:T(128)} %bitcast.refs_2_.refs_0_, f32[8,128]{1,0:T(8,128)S(1)} %get-tuple-element.21.refs_1_, bf16[320,1152]{1,0:T(8,128)(2,1)S(1)} %get-tuple-element.23.refs_2_, bf16[320,1152]{1,0:T(8,128)(2,1)S(1)} %get-tuple-element.57.refs_3_, ...), custom_call_target="tpu_custom_call" | custom-call | flops 4529848320 | bytes 1048576 | tf_op jit(solution)/shard_map/pallas_call | solution.py:268
  49.3 0.8 collective-permute-start.15
  50.2 6.3 %shard_map.62 = (f32[2,480,1152]{2,1,0:T(8,128)S(1)}, f32[2,640,1152]{2,1,0:T(8,128)S(1)}, bf16[2,1280,640]{2,1,0:T(8,128)(2,1)S(1)}) custom-call(s32[1]{0:T(128)} %bitcast.refs_2_.refs_0_, bf16[2,1280,512]{2,1,0:T(8,128)(2,1)S(1)} %get-tuple-element.26.refs_12_.refs_1_.refs_2_, bf16[2,1280,128]{2,1,0:T(8,128)(2,1)S(1)} %get-tuple-element.27.refs_2_.refs_3_, ...), custom_call_target="tpu_custom_call" | custom-call | flops 5284823040 | bytes 1048576 | tf_op jit(solution)/shard_map/pallas_call | solution.py:268
  56.5 0.1 collective-permute-start.14
  56.5 0.0 collective-permute-done.15.refs_1_
  56.6 4.5 %shard_map.63 = (bf16[320,1152]{1,0:T(8,128)(2,1)S(1)}, bf16[320,1152]{1,0:T(8,128)(2,1)S(1)}, bf16[320,1152]{1,0:T(8,128)(2,1)S(1)}, bf16[320,1152]{1,0:T(8,128)(2,1)S(1)}) custom-call(s32[1]{0:T(128)} %bitcast.refs_2_.refs_0_, bf16[2,1280,640]{2,1,0:T(8,128)(2,1)S(1)} %collective-permute-done.15.refs_1_, f32[2,640,1152]{2,1,0:T(8,128)S(1)} %get-tuple-element.31.refs_2_, ...), custom_call_target="tpu_custom_call" | custom-call | flops 3774873600 | bytes 1048576 | tf_op jit(solution)/shard_map/pallas_call | solution.py:268
  61.1 2.8 %collective-permute-start.16 = (bf16[320,1152]{1,0:T(8,128)(2,1)S(1)}, bf16[320,1152]{1,0:T(8,128)(2,1)S(1)}, u32[]{:S(2)}, u32[]{:S(2)}) collective-permute-start(bf16[320,1152]{1,0:T(8,128)(2,1)S(1)} %get-tuple-element.33), channel_id=1, source_target_pairs={{0,2},{1,67},{2,0},{3,65},{4,6},{5,71},{6,4},{7,69},{8,10},{9,75},... | collective-permute-start | bytes 2211848 | tf_op jit(solution)/shard_map/ppermute | solution.py:57
  63.8 1.7 %collective-permute-start.20 = (bf16[320,1152]{1,0:T(8,128)(2,1)S(1)}, bf16[320,1152]{1,0:T(8,128)(2,1)S(1)}, u32[]{:S(2)}, u32[]{:S(2)}) collective-permute-start(bf16[320,1152]{1,0:T(8,128)(2,1)S(1)} %get-tuple-element.38), channel_id=1, source_target_pairs={{0,12},{1,49},{2,14},{3,51},{4,0},{5,53},{6,2},{7,55},{8,4},{9,57}... | collective-permute-start | bytes 2211848 | tf_op jit(solution)/shard_map/ppermute | solution.py:48
  65.5 0.0 collective-permute-start.21
  65.5 0.0 collective-permute-done.14.refs_1_
  65.5 3.7 %shard_map.64 = (bf16[320,1152]{1,0:T(8,128)(2,1)S(1)}, bf16[320,1152]{1,0:T(8,128)(2,1)S(1)}, bf16[320,1152]{1,0:T(8,128)(2,1)S(1)}) custom-call(s32[1]{0:T(128)} %bitcast.refs_2_.refs_0_, bf16[2,1280,640]{2,1,0:T(8,128)(2,1)S(1)} %collective-permute-done.14.refs_1_, f32[2,480,1152]{2,1,0:T(8,128)S(1)} %get-tuple-element.34.refs_2_, ...), custom_call_target="tpu_custom_call" | custom-call | flops 3019898880 | bytes 1048576 | tf_op jit(solution)/shard_map/pallas_call | solution.py:268
  69.2 2.7 %collective-permute-start.18 = (bf16[320,1152]{1,0:T(8,128)(2,1)S(1)}, bf16[320,1152]{1,0:T(8,128)(2,1)S(1)}, u32[]{:S(2)}, u32[]{:S(2)}) collective-permute-start(bf16[320,1152]{1,0:T(8,128)(2,1)S(1)} %get-tuple-element.35.refs_2_), channel_id=1, source_target_pairs={{0,12},{1,49},{2,14},{3,51},{4,0},{5,53},{6,2},{7,55},{8,4},{9,57}... | collective-permute-start | bytes 2211848 | tf_op jit(solution)/shard_map/ppermute | solution.py:48
  71.9 0.0 collective-permute-start.19
  71.9 1.1 %collective-permute-done.16.refs_1_ = bf16[320,1152]{1,0:T(8,128)(2,1)S(1)} collective-permute-done((bf16[320,1152]{1,0:T(8,128)(2,1)S(1)}, bf16[320,1152]{1,0:T(8,128)(2,1)S(1)}, u32[]{:S(2)}, u32[]{:S(2)}) %collective-permute-start.16) | collective-permute-done | bytes 737312 | tf_op jit(solution)/shard_map/ppermute | solution.py:57
  73.0 0.2 shard_map.65.refs_7_
  73.2 2.1 %collective-permute-start.17 = (bf16[320,1152]{1,0:T(8,128)(2,1)S(1)}, bf16[320,1152]{1,0:T(8,128)(2,1)S(1)}, u32[]{:S(2)}, u32[]{:S(2)}) collective-permute-start(bf16[320,1152]{1,0:T(8,128)(2,1)S(1)} %shard_map.65.refs_7_), channel_id=1, source_target_pairs={{0,8},{1,33},{2,10},{3,35},{4,12},{5,37},{6,14},{7,39},{8,0},{9,41... | collective-permute-start | bytes 2211848 | tf_op jit(solution)/shard_map/ppermute | solution.py:48
  75.2 3.0 %shard_map.66.refs_0_.refs_3_ = f32[320,1152]{1,0:T(8,128)S(1)} custom-call(s32[1]{0:T(128)} %bitcast.refs_2_.refs_0_, bf16[2,1280,640]{2,1,0:T(8,128)(2,1)S(1)} %collective-permute-done.14.refs_1_, bf16[2,1280,512]{2,1,0:T(8,128)(2,1)S(1)} %get-tuple-element.26.refs_12_.refs_1_.refs_2_, bf16[2,1280,128]{2,1,0:T(8,128)(2,1)S(1)} %get-tuple-element.27.refs_2_.refs_3_, ...), custom_call_target="tpu_custom_call" | custom-call | flops 1887436800 | bytes 1048576 | tf_op jit(solution)/shard_map/pallas_call | solution.py:268
  78.2 0.0 collective-permute-done.20.refs_1_
  78.3 0.3 shard_map.68
  78.5 2.7 %collective-permute-start.22 = (bf16[320,1152]{1,0:T(8,128)(2,1)S(1)}, bf16[320,1152]{1,0:T(8,128)(2,1)S(1)}, u32[]{:S(2)}, u32[]{:S(2)}) collective-permute-start(bf16[320,1152]{1,0:T(8,128)(2,1)S(1)} %shard_map.68), channel_id=1, source_target_pairs={{0,2},{1,67},{2,0},{3,65},{4,6},{5,71},{6,4},{7,69},{8,10},{9,75},... | collective-permute-start | bytes 2211848 | tf_op jit(solution)/shard_map/ppermute | solution.py:57
  81.3 10.8 %collective-permute-done.17.refs_1_ = bf16[320,1152]{1,0:T(8,128)(2,1)S(1)} collective-permute-done((bf16[320,1152]{1,0:T(8,128)(2,1)S(1)}, bf16[320,1152]{1,0:T(8,128)(2,1)S(1)}, u32[]{:S(2)}, u32[]{:S(2)}) %collective-permute-start.17) | collective-permute-done | bytes 737312 | tf_op jit(solution)/shard_map/ppermute | solution.py:48
  92.1 0.2 shard_map.67.refs_3_
  92.3 0.6 collective-permute-done.19.refs_5_
  92.8 0.4 shard_map.69.refs_7_
  93.3 0.1 collective-permute-start.23
  93.3 0.5 shard_map.70
  93.8 1.2 %collective-permute-done.23 = bf16[160,1152]{1,0:T(8,128)(2,1)S(1)} collective-permute-done((bf16[160,1152]{1,0:T(8,128)(2,1)S(1)}, bf16[160,1152]{1,0:T(8,128)(2,1)S(1)}, u32[]{:S(2)}, u32[]{:S(2)}) %collective-permute-start.23) | collective-permute-done | bytes 368672 | tf_op jit(solution)/shard_map/ppermute | solution.py:61
  95.0 0.9 broadcast_select_fusion
  (10 shorter events, 0.0 us)
Async XLA Ops:
  1.8 2.8 %collective-permute-start = (bf16[160,1152]{1,0:T(8,128)(2,1)S(1)}, bf16[160,1152]{1,0:T(8,128)(2,1)S(1)}, u32[]{:S(2)}, u32[]{:S(2)}) collective-permute-start(bf16[160,1152]{1,0:T(8,128)(2,1)S(1)} %get-tuple-element.42), channel_id=1, source_target_pairs={{0,1},{1,0},{2,3},{3,2},{4,5},{5,4},{6,7},{7,6},{8,9},{9,8},{10,11... | collective-permute-start | bytes 1105928 | tf_op jit(solution)/shard_map/ppermute | solution.py:61
  5.0 9.5 %collective-permute-start.1 = (bf16[160,1152]{1,0:T(8,128)(2,1)S(1)}, bf16[160,1152]{1,0:T(8,128)(2,1)S(1)}, u32[]{:S(2)}, u32[]{:S(2)}) collective-permute-start(bf16[160,1152]{1,0:T(8,128)(2,1)S(1)} %get-tuple-element.24), channel_id=1, source_target_pairs={{0,4},{1,17},{2,6},{3,19},{4,8},{5,21},{6,10},{7,23},{8,12},{9,25}... | collective-permute-start | bytes 1105928 | tf_op jit(solution)/shard_map/ppermute | solution.py:48
  6.8 7.8 %collective-permute-start.4 = (bf16[160,1152]{1,0:T(8,128)(2,1)S(1)}, bf16[160,1152]{1,0:T(8,128)(2,1)S(1)}, u32[]{:S(2)}, u32[]{:S(2)}) collective-permute-start(bf16[160,1152]{1,0:T(8,128)(2,1)S(1)} %get-tuple-element.25), channel_id=1, source_target_pairs={{0,12},{1,49},{2,14},{3,51},{4,0},{5,53},{6,2},{7,55},{8,4},{9,57}... | collective-permute-start | bytes 1105928 | tf_op jit(solution)/shard_map/ppermute | solution.py:48
  9.0 8.8 %collective-permute-start.2 = (bf16[160,1152]{1,0:T(8,128)(2,1)S(1)}, bf16[160,1152]{1,0:T(8,128)(2,1)S(1)}, u32[]{:S(2)}, u32[]{:S(2)}) collective-permute-start(bf16[160,1152]{1,0:T(8,128)(2,1)S(1)} %get-tuple-element.25), channel_id=1, source_target_pairs={{0,4},{1,17},{2,6},{3,19},{4,8},{5,21},{6,10},{7,23},{8,12},{9,25}... | collective-permute-start | bytes 1105928 | tf_op jit(solution)/shard_map/ppermute | solution.py:48
  9.0 11.9 %collective-permute-start.5 = (bf16[320,1152]{1,0:T(8,128)(2,1)S(1)}, bf16[320,1152]{1,0:T(8,128)(2,1)S(1)}, u32[]{:S(2)}, u32[]{:S(2)}) collective-permute-start(bf16[320,1152]{1,0:T(8,128)(2,1)S(1)} %get-tuple-element.23.refs_2_), channel_id=1, source_target_pairs={{0,2},{1,67},{2,0},{3,65},{4,6},{5,71},{6,4},{7,69},{8,10},{9,75},... | collective-permute-start | bytes 2211848 | tf_op jit(solution)/shard_map/ppermute | solution.py:57
  11.8 7.2 %collective-permute-start.3 = (bf16[160,1152]{1,0:T(8,128)(2,1)S(1)}, bf16[160,1152]{1,0:T(8,128)(2,1)S(1)}, u32[]{:S(2)}, u32[]{:S(2)}) collective-permute-start(bf16[160,1152]{1,0:T(8,128)(2,1)S(1)} %get-tuple-element.24), channel_id=1, source_target_pairs={{0,12},{1,49},{2,14},{3,51},{4,0},{5,53},{6,2},{7,55},{8,4},{9,57}... | collective-permute-start | bytes 1105928 | tf_op jit(solution)/shard_map/ppermute | solution.py:48
  14.6 11.4 %collective-permute-start.6 = (bf16[160,1152]{1,0:T(8,128)(2,1)S(1)}, bf16[160,1152]{1,0:T(8,128)(2,1)S(1)}, u32[]{:S(2)}, u32[]{:S(2)}) collective-permute-start(bf16[160,1152]{1,0:T(8,128)(2,1)S(1)} %collective-permute-done.1), channel_id=1, source_target_pairs={{0,4},{1,17},{2,6},{3,19},{4,8},{5,21},{6,10},{7,23},{8,12},{9,25}... | collective-permute-start | bytes 1105928 | tf_op jit(solution)/shard_map/ppermute | solution.py:48
  14.6 14.1 %collective-permute-start.7 = (bf16[160,1152]{1,0:T(8,128)(2,1)S(1)}, bf16[160,1152]{1,0:T(8,128)(2,1)S(1)}, u32[]{:S(2)}, u32[]{:S(2)}) collective-permute-start(bf16[160,1152]{1,0:T(8,128)(2,1)S(1)} %collective-permute-done.4), channel_id=1, source_target_pairs={{0,12},{1,49},{2,14},{3,51},{4,0},{5,53},{6,2},{7,55},{8,4},{9,57}... | collective-permute-start | bytes 1105928 | tf_op jit(solution)/shard_map/ppermute | solution.py:48
  20.9 11.8 %collective-permute-start.8 = (bf16[320,1152]{1,0:T(8,128)(2,1)S(1)}, bf16[320,1152]{1,0:T(8,128)(2,1)S(1)}, u32[]{:S(2)}, u32[]{:S(2)}) collective-permute-start(bf16[320,1152]{1,0:T(8,128)(2,1)S(1)} %collective-permute-done.5.refs_5_), channel_id=1, source_target_pairs={{0,4},{1,17},{2,6},{3,19},{4,8},{5,21},{6,10},{7,23},{8,12},{9,25}... | collective-permute-start | bytes 2211848 | tf_op jit(solution)/shard_map/ppermute | solution.py:48
  21.9 16.0 %collective-permute-start.12 = (bf16[1280,1152]{1,0:T(8,128)(2,1)S(1)}, bf16[1280,1152]{1,0:T(8,128)(2,1)S(1)}, u32[]{:S(2)}, u32[]{:S(2)}) collective-permute-start(bf16[1280,1152]{1,0:T(8,128)(2,1)S(1)} %constant_dynamic-update-slice_fusion.8), channel_id=1, source_target_pairs={{0,1},{1,0},{2,3},{3,2},{4,5},{5,4},{6,7},{7,6},{8,9},{9,8},{10,11... | collective-permute-start | bytes 8847368 | tf_op jit(solution)/shard_map/ppermute | solution.py:61
  22.2 12.2 %collective-permute-start.9 = (bf16[320,1152]{1,0:T(8,128)(2,1)S(1)}, bf16[320,1152]{1,0:T(8,128)(2,1)S(1)}, u32[]{:S(2)}, u32[]{:S(2)}) collective-permute-start(bf16[320,1152]{1,0:T(8,128)(2,1)S(1)} %collective-permute-done.5.refs_5_), channel_id=1, source_target_pairs={{0,12},{1,49},{2,14},{3,51},{4,0},{5,53},{6,2},{7,55},{8,4},{9,57}... | collective-permute-start | bytes 2211848 | tf_op jit(solution)/shard_map/ppermute | solution.py:48
  26.0 8.5 %collective-permute-start.10 = (bf16[160,1152]{1,0:T(8,128)(2,1)S(1)}, bf16[160,1152]{1,0:T(8,128)(2,1)S(1)}, u32[]{:S(2)}, u32[]{:S(2)}) collective-permute-start(bf16[160,1152]{1,0:T(8,128)(2,1)S(1)} %collective-permute-done.6), channel_id=1, source_target_pairs={{0,2},{1,67},{2,0},{3,65},{4,6},{5,71},{6,4},{7,69},{8,10},{9,75},... | collective-permute-start | bytes 1105928 | tf_op jit(solution)/shard_map/ppermute | solution.py:57
  28.7 8.8 %collective-permute-start.11 = (bf16[160,1152]{1,0:T(8,128)(2,1)S(1)}, bf16[160,1152]{1,0:T(8,128)(2,1)S(1)}, u32[]{:S(2)}, u32[]{:S(2)}) collective-permute-start(bf16[160,1152]{1,0:T(8,128)(2,1)S(1)} %collective-permute-done.7), channel_id=1, source_target_pairs={{0,2},{1,67},{2,0},{3,65},{4,6},{5,71},{6,4},{7,69},{8,10},{9,75},... | collective-permute-start | bytes 1105928 | tf_op jit(solution)/shard_map/ppermute | solution.py:57
  37.6 5.9 %collective-permute-start.13 = (bf16[1280,1152]{1,0:T(8,128)(2,1)S(1)}, bf16[1280,1152]{1,0:T(8,128)(2,1)S(1)}, u32[]{:S(2)}, u32[]{:S(2)}) collective-permute-start(bf16[1280,1152]{1,0:T(8,128)(2,1)S(1)} %get-tuple-element.44), channel_id=1, source_target_pairs={{0,1},{1,0},{2,3},{3,2},{4,5},{5,4},{6,7},{7,6},{8,9},{9,8},{10,11... | collective-permute-start | bytes 8847368 | tf_op jit(solution)/shard_map/ppermute | solution.py:61
  49.3 7.2 %collective-permute-start.15 = (bf16[2,1280,640]{2,1,0:T(8,128)(2,1)S(1)}, bf16[2,1280,640]{2,1,0:T(8,128)(2,1)S(1)}, u32[]{:S(2)}, u32[]{:S(2)}) collective-permute-start(bf16[2,1280,640]{2,1,0:T(8,128)(2,1)S(1)} %get-tuple-element.28.refs_3_.refs_4_), channel_id=1, source_target_pairs={{0,1},{1,0},{2,3},{3,2},{4,5},{5,4},{6,7},{7,6},{8,9},{9,8},{10,11... | collective-permute-start | bytes 9830408 | tf_op jit(solution)/shard_map/ppermute | solution.py:61
  56.5 9.0 %collective-permute-start.14 = (bf16[2,1280,640]{2,1,0:T(8,128)(2,1)S(1)}, bf16[2,1280,640]{2,1,0:T(8,128)(2,1)S(1)}, u32[]{:S(2)}, u32[]{:S(2)}) collective-permute-start(bf16[2,1280,640]{2,1,0:T(8,128)(2,1)S(1)} %get-tuple-element.30), channel_id=1, source_target_pairs={{0,1},{1,0},{2,3},{3,2},{4,5},{5,4},{6,7},{7,6},{8,9},{9,8},{10,11... | collective-permute-start | bytes 9830408 | tf_op jit(solution)/shard_map/ppermute | solution.py:61
  61.1 11.9 %collective-permute-start.16 = (bf16[320,1152]{1,0:T(8,128)(2,1)S(1)}, bf16[320,1152]{1,0:T(8,128)(2,1)S(1)}, u32[]{:S(2)}, u32[]{:S(2)}) collective-permute-start(bf16[320,1152]{1,0:T(8,128)(2,1)S(1)} %get-tuple-element.33), channel_id=1, source_target_pairs={{0,2},{1,67},{2,0},{3,65},{4,6},{5,71},{6,4},{7,69},{8,10},{9,75},... | collective-permute-start | bytes 2211848 | tf_op jit(solution)/shard_map/ppermute | solution.py:57
  63.8 14.4 %collective-permute-start.20 = (bf16[320,1152]{1,0:T(8,128)(2,1)S(1)}, bf16[320,1152]{1,0:T(8,128)(2,1)S(1)}, u32[]{:S(2)}, u32[]{:S(2)}) collective-permute-start(bf16[320,1152]{1,0:T(8,128)(2,1)S(1)} %get-tuple-element.38), channel_id=1, source_target_pairs={{0,12},{1,49},{2,14},{3,51},{4,0},{5,53},{6,2},{7,55},{8,4},{9,57}... | collective-permute-start | bytes 2211848 | tf_op jit(solution)/shard_map/ppermute | solution.py:48
  65.5 12.8 %collective-permute-start.21 = (bf16[320,1152]{1,0:T(8,128)(2,1)S(1)}, bf16[320,1152]{1,0:T(8,128)(2,1)S(1)}, u32[]{:S(2)}, u32[]{:S(2)}) collective-permute-start(bf16[320,1152]{1,0:T(8,128)(2,1)S(1)} %get-tuple-element.39), channel_id=1, source_target_pairs={{0,4},{1,17},{2,6},{3,19},{4,8},{5,21},{6,10},{7,23},{8,12},{9,25}... | collective-permute-start | bytes 2211848 | tf_op jit(solution)/shard_map/ppermute | solution.py:48
  69.2 23.1 %collective-permute-start.18 = (bf16[320,1152]{1,0:T(8,128)(2,1)S(1)}, bf16[320,1152]{1,0:T(8,128)(2,1)S(1)}, u32[]{:S(2)}, u32[]{:S(2)}) collective-permute-start(bf16[320,1152]{1,0:T(8,128)(2,1)S(1)} %get-tuple-element.35.refs_2_), channel_id=1, source_target_pairs={{0,12},{1,49},{2,14},{3,51},{4,0},{5,53},{6,2},{7,55},{8,4},{9,57}... | collective-permute-start | bytes 2211848 | tf_op jit(solution)/shard_map/ppermute | solution.py:48
  71.9 20.9 %collective-permute-start.19 = (bf16[320,1152]{1,0:T(8,128)(2,1)S(1)}, bf16[320,1152]{1,0:T(8,128)(2,1)S(1)}, u32[]{:S(2)}, u32[]{:S(2)}) collective-permute-start(bf16[320,1152]{1,0:T(8,128)(2,1)S(1)} %get-tuple-element.36), channel_id=1, source_target_pairs={{0,4},{1,17},{2,6},{3,19},{4,8},{5,21},{6,10},{7,23},{8,12},{9,25}... | collective-permute-start | bytes 2211848 | tf_op jit(solution)/shard_map/ppermute | solution.py:48
  73.2 18.9 %collective-permute-start.17 = (bf16[320,1152]{1,0:T(8,128)(2,1)S(1)}, bf16[320,1152]{1,0:T(8,128)(2,1)S(1)}, u32[]{:S(2)}, u32[]{:S(2)}) collective-permute-start(bf16[320,1152]{1,0:T(8,128)(2,1)S(1)} %shard_map.65.refs_7_), channel_id=1, source_target_pairs={{0,8},{1,33},{2,10},{3,35},{4,12},{5,37},{6,14},{7,39},{8,0},{9,41... | collective-permute-start | bytes 2211848 | tf_op jit(solution)/shard_map/ppermute | solution.py:48
  78.5 14.3 %collective-permute-start.22 = (bf16[320,1152]{1,0:T(8,128)(2,1)S(1)}, bf16[320,1152]{1,0:T(8,128)(2,1)S(1)}, u32[]{:S(2)}, u32[]{:S(2)}) collective-permute-start(bf16[320,1152]{1,0:T(8,128)(2,1)S(1)} %shard_map.68), channel_id=1, source_target_pairs={{0,2},{1,67},{2,0},{3,65},{4,6},{5,71},{6,4},{7,69},{8,10},{9,75},... | collective-permute-start | bytes 2211848 | tf_op jit(solution)/shard_map/ppermute | solution.py:57
  93.3 1.8 %collective-permute-start.23 = (bf16[160,1152]{1,0:T(8,128)(2,1)S(1)}, bf16[160,1152]{1,0:T(8,128)(2,1)S(1)}, u32[]{:S(2)}, u32[]{:S(2)}) collective-permute-start(bf16[160,1152]{1,0:T(8,128)(2,1)S(1)} %shard_map.69.refs_7_), channel_id=1, source_target_pairs={{0,1},{1,0},{2,3},{3,2},{4,5},{5,4},{6,7},{7,6},{8,9},{9,8},{10,11... | collective-permute-start | bytes 1105928 | tf_op jit(solution)/shard_map/ppermute | solution.py:61

commit v11 on v10

--- a/solution.py
+++ b/solution.py
@@ -330,15 +330,19 @@
         (keep, got),
         kinds=(jnp.bfloat16,) * 4 + (jnp.float32,),
     )
+    across = pair(unit)
     left_low, right_high = ring(low, 1), ring(high, -1)
-    left = jnp.concatenate([left_low, ring(high, 1)], axis=0)
-    right = jnp.concatenate([ring(low, -1), right_high], axis=0)
-    across = pair(unit)
+    late_high, late_low, _ = lax.optimization_barrier((high, low, left_low[:8]))
+    left_high, right_low = ring(late_high, 1), ring(late_low, -1)
     distant_low, distant_high = ring(left_low, 1), ring(right_high, -1)
+    far_left, far_right = ring(across, 1), ring(across, -1)
+    low_far, high_far = pair(distant_low), pair(distant_high)
+    left = jnp.concatenate([left_low, left_high], axis=0)
+    right = jnp.concatenate([right_low, right_high], axis=0)
     distant = jnp.concatenate([distant_low, distant_high], axis=0)
-    far_distant = jnp.concatenate([pair(distant_low), pair(distant_high)], axis=0)
+    far_distant = jnp.concatenate([low_far, high_far], axis=0)
     near = [unit, left, right, across]
-    far = [distant, ring(across, 1), ring(across, -1), far_distant]
+    far = [distant, far_left, far_right, far_distant]
     mine = near + far
     other = [
         swap(jnp.concatenate(near, axis=0)),

time: 96.1 us -> 95.8 us (level)
    ppermute x5, waiting for transfers between devices: 5.81 us -> 4.04 us  [pair(): return lax.ppermute(value, axes, pairs_of(move))]
    ppermute x13, waiting for transfers between devices: 18.3 us -> 19.5 us  [ring(): return lax.ppermute(value, axes, ring_move(steps))]
  transfers between devices with their start and end apart: 24 -> 24, of which waited for: 10 -> 8; matrix products, arithmetic and copies ran while one was open for 1% -> 1% of each run, Pallas kernels for 25% -> 25%
where the time goes in v11:
time: 95.8 us; the launch traced here: 95.7 us
  starting transfers between devices  35 us (37%)
  Pallas kernels  30.7 us (32%)
  waiting for transfers between devices  24.8 us (26%)
  between operations  2.15 us (2%)
  other arithmetic  2.1 us (2%)
    pallas_call x12, Pallas kernels, call(): pl.pallas_call(body, in_specs=[pl.BlockSpec(memory_space=pltpu.SMEM)] * l...  30.7 us
    ppermute x13, starting transfers between devices, ring(): return lax.ppermute(value, axes, ring_move(steps))  21 us
    ppermute x13, waiting for transfers between devices, ring(): return lax.ppermute(value, axes, ring_move(steps))  19.5 us
    ppermute x5, starting transfers between devices, pair(): return lax.ppermute(value, axes, pairs_of(move))  11.1 us
    ppermute x5, waiting for transfers between devices, pair(): return lax.ppermute(value, axes, pairs_of(move))  4.04 us
    ppermute x6, starting transfers between devices, swap(): return lax.ppermute(value, 'core', [(0, 1), (1, 0)])  2.84 us
  transfers between devices with their start and end apart: 24, of which 8 were waited for; matrix products, arithmetic and copies ran while one was open for 1% of the time, Pallas kernels for 25%

profile of v11, /device:TPU:1, one launch (start us, length us, event | category | flops | bytes accessed | tf_op | source)
XLA Modules:
  0.0 95.7 jit_solution(13323559457945422187)
XLA Ops:
  0.6 1.2 %broadcast_select_fusion.2 = (bf16[160,1152]{1,0:T(8,128)(2,1)S(1)}, bf16[160,1152]{1,0:T(8,128)(2,1)S(1)}) fusion(bf16[160,1152]{1,0:T(8,128)(2,1)} %param.5, bf16[160,1152]{1,0:T(8,128)(2,1)} %param.4, pred[]{:T(512)S(6)} %eq.3), kind=kLoop, calls=%fused_computation.2 | loop fusion | flops 368640 | bytes 1474561 | tf_op jit(solution)/shard_map/jit(_where)/select_n | solution.py:323
  1.8 1.5 %collective-permute-start = (bf16[160,1152]{1,0:T(8,128)(2,1)S(1)}, bf16[160,1152]{1,0:T(8,128)(2,1)S(1)}, u32[]{:S(2)}, u32[]{:S(2)}) collective-permute-start(bf16[160,1152]{1,0:T(8,128)(2,1)S(1)} %get-tuple-element.46), channel_id=1, source_target_pairs={{0,1},{1,0},{2,3},{3,2},{4,5},{5,4},{6,7},{7,6},{8,9},{9,8},{10,11... | collective-permute-start | bytes 1105928 | tf_op jit(solution)/shard_map/ppermute | solution.py:61
  4.6 0.0 collective-permute-done.refs_4_
  4.6 0.4 shard_map.59
  5.0 1.8 %collective-permute-start.1 = (bf16[160,1152]{1,0:T(8,128)(2,1)S(1)}, bf16[160,1152]{1,0:T(8,128)(2,1)S(1)}, u32[]{:S(2)}, u32[]{:S(2)}) collective-permute-start(bf16[160,1152]{1,0:T(8,128)(2,1)S(1)} %get-tuple-element.29), channel_id=1, source_target_pairs={{0,4},{1,17},{2,6},{3,19},{4,8},{5,21},{6,10},{7,23},{8,12},{9,25}... | collective-permute-start | bytes 1105928 | tf_op jit(solution)/shard_map/ppermute | solution.py:48
  6.8 2.2 %collective-permute-start.4 = (bf16[160,1152]{1,0:T(8,128)(2,1)S(1)}, bf16[160,1152]{1,0:T(8,128)(2,1)S(1)}, u32[]{:S(2)}, u32[]{:S(2)}) collective-permute-start(bf16[160,1152]{1,0:T(8,128)(2,1)S(1)} %get-tuple-element.28), channel_id=1, source_target_pairs={{0,12},{1,49},{2,14},{3,51},{4,0},{5,53},{6,2},{7,55},{8,4},{9,57}... | collective-permute-start | bytes 1105928 | tf_op jit(solution)/shard_map/ppermute | solution.py:48
  9.0 2.7 %collective-permute-start.5 = (bf16[320,1152]{1,0:T(8,128)(2,1)S(1)}, bf16[320,1152]{1,0:T(8,128)(2,1)S(1)}, u32[]{:S(2)}, u32[]{:S(2)}) collective-permute-start(bf16[320,1152]{1,0:T(8,128)(2,1)S(1)} %get-tuple-element.25.refs_2_), channel_id=1, source_target_pairs={{0,2},{1,67},{2,0},{3,65},{4,6},{5,71},{6,4},{7,69},{8,10},{9,75},... | collective-permute-start | bytes 2211848 | tf_op jit(solution)/shard_map/ppermute | solution.py:57
  11.8 0.1 constant_dynamic-update-slice_fusion.13
  11.8 2.7 %collective-permute-start.3 = (bf16[160,1152]{1,0:T(8,128)(2,1)S(1)}, bf16[160,1152]{1,0:T(8,128)(2,1)S(1)}, u32[]{:S(2)}, u32[]{:S(2)}) collective-permute-start(bf16[160,1152]{1,0:T(8,128)(2,1)S(1)} %get-tuple-element.29), channel_id=1, source_target_pairs={{0,12},{1,49},{2,14},{3,51},{4,0},{5,53},{6,2},{7,55},{8,4},{9,57}... | collective-permute-start | bytes 1105928 | tf_op jit(solution)/shard_map/ppermute | solution.py:48
  14.6 0.0 collective-permute-start.6
  14.6 0.0 collective-permute-done.4
  14.6 2.7 %collective-permute-start.7 = (bf16[160,1152]{1,0:T(8,128)(2,1)S(1)}, bf16[160,1152]{1,0:T(8,128)(2,1)S(1)}, u32[]{:S(2)}, u32[]{:S(2)}) collective-permute-start(bf16[160,1152]{1,0:T(8,128)(2,1)S(1)} %collective-permute-done.4), channel_id=1, source_target_pairs={{0,12},{1,49},{2,14},{3,51},{4,0},{5,53},{6,2},{7,55},{8,4},{9,57}... | collective-permute-start | bytes 1105928 | tf_op jit(solution)/shard_map/ppermute | solution.py:48
  17.2 0.1 constant_dynamic-update-slice_fusion.12
  17.3 2.3 %collective-permute-done.2 = bf16[160,1152]{1,0:T(8,128)(2,1)S(1)} collective-permute-done((bf16[160,1152]{1,0:T(8,128)(2,1)S(1)}, bf16[160,1152]{1,0:T(8,128)(2,1)S(1)}, u32[]{:S(2)}, u32[]{:S(2)}) %collective-permute-start.2) | collective-permute-done | bytes 368672 | tf_op jit(solution)/shard_map/ppermute | solution.py:48
  19.6 0.1 constant_dynamic-update-slice_fusion.11
  19.7 0.0 collective-permute-done.3
  19.7 0.1 constant_dynamic-update-slice_fusion.10
  19.8 0.1 constant_dynamic-update-slice_fusion.9
  19.9 1.0 %collective-permute-done.5.refs_5_ = bf16[320,1152]{1,0:T(8,128)(2,1)S(1)} collective-permute-done((bf16[320,1152]{1,0:T(8,128)(2,1)S(1)}, bf16[320,1152]{1,0:T(8,128)(2,1)S(1)}, u32[]{:S(2)}, u32[]{:S(2)}) %collective-permute-start.5) | collective-permute-done | bytes 737312 | tf_op jit(solution)/shard_map/ppermute | solution.py:57
  20.9 0.1 constant_dynamic-update-slice_fusion.8
  21.0 0.1 collective-permute-start.12
  21.1 3.4 %collective-permute-start.9 = (bf16[320,1152]{1,0:T(8,128)(2,1)S(1)}, bf16[320,1152]{1,0:T(8,128)(2,1)S(1)}, u32[]{:S(2)}, u32[]{:S(2)}) collective-permute-start(bf16[320,1152]{1,0:T(8,128)(2,1)S(1)} %collective-permute-done.5.refs_5_), channel_id=1, source_target_pairs={{0,12},{1,49},{2,14},{3,51},{4,0},{5,53},{6,2},{7,55},{8,4},{9,57}... | collective-permute-start | bytes 2211848 | tf_op jit(solution)/shard_map/ppermute | solution.py:48
  24.5 2.7 %collective-permute-start.10 = (bf16[160,1152]{1,0:T(8,128)(2,1)S(1)}, bf16[160,1152]{1,0:T(8,128)(2,1)S(1)}, u32[]{:S(2)}, u32[]{:S(2)}) collective-permute-start(bf16[160,1152]{1,0:T(8,128)(2,1)S(1)} %collective-permute-done.6), channel_id=1, source_target_pairs={{0,2},{1,67},{2,0},{3,65},{4,6},{5,71},{6,4},{7,69},{8,10},{9,75},... | collective-permute-start | bytes 1105928 | tf_op jit(solution)/shard_map/ppermute | solution.py:57
  27.2 0.1 collective-permute-start.11
  27.3 0.1 constant_dynamic-update-slice_fusion.19
  27.4 0.1 constant_dynamic-update-slice_fusion.18
  27.4 5.0 %collective-permute-done.8.refs_7_ = bf16[320,1152]{1,0:T(8,128)(2,1)S(1)} collective-permute-done((bf16[320,1152]{1,0:T(8,128)(2,1)S(1)}, bf16[320,1152]{1,0:T(8,128)(2,1)S(1)}, u32[]{:S(2)}, u32[]{:S(2)}) %collective-permute-start.8) | collective-permute-done | bytes 737312 | tf_op jit(solution)/shard_map/ppermute | solution.py:48
  32.5 0.1 constant_dynamic-update-slice_fusion.17
  32.6 0.3 collective-permute-done.9.refs_8_
  32.9 0.1 constant_dynamic-update-slice_fusion.16
  33.0 0.0 collective-permute-done.10
  33.0 0.1 constant_dynamic-update-slice_fusion.15
  33.1 3.0 %collective-permute-done.11 = bf16[160,1152]{1,0:T(8,128)(2,1)S(1)} collective-permute-done((bf16[160,1152]{1,0:T(8,128)(2,1)S(1)}, bf16[160,1152]{1,0:T(8,128)(2,1)S(1)}, u32[]{:S(2)}, u32[]{:S(2)}) %collective-permute-start.11) | collective-permute-done | bytes 368672 | tf_op jit(solution)/shard_map/ppermute | solution.py:57
  36.1 0.1 constant_dynamic-update-slice_fusion.14
  36.1 0.3 collective-permute-start.13
  36.4 0.0 collective-permute-done.12.refs_10_.refs_5_.refs_3_
  36.4 5.6 %shard_map.60 = (bf16[2,1280,512]{2,1,0:T(8,128)(2,1)S(1)}, f32[2,640,1152]{2,1,0:T(8,128)S(1)}) custom-call(s32[1]{0:T(128)} %bitcast.refs_2_.refs_0_, f32[8,128]{1,0:T(8,128)S(1)} %get-tuple-element.23.refs_1_, bf16[320,1152]{1,0:T(8,128)(2,1)S(1)} %get-tuple-element.25.refs_2_, bf16[320,1152]{1,0:T(8,128)(2,1)S(1)} %get-tuple-element.61.refs_3_, ...), custom_call_target="tpu_custom_call" | custom-call | flops 4529848320 | bytes 1048576 | tf_op jit(solution)/shard_map/pallas_call | solution.py:268
  42.0 0.0 collective-permute-done.13.refs_11_.refs_6_.refs_4_
  42.1 5.8 %shard_map.61 = (bf16[2,1280,128]{2,1,0:T(8,128)(2,1)S(1)}, bf16[2,1280,640]{2,1,0:T(8,128)(2,1)S(1)}) custom-call(s32[1]{0:T(128)} %bitcast.refs_2_.refs_0_, f32[8,128]{1,0:T(8,128)S(1)} %get-tuple-element.23.refs_1_, bf16[320,1152]{1,0:T(8,128)(2,1)S(1)} %get-tuple-element.25.refs_2_, bf16[320,1152]{1,0:T(8,128)(2,1)S(1)} %get-tuple-element.61.refs_3_, ...), custom_call_target="tpu_custom_call" | custom-call | flops 4529848320 | bytes 1048576 | tf_op jit(solution)/shard_map/pallas_call | solution.py:268
  47.8 0.8 collective-permute-start.15
  48.7 6.3 %shard_map.62 = (f32[2,480,1152]{2,1,0:T(8,128)S(1)}, f32[2,640,1152]{2,1,0:T(8,128)S(1)}, bf16[2,1280,640]{2,1,0:T(8,128)(2,1)S(1)}) custom-call(s32[1]{0:T(128)} %bitcast.refs_2_.refs_0_, bf16[2,1280,512]{2,1,0:T(8,128)(2,1)S(1)} %get-tuple-element.30.refs_12_.refs_1_.refs_2_, bf16[2,1280,128]{2,1,0:T(8,128)(2,1)S(1)} %get-tuple-element.31.refs_2_.refs_3_, ...), custom_call_target="tpu_custom_call" | custom-call | flops 5284823040 | bytes 1048576 | tf_op jit(solution)/shard_map/pallas_call | solution.py:268
  55.0 0.1 collective-permute-start.14
  55.0 0.0 collective-permute-done.15.refs_1_
  55.1 4.5 %shard_map.63 = (bf16[320,1152]{1,0:T(8,128)(2,1)S(1)}, bf16[320,1152]{1,0:T(8,128)(2,1)S(1)}, bf16[320,1152]{1,0:T(8,128)(2,1)S(1)}, bf16[320,1152]{1,0:T(8,128)(2,1)S(1)}) custom-call(s32[1]{0:T(128)} %bitcast.refs_2_.refs_0_, bf16[2,1280,640]{2,1,0:T(8,128)(2,1)S(1)} %collective-permute-done.15.refs_1_, f32[2,640,1152]{2,1,0:T(8,128)S(1)} %get-tuple-element.35.refs_2_, ...), custom_call_target="tpu_custom_call" | custom-call | flops 3774873600 | bytes 1048576 | tf_op jit(solution)/shard_map/pallas_call | solution.py:268
  59.6 2.8 %collective-permute-start.16 = (bf16[320,1152]{1,0:T(8,128)(2,1)S(1)}, bf16[320,1152]{1,0:T(8,128)(2,1)S(1)}, u32[]{:S(2)}, u32[]{:S(2)}) collective-permute-start(bf16[320,1152]{1,0:T(8,128)(2,1)S(1)} %get-tuple-element.37), channel_id=1, source_target_pairs={{0,2},{1,67},{2,0},{3,65},{4,6},{5,71},{6,4},{7,69},{8,10},{9,75},... | collective-permute-start | bytes 2211848 | tf_op jit(solution)/shard_map/ppermute | solution.py:57
  62.3 2.9 %collective-permute-start.20 = (bf16[320,1152]{1,0:T(8,128)(2,1)S(1)}, bf16[320,1152]{1,0:T(8,128)(2,1)S(1)}, u32[]{:S(2)}, u32[]{:S(2)}) collective-permute-start(bf16[320,1152]{1,0:T(8,128)(2,1)S(1)} %get-tuple-element.42), channel_id=1, source_target_pairs={{0,12},{1,49},{2,14},{3,51},{4,0},{5,53},{6,2},{7,55},{8,4},{9,57}... | collective-permute-start | bytes 2211848 | tf_op jit(solution)/shard_map/ppermute | solution.py:48
  65.2 0.0 collective-permute-start.21
  65.2 0.0 collective-permute-done.14.refs_1_
  65.2 3.7 %shard_map.64 = (bf16[320,1152]{1,0:T(8,128)(2,1)S(1)}, bf16[320,1152]{1,0:T(8,128)(2,1)S(1)}, bf16[320,1152]{1,0:T(8,128)(2,1)S(1)}) custom-call(s32[1]{0:T(128)} %bitcast.refs_2_.refs_0_, bf16[2,1280,640]{2,1,0:T(8,128)(2,1)S(1)} %collective-permute-done.14.refs_1_, f32[2,480,1152]{2,1,0:T(8,128)S(1)} %get-tuple-element.38.refs_2_, ...), custom_call_target="tpu_custom_call" | custom-call | flops 3019898880 | bytes 1048576 | tf_op jit(solution)/shard_map/pallas_call | solution.py:268
  68.9 2.7 %collective-permute-start.18 = (bf16[320,1152]{1,0:T(8,128)(2,1)S(1)}, bf16[320,1152]{1,0:T(8,128)(2,1)S(1)}, u32[]{:S(2)}, u32[]{:S(2)}) collective-permute-start(bf16[320,1152]{1,0:T(8,128)(2,1)S(1)} %get-tuple-element.39.refs_2_), channel_id=1, source_target_pairs={{0,12},{1,49},{2,14},{3,51},{4,0},{5,53},{6,2},{7,55},{8,4},{9,57}... | collective-permute-start | bytes 2211848 | tf_op jit(solution)/shard_map/ppermute | solution.py:48
  71.6 0.0 collective-permute-start.19
  71.6 0.2 shard_map.65.refs_7_
  71.8 2.6 %collective-permute-start.17 = (bf16[320,1152]{1,0:T(8,128)(2,1)S(1)}, bf16[320,1152]{1,0:T(8,128)(2,1)S(1)}, u32[]{:S(2)}, u32[]{:S(2)}) collective-permute-start(bf16[320,1152]{1,0:T(8,128)(2,1)S(1)} %shard_map.65.refs_7_), channel_id=1, source_target_pairs={{0,8},{1,33},{2,10},{3,35},{4,12},{5,37},{6,14},{7,39},{8,0},{9,41... | collective-permute-start | bytes 2211848 | tf_op jit(solution)/shard_map/ppermute | solution.py:48
  74.4 3.0 %shard_map.66.refs_0_.refs_3_ = f32[320,1152]{1,0:T(8,128)S(1)} custom-call(s32[1]{0:T(128)} %bitcast.refs_2_.refs_0_, bf16[2,1280,640]{2,1,0:T(8,128)(2,1)S(1)} %collective-permute-done.14.refs_1_, bf16[2,1280,512]{2,1,0:T(8,128)(2,1)S(1)} %get-tuple-element.30.refs_12_.refs_1_.refs_2_, bf16[2,1280,128]{2,1,0:T(8,128)(2,1)S(1)} %get-tuple-element.31.refs_2_.refs_3_, ...), custom_call_target="tpu_custom_call" | custom-call | flops 1887436800 | bytes 1048576 | tf_op jit(solution)/shard_map/pallas_call | solution.py:268
  77.5 0.3 shard_map.68
  77.7 2.8 %collective-permute-start.22 = (bf16[320,1152]{1,0:T(8,128)(2,1)S(1)}, bf16[320,1152]{1,0:T(8,128)(2,1)S(1)}, u32[]{:S(2)}, u32[]{:S(2)}) collective-permute-start(bf16[320,1152]{1,0:T(8,128)(2,1)S(1)} %shard_map.68), channel_id=1, source_target_pairs={{0,2},{1,67},{2,0},{3,65},{4,6},{5,71},{6,4},{7,69},{8,10},{9,75},... | collective-permute-start | bytes 2211848 | tf_op jit(solution)/shard_map/ppermute | solution.py:57
  80.5 10.8 %collective-permute-done.17.refs_1_ = bf16[320,1152]{1,0:T(8,128)(2,1)S(1)} collective-permute-done((bf16[320,1152]{1,0:T(8,128)(2,1)S(1)}, bf16[320,1152]{1,0:T(8,128)(2,1)S(1)}, u32[]{:S(2)}, u32[]{:S(2)}) %collective-permute-start.17) | collective-permute-done | bytes 737312 | tf_op jit(solution)/shard_map/ppermute | solution.py:48
  91.3 0.2 shard_map.67.refs_3_
  91.5 1.1 %collective-permute-done.19.refs_5_ = bf16[320,1152]{1,0:T(8,128)(2,1)S(1)} collective-permute-done((bf16[320,1152]{1,0:T(8,128)(2,1)S(1)}, bf16[320,1152]{1,0:T(8,128)(2,1)S(1)}, u32[]{:S(2)}, u32[]{:S(2)}) %collective-permute-start.19) | collective-permute-done | bytes 737312 | tf_op jit(solution)/shard_map/ppermute | solution.py:48
  92.5 0.4 shard_map.69.refs_7_
  93.0 0.1 collective-permute-start.23
  93.1 0.5 shard_map.70
  93.5 1.2 %collective-permute-done.23 = bf16[160,1152]{1,0:T(8,128)(2,1)S(1)} collective-permute-done((bf16[160,1152]{1,0:T(8,128)(2,1)S(1)}, bf16[160,1152]{1,0:T(8,128)(2,1)S(1)}, u32[]{:S(2)}, u32[]{:S(2)}) %collective-permute-start.23) | collective-permute-done | bytes 368672 | tf_op jit(solution)/shard_map/ppermute | solution.py:61
  94.7 0.9 broadcast_select_fusion
  (10 shorter events, 0.0 us)
Async XLA Ops:
  1.8 2.8 %collective-permute-start = (bf16[160,1152]{1,0:T(8,128)(2,1)S(1)}, bf16[160,1152]{1,0:T(8,128)(2,1)S(1)}, u32[]{:S(2)}, u32[]{:S(2)}) collective-permute-start(bf16[160,1152]{1,0:T(8,128)(2,1)S(1)} %get-tuple-element.46), channel_id=1, source_target_pairs={{0,1},{1,0},{2,3},{3,2},{4,5},{5,4},{6,7},{7,6},{8,9},{9,8},{10,11... | collective-permute-start | bytes 1105928 | tf_op jit(solution)/shard_map/ppermute | solution.py:61
  5.0 9.5 %collective-permute-start.1 = (bf16[160,1152]{1,0:T(8,128)(2,1)S(1)}, bf16[160,1152]{1,0:T(8,128)(2,1)S(1)}, u32[]{:S(2)}, u32[]{:S(2)}) collective-permute-start(bf16[160,1152]{1,0:T(8,128)(2,1)S(1)} %get-tuple-element.29), channel_id=1, source_target_pairs={{0,4},{1,17},{2,6},{3,19},{4,8},{5,21},{6,10},{7,23},{8,12},{9,25}... | collective-permute-start | bytes 1105928 | tf_op jit(solution)/shard_map/ppermute | solution.py:48
  6.8 7.8 %collective-permute-start.4 = (bf16[160,1152]{1,0:T(8,128)(2,1)S(1)}, bf16[160,1152]{1,0:T(8,128)(2,1)S(1)}, u32[]{:S(2)}, u32[]{:S(2)}) collective-permute-start(bf16[160,1152]{1,0:T(8,128)(2,1)S(1)} %get-tuple-element.28), channel_id=1, source_target_pairs={{0,12},{1,49},{2,14},{3,51},{4,0},{5,53},{6,2},{7,55},{8,4},{9,57}... | collective-permute-start | bytes 1105928 | tf_op jit(solution)/shard_map/ppermute | solution.py:48
  9.0 11.9 %collective-permute-start.5 = (bf16[320,1152]{1,0:T(8,128)(2,1)S(1)}, bf16[320,1152]{1,0:T(8,128)(2,1)S(1)}, u32[]{:S(2)}, u32[]{:S(2)}) collective-permute-start(bf16[320,1152]{1,0:T(8,128)(2,1)S(1)} %get-tuple-element.25.refs_2_), channel_id=1, source_target_pairs={{0,2},{1,67},{2,0},{3,65},{4,6},{5,71},{6,4},{7,69},{8,10},{9,75},... | collective-permute-start | bytes 2211848 | tf_op jit(solution)/shard_map/ppermute | solution.py:57
  11.8 7.9 %collective-permute-start.2 = (bf16[160,1152]{1,0:T(8,128)(2,1)S(1)}, bf16[160,1152]{1,0:T(8,128)(2,1)S(1)}, u32[]{:S(2)}, u32[]{:S(2)}) collective-permute-start(bf16[160,1152]{1,0:T(8,128)(2,1)S(1)} %get-tuple-element.28), channel_id=1, source_target_pairs={{0,4},{1,17},{2,6},{3,19},{4,8},{5,21},{6,10},{7,23},{8,12},{9,25}... | collective-permute-start | bytes 1105928 | tf_op jit(solution)/shard_map/ppermute | solution.py:48
  11.8 7.9 %collective-permute-start.3 = (bf16[160,1152]{1,0:T(8,128)(2,1)S(1)}, bf16[160,1152]{1,0:T(8,128)(2,1)S(1)}, u32[]{:S(2)}, u32[]{:S(2)}) collective-permute-start(bf16[160,1152]{1,0:T(8,128)(2,1)S(1)} %get-tuple-element.29), channel_id=1, source_target_pairs={{0,12},{1,49},{2,14},{3,51},{4,0},{5,53},{6,2},{7,55},{8,4},{9,57}... | collective-permute-start | bytes 1105928 | tf_op jit(solution)/shard_map/ppermute | solution.py:48
  14.6 9.9 %collective-permute-start.6 = (bf16[160,1152]{1,0:T(8,128)(2,1)S(1)}, bf16[160,1152]{1,0:T(8,128)(2,1)S(1)}, u32[]{:S(2)}, u32[]{:S(2)}) collective-permute-start(bf16[160,1152]{1,0:T(8,128)(2,1)S(1)} %collective-permute-done.1), channel_id=1, source_target_pairs={{0,4},{1,17},{2,6},{3,19},{4,8},{5,21},{6,10},{7,23},{8,12},{9,25}... | collective-permute-start | bytes 1105928 | tf_op jit(solution)/shard_map/ppermute | solution.py:48
  14.6 12.6 %collective-permute-start.7 = (bf16[160,1152]{1,0:T(8,128)(2,1)S(1)}, bf16[160,1152]{1,0:T(8,128)(2,1)S(1)}, u32[]{:S(2)}, u32[]{:S(2)}) collective-permute-start(bf16[160,1152]{1,0:T(8,128)(2,1)S(1)} %collective-permute-done.4), channel_id=1, source_target_pairs={{0,12},{1,49},{2,14},{3,51},{4,0},{5,53},{6,2},{7,55},{8,4},{9,57}... | collective-permute-start | bytes 1105928 | tf_op jit(solution)/shard_map/ppermute | solution.py:48
  20.9 11.6 %collective-permute-start.8 = (bf16[320,1152]{1,0:T(8,128)(2,1)S(1)}, bf16[320,1152]{1,0:T(8,128)(2,1)S(1)}, u32[]{:S(2)}, u32[]{:S(2)}) collective-permute-start(bf16[320,1152]{1,0:T(8,128)(2,1)S(1)} %collective-permute-done.5.refs_5_), channel_id=1, source_target_pairs={{0,4},{1,17},{2,6},{3,19},{4,8},{5,21},{6,10},{7,23},{8,12},{9,25}... | collective-permute-start | bytes 2211848 | tf_op jit(solution)/shard_map/ppermute | solution.py:48
  21.0 15.4 %collective-permute-start.12 = (bf16[1280,1152]{1,0:T(8,128)(2,1)S(1)}, bf16[1280,1152]{1,0:T(8,128)(2,1)S(1)}, u32[]{:S(2)}, u32[]{:S(2)}) collective-permute-start(bf16[1280,1152]{1,0:T(8,128)(2,1)S(1)} %constant_dynamic-update-slice_fusion.8), channel_id=1, source_target_pairs={{0,1},{1,0},{2,3},{3,2},{4,5},{5,4},{6,7},{7,6},{8,9},{9,8},{10,11... | collective-permute-start | bytes 8847368 | tf_op jit(solution)/shard_map/ppermute | solution.py:61
  21.1 11.8 %collective-permute-start.9 = (bf16[320,1152]{1,0:T(8,128)(2,1)S(1)}, bf16[320,1152]{1,0:T(8,128)(2,1)S(1)}, u32[]{:S(2)}, u32[]{:S(2)}) collective-permute-start(bf16[320,1152]{1,0:T(8,128)(2,1)S(1)} %collective-permute-done.5.refs_5_), channel_id=1, source_target_pairs={{0,12},{1,49},{2,14},{3,51},{4,0},{5,53},{6,2},{7,55},{8,4},{9,57}... | collective-permute-start | bytes 2211848 | tf_op jit(solution)/shard_map/ppermute | solution.py:48
  24.5 8.5 %collective-permute-start.10 = (bf16[160,1152]{1,0:T(8,128)(2,1)S(1)}, bf16[160,1152]{1,0:T(8,128)(2,1)S(1)}, u32[]{:S(2)}, u32[]{:S(2)}) collective-permute-start(bf16[160,1152]{1,0:T(8,128)(2,1)S(1)} %collective-permute-done.6), channel_id=1, source_target_pairs={{0,2},{1,67},{2,0},{3,65},{4,6},{5,71},{6,4},{7,69},{8,10},{9,75},... | collective-permute-start | bytes 1105928 | tf_op jit(solution)/shard_map/ppermute | solution.py:57
  27.2 8.8 %collective-permute-start.11 = (bf16[160,1152]{1,0:T(8,128)(2,1)S(1)}, bf16[160,1152]{1,0:T(8,128)(2,1)S(1)}, u32[]{:S(2)}, u32[]{:S(2)}) collective-permute-start(bf16[160,1152]{1,0:T(8,128)(2,1)S(1)} %collective-permute-done.7), channel_id=1, source_target_pairs={{0,2},{1,67},{2,0},{3,65},{4,6},{5,71},{6,4},{7,69},{8,10},{9,75},... | collective-permute-start | bytes 1105928 | tf_op jit(solution)/shard_map/ppermute | solution.py:57
  36.1 5.9 %collective-permute-start.13 = (bf16[1280,1152]{1,0:T(8,128)(2,1)S(1)}, bf16[1280,1152]{1,0:T(8,128)(2,1)S(1)}, u32[]{:S(2)}, u32[]{:S(2)}) collective-permute-start(bf16[1280,1152]{1,0:T(8,128)(2,1)S(1)} %get-tuple-element.48), channel_id=1, source_target_pairs={{0,1},{1,0},{2,3},{3,2},{4,5},{5,4},{6,7},{7,6},{8,9},{9,8},{10,11... | collective-permute-start | bytes 8847368 | tf_op jit(solution)/shard_map/ppermute | solution.py:61
  47.8 7.2 %collective-permute-start.15 = (bf16[2,1280,640]{2,1,0:T(8,128)(2,1)S(1)}, bf16[2,1280,640]{2,1,0:T(8,128)(2,1)S(1)}, u32[]{:S(2)}, u32[]{:S(2)}) collective-permute-start(bf16[2,1280,640]{2,1,0:T(8,128)(2,1)S(1)} %get-tuple-element.32.refs_3_.refs_4_), channel_id=1, source_target_pairs={{0,1},{1,0},{2,3},{3,2},{4,5},{5,4},{6,7},{7,6},{8,9},{9,8},{10,11... | collective-permute-start | bytes 9830408 | tf_op jit(solution)/shard_map/ppermute | solution.py:61
  55.0 10.3 %collective-permute-start.14 = (bf16[2,1280,640]{2,1,0:T(8,128)(2,1)S(1)}, bf16[2,1280,640]{2,1,0:T(8,128)(2,1)S(1)}, u32[]{:S(2)}, u32[]{:S(2)}) collective-permute-start(bf16[2,1280,640]{2,1,0:T(8,128)(2,1)S(1)} %get-tuple-element.34), channel_id=1, source_target_pairs={{0,1},{1,0},{2,3},{3,2},{4,5},{5,4},{6,7},{7,6},{8,9},{9,8},{10,11... | collective-permute-start | bytes 9830408 | tf_op jit(solution)/shard_map/ppermute | solution.py:61
  59.6 12.1 %collective-permute-start.16 = (bf16[320,1152]{1,0:T(8,128)(2,1)S(1)}, bf16[320,1152]{1,0:T(8,128)(2,1)S(1)}, u32[]{:S(2)}, u32[]{:S(2)}) collective-permute-start(bf16[320,1152]{1,0:T(8,128)(2,1)S(1)} %get-tuple-element.37), channel_id=1, source_target_pairs={{0,2},{1,67},{2,0},{3,65},{4,6},{5,71},{6,4},{7,69},{8,10},{9,75},... | collective-permute-start | bytes 2211848 | tf_op jit(solution)/shard_map/ppermute | solution.py:57
  62.3 15.1 %collective-permute-start.20 = (bf16[320,1152]{1,0:T(8,128)(2,1)S(1)}, bf16[320,1152]{1,0:T(8,128)(2,1)S(1)}, u32[]{:S(2)}, u32[]{:S(2)}) collective-permute-start(bf16[320,1152]{1,0:T(8,128)(2,1)S(1)} %get-tuple-element.42), channel_id=1, source_target_pairs={{0,12},{1,49},{2,14},{3,51},{4,0},{5,53},{6,2},{7,55},{8,4},{9,57}... | collective-permute-start | bytes 2211848 | tf_op jit(solution)/shard_map/ppermute | solution.py:48
  65.2 12.2 %collective-permute-start.21 = (bf16[320,1152]{1,0:T(8,128)(2,1)S(1)}, bf16[320,1152]{1,0:T(8,128)(2,1)S(1)}, u32[]{:S(2)}, u32[]{:S(2)}) collective-permute-start(bf16[320,1152]{1,0:T(8,128)(2,1)S(1)} %get-tuple-element.43), channel_id=1, source_target_pairs={{0,4},{1,17},{2,6},{3,19},{4,8},{5,21},{6,10},{7,23},{8,12},{9,25}... | collective-permute-start | bytes 2211848 | tf_op jit(solution)/shard_map/ppermute | solution.py:48
  68.9 22.6 %collective-permute-start.18 = (bf16[320,1152]{1,0:T(8,128)(2,1)S(1)}, bf16[320,1152]{1,0:T(8,128)(2,1)S(1)}, u32[]{:S(2)}, u32[]{:S(2)}) collective-permute-start(bf16[320,1152]{1,0:T(8,128)(2,1)S(1)} %get-tuple-element.39.refs_2_), channel_id=1, source_target_pairs={{0,12},{1,49},{2,14},{3,51},{4,0},{5,53},{6,2},{7,55},{8,4},{9,57}... | collective-permute-start | bytes 2211848 | tf_op jit(solution)/shard_map/ppermute | solution.py:48
  71.6 20.9 %collective-permute-start.19 = (bf16[320,1152]{1,0:T(8,128)(2,1)S(1)}, bf16[320,1152]{1,0:T(8,128)(2,1)S(1)}, u32[]{:S(2)}, u32[]{:S(2)}) collective-permute-start(bf16[320,1152]{1,0:T(8,128)(2,1)S(1)} %get-tuple-element.40), channel_id=1, source_target_pairs={{0,4},{1,17},{2,6},{3,19},{4,8},{5,21},{6,10},{7,23},{8,12},{9,25}... | collective-permute-start | bytes 2211848 | tf_op jit(solution)/shard_map/ppermute | solution.py:48
  71.8 19.5 %collective-permute-start.17 = (bf16[320,1152]{1,0:T(8,128)(2,1)S(1)}, bf16[320,1152]{1,0:T(8,128)(2,1)S(1)}, u32[]{:S(2)}, u32[]{:S(2)}) collective-permute-start(bf16[320,1152]{1,0:T(8,128)(2,1)S(1)} %shard_map.65.refs_7_), channel_id=1, source_target_pairs={{0,8},{1,33},{2,10},{3,35},{4,12},{5,37},{6,14},{7,39},{8,0},{9,41... | collective-permute-start | bytes 2211848 | tf_op jit(solution)/shard_map/ppermute | solution.py:48
  77.7 14.8 %collective-permute-start.22 = (bf16[320,1152]{1,0:T(8,128)(2,1)S(1)}, bf16[320,1152]{1,0:T(8,128)(2,1)S(1)}, u32[]{:S(2)}, u32[]{:S(2)}) collective-permute-start(bf16[320,1152]{1,0:T(8,128)(2,1)S(1)} %shard_map.68), channel_id=1, source_target_pairs={{0,2},{1,67},{2,0},{3,65},{4,6},{5,71},{6,4},{7,69},{8,10},{9,75},... | collective-permute-start | bytes 2211848 | tf_op jit(solution)/shard_map/ppermute | solution.py:57
  93.0 1.8 %collective-permute-start.23 = (bf16[160,1152]{1,0:T(8,128)(2,1)S(1)}, bf16[160,1152]{1,0:T(8,128)(2,1)S(1)}, u32[]{:S(2)}, u32[]{:S(2)}) collective-permute-start(bf16[160,1152]{1,0:T(8,128)(2,1)S(1)} %shard_map.69.refs_7_), channel_id=1, source_target_pairs={{0,1},{1,0},{2,3},{3,2},{4,5},{5,4},{6,7},{7,6},{8,9},{9,8},{10,11... | collective-permute-start | bytes 1105928 | tf_op jit(solution)/shard_map/ppermute | solution.py:61

commit v12 on v11

--- a/solution.py
+++ b/solution.py
@@ -321,7 +321,8 @@
     first_core = core == 0
     cores = core.astype(jnp.int32).reshape(1)
     give = jnp.where(first_core, text_embeds, image_embeds)
-    keep = jnp.where(first_core, image_embeds, text_embeds)
+    first_image, first_text = lax.optimization_barrier((image_embeds, text_embeds))
+    keep = jnp.where(first_core, first_image, first_text)
     got = swap(give)
     unit, low, high, raw, factors = call(
         pack_kernel,
@@ -394,7 +395,8 @@
         (near_received, near_part, *other),
         8 * share,
     )
-    (distant_total,) = add([(far_sums[0], arrived[2])], (near_sums[0],))
+    (across_total,) = add([(near_sums[2], arrived[0], arrived[1])], (near_sums[0],))
+    (distant_total,) = add([(far_sums[0], arrived[2])], (across_total,))
     (own_sum,) = call(
         functools.partial(self_kernel, len(other)),
         [block],
@@ -404,10 +406,9 @@
         (distant_total,),
         (jnp.float32,),
     )
-    (across_total,) = add([(near_sums[2], arrived[0], arrived[1])], (own_sum,))
-    (own_part,) = add([(own_sum, ring(distant_total, 2))], kind=jnp.float32)
     parts = [
-        own_part,
+        own_sum,
+        ring(distant_total, 2),
         ring(near_sums[0], -1),
         ring(near_sums[1], 1),
         pair(across_total),

time: 95.8 us -> 95.1 us (level)
  starting transfers between devices: 35 us -> 33.5 us
    ppermute x13, starting transfers between devices: 21 us -> 19.4 us  [ring(): return lax.ppermute(value, axes, ring_move(steps))]
    select_n x0 -> x1, other arithmetic: none -> 1.05 us  [on_device(): keep = jnp.where(first_core, first_image, first_text)]
    pallas_call x12 -> x11, Pallas kernels: 30.7 us -> 30.6 us  [call(): pl.pallas_call(body, in_specs=[pl.BlockSpec(memory_space=pltpu.SMEM)] * l...]
  transfers between devices with their start and end apart: 24 -> 24, of which waited for: 8 -> 8; matrix products, arithmetic and copies ran while one was open for 1% -> 2% of each run, Pallas kernels for 25% -> 25%
where the time goes in v12:
time: 95.1 us; the launch traced here: 94.9 us
  starting transfers between devices  33.5 us (35%)
  Pallas kernels  30.6 us (32%)
  waiting for transfers between devices  24.8 us (26%)
  other arithmetic  3.02 us (3%)
  between operations  2.12 us (2%)
    pallas_call x11, Pallas kernels, call(): pl.pallas_call(body, in_specs=[pl.BlockSpec(memory_space=pltpu.SMEM)] * l...  30.6 us
    ppermute x13, waiting for transfers between devices, ring(): return lax.ppermute(value, axes, ring_move(steps))  19.9 us
    ppermute x13, starting transfers between devices, ring(): return lax.ppermute(value, axes, ring_move(steps))  19.4 us
    ppermute x5, starting transfers between devices, pair(): return lax.ppermute(value, axes, pairs_of(move))  10.7 us
    ppermute x5, waiting for transfers between devices, pair(): return lax.ppermute(value, axes, pairs_of(move))  4.01 us
    ppermute x6, starting transfers between devices, swap(): return lax.ppermute(value, 'core', [(0, 1), (1, 0)])  3.31 us
  transfers between devices with their start and end apart: 24, of which 8 were waited for; matrix products, arithmetic and copies ran while one was open for 2% of the time, Pallas kernels for 25%

profile of v12, /device:TPU:1, one launch (start us, length us, event | category | flops | bytes accessed | tf_op | source)
XLA Modules:
  0.0 94.9 jit_solution(61229110629455361)
XLA Ops:
  0.6 1.0 %broadcast_select_fusion.2 = bf16[160,1152]{1,0:T(8,128)(2,1)S(1)} fusion(bf16[160,1152]{1,0:T(8,128)(2,1)} %param.5, bf16[160,1152]{1,0:T(8,128)(2,1)} %param.4, pred[]{:T(512)S(6)} %eq.3), kind=kLoop, calls=%fused_computation.2 | loop fusion | flops 184320 | bytes 1105921 | tf_op jit(solution)/shard_map/jit(_where)/select_n | solution.py:323
  1.7 1.5 %collective-permute-start = (bf16[160,1152]{1,0:T(8,128)(2,1)S(1)}, bf16[160,1152]{1,0:T(8,128)(2,1)S(1)}, u32[]{:S(2)}, u32[]{:S(2)}) collective-permute-start(bf16[160,1152]{1,0:T(8,128)(2,1)S(1)} %broadcast_select_fusion.2), channel_id=1, source_target_pairs={{0,1},{1,0},{2,3},{3,2},{4,5},{5,4},{6,7},{7,6},{8,9},{9,8},{10,11... | collective-permute-start | bytes 1105928 | tf_op jit(solution)/shard_map/ppermute | solution.py:61
  4.5 1.0 %broadcast_select_fusion.3.refs_3_ = bf16[160,1152]{1,0:T(8,128)(2,1)S(1)} fusion(bf16[160,1152]{1,0:T(8,128)(2,1)} %param.4, bf16[160,1152]{1,0:T(8,128)(2,1)} %param.5, pred[]{:T(512)S(6)} %eq.3), kind=kLoop, calls=%fused_computation.3 | loop fusion | flops 184320 | bytes 1105921 | tf_op jit(solution)/shard_map/jit(_where)/select_n | solution.py:325
  5.5 0.4 shard_map.59
  6.0 1.8 %collective-permute-start.1 = (bf16[160,1152]{1,0:T(8,128)(2,1)S(1)}, bf16[160,1152]{1,0:T(8,128)(2,1)S(1)}, u32[]{:S(2)}, u32[]{:S(2)}) collective-permute-start(bf16[160,1152]{1,0:T(8,128)(2,1)S(1)} %get-tuple-element.33), channel_id=1, source_target_pairs={{0,4},{1,17},{2,6},{3,19},{4,8},{5,21},{6,10},{7,23},{8,12},{9,25}... | collective-permute-start | bytes 1105928 | tf_op jit(solution)/shard_map/ppermute | solution.py:48
  7.7 2.2 %collective-permute-start.4 = (bf16[160,1152]{1,0:T(8,128)(2,1)S(1)}, bf16[160,1152]{1,0:T(8,128)(2,1)S(1)}, u32[]{:S(2)}, u32[]{:S(2)}) collective-permute-start(bf16[160,1152]{1,0:T(8,128)(2,1)S(1)} %get-tuple-element.32), channel_id=1, source_target_pairs={{0,12},{1,49},{2,14},{3,51},{4,0},{5,53},{6,2},{7,55},{8,4},{9,57}... | collective-permute-start | bytes 1105928 | tf_op jit(solution)/shard_map/ppermute | solution.py:48
  9.9 2.7 %collective-permute-start.5 = (bf16[320,1152]{1,0:T(8,128)(2,1)S(1)}, bf16[320,1152]{1,0:T(8,128)(2,1)S(1)}, u32[]{:S(2)}, u32[]{:S(2)}) collective-permute-start(bf16[320,1152]{1,0:T(8,128)(2,1)S(1)} %get-tuple-element.29.refs_2_), channel_id=1, source_target_pairs={{0,2},{1,67},{2,0},{3,65},{4,6},{5,71},{6,4},{7,69},{8,10},{9,75},... | collective-permute-start | bytes 2211848 | tf_op jit(solution)/shard_map/ppermute | solution.py:57
  12.7 0.1 constant_dynamic-update-slice_fusion.13
  12.7 2.7 %collective-permute-start.3 = (bf16[160,1152]{1,0:T(8,128)(2,1)S(1)}, bf16[160,1152]{1,0:T(8,128)(2,1)S(1)}, u32[]{:S(2)}, u32[]{:S(2)}) collective-permute-start(bf16[160,1152]{1,0:T(8,128)(2,1)S(1)} %get-tuple-element.33), channel_id=1, source_target_pairs={{0,12},{1,49},{2,14},{3,51},{4,0},{5,53},{6,2},{7,55},{8,4},{9,57}... | collective-permute-start | bytes 1105928 | tf_op jit(solution)/shard_map/ppermute | solution.py:48
  15.5 0.0 collective-permute-done.1
  15.5 0.0 collective-permute-start.6
  15.5 0.0 collective-permute-done.4
  15.5 2.7 %collective-permute-start.7 = (bf16[160,1152]{1,0:T(8,128)(2,1)S(1)}, bf16[160,1152]{1,0:T(8,128)(2,1)S(1)}, u32[]{:S(2)}, u32[]{:S(2)}) collective-permute-start(bf16[160,1152]{1,0:T(8,128)(2,1)S(1)} %collective-permute-done.4), channel_id=1, source_target_pairs={{0,12},{1,49},{2,14},{3,51},{4,0},{5,53},{6,2},{7,55},{8,4},{9,57}... | collective-permute-start | bytes 1105928 | tf_op jit(solution)/shard_map/ppermute | solution.py:48
  18.2 0.1 constant_dynamic-update-slice_fusion.12
  18.2 2.3 %collective-permute-done.2 = bf16[160,1152]{1,0:T(8,128)(2,1)S(1)} collective-permute-done((bf16[160,1152]{1,0:T(8,128)(2,1)S(1)}, bf16[160,1152]{1,0:T(8,128)(2,1)S(1)}, u32[]{:S(2)}, u32[]{:S(2)}) %collective-permute-start.2) | collective-permute-done | bytes 368672 | tf_op jit(solution)/shard_map/ppermute | solution.py:48
  20.5 0.1 constant_dynamic-update-slice_fusion.11
  20.6 0.0 collective-permute-done.3
  20.6 0.1 constant_dynamic-update-slice_fusion.10
  20.7 0.1 constant_dynamic-update-slice_fusion.9
  20.8 1.0 %collective-permute-done.5.refs_5_ = bf16[320,1152]{1,0:T(8,128)(2,1)S(1)} collective-permute-done((bf16[320,1152]{1,0:T(8,128)(2,1)S(1)}, bf16[320,1152]{1,0:T(8,128)(2,1)S(1)}, u32[]{:S(2)}, u32[]{:S(2)}) %collective-permute-start.5) | collective-permute-done | bytes 737312 | tf_op jit(solution)/shard_map/ppermute | solution.py:57
  21.8 0.1 constant_dynamic-update-slice_fusion.8
  21.9 0.1 collective-permute-start.12
  22.0 3.0 %collective-permute-start.9 = (bf16[320,1152]{1,0:T(8,128)(2,1)S(1)}, bf16[320,1152]{1,0:T(8,128)(2,1)S(1)}, u32[]{:S(2)}, u32[]{:S(2)}) collective-permute-start(bf16[320,1152]{1,0:T(8,128)(2,1)S(1)} %collective-permute-done.5.refs_5_), channel_id=1, source_target_pairs={{0,12},{1,49},{2,14},{3,51},{4,0},{5,53},{6,2},{7,55},{8,4},{9,57}... | collective-permute-start | bytes 2211848 | tf_op jit(solution)/shard_map/ppermute | solution.py:48
  25.0 2.7 %collective-permute-start.10 = (bf16[160,1152]{1,0:T(8,128)(2,1)S(1)}, bf16[160,1152]{1,0:T(8,128)(2,1)S(1)}, u32[]{:S(2)}, u32[]{:S(2)}) collective-permute-start(bf16[160,1152]{1,0:T(8,128)(2,1)S(1)} %collective-permute-done.6), channel_id=1, source_target_pairs={{0,2},{1,67},{2,0},{3,65},{4,6},{5,71},{6,4},{7,69},{8,10},{9,75},... | collective-permute-start | bytes 1105928 | tf_op jit(solution)/shard_map/ppermute | solution.py:57
  27.8 0.0 collective-permute-done.7
  27.8 0.1 collective-permute-start.11
  27.9 0.1 constant_dynamic-update-slice_fusion.19
  27.9 0.1 constant_dynamic-update-slice_fusion.18
  28.0 5.4 %collective-permute-done.8.refs_7_ = bf16[320,1152]{1,0:T(8,128)(2,1)S(1)} collective-permute-done((bf16[320,1152]{1,0:T(8,128)(2,1)S(1)}, bf16[320,1152]{1,0:T(8,128)(2,1)S(1)}, u32[]{:S(2)}, u32[]{:S(2)}) %collective-permute-start.8) | collective-permute-done | bytes 737312 | tf_op jit(solution)/shard_map/ppermute | solution.py:48
  33.3 0.1 constant_dynamic-update-slice_fusion.17
  33.4 0.0 collective-permute-done.9.refs_8_
  33.5 0.1 constant_dynamic-update-slice_fusion.16
  33.6 0.1 constant_dynamic-update-slice_fusion.15
  33.6 3.0 %collective-permute-done.11 = bf16[160,1152]{1,0:T(8,128)(2,1)S(1)} collective-permute-done((bf16[160,1152]{1,0:T(8,128)(2,1)S(1)}, bf16[160,1152]{1,0:T(8,128)(2,1)S(1)}, u32[]{:S(2)}, u32[]{:S(2)}) %collective-permute-start.11) | collective-permute-done | bytes 368672 | tf_op jit(solution)/shard_map/ppermute | solution.py:57
  36.6 0.1 constant_dynamic-update-slice_fusion.14
  36.7 0.4 collective-permute-start.13
  37.1 0.0 collective-permute-done.12.refs_10_.refs_5_.refs_3_
  37.1 5.6 %shard_map.60 = (bf16[2,1280,512]{2,1,0:T(8,128)(2,1)S(1)}, f32[2,640,1152]{2,1,0:T(8,128)S(1)}) custom-call(s32[1]{0:T(128)} %bitcast.refs_2_.refs_0_, f32[8,128]{1,0:T(8,128)S(1)} %get-tuple-element.27.refs_1_, bf16[320,1152]{1,0:T(8,128)(2,1)S(1)} %get-tuple-element.29.refs_2_, bf16[320,1152]{1,0:T(8,128)(2,1)S(1)} %get-tuple-element.63.refs_3_, ...), custom_call_target="tpu_custom_call" | custom-call | flops 4529848320 | bytes 1048576 | tf_op jit(solution)/shard_map/pallas_call | solution.py:268
  42.7 5.8 %shard_map.61 = (bf16[2,1280,128]{2,1,0:T(8,128)(2,1)S(1)}, bf16[2,1280,640]{2,1,0:T(8,128)(2,1)S(1)}) custom-call(s32[1]{0:T(128)} %bitcast.refs_2_.refs_0_, f32[8,128]{1,0:T(8,128)S(1)} %get-tuple-element.27.refs_1_, bf16[320,1152]{1,0:T(8,128)(2,1)S(1)} %get-tuple-element.29.refs_2_, bf16[320,1152]{1,0:T(8,128)(2,1)S(1)} %get-tuple-element.63.refs_3_, ...), custom_call_target="tpu_custom_call" | custom-call | flops 4529848320 | bytes 1048576 | tf_op jit(solution)/shard_map/pallas_call | solution.py:268
  48.5 0.7 collective-permute-start.15
  49.2 6.3 %shard_map.62 = (f32[2,480,1152]{2,1,0:T(8,128)S(1)}, f32[2,640,1152]{2,1,0:T(8,128)S(1)}, bf16[2,1280,640]{2,1,0:T(8,128)(2,1)S(1)}) custom-call(s32[1]{0:T(128)} %bitcast.refs_2_.refs_0_, bf16[2,1280,512]{2,1,0:T(8,128)(2,1)S(1)} %get-tuple-element.34.refs_12_.refs_1_.refs_2_, bf16[2,1280,128]{2,1,0:T(8,128)(2,1)S(1)} %get-tuple-element.35.refs_2_.refs_3_, ...), custom_call_target="tpu_custom_call" | custom-call | flops 5284823040 | bytes 1048576 | tf_op jit(solution)/shard_map/pallas_call | solution.py:268
  55.5 0.1 collective-permute-start.14
  55.6 0.0 collective-permute-done.15.refs_1_
  55.6 4.5 %shard_map.63 = (bf16[320,1152]{1,0:T(8,128)(2,1)S(1)}, bf16[320,1152]{1,0:T(8,128)(2,1)S(1)}, bf16[320,1152]{1,0:T(8,128)(2,1)S(1)}, bf16[320,1152]{1,0:T(8,128)(2,1)S(1)}) custom-call(s32[1]{0:T(128)} %bitcast.refs_2_.refs_0_, bf16[2,1280,640]{2,1,0:T(8,128)(2,1)S(1)} %collective-permute-done.15.refs_1_, f32[2,640,1152]{2,1,0:T(8,128)S(1)} %get-tuple-element.39.refs_2_, ...), custom_call_target="tpu_custom_call" | custom-call | flops 3774873600 | bytes 1048576 | tf_op jit(solution)/shard_map/pallas_call | solution.py:268
  60.1 2.9 %collective-permute-start.17 = (bf16[320,1152]{1,0:T(8,128)(2,1)S(1)}, bf16[320,1152]{1,0:T(8,128)(2,1)S(1)}, u32[]{:S(2)}, u32[]{:S(2)}) collective-permute-start(bf16[320,1152]{1,0:T(8,128)(2,1)S(1)} %get-tuple-element.44), channel_id=1, source_target_pairs={{0,12},{1,49},{2,14},{3,51},{4,0},{5,53},{6,2},{7,55},{8,4},{9,57}... | collective-permute-start | bytes 2211848 | tf_op jit(solution)/shard_map/ppermute | solution.py:48
  63.0 0.0 collective-permute-start.18
  63.0 2.7 %collective-permute-start.16 = (bf16[320,1152]{1,0:T(8,128)(2,1)S(1)}, bf16[320,1152]{1,0:T(8,128)(2,1)S(1)}, u32[]{:S(2)}, u32[]{:S(2)}) collective-permute-start(bf16[320,1152]{1,0:T(8,128)(2,1)S(1)} %get-tuple-element.41), channel_id=1, source_target_pairs={{0,2},{1,67},{2,0},{3,65},{4,6},{5,71},{6,4},{7,69},{8,10},{9,75},... | collective-permute-start | bytes 2211848 | tf_op jit(solution)/shard_map/ppermute | solution.py:57
  65.7 3.7 %shard_map.64 = (bf16[320,1152]{1,0:T(8,128)(2,1)S(1)}, bf16[320,1152]{1,0:T(8,128)(2,1)S(1)}, bf16[320,1152]{1,0:T(8,128)(2,1)S(1)}) custom-call(s32[1]{0:T(128)} %bitcast.refs_2_.refs_0_, bf16[2,1280,640]{2,1,0:T(8,128)(2,1)S(1)} %collective-permute-done.14.refs_1_, f32[2,480,1152]{2,1,0:T(8,128)S(1)} %get-tuple-element.42.refs_2_, ...), custom_call_target="tpu_custom_call" | custom-call | flops 3019898880 | bytes 1048576 | tf_op jit(solution)/shard_map/pallas_call | solution.py:268
  69.4 2.7 %collective-permute-start.20 = (bf16[320,1152]{1,0:T(8,128)(2,1)S(1)}, bf16[320,1152]{1,0:T(8,128)(2,1)S(1)}, u32[]{:S(2)}, u32[]{:S(2)}) collective-permute-start(bf16[320,1152]{1,0:T(8,128)(2,1)S(1)} %get-tuple-element.46.refs_3_), channel_id=1, source_target_pairs={{0,12},{1,49},{2,14},{3,51},{4,0},{5,53},{6,2},{7,55},{8,4},{9,57}... | collective-permute-start | bytes 2211848 | tf_op jit(solution)/shard_map/ppermute | solution.py:48
  72.1 0.0 collective-permute-start.21
  72.2 0.0 collective-permute-done.17.refs_1_
  72.2 2.7 %collective-permute-done.18.refs_2_ = bf16[320,1152]{1,0:T(8,128)(2,1)S(1)} collective-permute-done((bf16[320,1152]{1,0:T(8,128)(2,1)S(1)}, bf16[320,1152]{1,0:T(8,128)(2,1)S(1)}, u32[]{:S(2)}, u32[]{:S(2)}) %collective-permute-start.18) | collective-permute-done | bytes 737312 | tf_op jit(solution)/shard_map/ppermute | solution.py:48
  74.8 0.3 shard_map.65.refs_2_
  75.1 0.2 shard_map.66.refs_7_
  75.3 1.4 %collective-permute-start.19 = (bf16[320,1152]{1,0:T(8,128)(2,1)S(1)}, bf16[320,1152]{1,0:T(8,128)(2,1)S(1)}, u32[]{:S(2)}, u32[]{:S(2)}) collective-permute-start(bf16[320,1152]{1,0:T(8,128)(2,1)S(1)} %shard_map.66.refs_7_), channel_id=1, source_target_pairs={{0,8},{1,33},{2,10},{3,35},{4,12},{5,37},{6,14},{7,39},{8,0},{9,41... | collective-permute-start | bytes 2211848 | tf_op jit(solution)/shard_map/ppermute | solution.py:48
  76.7 2.4 %collective-permute-start.22 = (bf16[320,1152]{1,0:T(8,128)(2,1)S(1)}, bf16[320,1152]{1,0:T(8,128)(2,1)S(1)}, u32[]{:S(2)}, u32[]{:S(2)}) collective-permute-start(bf16[320,1152]{1,0:T(8,128)(2,1)S(1)} %shard_map.65.refs_2_), channel_id=1, source_target_pairs={{0,2},{1,67},{2,0},{3,65},{4,6},{5,71},{6,4},{7,69},{8,10},{9,75},... | collective-permute-start | bytes 2211848 | tf_op jit(solution)/shard_map/ppermute | solution.py:57
  79.1 3.0 %shard_map.67.refs_3_ = f32[320,1152]{1,0:T(8,128)S(1)} custom-call(s32[1]{0:T(128)} %bitcast.refs_2_.refs_0_, bf16[2,1280,640]{2,1,0:T(8,128)(2,1)S(1)} %collective-permute-done.14.refs_1_, bf16[2,1280,512]{2,1,0:T(8,128)(2,1)S(1)} %get-tuple-element.34.refs_12_.refs_1_.refs_2_, bf16[2,1280,128]{2,1,0:T(8,128)(2,1)S(1)} %get-tuple-element.35.refs_2_.refs_3_, ...), custom_call_target="tpu_custom_call" | custom-call | flops 1887436800 | bytes 1048576 | tf_op jit(solution)/shard_map/pallas_call | solution.py:268
  82.1 6.3 %collective-permute-done.20.refs_5_ = bf16[320,1152]{1,0:T(8,128)(2,1)S(1)} collective-permute-done((bf16[320,1152]{1,0:T(8,128)(2,1)S(1)}, bf16[320,1152]{1,0:T(8,128)(2,1)S(1)}, u32[]{:S(2)}, u32[]{:S(2)}) %collective-permute-start.20) | collective-permute-done | bytes 737312 | tf_op jit(solution)/shard_map/ppermute | solution.py:48
  88.5 3.3 %collective-permute-done.21.refs_6_ = bf16[320,1152]{1,0:T(8,128)(2,1)S(1)} collective-permute-done((bf16[320,1152]{1,0:T(8,128)(2,1)S(1)}, bf16[320,1152]{1,0:T(8,128)(2,1)S(1)}, u32[]{:S(2)}, u32[]{:S(2)}) %collective-permute-start.21) | collective-permute-done | bytes 737312 | tf_op jit(solution)/shard_map/ppermute | solution.py:48
  91.7 0.5 shard_map.68.refs_8_
  92.2 0.5 collective-permute-start.23
  92.7 0.5 shard_map.69
  93.2 0.8 collective-permute-done.23
  94.0 0.9 broadcast_select_fusion
  (10 shorter events, 0.0 us)
Async XLA Ops:
  1.7 3.8 %collective-permute-start = (bf16[160,1152]{1,0:T(8,128)(2,1)S(1)}, bf16[160,1152]{1,0:T(8,128)(2,1)S(1)}, u32[]{:S(2)}, u32[]{:S(2)}) collective-permute-start(bf16[160,1152]{1,0:T(8,128)(2,1)S(1)} %broadcast_select_fusion.2), channel_id=1, source_target_pairs={{0,1},{1,0},{2,3},{3,2},{4,5},{5,4},{6,7},{7,6},{8,9},{9,8},{10,11... | collective-permute-start | bytes 1105928 | tf_op jit(solution)/shard_map/ppermute | solution.py:61
  6.0 9.5 %collective-permute-start.1 = (bf16[160,1152]{1,0:T(8,128)(2,1)S(1)}, bf16[160,1152]{1,0:T(8,128)(2,1)S(1)}, u32[]{:S(2)}, u32[]{:S(2)}) collective-permute-start(bf16[160,1152]{1,0:T(8,128)(2,1)S(1)} %get-tuple-element.33), channel_id=1, source_target_pairs={{0,4},{1,17},{2,6},{3,19},{4,8},{5,21},{6,10},{7,23},{8,12},{9,25}... | collective-permute-start | bytes 1105928 | tf_op jit(solution)/shard_map/ppermute | solution.py:48
  7.7 7.8 %collective-permute-start.4 = (bf16[160,1152]{1,0:T(8,128)(2,1)S(1)}, bf16[160,1152]{1,0:T(8,128)(2,1)S(1)}, u32[]{:S(2)}, u32[]{:S(2)}) collective-permute-start(bf16[160,1152]{1,0:T(8,128)(2,1)S(1)} %get-tuple-element.32), channel_id=1, source_target_pairs={{0,12},{1,49},{2,14},{3,51},{4,0},{5,53},{6,2},{7,55},{8,4},{9,57}... | collective-permute-start | bytes 1105928 | tf_op jit(solution)/shard_map/ppermute | solution.py:48
  9.9 11.9 %collective-permute-start.5 = (bf16[320,1152]{1,0:T(8,128)(2,1)S(1)}, bf16[320,1152]{1,0:T(8,128)(2,1)S(1)}, u32[]{:S(2)}, u32[]{:S(2)}) collective-permute-start(bf16[320,1152]{1,0:T(8,128)(2,1)S(1)} %get-tuple-element.29.refs_2_), channel_id=1, source_target_pairs={{0,2},{1,67},{2,0},{3,65},{4,6},{5,71},{6,4},{7,69},{8,10},{9,75},... | collective-permute-start | bytes 2211848 | tf_op jit(solution)/shard_map/ppermute | solution.py:57
  12.7 7.9 %collective-permute-start.2 = (bf16[160,1152]{1,0:T(8,128)(2,1)S(1)}, bf16[160,1152]{1,0:T(8,128)(2,1)S(1)}, u32[]{:S(2)}, u32[]{:S(2)}) collective-permute-start(bf16[160,1152]{1,0:T(8,128)(2,1)S(1)} %get-tuple-element.32), channel_id=1, source_target_pairs={{0,4},{1,17},{2,6},{3,19},{4,8},{5,21},{6,10},{7,23},{8,12},{9,25}... | collective-permute-start | bytes 1105928 | tf_op jit(solution)/shard_map/ppermute | solution.py:48
  12.7 7.9 %collective-permute-start.3 = (bf16[160,1152]{1,0:T(8,128)(2,1)S(1)}, bf16[160,1152]{1,0:T(8,128)(2,1)S(1)}, u32[]{:S(2)}, u32[]{:S(2)}) collective-permute-start(bf16[160,1152]{1,0:T(8,128)(2,1)S(1)} %get-tuple-element.33), channel_id=1, source_target_pairs={{0,12},{1,49},{2,14},{3,51},{4,0},{5,53},{6,2},{7,55},{8,4},{9,57}... | collective-permute-start | bytes 1105928 | tf_op jit(solution)/shard_map/ppermute | solution.py:48
  15.5 9.5 %collective-permute-start.6 = (bf16[160,1152]{1,0:T(8,128)(2,1)S(1)}, bf16[160,1152]{1,0:T(8,128)(2,1)S(1)}, u32[]{:S(2)}, u32[]{:S(2)}) collective-permute-start(bf16[160,1152]{1,0:T(8,128)(2,1)S(1)} %collective-permute-done.1), channel_id=1, source_target_pairs={{0,4},{1,17},{2,6},{3,19},{4,8},{5,21},{6,10},{7,23},{8,12},{9,25}... | collective-permute-start | bytes 1105928 | tf_op jit(solution)/shard_map/ppermute | solution.py:48
  15.5 12.3 %collective-permute-start.7 = (bf16[160,1152]{1,0:T(8,128)(2,1)S(1)}, bf16[160,1152]{1,0:T(8,128)(2,1)S(1)}, u32[]{:S(2)}, u32[]{:S(2)}) collective-permute-start(bf16[160,1152]{1,0:T(8,128)(2,1)S(1)} %collective-permute-done.4), channel_id=1, source_target_pairs={{0,12},{1,49},{2,14},{3,51},{4,0},{5,53},{6,2},{7,55},{8,4},{9,57}... | collective-permute-start | bytes 1105928 | tf_op jit(solution)/shard_map/ppermute | solution.py:48
  21.8 11.5 %collective-permute-start.8 = (bf16[320,1152]{1,0:T(8,128)(2,1)S(1)}, bf16[320,1152]{1,0:T(8,128)(2,1)S(1)}, u32[]{:S(2)}, u32[]{:S(2)}) collective-permute-start(bf16[320,1152]{1,0:T(8,128)(2,1)S(1)} %collective-permute-done.5.refs_5_), channel_id=1, source_target_pairs={{0,4},{1,17},{2,6},{3,19},{4,8},{5,21},{6,10},{7,23},{8,12},{9,25}... | collective-permute-start | bytes 2211848 | tf_op jit(solution)/shard_map/ppermute | solution.py:48
  21.9 15.2 %collective-permute-start.12 = (bf16[1280,1152]{1,0:T(8,128)(2,1)S(1)}, bf16[1280,1152]{1,0:T(8,128)(2,1)S(1)}, u32[]{:S(2)}, u32[]{:S(2)}) collective-permute-start(bf16[1280,1152]{1,0:T(8,128)(2,1)S(1)} %constant_dynamic-update-slice_fusion.8), channel_id=1, source_target_pairs={{0,1},{1,0},{2,3},{3,2},{4,5},{5,4},{6,7},{7,6},{8,9},{9,8},{10,11... | collective-permute-start | bytes 8847368 | tf_op jit(solution)/shard_map/ppermute | solution.py:61
  22.0 11.4 %collective-permute-start.9 = (bf16[320,1152]{1,0:T(8,128)(2,1)S(1)}, bf16[320,1152]{1,0:T(8,128)(2,1)S(1)}, u32[]{:S(2)}, u32[]{:S(2)}) collective-permute-start(bf16[320,1152]{1,0:T(8,128)(2,1)S(1)} %collective-permute-done.5.refs_5_), channel_id=1, source_target_pairs={{0,12},{1,49},{2,14},{3,51},{4,0},{5,53},{6,2},{7,55},{8,4},{9,57}... | collective-permute-start | bytes 2211848 | tf_op jit(solution)/shard_map/ppermute | solution.py:48
  25.0 8.5 %collective-permute-start.10 = (bf16[160,1152]{1,0:T(8,128)(2,1)S(1)}, bf16[160,1152]{1,0:T(8,128)(2,1)S(1)}, u32[]{:S(2)}, u32[]{:S(2)}) collective-permute-start(bf16[160,1152]{1,0:T(8,128)(2,1)S(1)} %collective-permute-done.6), channel_id=1, source_target_pairs={{0,2},{1,67},{2,0},{3,65},{4,6},{5,71},{6,4},{7,69},{8,10},{9,75},... | collective-permute-start | bytes 1105928 | tf_op jit(solution)/shard_map/ppermute | solution.py:57
  27.8 8.8 %collective-permute-start.11 = (bf16[160,1152]{1,0:T(8,128)(2,1)S(1)}, bf16[160,1152]{1,0:T(8,128)(2,1)S(1)}, u32[]{:S(2)}, u32[]{:S(2)}) collective-permute-start(bf16[160,1152]{1,0:T(8,128)(2,1)S(1)} %collective-permute-done.7), channel_id=1, source_target_pairs={{0,2},{1,67},{2,0},{3,65},{4,6},{5,71},{6,4},{7,69},{8,10},{9,75},... | collective-permute-start | bytes 1105928 | tf_op jit(solution)/shard_map/ppermute | solution.py:57
  36.7 6.0 %collective-permute-start.13 = (bf16[1280,1152]{1,0:T(8,128)(2,1)S(1)}, bf16[1280,1152]{1,0:T(8,128)(2,1)S(1)}, u32[]{:S(2)}, u32[]{:S(2)}) collective-permute-start(bf16[1280,1152]{1,0:T(8,128)(2,1)S(1)} %get-tuple-element.50), channel_id=1, source_target_pairs={{0,1},{1,0},{2,3},{3,2},{4,5},{5,4},{6,7},{7,6},{8,9},{9,8},{10,11... | collective-permute-start | bytes 8847368 | tf_op jit(solution)/shard_map/ppermute | solution.py:61
  48.5 7.1 %collective-permute-start.15 = (bf16[2,1280,640]{2,1,0:T(8,128)(2,1)S(1)}, bf16[2,1280,640]{2,1,0:T(8,128)(2,1)S(1)}, u32[]{:S(2)}, u32[]{:S(2)}) collective-permute-start(bf16[2,1280,640]{2,1,0:T(8,128)(2,1)S(1)} %get-tuple-element.36.refs_3_.refs_4_), channel_id=1, source_target_pairs={{0,1},{1,0},{2,3},{3,2},{4,5},{5,4},{6,7},{7,6},{8,9},{9,8},{10,11... | collective-permute-start | bytes 9830408 | tf_op jit(solution)/shard_map/ppermute | solution.py:61
  55.5 10.2 %collective-permute-start.14 = (bf16[2,1280,640]{2,1,0:T(8,128)(2,1)S(1)}, bf16[2,1280,640]{2,1,0:T(8,128)(2,1)S(1)}, u32[]{:S(2)}, u32[]{:S(2)}) collective-permute-start(bf16[2,1280,640]{2,1,0:T(8,128)(2,1)S(1)} %get-tuple-element.38), channel_id=1, source_target_pairs={{0,1},{1,0},{2,3},{3,2},{4,5},{5,4},{6,7},{7,6},{8,9},{9,8},{10,11... | collective-permute-start | bytes 9830408 | tf_op jit(solution)/shard_map/ppermute | solution.py:61
  60.1 12.0 %collective-permute-start.17 = (bf16[320,1152]{1,0:T(8,128)(2,1)S(1)}, bf16[320,1152]{1,0:T(8,128)(2,1)S(1)}, u32[]{:S(2)}, u32[]{:S(2)}) collective-permute-start(bf16[320,1152]{1,0:T(8,128)(2,1)S(1)} %get-tuple-element.44), channel_id=1, source_target_pairs={{0,12},{1,49},{2,14},{3,51},{4,0},{5,53},{6,2},{7,55},{8,4},{9,57}... | collective-permute-start | bytes 2211848 | tf_op jit(solution)/shard_map/ppermute | solution.py:48
  63.0 11.8 %collective-permute-start.18 = (bf16[320,1152]{1,0:T(8,128)(2,1)S(1)}, bf16[320,1152]{1,0:T(8,128)(2,1)S(1)}, u32[]{:S(2)}, u32[]{:S(2)}) collective-permute-start(bf16[320,1152]{1,0:T(8,128)(2,1)S(1)} %get-tuple-element.45), channel_id=1, source_target_pairs={{0,4},{1,17},{2,6},{3,19},{4,8},{5,21},{6,10},{7,23},{8,12},{9,25}... | collective-permute-start | bytes 2211848 | tf_op jit(solution)/shard_map/ppermute | solution.py:48
  63.0 12.1 %collective-permute-start.16 = (bf16[320,1152]{1,0:T(8,128)(2,1)S(1)}, bf16[320,1152]{1,0:T(8,128)(2,1)S(1)}, u32[]{:S(2)}, u32[]{:S(2)}) collective-permute-start(bf16[320,1152]{1,0:T(8,128)(2,1)S(1)} %get-tuple-element.41), channel_id=1, source_target_pairs={{0,2},{1,67},{2,0},{3,65},{4,6},{5,71},{6,4},{7,69},{8,10},{9,75},... | collective-permute-start | bytes 2211848 | tf_op jit(solution)/shard_map/ppermute | solution.py:57
  69.4 19.1 %collective-permute-start.20 = (bf16[320,1152]{1,0:T(8,128)(2,1)S(1)}, bf16[320,1152]{1,0:T(8,128)(2,1)S(1)}, u32[]{:S(2)}, u32[]{:S(2)}) collective-permute-start(bf16[320,1152]{1,0:T(8,128)(2,1)S(1)} %get-tuple-element.46.refs_3_), channel_id=1, source_target_pairs={{0,12},{1,49},{2,14},{3,51},{4,0},{5,53},{6,2},{7,55},{8,4},{9,57}... | collective-permute-start | bytes 2211848 | tf_op jit(solution)/shard_map/ppermute | solution.py:48
  72.1 19.6 %collective-permute-start.21 = (bf16[320,1152]{1,0:T(8,128)(2,1)S(1)}, bf16[320,1152]{1,0:T(8,128)(2,1)S(1)}, u32[]{:S(2)}, u32[]{:S(2)}) collective-permute-start(bf16[320,1152]{1,0:T(8,128)(2,1)S(1)} %get-tuple-element.47), channel_id=1, source_target_pairs={{0,4},{1,17},{2,6},{3,19},{4,8},{5,21},{6,10},{7,23},{8,12},{9,25}... | collective-permute-start | bytes 2211848 | tf_op jit(solution)/shard_map/ppermute | solution.py:48
  75.3 16.4 %collective-permute-start.19 = (bf16[320,1152]{1,0:T(8,128)(2,1)S(1)}, bf16[320,1152]{1,0:T(8,128)(2,1)S(1)}, u32[]{:S(2)}, u32[]{:S(2)}) collective-permute-start(bf16[320,1152]{1,0:T(8,128)(2,1)S(1)} %shard_map.66.refs_7_), channel_id=1, source_target_pairs={{0,8},{1,33},{2,10},{3,35},{4,12},{5,37},{6,14},{7,39},{8,0},{9,41... | collective-permute-start | bytes 2211848 | tf_op jit(solution)/shard_map/ppermute | solution.py:48
  76.7 15.0 %collective-permute-start.22 = (bf16[320,1152]{1,0:T(8,128)(2,1)S(1)}, bf16[320,1152]{1,0:T(8,128)(2,1)S(1)}, u32[]{:S(2)}, u32[]{:S(2)}) collective-permute-start(bf16[320,1152]{1,0:T(8,128)(2,1)S(1)} %shard_map.65.refs_2_), channel_id=1, source_target_pairs={{0,2},{1,67},{2,0},{3,65},{4,6},{5,71},{6,4},{7,69},{8,10},{9,75},... | collective-permute-start | bytes 2211848 | tf_op jit(solution)/shard_map/ppermute | solution.py:57
  92.2 1.8 %collective-permute-start.23 = (bf16[160,1152]{1,0:T(8,128)(2,1)S(1)}, bf16[160,1152]{1,0:T(8,128)(2,1)S(1)}, u32[]{:S(2)}, u32[]{:S(2)}) collective-permute-start(bf16[160,1152]{1,0:T(8,128)(2,1)S(1)} %shard_map.68.refs_8_), channel_id=1, source_target_pairs={{0,1},{1,0},{2,3},{3,2},{4,5},{5,4},{6,7},{7,6},{8,9},{9,8},{10,11... | collective-permute-start | bytes 1105928 | tf_op jit(solution)/shard_map/ppermute | solution.py:61

commit v13 on v12

--- a/solution.py
+++ b/solution.py
@@ -321,8 +321,7 @@
     first_core = core == 0
     cores = core.astype(jnp.int32).reshape(1)
     give = jnp.where(first_core, text_embeds, image_embeds)
-    first_image, first_text = lax.optimization_barrier((image_embeds, text_embeds))
-    keep = jnp.where(first_core, first_image, first_text)
+    keep = jnp.where(first_core, image_embeds, text_embeds)
     got = swap(give)
     unit, low, high, raw, factors = call(
         pack_kernel,

time: 95.1 us -> 94.5 us (level)
    select_n x1 -> x0, other arithmetic: 1.05 us -> none  [on_device(): keep = jnp.where(first_core, first_image, first_text)]
  transfers between devices with their start and end apart: 24 -> 24, of which waited for: 8 -> 9; matrix products, arithmetic and copies ran while one was open for 2% -> 1% of each run, Pallas kernels for 25% -> 25%
where the time goes in v13:
time: 94.5 us; the launch traced here: 94.3 us
  starting transfers between devices  33.8 us (36%)
  Pallas kernels  30.7 us (32%)
  waiting for transfers between devices  24.8 us (26%)
  between operations  2.12 us (2%)
  other arithmetic  2.1 us (2%)
    pallas_call x11, Pallas kernels, call(): pl.pallas_call(body, in_specs=[pl.BlockSpec(memory_space=pltpu.SMEM)] * l...  30.7 us
    ppermute x13, waiting for transfers between devices, ring(): return lax.ppermute(value, axes, ring_move(steps))  19.9 us
    ppermute x13, starting transfers between devices, ring(): return lax.ppermute(value, axes, ring_move(steps))  19.6 us
    ppermute x5, starting transfers between devices, pair(): return lax.ppermute(value, axes, pairs_of(move))  11 us
    ppermute x5, waiting for transfers between devices, pair(): return lax.ppermute(value, axes, pairs_of(move))  4.04 us
    ppermute x6, starting transfers between devices, swap(): return lax.ppermute(value, 'core', [(0, 1), (1, 0)])  3.23 us
  transfers between devices with their start and end apart: 24, of which 9 were waited for; matrix products, arithmetic and copies ran while one was open for 1% of the time, Pallas kernels for 25%

profile of v13, /device:TPU:1, one launch (start us, length us, event | category | flops | bytes accessed | tf_op | source)
XLA Modules:
  0.0 94.3 jit_solution(12212915633882191872)
XLA Ops:
  0.6 1.2 %broadcast_select_fusion.2 = (bf16[160,1152]{1,0:T(8,128)(2,1)S(1)}, bf16[160,1152]{1,0:T(8,128)(2,1)S(1)}) fusion(bf16[160,1152]{1,0:T(8,128)(2,1)} %param.5, bf16[160,1152]{1,0:T(8,128)(2,1)} %param.4, pred[]{:T(512)S(6)} %eq.3), kind=kLoop, calls=%fused_computation.2 | loop fusion | flops 368640 | bytes 1474561 | tf_op jit(solution)/shard_map/jit(_where)/select_n | solution.py:323
  1.8 1.5 %collective-permute-start = (bf16[160,1152]{1,0:T(8,128)(2,1)S(1)}, bf16[160,1152]{1,0:T(8,128)(2,1)S(1)}, u32[]{:S(2)}, u32[]{:S(2)}) collective-permute-start(bf16[160,1152]{1,0:T(8,128)(2,1)S(1)} %get-tuple-element.46), channel_id=1, source_target_pairs={{0,1},{1,0},{2,3},{3,2},{4,5},{5,4},{6,7},{7,6},{8,9},{9,8},{10,11... | collective-permute-start | bytes 1105928 | tf_op jit(solution)/shard_map/ppermute | solution.py:61
  4.6 0.0 collective-permute-done.refs_4_
  4.6 0.4 shard_map.59
  5.0 1.8 %collective-permute-start.1 = (bf16[160,1152]{1,0:T(8,128)(2,1)S(1)}, bf16[160,1152]{1,0:T(8,128)(2,1)S(1)}, u32[]{:S(2)}, u32[]{:S(2)}) collective-permute-start(bf16[160,1152]{1,0:T(8,128)(2,1)S(1)} %get-tuple-element.29), channel_id=1, source_target_pairs={{0,4},{1,17},{2,6},{3,19},{4,8},{5,21},{6,10},{7,23},{8,12},{9,25}... | collective-permute-start | bytes 1105928 | tf_op jit(solution)/shard_map/ppermute | solution.py:48
  6.8 2.2 %collective-permute-start.4 = (bf16[160,1152]{1,0:T(8,128)(2,1)S(1)}, bf16[160,1152]{1,0:T(8,128)(2,1)S(1)}, u32[]{:S(2)}, u32[]{:S(2)}) collective-permute-start(bf16[160,1152]{1,0:T(8,128)(2,1)S(1)} %get-tuple-element.28), channel_id=1, source_target_pairs={{0,12},{1,49},{2,14},{3,51},{4,0},{5,53},{6,2},{7,55},{8,4},{9,57}... | collective-permute-start | bytes 1105928 | tf_op jit(solution)/shard_map/ppermute | solution.py:48
  9.0 2.7 %collective-permute-start.5 = (bf16[320,1152]{1,0:T(8,128)(2,1)S(1)}, bf16[320,1152]{1,0:T(8,128)(2,1)S(1)}, u32[]{:S(2)}, u32[]{:S(2)}) collective-permute-start(bf16[320,1152]{1,0:T(8,128)(2,1)S(1)} %get-tuple-element.25.refs_2_), channel_id=1, source_target_pairs={{0,2},{1,67},{2,0},{3,65},{4,6},{5,71},{6,4},{7,69},{8,10},{9,75},... | collective-permute-start | bytes 2211848 | tf_op jit(solution)/shard_map/ppermute | solution.py:57
  11.8 0.1 constant_dynamic-update-slice_fusion.13
  11.8 2.7 %collective-permute-start.3 = (bf16[160,1152]{1,0:T(8,128)(2,1)S(1)}, bf16[160,1152]{1,0:T(8,128)(2,1)S(1)}, u32[]{:S(2)}, u32[]{:S(2)}) collective-permute-start(bf16[160,1152]{1,0:T(8,128)(2,1)S(1)} %get-tuple-element.29), channel_id=1, source_target_pairs={{0,12},{1,49},{2,14},{3,51},{4,0},{5,53},{6,2},{7,55},{8,4},{9,57}... | collective-permute-start | bytes 1105928 | tf_op jit(solution)/shard_map/ppermute | solution.py:48
  14.6 0.0 collective-permute-done.1
  14.6 0.0 collective-permute-start.6
  14.6 0.0 collective-permute-done.4
  14.6 2.7 %collective-permute-start.7 = (bf16[160,1152]{1,0:T(8,128)(2,1)S(1)}, bf16[160,1152]{1,0:T(8,128)(2,1)S(1)}, u32[]{:S(2)}, u32[]{:S(2)}) collective-permute-start(bf16[160,1152]{1,0:T(8,128)(2,1)S(1)} %collective-permute-done.4), channel_id=1, source_target_pairs={{0,12},{1,49},{2,14},{3,51},{4,0},{5,53},{6,2},{7,55},{8,4},{9,57}... | collective-permute-start | bytes 1105928 | tf_op jit(solution)/shard_map/ppermute | solution.py:48
  17.2 0.1 constant_dynamic-update-slice_fusion.12
  17.3 2.3 %collective-permute-done.2 = bf16[160,1152]{1,0:T(8,128)(2,1)S(1)} collective-permute-done((bf16[160,1152]{1,0:T(8,128)(2,1)S(1)}, bf16[160,1152]{1,0:T(8,128)(2,1)S(1)}, u32[]{:S(2)}, u32[]{:S(2)}) %collective-permute-start.2) | collective-permute-done | bytes 368672 | tf_op jit(solution)/shard_map/ppermute | solution.py:48
  19.6 0.1 constant_dynamic-update-slice_fusion.11
  19.7 0.0 collective-permute-done.3
  19.7 0.1 constant_dynamic-update-slice_fusion.10
  19.8 0.1 constant_dynamic-update-slice_fusion.9
  19.9 1.0 %collective-permute-done.5.refs_5_ = bf16[320,1152]{1,0:T(8,128)(2,1)S(1)} collective-permute-done((bf16[320,1152]{1,0:T(8,128)(2,1)S(1)}, bf16[320,1152]{1,0:T(8,128)(2,1)S(1)}, u32[]{:S(2)}, u32[]{:S(2)}) %collective-permute-start.5) | collective-permute-done | bytes 737312 | tf_op jit(solution)/shard_map/ppermute | solution.py:57
  20.9 0.1 constant_dynamic-update-slice_fusion.8
  21.0 0.1 collective-permute-start.12
  21.1 3.4 %collective-permute-start.9 = (bf16[320,1152]{1,0:T(8,128)(2,1)S(1)}, bf16[320,1152]{1,0:T(8,128)(2,1)S(1)}, u32[]{:S(2)}, u32[]{:S(2)}) collective-permute-start(bf16[320,1152]{1,0:T(8,128)(2,1)S(1)} %collective-permute-done.5.refs_5_), channel_id=1, source_target_pairs={{0,12},{1,49},{2,14},{3,51},{4,0},{5,53},{6,2},{7,55},{8,4},{9,57}... | collective-permute-start | bytes 2211848 | tf_op jit(solution)/shard_map/ppermute | solution.py:48
  24.5 2.7 %collective-permute-start.10 = (bf16[160,1152]{1,0:T(8,128)(2,1)S(1)}, bf16[160,1152]{1,0:T(8,128)(2,1)S(1)}, u32[]{:S(2)}, u32[]{:S(2)}) collective-permute-start(bf16[160,1152]{1,0:T(8,128)(2,1)S(1)} %collective-permute-done.6), channel_id=1, source_target_pairs={{0,2},{1,67},{2,0},{3,65},{4,6},{5,71},{6,4},{7,69},{8,10},{9,75},... | collective-permute-start | bytes 1105928 | tf_op jit(solution)/shard_map/ppermute | solution.py:57
  27.2 0.0 collective-permute-done.7
  27.2 0.1 collective-permute-start.11
  27.3 0.1 constant_dynamic-update-slice_fusion.19
  27.4 0.1 constant_dynamic-update-slice_fusion.18
  27.4 5.0 %collective-permute-done.8.refs_7_ = bf16[320,1152]{1,0:T(8,128)(2,1)S(1)} collective-permute-done((bf16[320,1152]{1,0:T(8,128)(2,1)S(1)}, bf16[320,1152]{1,0:T(8,128)(2,1)S(1)}, u32[]{:S(2)}, u32[]{:S(2)}) %collective-permute-start.8) | collective-permute-done | bytes 737312 | tf_op jit(solution)/shard_map/ppermute | solution.py:48
  32.5 0.1 constant_dynamic-update-slice_fusion.17
  32.6 0.3 collective-permute-done.9.refs_8_
  32.9 0.1 constant_dynamic-update-slice_fusion.16
  33.0 0.0 collective-permute-done.10
  33.0 0.1 constant_dynamic-update-slice_fusion.15
  33.1 3.0 %collective-permute-done.11 = bf16[160,1152]{1,0:T(8,128)(2,1)S(1)} collective-permute-done((bf16[160,1152]{1,0:T(8,128)(2,1)S(1)}, bf16[160,1152]{1,0:T(8,128)(2,1)S(1)}, u32[]{:S(2)}, u32[]{:S(2)}) %collective-permute-start.11) | collective-permute-done | bytes 368672 | tf_op jit(solution)/shard_map/ppermute | solution.py:57
  36.1 0.1 constant_dynamic-update-slice_fusion.14
  36.1 0.3 collective-permute-start.13
  36.4 5.6 %shard_map.60 = (bf16[2,1280,512]{2,1,0:T(8,128)(2,1)S(1)}, f32[2,640,1152]{2,1,0:T(8,128)S(1)}) custom-call(s32[1]{0:T(128)} %bitcast.refs_2_.refs_0_, f32[8,128]{1,0:T(8,128)S(1)} %get-tuple-element.23.refs_1_, bf16[320,1152]{1,0:T(8,128)(2,1)S(1)} %get-tuple-element.25.refs_2_, bf16[320,1152]{1,0:T(8,128)(2,1)S(1)} %get-tuple-element.61.refs_3_, ...), custom_call_target="tpu_custom_call" | custom-call | flops 4529848320 | bytes 1048576 | tf_op jit(solution)/shard_map/pallas_call | solution.py:268
  42.0 0.0 collective-permute-done.13.refs_11_.refs_6_.refs_4_
  42.1 5.8 %shard_map.61 = (bf16[2,1280,128]{2,1,0:T(8,128)(2,1)S(1)}, bf16[2,1280,640]{2,1,0:T(8,128)(2,1)S(1)}) custom-call(s32[1]{0:T(128)} %bitcast.refs_2_.refs_0_, f32[8,128]{1,0:T(8,128)S(1)} %get-tuple-element.23.refs_1_, bf16[320,1152]{1,0:T(8,128)(2,1)S(1)} %get-tuple-element.25.refs_2_, bf16[320,1152]{1,0:T(8,128)(2,1)S(1)} %get-tuple-element.61.refs_3_, ...), custom_call_target="tpu_custom_call" | custom-call | flops 4529848320 | bytes 1048576 | tf_op jit(solution)/shard_map/pallas_call | solution.py:268
  47.8 0.8 collective-permute-start.15
  48.7 6.3 %shard_map.62 = (f32[2,480,1152]{2,1,0:T(8,128)S(1)}, f32[2,640,1152]{2,1,0:T(8,128)S(1)}, bf16[2,1280,640]{2,1,0:T(8,128)(2,1)S(1)}) custom-call(s32[1]{0:T(128)} %bitcast.refs_2_.refs_0_, bf16[2,1280,512]{2,1,0:T(8,128)(2,1)S(1)} %get-tuple-element.30.refs_12_.refs_1_.refs_2_, bf16[2,1280,128]{2,1,0:T(8,128)(2,1)S(1)} %get-tuple-element.31.refs_2_.refs_3_, ...), custom_call_target="tpu_custom_call" | custom-call | flops 5284823040 | bytes 1048576 | tf_op jit(solution)/shard_map/pallas_call | solution.py:268
  54.9 0.1 collective-permute-start.14
  55.0 0.0 collective-permute-done.15.refs_1_
  55.0 4.5 %shard_map.63 = (bf16[320,1152]{1,0:T(8,128)(2,1)S(1)}, bf16[320,1152]{1,0:T(8,128)(2,1)S(1)}, bf16[320,1152]{1,0:T(8,128)(2,1)S(1)}, bf16[320,1152]{1,0:T(8,128)(2,1)S(1)}) custom-call(s32[1]{0:T(128)} %bitcast.refs_2_.refs_0_, bf16[2,1280,640]{2,1,0:T(8,128)(2,1)S(1)} %collective-permute-done.15.refs_1_, f32[2,640,1152]{2,1,0:T(8,128)S(1)} %get-tuple-element.35.refs_2_, ...), custom_call_target="tpu_custom_call" | custom-call | flops 3774873600 | bytes 1048576 | tf_op jit(solution)/shard_map/pallas_call | solution.py:268
  59.6 2.9 %collective-permute-start.17 = (bf16[320,1152]{1,0:T(8,128)(2,1)S(1)}, bf16[320,1152]{1,0:T(8,128)(2,1)S(1)}, u32[]{:S(2)}, u32[]{:S(2)}) collective-permute-start(bf16[320,1152]{1,0:T(8,128)(2,1)S(1)} %get-tuple-element.40), channel_id=1, source_target_pairs={{0,12},{1,49},{2,14},{3,51},{4,0},{5,53},{6,2},{7,55},{8,4},{9,57}... | collective-permute-start | bytes 2211848 | tf_op jit(solution)/shard_map/ppermute | solution.py:48
  62.4 0.0 collective-permute-start.18
  62.4 2.7 %collective-permute-start.16 = (bf16[320,1152]{1,0:T(8,128)(2,1)S(1)}, bf16[320,1152]{1,0:T(8,128)(2,1)S(1)}, u32[]{:S(2)}, u32[]{:S(2)}) collective-permute-start(bf16[320,1152]{1,0:T(8,128)(2,1)S(1)} %get-tuple-element.37), channel_id=1, source_target_pairs={{0,2},{1,67},{2,0},{3,65},{4,6},{5,71},{6,4},{7,69},{8,10},{9,75},... | collective-permute-start | bytes 2211848 | tf_op jit(solution)/shard_map/ppermute | solution.py:57
  65.2 3.7 %shard_map.64 = (bf16[320,1152]{1,0:T(8,128)(2,1)S(1)}, bf16[320,1152]{1,0:T(8,128)(2,1)S(1)}, bf16[320,1152]{1,0:T(8,128)(2,1)S(1)}) custom-call(s32[1]{0:T(128)} %bitcast.refs_2_.refs_0_, bf16[2,1280,640]{2,1,0:T(8,128)(2,1)S(1)} %collective-permute-done.14.refs_1_, f32[2,480,1152]{2,1,0:T(8,128)S(1)} %get-tuple-element.38.refs_2_, ...), custom_call_target="tpu_custom_call" | custom-call | flops 3019898880 | bytes 1048576 | tf_op jit(solution)/shard_map/pallas_call | solution.py:268
  68.9 2.7 %collective-permute-start.20 = (bf16[320,1152]{1,0:T(8,128)(2,1)S(1)}, bf16[320,1152]{1,0:T(8,128)(2,1)S(1)}, u32[]{:S(2)}, u32[]{:S(2)}) collective-permute-start(bf16[320,1152]{1,0:T(8,128)(2,1)S(1)} %get-tuple-element.42.refs_3_), channel_id=1, source_target_pairs={{0,12},{1,49},{2,14},{3,51},{4,0},{5,53},{6,2},{7,55},{8,4},{9,57}... | collective-permute-start | bytes 2211848 | tf_op jit(solution)/shard_map/ppermute | solution.py:48
  71.6 0.0 collective-permute-start.21
  71.6 2.7 %collective-permute-done.18.refs_2_ = bf16[320,1152]{1,0:T(8,128)(2,1)S(1)} collective-permute-done((bf16[320,1152]{1,0:T(8,128)(2,1)S(1)}, bf16[320,1152]{1,0:T(8,128)(2,1)S(1)}, u32[]{:S(2)}, u32[]{:S(2)}) %collective-permute-start.18) | collective-permute-done | bytes 737312 | tf_op jit(solution)/shard_map/ppermute | solution.py:48
  74.3 0.3 shard_map.65.refs_2_
  74.6 0.2 shard_map.66.refs_7_
  74.8 1.2 %collective-permute-start.19 = (bf16[320,1152]{1,0:T(8,128)(2,1)S(1)}, bf16[320,1152]{1,0:T(8,128)(2,1)S(1)}, u32[]{:S(2)}, u32[]{:S(2)}) collective-permute-start(bf16[320,1152]{1,0:T(8,128)(2,1)S(1)} %shard_map.66.refs_7_), channel_id=1, source_target_pairs={{0,8},{1,33},{2,10},{3,35},{4,12},{5,37},{6,14},{7,39},{8,0},{9,41... | collective-permute-start | bytes 2211848 | tf_op jit(solution)/shard_map/ppermute | solution.py:48
  75.9 2.7 %collective-permute-start.22 = (bf16[320,1152]{1,0:T(8,128)(2,1)S(1)}, bf16[320,1152]{1,0:T(8,128)(2,1)S(1)}, u32[]{:S(2)}, u32[]{:S(2)}) collective-permute-start(bf16[320,1152]{1,0:T(8,128)(2,1)S(1)} %shard_map.65.refs_2_), channel_id=1, source_target_pairs={{0,2},{1,67},{2,0},{3,65},{4,6},{5,71},{6,4},{7,69},{8,10},{9,75},... | collective-permute-start | bytes 2211848 | tf_op jit(solution)/shard_map/ppermute | solution.py:57
  78.6 3.0 %shard_map.67.refs_3_ = f32[320,1152]{1,0:T(8,128)S(1)} custom-call(s32[1]{0:T(128)} %bitcast.refs_2_.refs_0_, bf16[2,1280,640]{2,1,0:T(8,128)(2,1)S(1)} %collective-permute-done.14.refs_1_, bf16[2,1280,512]{2,1,0:T(8,128)(2,1)S(1)} %get-tuple-element.30.refs_12_.refs_1_.refs_2_, bf16[2,1280,128]{2,1,0:T(8,128)(2,1)S(1)} %get-tuple-element.31.refs_2_.refs_3_, ...), custom_call_target="tpu_custom_call" | custom-call | flops 1887436800 | bytes 1048576 | tf_op jit(solution)/shard_map/pallas_call | solution.py:268
  81.6 6.3 %collective-permute-done.20.refs_5_ = bf16[320,1152]{1,0:T(8,128)(2,1)S(1)} collective-permute-done((bf16[320,1152]{1,0:T(8,128)(2,1)S(1)}, bf16[320,1152]{1,0:T(8,128)(2,1)S(1)}, u32[]{:S(2)}, u32[]{:S(2)}) %collective-permute-start.20) | collective-permute-done | bytes 737312 | tf_op jit(solution)/shard_map/ppermute | solution.py:48
  87.9 3.2 %collective-permute-done.21.refs_6_ = bf16[320,1152]{1,0:T(8,128)(2,1)S(1)} collective-permute-done((bf16[320,1152]{1,0:T(8,128)(2,1)S(1)}, bf16[320,1152]{1,0:T(8,128)(2,1)S(1)}, u32[]{:S(2)}, u32[]{:S(2)}) %collective-permute-start.21) | collective-permute-done | bytes 737312 | tf_op jit(solution)/shard_map/ppermute | solution.py:48
  91.1 0.5 shard_map.68.refs_8_
  91.6 0.5 collective-permute-start.23
  92.1 0.5 shard_map.69
  92.6 0.8 collective-permute-done.23
  93.4 0.9 broadcast_select_fusion
  (9 shorter events, 0.0 us)
Async XLA Ops:
  1.8 2.8 %collective-permute-start = (bf16[160,1152]{1,0:T(8,128)(2,1)S(1)}, bf16[160,1152]{1,0:T(8,128)(2,1)S(1)}, u32[]{:S(2)}, u32[]{:S(2)}) collective-permute-start(bf16[160,1152]{1,0:T(8,128)(2,1)S(1)} %get-tuple-element.46), channel_id=1, source_target_pairs={{0,1},{1,0},{2,3},{3,2},{4,5},{5,4},{6,7},{7,6},{8,9},{9,8},{10,11... | collective-permute-start | bytes 1105928 | tf_op jit(solution)/shard_map/ppermute | solution.py:61
  5.0 9.5 %collective-permute-start.1 = (bf16[160,1152]{1,0:T(8,128)(2,1)S(1)}, bf16[160,1152]{1,0:T(8,128)(2,1)S(1)}, u32[]{:S(2)}, u32[]{:S(2)}) collective-permute-start(bf16[160,1152]{1,0:T(8,128)(2,1)S(1)} %get-tuple-element.29), channel_id=1, source_target_pairs={{0,4},{1,17},{2,6},{3,19},{4,8},{5,21},{6,10},{7,23},{8,12},{9,25}... | collective-permute-start | bytes 1105928 | tf_op jit(solution)/shard_map/ppermute | solution.py:48
  6.8 7.8 %collective-permute-start.4 = (bf16[160,1152]{1,0:T(8,128)(2,1)S(1)}, bf16[160,1152]{1,0:T(8,128)(2,1)S(1)}, u32[]{:S(2)}, u32[]{:S(2)}) collective-permute-start(bf16[160,1152]{1,0:T(8,128)(2,1)S(1)} %get-tuple-element.28), channel_id=1, source_target_pairs={{0,12},{1,49},{2,14},{3,51},{4,0},{5,53},{6,2},{7,55},{8,4},{9,57}... | collective-permute-start | bytes 1105928 | tf_op jit(solution)/shard_map/ppermute | solution.py:48
  9.0 11.9 %collective-permute-start.5 = (bf16[320,1152]{1,0:T(8,128)(2,1)S(1)}, bf16[320,1152]{1,0:T(8,128)(2,1)S(1)}, u32[]{:S(2)}, u32[]{:S(2)}) collective-permute-start(bf16[320,1152]{1,0:T(8,128)(2,1)S(1)} %get-tuple-element.25.refs_2_), channel_id=1, source_target_pairs={{0,2},{1,67},{2,0},{3,65},{4,6},{5,71},{6,4},{7,69},{8,10},{9,75},... | collective-permute-start | bytes 2211848 | tf_op jit(solution)/shard_map/ppermute | solution.py:57
  11.8 7.9 %collective-permute-start.2 = (bf16[160,1152]{1,0:T(8,128)(2,1)S(1)}, bf16[160,1152]{1,0:T(8,128)(2,1)S(1)}, u32[]{:S(2)}, u32[]{:S(2)}) collective-permute-start(bf16[160,1152]{1,0:T(8,128)(2,1)S(1)} %get-tuple-element.28), channel_id=1, source_target_pairs={{0,4},{1,17},{2,6},{3,19},{4,8},{5,21},{6,10},{7,23},{8,12},{9,25}... | collective-permute-start | bytes 1105928 | tf_op jit(solution)/shard_map/ppermute | solution.py:48
  11.8 7.9 %collective-permute-start.3 = (bf16[160,1152]{1,0:T(8,128)(2,1)S(1)}, bf16[160,1152]{1,0:T(8,128)(2,1)S(1)}, u32[]{:S(2)}, u32[]{:S(2)}) collective-permute-start(bf16[160,1152]{1,0:T(8,128)(2,1)S(1)} %get-tuple-element.29), channel_id=1, source_target_pairs={{0,12},{1,49},{2,14},{3,51},{4,0},{5,53},{6,2},{7,55},{8,4},{9,57}... | collective-permute-start | bytes 1105928 | tf_op jit(solution)/shard_map/ppermute | solution.py:48
  14.6 9.9 %collective-permute-start.6 = (bf16[160,1152]{1,0:T(8,128)(2,1)S(1)}, bf16[160,1152]{1,0:T(8,128)(2,1)S(1)}, u32[]{:S(2)}, u32[]{:S(2)}) collective-permute-start(bf16[160,1152]{1,0:T(8,128)(2,1)S(1)} %collective-permute-done.1), channel_id=1, source_target_pairs={{0,4},{1,17},{2,6},{3,19},{4,8},{5,21},{6,10},{7,23},{8,12},{9,25}... | collective-permute-start | bytes 1105928 | tf_op jit(solution)/shard_map/ppermute | solution.py:48
  14.6 12.6 %collective-permute-start.7 = (bf16[160,1152]{1,0:T(8,128)(2,1)S(1)}, bf16[160,1152]{1,0:T(8,128)(2,1)S(1)}, u32[]{:S(2)}, u32[]{:S(2)}) collective-permute-start(bf16[160,1152]{1,0:T(8,128)(2,1)S(1)} %collective-permute-done.4), channel_id=1, source_target_pairs={{0,12},{1,49},{2,14},{3,51},{4,0},{5,53},{6,2},{7,55},{8,4},{9,57}... | collective-permute-start | bytes 1105928 | tf_op jit(solution)/shard_map/ppermute | solution.py:48
  20.9 11.6 %collective-permute-start.8 = (bf16[320,1152]{1,0:T(8,128)(2,1)S(1)}, bf16[320,1152]{1,0:T(8,128)(2,1)S(1)}, u32[]{:S(2)}, u32[]{:S(2)}) collective-permute-start(bf16[320,1152]{1,0:T(8,128)(2,1)S(1)} %collective-permute-done.5.refs_5_), channel_id=1, source_target_pairs={{0,4},{1,17},{2,6},{3,19},{4,8},{5,21},{6,10},{7,23},{8,12},{9,25}... | collective-permute-start | bytes 2211848 | tf_op jit(solution)/shard_map/ppermute | solution.py:48
  21.0 15.4 %collective-permute-start.12 = (bf16[1280,1152]{1,0:T(8,128)(2,1)S(1)}, bf16[1280,1152]{1,0:T(8,128)(2,1)S(1)}, u32[]{:S(2)}, u32[]{:S(2)}) collective-permute-start(bf16[1280,1152]{1,0:T(8,128)(2,1)S(1)} %constant_dynamic-update-slice_fusion.8), channel_id=1, source_target_pairs={{0,1},{1,0},{2,3},{3,2},{4,5},{5,4},{6,7},{7,6},{8,9},{9,8},{10,11... | collective-permute-start | bytes 8847368 | tf_op jit(solution)/shard_map/ppermute | solution.py:61
  21.1 11.8 %collective-permute-start.9 = (bf16[320,1152]{1,0:T(8,128)(2,1)S(1)}, bf16[320,1152]{1,0:T(8,128)(2,1)S(1)}, u32[]{:S(2)}, u32[]{:S(2)}) collective-permute-start(bf16[320,1152]{1,0:T(8,128)(2,1)S(1)} %collective-permute-done.5.refs_5_), channel_id=1, source_target_pairs={{0,12},{1,49},{2,14},{3,51},{4,0},{5,53},{6,2},{7,55},{8,4},{9,57}... | collective-permute-start | bytes 2211848 | tf_op jit(solution)/shard_map/ppermute | solution.py:48
  24.5 8.5 %collective-permute-start.10 = (bf16[160,1152]{1,0:T(8,128)(2,1)S(1)}, bf16[160,1152]{1,0:T(8,128)(2,1)S(1)}, u32[]{:S(2)}, u32[]{:S(2)}) collective-permute-start(bf16[160,1152]{1,0:T(8,128)(2,1)S(1)} %collective-permute-done.6), channel_id=1, source_target_pairs={{0,2},{1,67},{2,0},{3,65},{4,6},{5,71},{6,4},{7,69},{8,10},{9,75},... | collective-permute-start | bytes 1105928 | tf_op jit(solution)/shard_map/ppermute | solution.py:57
  27.2 8.8 %collective-permute-start.11 = (bf16[160,1152]{1,0:T(8,128)(2,1)S(1)}, bf16[160,1152]{1,0:T(8,128)(2,1)S(1)}, u32[]{:S(2)}, u32[]{:S(2)}) collective-permute-start(bf16[160,1152]{1,0:T(8,128)(2,1)S(1)} %collective-permute-done.7), channel_id=1, source_target_pairs={{0,2},{1,67},{2,0},{3,65},{4,6},{5,71},{6,4},{7,69},{8,10},{9,75},... | collective-permute-start | bytes 1105928 | tf_op jit(solution)/shard_map/ppermute | solution.py:57
  36.1 5.9 %collective-permute-start.13 = (bf16[1280,1152]{1,0:T(8,128)(2,1)S(1)}, bf16[1280,1152]{1,0:T(8,128)(2,1)S(1)}, u32[]{:S(2)}, u32[]{:S(2)}) collective-permute-start(bf16[1280,1152]{1,0:T(8,128)(2,1)S(1)} %get-tuple-element.48), channel_id=1, source_target_pairs={{0,1},{1,0},{2,3},{3,2},{4,5},{5,4},{6,7},{7,6},{8,9},{9,8},{10,11... | collective-permute-start | bytes 8847368 | tf_op jit(solution)/shard_map/ppermute | solution.py:61
  47.8 7.2 %collective-permute-start.15 = (bf16[2,1280,640]{2,1,0:T(8,128)(2,1)S(1)}, bf16[2,1280,640]{2,1,0:T(8,128)(2,1)S(1)}, u32[]{:S(2)}, u32[]{:S(2)}) collective-permute-start(bf16[2,1280,640]{2,1,0:T(8,128)(2,1)S(1)} %get-tuple-element.32.refs_3_.refs_4_), channel_id=1, source_target_pairs={{0,1},{1,0},{2,3},{3,2},{4,5},{5,4},{6,7},{7,6},{8,9},{9,8},{10,11... | collective-permute-start | bytes 9830408 | tf_op jit(solution)/shard_map/ppermute | solution.py:61
  54.9 10.3 %collective-permute-start.14 = (bf16[2,1280,640]{2,1,0:T(8,128)(2,1)S(1)}, bf16[2,1280,640]{2,1,0:T(8,128)(2,1)S(1)}, u32[]{:S(2)}, u32[]{:S(2)}) collective-permute-start(bf16[2,1280,640]{2,1,0:T(8,128)(2,1)S(1)} %get-tuple-element.34), channel_id=1, source_target_pairs={{0,1},{1,0},{2,3},{3,2},{4,5},{5,4},{6,7},{7,6},{8,9},{9,8},{10,11... | collective-permute-start | bytes 9830408 | tf_op jit(solution)/shard_map/ppermute | solution.py:61
  59.6 12.0 %collective-permute-start.17 = (bf16[320,1152]{1,0:T(8,128)(2,1)S(1)}, bf16[320,1152]{1,0:T(8,128)(2,1)S(1)}, u32[]{:S(2)}, u32[]{:S(2)}) collective-permute-start(bf16[320,1152]{1,0:T(8,128)(2,1)S(1)} %get-tuple-element.40), channel_id=1, source_target_pairs={{0,12},{1,49},{2,14},{3,51},{4,0},{5,53},{6,2},{7,55},{8,4},{9,57}... | collective-permute-start | bytes 2211848 | tf_op jit(solution)/shard_map/ppermute | solution.py:48
  62.4 11.8 %collective-permute-start.18 = (bf16[320,1152]{1,0:T(8,128)(2,1)S(1)}, bf16[320,1152]{1,0:T(8,128)(2,1)S(1)}, u32[]{:S(2)}, u32[]{:S(2)}) collective-permute-start(bf16[320,1152]{1,0:T(8,128)(2,1)S(1)} %get-tuple-element.41), channel_id=1, source_target_pairs={{0,4},{1,17},{2,6},{3,19},{4,8},{5,21},{6,10},{7,23},{8,12},{9,25}... | collective-permute-start | bytes 2211848 | tf_op jit(solution)/shard_map/ppermute | solution.py:48
  62.4 12.1 %collective-permute-start.16 = (bf16[320,1152]{1,0:T(8,128)(2,1)S(1)}, bf16[320,1152]{1,0:T(8,128)(2,1)S(1)}, u32[]{:S(2)}, u32[]{:S(2)}) collective-permute-start(bf16[320,1152]{1,0:T(8,128)(2,1)S(1)} %get-tuple-element.37), channel_id=1, source_target_pairs={{0,2},{1,67},{2,0},{3,65},{4,6},{5,71},{6,4},{7,69},{8,10},{9,75},... | collective-permute-start | bytes 2211848 | tf_op jit(solution)/shard_map/ppermute | solution.py:57
  68.9 19.1 %collective-permute-start.20 = (bf16[320,1152]{1,0:T(8,128)(2,1)S(1)}, bf16[320,1152]{1,0:T(8,128)(2,1)S(1)}, u32[]{:S(2)}, u32[]{:S(2)}) collective-permute-start(bf16[320,1152]{1,0:T(8,128)(2,1)S(1)} %get-tuple-element.42.refs_3_), channel_id=1, source_target_pairs={{0,12},{1,49},{2,14},{3,51},{4,0},{5,53},{6,2},{7,55},{8,4},{9,57}... | collective-permute-start | bytes 2211848 | tf_op jit(solution)/shard_map/ppermute | solution.py:48
  71.6 19.5 %collective-permute-start.21 = (bf16[320,1152]{1,0:T(8,128)(2,1)S(1)}, bf16[320,1152]{1,0:T(8,128)(2,1)S(1)}, u32[]{:S(2)}, u32[]{:S(2)}) collective-permute-start(bf16[320,1152]{1,0:T(8,128)(2,1)S(1)} %get-tuple-element.43), channel_id=1, source_target_pairs={{0,4},{1,17},{2,6},{3,19},{4,8},{5,21},{6,10},{7,23},{8,12},{9,25}... | collective-permute-start | bytes 2211848 | tf_op jit(solution)/shard_map/ppermute | solution.py:48
  74.8 16.4 %collective-permute-start.19 = (bf16[320,1152]{1,0:T(8,128)(2,1)S(1)}, bf16[320,1152]{1,0:T(8,128)(2,1)S(1)}, u32[]{:S(2)}, u32[]{:S(2)}) collective-permute-start(bf16[320,1152]{1,0:T(8,128)(2,1)S(1)} %shard_map.66.refs_7_), channel_id=1, source_target_pairs={{0,8},{1,33},{2,10},{3,35},{4,12},{5,37},{6,14},{7,39},{8,0},{9,41... | collective-permute-start | bytes 2211848 | tf_op jit(solution)/shard_map/ppermute | solution.py:48
  75.9 15.2 %collective-permute-start.22 = (bf16[320,1152]{1,0:T(8,128)(2,1)S(1)}, bf16[320,1152]{1,0:T(8,128)(2,1)S(1)}, u32[]{:S(2)}, u32[]{:S(2)}) collective-permute-start(bf16[320,1152]{1,0:T(8,128)(2,1)S(1)} %shard_map.65.refs_2_), channel_id=1, source_target_pairs={{0,2},{1,67},{2,0},{3,65},{4,6},{5,71},{6,4},{7,69},{8,10},{9,75},... | collective-permute-start | bytes 2211848 | tf_op jit(solution)/shard_map/ppermute | solution.py:57
  91.6 1.8 %collective-permute-start.23 = (bf16[160,1152]{1,0:T(8,128)(2,1)S(1)}, bf16[160,1152]{1,0:T(8,128)(2,1)S(1)}, u32[]{:S(2)}, u32[]{:S(2)}) collective-permute-start(bf16[160,1152]{1,0:T(8,128)(2,1)S(1)} %shard_map.68.refs_8_), channel_id=1, source_target_pairs={{0,1},{1,0},{2,3},{3,2},{4,5},{5,4},{6,7},{7,6},{8,9},{9,8},{10,11... | collective-permute-start | bytes 1105928 | tf_op jit(solution)/shard_map/ppermute | solution.py:61

commit v14 on v13

--- a/solution.py
+++ b/solution.py
@@ -169,7 +169,7 @@
     mine, other = places_of(refs[: pieces[0]]), places_of(refs[pieces[0] : sum(pieces)])
     edge_ref, far_ref = refs[sum(pieces) :]
     edge = edge_ref.shape[2]
-    first = 4 * rows - edge
+    first = 8 * rows - edge - far_ref.shape[2]
     for half in range(2):
         mine_rows = stacked(mine, half * rows)
         other_rows = stacked(other, opposite_rows(core_ref[0], half))
@@ -178,9 +178,8 @@
             weights = weights_of(
                 factors_ref, mine_rows, other_rows[start : start + size]
             )
-            if begin == 0:
-                edge_ref[half] = weights[:, :edge]
-                far_ref[half, :, pl.ds(0, size - edge)] = weights[:, edge:]
+            if begin < edge:
+                edge_ref[half, :, pl.ds(begin, size)] = weights
             else:
                 far_ref[half, :, pl.ds(begin - edge, size)] = weights
 
@@ -194,15 +193,14 @@
 
 def own_kernel(pieces, core_ref, *refs):
     weights_refs, begun_ref, other = refs[:3], refs[3], places_of(refs[4 : 4 + pieces])
-    near_ref, far_ref, joined_ref = refs[4 + pieces :]
+    near_ref, far_ref, low_ref, high_ref = refs[4 + pieces :]
     count = weights_refs[0].shape[2]
-    edge = 4 * rows - weights_refs[1].shape[2]
+    low_ref[...] = weights_refs[0][...]
+    high_ref[...] = weights_refs[1][...]
     for half in range(2):
         other_rows = stacked(other, opposite_rows(core_ref[0], half))
-        joined_ref[half, :, pl.ds(0, edge)] = weights_refs[0][half]
-        joined_ref[half, :, pl.ds(edge, 4 * rows - edge)] = weights_refs[1][half]
-        far_ref[half] = begun_ref[half] + own_product(
-            half, 4 * rows, 4 * rows, weights_refs[1:], other_rows[count:]
+        far_ref[half] = begun_ref[half, pl.ds(rows, 3 * rows), :] + own_product(
+            half, 5 * rows, 3 * rows, weights_refs[1:], other_rows[count:]
         )
         near_ref[half] = own_product(half, rows, 3 * rows, weights_refs, other_rows)
 
@@ -217,21 +215,40 @@
 
 
 def far_kernel(pieces, core_ref, weights_ref, part_ref, *refs):
-    other, sums = places_of(refs[:pieces]), places_of(refs[pieces:])
-    for half in range(2):
-        columns = [(weights_ref, 0, 4 * rows)]
-        total = part_ref[half] + received(core_ref[0], half, columns, other)
-        store_chips(sums, half * rows, 0, total)
-
-
-def near_kernel(pieces, core_ref, weights_ref, part_ref, *refs):
+    other, sums = places_of(refs[:pieces]), places_of(refs[pieces:-1])
+    tail_ref = refs[-1]
+    tail = tail_ref.shape[1]
+    for half in range(2):
+        columns = [(weights_ref, 0, weights_ref.shape[2])]
+        total = received(core_ref[0], half, columns, other)
+        tail_ref[half] = total[:tail]
+        store_chips(sums, half * rows, 0, total[tail:] + part_ref[half])
+
+
+def near_kernel(pieces, core_ref, low_ref, high_ref, part_ref, *refs):
     other, sums = places_of(refs[:pieces]), places_of(refs[pieces:])
     first = rows // 128 * 128
-    columns = [(weights_ref, first, 4 * rows - first)]
+    count = low_ref.shape[2]
+    columns = [(low_ref, first, count - first), (high_ref, 0, 4 * rows - count)]
+    for half in range(2):
+        total = received(core_ref[0], half, columns, other)[rows - first :]
+        store_chips(sums, half * rows, 0, total + part_ref[half])
+
+
+def distant_kernel(pieces, core_ref, high_ref, tail_ref, begun_ref, *refs):
+    weights_refs, other = refs[:2], places_of(refs[2 : 2 + pieces])
+    sums = places_of(refs[2 + pieces :])
+    size = rows - tail_ref.shape[1]
+    columns = [(high_ref, high_ref.shape[2] - size, size)]
+    count = sum(ref.shape[2] for ref in weights_refs)
     for half in range(2):
         total = received(core_ref[0], half, columns, other)
-        total = total[rows - first :] + part_ref[half]
-        store_chips(sums, half * rows, 0, total)
+        total = jnp.concatenate([total, tail_ref[half]], axis=0)
+        other_rows = stacked(other, opposite_rows(core_ref[0], half))
+        own = begun_ref[half, pl.ds(0, rows), :] + own_product(
+            half, 4 * rows, rows, weights_refs, other_rows[8 * rows - count :]
+        )
+        store_chips(sums, half * rows, 0, total + own)
 
 
 def self_kernel(pieces, core_ref, received_ref, *refs):
@@ -362,7 +379,7 @@
     )
     edge_weights, far_weights = call(
         functools.partial(far_weights_kernel, (len(mine), len(other))),
-        [(2, all_rows, edge), (2, all_rows, near_rows)],
+        [(2, all_rows, chunk), (2, all_rows, 2 * chunk)],
         (cores,),
         (factors, *mine, *other),
         12 * share,
@@ -370,32 +387,42 @@
     )
     far_received = swap(far_weights)
     weights = (near_weights, edge_weights, far_weights)
-    near_part, far_part, near_joined = call(
+    near_part, far_part, near_copy, edge_copy = call(
         functools.partial(own_kernel, len(other)),
-        [(2, 3 * rows, width), (2, 4 * rows, width), (2, all_rows, near_rows)],
+        [(2, 3 * rows, width)] * 2
+        + [(2, all_rows, 2 * chunk), (2, all_rows, chunk)],
         (cores,),
         (*weights, far_begun, *other),
         14 * share,
-        kinds=(jnp.float32, jnp.float32, jnp.bfloat16),
-    )
-    near_received = swap(near_joined)
-    far_sums = call(
+        kinds=(jnp.float32,) * 2 + (jnp.bfloat16,) * 2,
+    )
+    near_received, edge_received = swap(near_copy), swap(edge_copy)
+    *far_sums, tail = call(
         functools.partial(far_kernel, len(other)),
-        [block] * 4,
+        [block] * 3 + [(2, 5 * rows - 3 * chunk, width)],
         (cores,),
         (far_received, far_part, *other),
         10 * share,
-    )
-    arrived = [ring(far_sums[1], -1), ring(far_sums[2], 1), pair(far_sums[3])]
+        kinds=[jnp.bfloat16] * 3 + [jnp.float32],
+    )
+    arrived = [ring(far_sums[0], -1), ring(far_sums[1], 1), pair(far_sums[2])]
     near_sums = call(
         functools.partial(near_kernel, len(other)),
         [block] * 3,
         (cores,),
-        (near_received, near_part, *other),
+        (near_received, edge_received, near_part, *other),
         8 * share,
     )
     (across_total,) = add([(near_sums[2], arrived[0], arrived[1])], (near_sums[0],))
-    (distant_total,) = add([(far_sums[0], arrived[2])], (across_total,))
+    (distant_sum,) = call(
+        functools.partial(distant_kernel, len(other)),
+        [block],
+        (cores,),
+        (edge_received, tail, far_begun, edge_weights, far_weights, *other),
+        4 * share,
+        (across_total,),
+    )
+    (distant_total,) = add([(distant_sum, arrived[2])])
     (own_sum,) = call(
         functools.partial(self_kernel, len(other)),
         [block],

time: 94.5 us -> 92.9 us (0.983)
    ppermute x13, starting transfers between devices: 19.6 us -> 18.1 us  [ring(): return lax.ppermute(value, axes, ring_move(steps))]
    ppermute x6 -> x7, starting transfers between devices: 3.23 us -> 3.74 us  [swap(): return lax.ppermute(value, 'core', [(0, 1), (1, 0)])]
    pallas_call x11 -> x12, Pallas kernels: 30.7 us -> 30.6 us  [call(): pl.pallas_call(body, in_specs=[pl.BlockSpec(memory_space=pltpu.SMEM)] * l...]
  transfers between devices with their start and end apart: 24 -> 25, of which waited for: 9 -> 9; matrix products, arithmetic and copies ran while one was open for 1% -> 1% of each run, Pallas kernels for 25% -> 26%
where the time goes in v14:
time: 92.9 us; the launch traced here: 92.7 us
  starting transfers between devices  33 us (36%)
  Pallas kernels  30.6 us (33%)
  waiting for transfers between devices  23.9 us (26%)
  between operations  2.14 us (2%)
  other arithmetic  2.13 us (2%)
    pallas_call x12, Pallas kernels, call(): pl.pallas_call(body, in_specs=[pl.BlockSpec(memory_space=pltpu.SMEM)] * l...  30.6 us
    ppermute x13, waiting for transfers between devices, ring(): return lax.ppermute(value, axes, ring_move(steps))  19 us
    ppermute x13, starting transfers between devices, ring(): return lax.ppermute(value, axes, ring_move(steps))  18.1 us
    ppermute x5, starting transfers between devices, pair(): return lax.ppermute(value, axes, pairs_of(move))  11.1 us
    ppermute x5, waiting for transfers between devices, pair(): return lax.ppermute(value, axes, pairs_of(move))  4.04 us
    ppermute x7, starting transfers between devices, swap(): return lax.ppermute(value, 'core', [(0, 1), (1, 0)])  3.74 us
  transfers between devices with their start and end apart: 25, of which 9 were waited for; matrix products, arithmetic and copies ran while one was open for 1% of the time, Pallas kernels for 26%

profile of v14, /device:TPU:1, one launch (start us, length us, event | category | flops | bytes accessed | tf_op | source)
XLA Modules:
  0.0 92.7 jit_solution(17471547463407763963)
XLA Ops:
  0.6 1.2 %broadcast_select_fusion.2 = (bf16[160,1152]{1,0:T(8,128)(2,1)S(1)}, bf16[160,1152]{1,0:T(8,128)(2,1)S(1)}) fusion(bf16[160,1152]{1,0:T(8,128)(2,1)} %param.5, bf16[160,1152]{1,0:T(8,128)(2,1)} %param.4, pred[]{:T(512)S(6)} %eq.3), kind=kLoop, calls=%fused_computation.2 | loop fusion | flops 368640 | bytes 1474561 | tf_op jit(solution)/shard_map/jit(_where)/select_n | solution.py:340
  1.8 1.5 %collective-permute-start = (bf16[160,1152]{1,0:T(8,128)(2,1)S(1)}, bf16[160,1152]{1,0:T(8,128)(2,1)S(1)}, u32[]{:S(2)}, u32[]{:S(2)}) collective-permute-start(bf16[160,1152]{1,0:T(8,128)(2,1)S(1)} %get-tuple-element.48), channel_id=1, source_target_pairs={{0,1},{1,0},{2,3},{3,2},{4,5},{5,4},{6,7},{7,6},{8,9},{9,8},{10,11... | collective-permute-start | bytes 1105928 | tf_op jit(solution)/shard_map/ppermute | solution.py:61
  4.6 0.0 collective-permute-done.refs_4_
  4.6 0.4 shard_map.59
  5.0 1.8 %collective-permute-start.1 = (bf16[160,1152]{1,0:T(8,128)(2,1)S(1)}, bf16[160,1152]{1,0:T(8,128)(2,1)S(1)}, u32[]{:S(2)}, u32[]{:S(2)}) collective-permute-start(bf16[160,1152]{1,0:T(8,128)(2,1)S(1)} %get-tuple-element.30), channel_id=1, source_target_pairs={{0,4},{1,17},{2,6},{3,19},{4,8},{5,21},{6,10},{7,23},{8,12},{9,25}... | collective-permute-start | bytes 1105928 | tf_op jit(solution)/shard_map/ppermute | solution.py:48
  6.8 2.2 %collective-permute-start.4 = (bf16[160,1152]{1,0:T(8,128)(2,1)S(1)}, bf16[160,1152]{1,0:T(8,128)(2,1)S(1)}, u32[]{:S(2)}, u32[]{:S(2)}) collective-permute-start(bf16[160,1152]{1,0:T(8,128)(2,1)S(1)} %get-tuple-element.29), channel_id=1, source_target_pairs={{0,12},{1,49},{2,14},{3,51},{4,0},{5,53},{6,2},{7,55},{8,4},{9,57}... | collective-permute-start | bytes 1105928 | tf_op jit(solution)/shard_map/ppermute | solution.py:48
  9.0 2.7 %collective-permute-start.5 = (bf16[320,1152]{1,0:T(8,128)(2,1)S(1)}, bf16[320,1152]{1,0:T(8,128)(2,1)S(1)}, u32[]{:S(2)}, u32[]{:S(2)}) collective-permute-start(bf16[320,1152]{1,0:T(8,128)(2,1)S(1)} %get-tuple-element.26.refs_2_), channel_id=1, source_target_pairs={{0,2},{1,67},{2,0},{3,65},{4,6},{5,71},{6,4},{7,69},{8,10},{9,75},... | collective-permute-start | bytes 2211848 | tf_op jit(solution)/shard_map/ppermute | solution.py:57
  11.8 0.0 collective-permute-start.2
  11.8 0.1 constant_dynamic-update-slice_fusion.13
  11.8 2.7 %collective-permute-start.3 = (bf16[160,1152]{1,0:T(8,128)(2,1)S(1)}, bf16[160,1152]{1,0:T(8,128)(2,1)S(1)}, u32[]{:S(2)}, u32[]{:S(2)}) collective-permute-start(bf16[160,1152]{1,0:T(8,128)(2,1)S(1)} %get-tuple-element.30), channel_id=1, source_target_pairs={{0,12},{1,49},{2,14},{3,51},{4,0},{5,53},{6,2},{7,55},{8,4},{9,57}... | collective-permute-start | bytes 1105928 | tf_op jit(solution)/shard_map/ppermute | solution.py:48
  14.6 2.7 %collective-permute-start.7 = (bf16[160,1152]{1,0:T(8,128)(2,1)S(1)}, bf16[160,1152]{1,0:T(8,128)(2,1)S(1)}, u32[]{:S(2)}, u32[]{:S(2)}) collective-permute-start(bf16[160,1152]{1,0:T(8,128)(2,1)S(1)} %collective-permute-done.4), channel_id=1, source_target_pairs={{0,12},{1,49},{2,14},{3,51},{4,0},{5,53},{6,2},{7,55},{8,4},{9,57}... | collective-permute-start | bytes 1105928 | tf_op jit(solution)/shard_map/ppermute | solution.py:48
  17.2 0.1 constant_dynamic-update-slice_fusion.12
  17.3 2.3 %collective-permute-done.2 = bf16[160,1152]{1,0:T(8,128)(2,1)S(1)} collective-permute-done((bf16[160,1152]{1,0:T(8,128)(2,1)S(1)}, bf16[160,1152]{1,0:T(8,128)(2,1)S(1)}, u32[]{:S(2)}, u32[]{:S(2)}) %collective-permute-start.2) | collective-permute-done | bytes 368672 | tf_op jit(solution)/shard_map/ppermute | solution.py:48
  19.6 0.1 constant_dynamic-update-slice_fusion.11
  19.7 0.0 collective-permute-done.3
  19.7 0.1 constant_dynamic-update-slice_fusion.10
  19.8 0.1 constant_dynamic-update-slice_fusion.9
  19.9 1.0 %collective-permute-done.5.refs_5_ = bf16[320,1152]{1,0:T(8,128)(2,1)S(1)} collective-permute-done((bf16[320,1152]{1,0:T(8,128)(2,1)S(1)}, bf16[320,1152]{1,0:T(8,128)(2,1)S(1)}, u32[]{:S(2)}, u32[]{:S(2)}) %collective-permute-start.5) | collective-permute-done | bytes 737312 | tf_op jit(solution)/shard_map/ppermute | solution.py:57
  20.9 0.0 collective-permute-start.8
  20.9 0.1 constant_dynamic-update-slice_fusion.8
  21.0 0.1 collective-permute-start.12
  21.1 3.4 %collective-permute-start.9 = (bf16[320,1152]{1,0:T(8,128)(2,1)S(1)}, bf16[320,1152]{1,0:T(8,128)(2,1)S(1)}, u32[]{:S(2)}, u32[]{:S(2)}) collective-permute-start(bf16[320,1152]{1,0:T(8,128)(2,1)S(1)} %collective-permute-done.5.refs_5_), channel_id=1, source_target_pairs={{0,12},{1,49},{2,14},{3,51},{4,0},{5,53},{6,2},{7,55},{8,4},{9,57}... | collective-permute-start | bytes 2211848 | tf_op jit(solution)/shard_map/ppermute | solution.py:48
  24.5 0.0 collective-permute-done.6
  24.5 2.7 %collective-permute-start.10 = (bf16[160,1152]{1,0:T(8,128)(2,1)S(1)}, bf16[160,1152]{1,0:T(8,128)(2,1)S(1)}, u32[]{:S(2)}, u32[]{:S(2)}) collective-permute-start(bf16[160,1152]{1,0:T(8,128)(2,1)S(1)} %collective-permute-done.6), channel_id=1, source_target_pairs={{0,2},{1,67},{2,0},{3,65},{4,6},{5,71},{6,4},{7,69},{8,10},{9,75},... | collective-permute-start | bytes 1105928 | tf_op jit(solution)/shard_map/ppermute | solution.py:57
  27.2 0.1 collective-permute-start.11
  27.3 0.1 constant_dynamic-update-slice_fusion.19
  27.4 0.1 constant_dynamic-update-slice_fusion.18
  27.4 5.0 %collective-permute-done.8.refs_7_ = bf16[320,1152]{1,0:T(8,128)(2,1)S(1)} collective-permute-done((bf16[320,1152]{1,0:T(8,128)(2,1)S(1)}, bf16[320,1152]{1,0:T(8,128)(2,1)S(1)}, u32[]{:S(2)}, u32[]{:S(2)}) %collective-permute-start.8) | collective-permute-done | bytes 737312 | tf_op jit(solution)/shard_map/ppermute | solution.py:48
  32.5 0.1 constant_dynamic-update-slice_fusion.17
  32.6 0.3 collective-permute-done.9.refs_8_
  32.9 0.1 constant_dynamic-update-slice_fusion.16
  33.0 0.1 constant_dynamic-update-slice_fusion.15
  33.1 3.0 %collective-permute-done.11 = bf16[160,1152]{1,0:T(8,128)(2,1)S(1)} collective-permute-done((bf16[160,1152]{1,0:T(8,128)(2,1)S(1)}, bf16[160,1152]{1,0:T(8,128)(2,1)S(1)}, u32[]{:S(2)}, u32[]{:S(2)}) %collective-permute-start.11) | collective-permute-done | bytes 368672 | tf_op jit(solution)/shard_map/ppermute | solution.py:57
  36.1 0.1 constant_dynamic-update-slice_fusion.14
  36.1 0.3 collective-permute-start.13
  36.4 5.6 %shard_map.60 = (bf16[2,1280,512]{2,1,0:T(8,128)(2,1)S(1)}, f32[2,640,1152]{2,1,0:T(8,128)S(1)}) custom-call(s32[1]{0:T(128)} %bitcast.refs_2_.refs_0_, f32[8,128]{1,0:T(8,128)S(1)} %get-tuple-element.24.refs_1_, bf16[320,1152]{1,0:T(8,128)(2,1)S(1)} %get-tuple-element.26.refs_2_, bf16[320,1152]{1,0:T(8,128)(2,1)S(1)} %get-tuple-element.63.refs_3_, ...), custom_call_target="tpu_custom_call" | custom-call | flops 4529848320 | bytes 1048576 | tf_op jit(solution)/shard_map/pallas_call | solution.py:285
  42.0 0.0 collective-permute-done.13.refs_11_.refs_6_.refs_4_.refs_5_.refs_7_
  42.0 5.7 %shard_map.61 = (bf16[2,1280,256]{2,1,0:T(8,128)(2,1)S(1)}, bf16[2,1280,512]{2,1,0:T(8,128)(2,1)S(1)}) custom-call(s32[1]{0:T(128)} %bitcast.refs_2_.refs_0_, f32[8,128]{1,0:T(8,128)S(1)} %get-tuple-element.24.refs_1_, bf16[320,1152]{1,0:T(8,128)(2,1)S(1)} %get-tuple-element.26.refs_2_, bf16[320,1152]{1,0:T(8,128)(2,1)S(1)} %get-tuple-element.63.refs_3_, ...), custom_call_target="tpu_custom_call" | custom-call | flops 4529848320 | bytes 1048576 | tf_op jit(solution)/shard_map/pallas_call | solution.py:285
  47.7 0.8 collective-permute-start.16
  48.5 5.5 %shard_map.62 = (f32[2,480,1152]{2,1,0:T(8,128)S(1)}, f32[2,480,1152]{2,1,0:T(8,128)S(1)}, bf16[2,1280,512]{2,1,0:T(8,128)(2,1)S(1)}, bf16[2,1280,256]{2,1,0:T(8,128)(2,1)S(1)}) custom-call(s32[1]{0:T(128)} %bitcast.refs_2_.refs_0_, bf16[2,1280,512]{2,1,0:T(8,128)(2,1)S(1)} %get-tuple-element.31.refs_12_.refs_1_.refs_2_, ...), custom_call_target="tpu_custom_call" | custom-call | flops 5284823040 | bytes 1048576 | tf_op jit(solution)/shard_map/pallas_call | solution.py:285
  54.1 0.1 collective-permute-start.14
  54.2 0.5 collective-permute-start.15
  54.7 0.0 collective-permute-done.16.refs_1_
  54.7 3.7 %shard_map.63 = (bf16[320,1152]{1,0:T(8,128)(2,1)S(1)}, bf16[320,1152]{1,0:T(8,128)(2,1)S(1)}, bf16[320,1152]{1,0:T(8,128)(2,1)S(1)}, f32[2,32,1152]{2,1,0:T(8,128)S(1)}) custom-call(s32[1]{0:T(128)} %bitcast.refs_2_.refs_0_, bf16[2,1280,512]{2,1,0:T(8,128)(2,1)S(1)} %collective-permute-done.16.refs_1_, f32[2,480,1152]{2,1,0:T(8,128)S(1)} %get-tuple-element.37.refs_2_, ...), custom_call_target="tpu_custom_call" | custom-call | flops 3774873600 | bytes 1048576 | tf_op jit(solution)/shard_map/pallas_call | solution.py:285
  58.3 2.5 %collective-permute-start.17 = (bf16[320,1152]{1,0:T(8,128)(2,1)S(1)}, bf16[320,1152]{1,0:T(8,128)(2,1)S(1)}, u32[]{:S(2)}, u32[]{:S(2)}) collective-permute-start(bf16[320,1152]{1,0:T(8,128)(2,1)S(1)} %get-tuple-element.41), channel_id=1, source_target_pairs={{0,12},{1,49},{2,14},{3,51},{4,0},{5,53},{6,2},{7,55},{8,4},{9,57}... | collective-permute-start | bytes 2211848 | tf_op jit(solution)/shard_map/ppermute | solution.py:48
  60.8 0.0 collective-permute-start.18
  60.8 2.7 %collective-permute-start.19 = (bf16[320,1152]{1,0:T(8,128)(2,1)S(1)}, bf16[320,1152]{1,0:T(8,128)(2,1)S(1)}, u32[]{:S(2)}, u32[]{:S(2)}) collective-permute-start(bf16[320,1152]{1,0:T(8,128)(2,1)S(1)} %get-tuple-element.44), channel_id=1, source_target_pairs={{0,2},{1,67},{2,0},{3,65},{4,6},{5,71},{6,4},{7,69},{8,10},{9,75},... | collective-permute-start | bytes 2211848 | tf_op jit(solution)/shard_map/ppermute | solution.py:57
  63.6 3.7 %shard_map.64 = (bf16[320,1152]{1,0:T(8,128)(2,1)S(1)}, bf16[320,1152]{1,0:T(8,128)(2,1)S(1)}, bf16[320,1152]{1,0:T(8,128)(2,1)S(1)}) custom-call(s32[1]{0:T(128)} %bitcast.refs_2_.refs_0_, bf16[2,1280,512]{2,1,0:T(8,128)(2,1)S(1)} %collective-permute-done.14.refs_1_, bf16[2,1280,256]{2,1,0:T(8,128)(2,1)S(1)} %collective-permute-done.15.refs_2_.refs_1_, ...), custom_call_target="tpu_custom_call" | custom-call | flops 3019898880 | bytes 1048576 | tf_op jit(solution)/shard_map/pallas_call | solution.py:285
  67.3 2.7 %collective-permute-start.21 = (bf16[320,1152]{1,0:T(8,128)(2,1)S(1)}, bf16[320,1152]{1,0:T(8,128)(2,1)S(1)}, u32[]{:S(2)}, u32[]{:S(2)}) collective-permute-start(bf16[320,1152]{1,0:T(8,128)(2,1)S(1)} %get-tuple-element.43.refs_3_), channel_id=1, source_target_pairs={{0,12},{1,49},{2,14},{3,51},{4,0},{5,53},{6,2},{7,55},{8,4},{9,57}... | collective-permute-start | bytes 2211848 | tf_op jit(solution)/shard_map/ppermute | solution.py:48
  70.0 0.0 collective-permute-start.22
  70.0 2.7 %collective-permute-done.18.refs_2_ = bf16[320,1152]{1,0:T(8,128)(2,1)S(1)} collective-permute-done((bf16[320,1152]{1,0:T(8,128)(2,1)S(1)}, bf16[320,1152]{1,0:T(8,128)(2,1)S(1)}, u32[]{:S(2)}, u32[]{:S(2)}) %collective-permute-start.18) | collective-permute-done | bytes 737312 | tf_op jit(solution)/shard_map/ppermute | solution.py:48
  72.7 0.3 shard_map.65.refs_8_
  72.9 1.8 %shard_map.66.refs_0_ = bf16[320,1152]{1,0:T(8,128)(2,1)S(1)} custom-call(s32[1]{0:T(128)} %bitcast.refs_2_.refs_0_, bf16[2,1280,256]{2,1,0:T(8,128)(2,1)S(1)} %collective-permute-done.15.refs_2_.refs_1_, f32[2,32,1152]{2,1,0:T(8,128)S(1)} %get-tuple-element.38.refs_2_, f32[2,640,1152]{2,1,0:T(8,128)S(1)} %get-tuple-element.34.refs_4_.refs_3_, ...), custom_call_target="tpu_custom_call" | custom-call | flops 1509949440 | bytes 1048576 | tf_op jit(solution)/shard_map/pallas_call | solution.py:285
  74.7 0.2 shard_map.67.refs_7_
  74.9 0.1 collective-permute-start.20
  75.0 2.8 %collective-permute-start.23 = (bf16[320,1152]{1,0:T(8,128)(2,1)S(1)}, bf16[320,1152]{1,0:T(8,128)(2,1)S(1)}, u32[]{:S(2)}, u32[]{:S(2)}) collective-permute-start(bf16[320,1152]{1,0:T(8,128)(2,1)S(1)} %shard_map.65.refs_8_), channel_id=1, source_target_pairs={{0,2},{1,67},{2,0},{3,65},{4,6},{5,71},{6,4},{7,69},{8,10},{9,75},... | collective-permute-start | bytes 2211848 | tf_op jit(solution)/shard_map/ppermute | solution.py:57
  77.8 3.0 %shard_map.68.refs_3_ = f32[320,1152]{1,0:T(8,128)S(1)} custom-call(s32[1]{0:T(128)} %bitcast.refs_2_.refs_0_, bf16[2,1280,512]{2,1,0:T(8,128)(2,1)S(1)} %collective-permute-done.14.refs_1_, bf16[2,1280,512]{2,1,0:T(8,128)(2,1)S(1)} %get-tuple-element.31.refs_12_.refs_1_.refs_2_, bf16[2,1280,256]{2,1,0:T(8,128)(2,1)S(1)} %get-tuple-element.32.refs_2_.refs_4_.refs_3_, ...), custom_call_target="tpu_custom_call" | custom-call | flops 1887436800 | bytes 1048576 | tf_op jit(solution)/shard_map/pallas_call | solution.py:285
  80.8 5.5 %collective-permute-done.21.refs_5_ = bf16[320,1152]{1,0:T(8,128)(2,1)S(1)} collective-permute-done((bf16[320,1152]{1,0:T(8,128)(2,1)S(1)}, bf16[320,1152]{1,0:T(8,128)(2,1)S(1)}, u32[]{:S(2)}, u32[]{:S(2)}) %collective-permute-start.21) | collective-permute-done | bytes 737312 | tf_op jit(solution)/shard_map/ppermute | solution.py:48
  86.3 3.2 %collective-permute-done.22.refs_6_ = bf16[320,1152]{1,0:T(8,128)(2,1)S(1)} collective-permute-done((bf16[320,1152]{1,0:T(8,128)(2,1)S(1)}, bf16[320,1152]{1,0:T(8,128)(2,1)S(1)}, u32[]{:S(2)}, u32[]{:S(2)}) %collective-permute-start.22) | collective-permute-done | bytes 737312 | tf_op jit(solution)/shard_map/ppermute | solution.py:48
  89.5 0.5 shard_map.69.refs_8_
  90.0 0.5 collective-permute-start.24
  90.5 0.5 shard_map.70
  90.9 0.8 collective-permute-done.24
  91.8 1.0 %broadcast_select_fusion = (bf16[160,1152]{1,0:T(8,128)(2,1)}, bf16[160,1152]{1,0:T(8,128)(2,1)}) fusion(bf16[160,1152]{1,0:T(8,128)(2,1)S(1)} %collective-permute-done.24, bf16[160,1152]{1,0:T(8,128)(2,1)S(1)} %shard_map.70, pred[]{:T(512)S(6)} %eq.3), kind=kLoop, calls=%fused_computation | loop fusion | flops 368640 | bytes 1474561 | tf_op jit(solution)/shard_map/jit(_where)/select_n | solution.py:457
  (12 shorter events, 0.0 us)
Async XLA Ops:
  1.8 2.8 %collective-permute-start = (bf16[160,1152]{1,0:T(8,128)(2,1)S(1)}, bf16[160,1152]{1,0:T(8,128)(2,1)S(1)}, u32[]{:S(2)}, u32[]{:S(2)}) collective-permute-start(bf16[160,1152]{1,0:T(8,128)(2,1)S(1)} %get-tuple-element.48), channel_id=1, source_target_pairs={{0,1},{1,0},{2,3},{3,2},{4,5},{5,4},{6,7},{7,6},{8,9},{9,8},{10,11... | collective-permute-start | bytes 1105928 | tf_op jit(solution)/shard_map/ppermute | solution.py:61
  5.0 9.5 %collective-permute-start.1 = (bf16[160,1152]{1,0:T(8,128)(2,1)S(1)}, bf16[160,1152]{1,0:T(8,128)(2,1)S(1)}, u32[]{:S(2)}, u32[]{:S(2)}) collective-permute-start(bf16[160,1152]{1,0:T(8,128)(2,1)S(1)} %get-tuple-element.30), channel_id=1, source_target_pairs={{0,4},{1,17},{2,6},{3,19},{4,8},{5,21},{6,10},{7,23},{8,12},{9,25}... | collective-permute-start | bytes 1105928 | tf_op jit(solution)/shard_map/ppermute | solution.py:48
  6.8 7.8 %collective-permute-start.4 = (bf16[160,1152]{1,0:T(8,128)(2,1)S(1)}, bf16[160,1152]{1,0:T(8,128)(2,1)S(1)}, u32[]{:S(2)}, u32[]{:S(2)}) collective-permute-start(bf16[160,1152]{1,0:T(8,128)(2,1)S(1)} %get-tuple-element.29), channel_id=1, source_target_pairs={{0,12},{1,49},{2,14},{3,51},{4,0},{5,53},{6,2},{7,55},{8,4},{9,57}... | collective-permute-start | bytes 1105928 | tf_op jit(solution)/shard_map/ppermute | solution.py:48
  9.0 11.9 %collective-permute-start.5 = (bf16[320,1152]{1,0:T(8,128)(2,1)S(1)}, bf16[320,1152]{1,0:T(8,128)(2,1)S(1)}, u32[]{:S(2)}, u32[]{:S(2)}) collective-permute-start(bf16[320,1152]{1,0:T(8,128)(2,1)S(1)} %get-tuple-element.26.refs_2_), channel_id=1, source_target_pairs={{0,2},{1,67},{2,0},{3,65},{4,6},{5,71},{6,4},{7,69},{8,10},{9,75},... | collective-permute-start | bytes 2211848 | tf_op jit(solution)/shard_map/ppermute | solution.py:57
  11.8 7.9 %collective-permute-start.2 = (bf16[160,1152]{1,0:T(8,128)(2,1)S(1)}, bf16[160,1152]{1,0:T(8,128)(2,1)S(1)}, u32[]{:S(2)}, u32[]{:S(2)}) collective-permute-start(bf16[160,1152]{1,0:T(8,128)(2,1)S(1)} %get-tuple-element.29), channel_id=1, source_target_pairs={{0,4},{1,17},{2,6},{3,19},{4,8},{5,21},{6,10},{7,23},{8,12},{9,25}... | collective-permute-start | bytes 1105928 | tf_op jit(solution)/shard_map/ppermute | solution.py:48
  11.8 7.9 %collective-permute-start.3 = (bf16[160,1152]{1,0:T(8,128)(2,1)S(1)}, bf16[160,1152]{1,0:T(8,128)(2,1)S(1)}, u32[]{:S(2)}, u32[]{:S(2)}) collective-permute-start(bf16[160,1152]{1,0:T(8,128)(2,1)S(1)} %get-tuple-element.30), channel_id=1, source_target_pairs={{0,12},{1,49},{2,14},{3,51},{4,0},{5,53},{6,2},{7,55},{8,4},{9,57}... | collective-permute-start | bytes 1105928 | tf_op jit(solution)/shard_map/ppermute | solution.py:48
  14.6 9.9 %collective-permute-start.6 = (bf16[160,1152]{1,0:T(8,128)(2,1)S(1)}, bf16[160,1152]{1,0:T(8,128)(2,1)S(1)}, u32[]{:S(2)}, u32[]{:S(2)}) collective-permute-start(bf16[160,1152]{1,0:T(8,128)(2,1)S(1)} %collective-permute-done.1), channel_id=1, source_target_pairs={{0,4},{1,17},{2,6},{3,19},{4,8},{5,21},{6,10},{7,23},{8,12},{9,25}... | collective-permute-start | bytes 1105928 | tf_op jit(solution)/shard_map/ppermute | solution.py:48
  14.6 12.6 %collective-permute-start.7 = (bf16[160,1152]{1,0:T(8,128)(2,1)S(1)}, bf16[160,1152]{1,0:T(8,128)(2,1)S(1)}, u32[]{:S(2)}, u32[]{:S(2)}) collective-permute-start(bf16[160,1152]{1,0:T(8,128)(2,1)S(1)} %collective-permute-done.4), channel_id=1, source_target_pairs={{0,12},{1,49},{2,14},{3,51},{4,0},{5,53},{6,2},{7,55},{8,4},{9,57}... | collective-permute-start | bytes 1105928 | tf_op jit(solution)/shard_map/ppermute | solution.py:48
  20.9 11.6 %collective-permute-start.8 = (bf16[320,1152]{1,0:T(8,128)(2,1)S(1)}, bf16[320,1152]{1,0:T(8,128)(2,1)S(1)}, u32[]{:S(2)}, u32[]{:S(2)}) collective-permute-start(bf16[320,1152]{1,0:T(8,128)(2,1)S(1)} %collective-permute-done.5.refs_5_), channel_id=1, source_target_pairs={{0,4},{1,17},{2,6},{3,19},{4,8},{5,21},{6,10},{7,23},{8,12},{9,25}... | collective-permute-start | bytes 2211848 | tf_op jit(solution)/shard_map/ppermute | solution.py:48
  21.0 15.4 %collective-permute-start.12 = (bf16[1280,1152]{1,0:T(8,128)(2,1)S(1)}, bf16[1280,1152]{1,0:T(8,128)(2,1)S(1)}, u32[]{:S(2)}, u32[]{:S(2)}) collective-permute-start(bf16[1280,1152]{1,0:T(8,128)(2,1)S(1)} %constant_dynamic-update-slice_fusion.8), channel_id=1, source_target_pairs={{0,1},{1,0},{2,3},{3,2},{4,5},{5,4},{6,7},{7,6},{8,9},{9,8},{10,11... | collective-permute-start | bytes 8847368 | tf_op jit(solution)/shard_map/ppermute | solution.py:61
  21.1 11.8 %collective-permute-start.9 = (bf16[320,1152]{1,0:T(8,128)(2,1)S(1)}, bf16[320,1152]{1,0:T(8,128)(2,1)S(1)}, u32[]{:S(2)}, u32[]{:S(2)}) collective-permute-start(bf16[320,1152]{1,0:T(8,128)(2,1)S(1)} %collective-permute-done.5.refs_5_), channel_id=1, source_target_pairs={{0,12},{1,49},{2,14},{3,51},{4,0},{5,53},{6,2},{7,55},{8,4},{9,57}... | collective-permute-start | bytes 2211848 | tf_op jit(solution)/shard_map/ppermute | solution.py:48
  24.5 8.5 %collective-permute-start.10 = (bf16[160,1152]{1,0:T(8,128)(2,1)S(1)}, bf16[160,1152]{1,0:T(8,128)(2,1)S(1)}, u32[]{:S(2)}, u32[]{:S(2)}) collective-permute-start(bf16[160,1152]{1,0:T(8,128)(2,1)S(1)} %collective-permute-done.6), channel_id=1, source_target_pairs={{0,2},{1,67},{2,0},{3,65},{4,6},{5,71},{6,4},{7,69},{8,10},{9,75},... | collective-permute-start | bytes 1105928 | tf_op jit(solution)/shard_map/ppermute | solution.py:57
  27.2 8.8 %collective-permute-start.11 = (bf16[160,1152]{1,0:T(8,128)(2,1)S(1)}, bf16[160,1152]{1,0:T(8,128)(2,1)S(1)}, u32[]{:S(2)}, u32[]{:S(2)}) collective-permute-start(bf16[160,1152]{1,0:T(8,128)(2,1)S(1)} %collective-permute-done.7), channel_id=1, source_target_pairs={{0,2},{1,67},{2,0},{3,65},{4,6},{5,71},{6,4},{7,69},{8,10},{9,75},... | collective-permute-start | bytes 1105928 | tf_op jit(solution)/shard_map/ppermute | solution.py:57
  36.1 5.9 %collective-permute-start.13 = (bf16[1280,1152]{1,0:T(8,128)(2,1)S(1)}, bf16[1280,1152]{1,0:T(8,128)(2,1)S(1)}, u32[]{:S(2)}, u32[]{:S(2)}) collective-permute-start(bf16[1280,1152]{1,0:T(8,128)(2,1)S(1)} %get-tuple-element.50), channel_id=1, source_target_pairs={{0,1},{1,0},{2,3},{3,2},{4,5},{5,4},{6,7},{7,6},{8,9},{9,8},{10,11... | collective-permute-start | bytes 8847368 | tf_op jit(solution)/shard_map/ppermute | solution.py:61
  47.7 6.9 %collective-permute-start.16 = (bf16[2,1280,512]{2,1,0:T(8,128)(2,1)S(1)}, bf16[2,1280,512]{2,1,0:T(8,128)(2,1)S(1)}, u32[]{:S(2)}, u32[]{:S(2)}) collective-permute-start(bf16[2,1280,512]{2,1,0:T(8,128)(2,1)S(1)} %get-tuple-element.33.refs_3_.refs_5_.refs_4_), channel_id=1, source_target_pairs={{0,1},{1,0},{2,3},{3,2},{4,5},{5,4},{6,7},{7,6},{8,9},{9,8},{10,11... | collective-permute-start | bytes 7864328 | tf_op jit(solution)/shard_map/ppermute | solution.py:61
  54.1 9.5 %collective-permute-start.14 = (bf16[2,1280,512]{2,1,0:T(8,128)(2,1)S(1)}, bf16[2,1280,512]{2,1,0:T(8,128)(2,1)S(1)}, u32[]{:S(2)}, u32[]{:S(2)}) collective-permute-start(bf16[2,1280,512]{2,1,0:T(8,128)(2,1)S(1)} %get-tuple-element.35), channel_id=1, source_target_pairs={{0,1},{1,0},{2,3},{3,2},{4,5},{5,4},{6,7},{7,6},{8,9},{9,8},{10,11... | collective-permute-start | bytes 7864328 | tf_op jit(solution)/shard_map/ppermute | solution.py:61
  54.2 9.4 %collective-permute-start.15 = (bf16[2,1280,256]{2,1,0:T(8,128)(2,1)S(1)}, bf16[2,1280,256]{2,1,0:T(8,128)(2,1)S(1)}, u32[]{:S(2)}, u32[]{:S(2)}) collective-permute-start(bf16[2,1280,256]{2,1,0:T(8,128)(2,1)S(1)} %get-tuple-element.36), channel_id=1, source_target_pairs={{0,1},{1,0},{2,3},{3,2},{4,5},{5,4},{6,7},{7,6},{8,9},{9,8},{10,11... | collective-permute-start | bytes 3932168 | tf_op jit(solution)/shard_map/ppermute | solution.py:61
  58.3 11.7 %collective-permute-start.17 = (bf16[320,1152]{1,0:T(8,128)(2,1)S(1)}, bf16[320,1152]{1,0:T(8,128)(2,1)S(1)}, u32[]{:S(2)}, u32[]{:S(2)}) collective-permute-start(bf16[320,1152]{1,0:T(8,128)(2,1)S(1)} %get-tuple-element.41), channel_id=1, source_target_pairs={{0,12},{1,49},{2,14},{3,51},{4,0},{5,53},{6,2},{7,55},{8,4},{9,57}... | collective-permute-start | bytes 2211848 | tf_op jit(solution)/shard_map/ppermute | solution.py:48
  60.8 11.8 %collective-permute-start.18 = (bf16[320,1152]{1,0:T(8,128)(2,1)S(1)}, bf16[320,1152]{1,0:T(8,128)(2,1)S(1)}, u32[]{:S(2)}, u32[]{:S(2)}) collective-permute-start(bf16[320,1152]{1,0:T(8,128)(2,1)S(1)} %get-tuple-element.42), channel_id=1, source_target_pairs={{0,4},{1,17},{2,6},{3,19},{4,8},{5,21},{6,10},{7,23},{8,12},{9,25}... | collective-permute-start | bytes 2211848 | tf_op jit(solution)/shard_map/ppermute | solution.py:48
  60.8 13.9 %collective-permute-start.19 = (bf16[320,1152]{1,0:T(8,128)(2,1)S(1)}, bf16[320,1152]{1,0:T(8,128)(2,1)S(1)}, u32[]{:S(2)}, u32[]{:S(2)}) collective-permute-start(bf16[320,1152]{1,0:T(8,128)(2,1)S(1)} %get-tuple-element.44), channel_id=1, source_target_pairs={{0,2},{1,67},{2,0},{3,65},{4,6},{5,71},{6,4},{7,69},{8,10},{9,75},... | collective-permute-start | bytes 2211848 | tf_op jit(solution)/shard_map/ppermute | solution.py:57
  67.3 19.1 %collective-permute-start.21 = (bf16[320,1152]{1,0:T(8,128)(2,1)S(1)}, bf16[320,1152]{1,0:T(8,128)(2,1)S(1)}, u32[]{:S(2)}, u32[]{:S(2)}) collective-permute-start(bf16[320,1152]{1,0:T(8,128)(2,1)S(1)} %get-tuple-element.43.refs_3_), channel_id=1, source_target_pairs={{0,12},{1,49},{2,14},{3,51},{4,0},{5,53},{6,2},{7,55},{8,4},{9,57}... | collective-permute-start | bytes 2211848 | tf_op jit(solution)/shard_map/ppermute | solution.py:48
  70.0 19.5 %collective-permute-start.22 = (bf16[320,1152]{1,0:T(8,128)(2,1)S(1)}, bf16[320,1152]{1,0:T(8,128)(2,1)S(1)}, u32[]{:S(2)}, u32[]{:S(2)}) collective-permute-start(bf16[320,1152]{1,0:T(8,128)(2,1)S(1)} %get-tuple-element.45), channel_id=1, source_target_pairs={{0,4},{1,17},{2,6},{3,19},{4,8},{5,21},{6,10},{7,23},{8,12},{9,25}... | collective-permute-start | bytes 2211848 | tf_op jit(solution)/shard_map/ppermute | solution.py:48
  74.9 14.6 %collective-permute-start.20 = (bf16[320,1152]{1,0:T(8,128)(2,1)S(1)}, bf16[320,1152]{1,0:T(8,128)(2,1)S(1)}, u32[]{:S(2)}, u32[]{:S(2)}) collective-permute-start(bf16[320,1152]{1,0:T(8,128)(2,1)S(1)} %shard_map.67.refs_7_), channel_id=1, source_target_pairs={{0,8},{1,33},{2,10},{3,35},{4,12},{5,37},{6,14},{7,39},{8,0},{9,41... | collective-permute-start | bytes 2211848 | tf_op jit(solution)/shard_map/ppermute | solution.py:48
  75.0 14.5 %collective-permute-start.23 = (bf16[320,1152]{1,0:T(8,128)(2,1)S(1)}, bf16[320,1152]{1,0:T(8,128)(2,1)S(1)}, u32[]{:S(2)}, u32[]{:S(2)}) collective-permute-start(bf16[320,1152]{1,0:T(8,128)(2,1)S(1)} %shard_map.65.refs_8_), channel_id=1, source_target_pairs={{0,2},{1,67},{2,0},{3,65},{4,6},{5,71},{6,4},{7,69},{8,10},{9,75},... | collective-permute-start | bytes 2211848 | tf_op jit(solution)/shard_map/ppermute | solution.py:57
  90.0 1.8 %collective-permute-start.24 = (bf16[160,1152]{1,0:T(8,128)(2,1)S(1)}, bf16[160,1152]{1,0:T(8,128)(2,1)S(1)}, u32[]{:S(2)}, u32[]{:S(2)}) collective-permute-start(bf16[160,1152]{1,0:T(8,128)(2,1)S(1)} %shard_map.69.refs_8_), channel_id=1, source_target_pairs={{0,1},{1,0},{2,3},{3,2},{4,5},{5,4},{6,7},{7,6},{8,9},{9,8},{10,11... | collective-permute-start | bytes 1105928 | tf_op jit(solution)/shard_map/ppermute | solution.py:61

commit v15 on v14

--- a/solution.py
+++ b/solution.py
@@ -167,21 +167,16 @@
 
 def far_weights_kernel(pieces, core_ref, factors_ref, *refs):
     mine, other = places_of(refs[: pieces[0]]), places_of(refs[pieces[0] : sum(pieces)])
-    edge_ref, far_ref = refs[sum(pieces) :]
-    edge = edge_ref.shape[2]
-    first = 8 * rows - edge - far_ref.shape[2]
+    (far_ref,) = refs[sum(pieces) :]
+    first = 8 * rows - far_ref.shape[2]
     for half in range(2):
         mine_rows = stacked(mine, half * rows)
         other_rows = stacked(other, opposite_rows(core_ref[0], half))
-        for begin, size in spans(edge + far_ref.shape[2]):
+        for begin, size in spans(far_ref.shape[2]):
             start = first + begin
-            weights = weights_of(
+            far_ref[half, :, pl.ds(begin, size)] = weights_of(
                 factors_ref, mine_rows, other_rows[start : start + size]
             )
-            if begin < edge:
-                edge_ref[half, :, pl.ds(begin, size)] = weights
-            else:
-                far_ref[half, :, pl.ds(begin - edge, size)] = weights
 
 
 def own_product(half, first, count, weights_refs, other_rows):
@@ -191,18 +186,24 @@
     return jnp.dot(weights, other_rows, preferred_element_type=jnp.float32)
 
 
-def own_kernel(pieces, core_ref, *refs):
-    weights_refs, begun_ref, other = refs[:3], refs[3], places_of(refs[4 : 4 + pieces])
-    near_ref, far_ref, low_ref, high_ref = refs[4 + pieces :]
-    count = weights_refs[0].shape[2]
-    low_ref[...] = weights_refs[0][...]
-    high_ref[...] = weights_refs[1][...]
-    for half in range(2):
+def own_kernel(pieces, core_ref, factors_ref, *refs):
+    mine, other = places_of(refs[: pieces[0]]), places_of(refs[pieces[0] : sum(pieces)])
+    first_ref, last_ref, begun_ref, near_ref, far_ref, copy_ref, edge_ref = refs[
+        sum(pieces) :
+    ]
+    count, edge = first_ref.shape[2], edge_ref.shape[2]
+    copy_ref[...] = first_ref[...]
+    for half in range(2):
+        mine_rows = stacked(mine, half * rows)
         other_rows = stacked(other, opposite_rows(core_ref[0], half))
+        edge_ref[half] = weights_of(
+            factors_ref, mine_rows, other_rows[count : count + edge]
+        )
+        weights_refs = (first_ref, edge_ref, last_ref)
         far_ref[half] = begun_ref[half, pl.ds(rows, 3 * rows), :] + own_product(
             half, 5 * rows, 3 * rows, weights_refs[1:], other_rows[count:]
         )
-        near_ref[half] = own_product(half, rows, 3 * rows, weights_refs, other_rows)
+        near_ref[half] = own_product(half, rows, 2 * rows, weights_refs, other_rows)
 
 
 def received(core, half, columns, other):
@@ -226,13 +227,17 @@
 
 
 def near_kernel(pieces, core_ref, low_ref, high_ref, part_ref, *refs):
-    other, sums = places_of(refs[:pieces]), places_of(refs[pieces:])
+    weights_refs, other = refs[:3], places_of(refs[3 : 3 + pieces])
+    sums = places_of(refs[3 + pieces :])
     first = rows // 128 * 128
     count = low_ref.shape[2]
     columns = [(low_ref, first, count - first), (high_ref, 0, 4 * rows - count)]
     for half in range(2):
         total = received(core_ref[0], half, columns, other)[rows - first :]
-        store_chips(sums, half * rows, 0, total + part_ref[half])
+        other_rows = stacked(other, opposite_rows(core_ref[0], half))
+        own = own_product(half, 3 * rows, rows, weights_refs, other_rows)
+        store_chips(sums[:2], half * rows, 0, total[: 2 * rows] + part_ref[half])
+        store_chips(sums[2:], half * rows, 0, total[2 * rows :] + own)
 
 
 def distant_kernel(pieces, core_ref, high_ref, tail_ref, begun_ref, *refs):
@@ -377,26 +382,26 @@
         12 * share,
         kinds=(jnp.bfloat16, jnp.float32),
     )
-    edge_weights, far_weights = call(
+    (far_weights,) = call(
         functools.partial(far_weights_kernel, (len(mine), len(other))),
-        [(2, all_rows, chunk), (2, all_rows, 2 * chunk)],
+        [(2, all_rows, 2 * chunk)],
         (cores,),
         (factors, *mine, *other),
-        12 * share,
+        8 * share,
         (near_weights,),
     )
     far_received = swap(far_weights)
+    near_part, far_part, near_copy, edge_weights = call(
+        functools.partial(own_kernel, (len(mine), len(other))),
+        [(2, 2 * rows, width), (2, 3 * rows, width)]
+        + [(2, all_rows, 2 * chunk), (2, all_rows, chunk)],
+        (cores,),
+        (factors, *mine, *other, near_weights, far_weights, far_begun),
+        16 * share,
+        kinds=(jnp.float32,) * 2 + (jnp.bfloat16,) * 2,
+    )
     weights = (near_weights, edge_weights, far_weights)
-    near_part, far_part, near_copy, edge_copy = call(
-        functools.partial(own_kernel, len(other)),
-        [(2, 3 * rows, width)] * 2
-        + [(2, all_rows, 2 * chunk), (2, all_rows, chunk)],
-        (cores,),
-        (*weights, far_begun, *other),
-        14 * share,
-        kinds=(jnp.float32,) * 2 + (jnp.bfloat16,) * 2,
-    )
-    near_received, edge_received = swap(near_copy), swap(edge_copy)
+    near_received, edge_received = swap(near_copy), swap(edge_weights)
     *far_sums, tail = call(
         functools.partial(far_kernel, len(other)),
         [block] * 3 + [(2, 5 * rows - 3 * chunk, width)],
@@ -410,7 +415,7 @@
         functools.partial(near_kernel, len(other)),
         [block] * 3,
         (cores,),
-        (near_received, edge_received, near_part, *other),
+        (near_received, edge_received, near_part, *weights, *other),
         8 * share,
     )
     (across_total,) = add([(near_sums[2], arrived[0], arrived[1])], (near_sums[0],))

time: 92.9 us -> 93 us (level)
  transfers between devices with their start and end apart: 25 -> 25, of which waited for: 9 -> 9; matrix products, arithmetic and copies ran while one was open for 1% -> 1% of each run, Pallas kernels for 26% -> 28%
where the time goes in v15:
time: 93 us; the launch traced here: 92.9 us
  starting transfers between devices  32.6 us (35%)
  Pallas kernels  30.9 us (33%)
  waiting for transfers between devices  24.2 us (26%)
  between operations  2.14 us (2%)
  other arithmetic  2.11 us (2%)
    pallas_call x12, Pallas kernels, call(): pl.pallas_call(body, in_specs=[pl.BlockSpec(memory_space=pltpu.SMEM)] * l...  30.9 us
    ppermute x13, waiting for transfers between devices, ring(): return lax.ppermute(value, axes, ring_move(steps))  18.9 us
    ppermute x13, starting transfers between devices, ring(): return lax.ppermute(value, axes, ring_move(steps))  18.2 us
    ppermute x5, starting transfers between devices, pair(): return lax.ppermute(value, axes, pairs_of(move))  11.1 us
    ppermute x5, waiting for transfers between devices, pair(): return lax.ppermute(value, axes, pairs_of(move))  4.04 us
    ppermute x7, starting transfers between devices, swap(): return lax.ppermute(value, 'core', [(0, 1), (1, 0)])  3.31 us
  transfers between devices with their start and end apart: 25, of which 9 were waited for; matrix products, arithmetic and copies ran while one was open for 1% of the time, Pallas kernels for 28%

profile of v15, /device:TPU:1, one launch (start us, length us, event | category | flops | bytes accessed | tf_op | source)
XLA Modules:
  0.0 92.9 jit_solution(13909942526700104702)
XLA Ops:
  0.6 1.2 %broadcast_select_fusion.2 = (bf16[160,1152]{1,0:T(8,128)(2,1)S(1)}, bf16[160,1152]{1,0:T(8,128)(2,1)S(1)}) fusion(bf16[160,1152]{1,0:T(8,128)(2,1)} %param.5, bf16[160,1152]{1,0:T(8,128)(2,1)} %param.4, pred[]{:T(512)S(6)} %eq.3), kind=kLoop, calls=%fused_computation.2 | loop fusion | flops 368640 | bytes 1474561 | tf_op jit(solution)/shard_map/jit(_where)/select_n | solution.py:345
  1.8 1.5 %collective-permute-start = (bf16[160,1152]{1,0:T(8,128)(2,1)S(1)}, bf16[160,1152]{1,0:T(8,128)(2,1)S(1)}, u32[]{:S(2)}, u32[]{:S(2)}) collective-permute-start(bf16[160,1152]{1,0:T(8,128)(2,1)S(1)} %get-tuple-element.44), channel_id=1, source_target_pairs={{0,1},{1,0},{2,3},{3,2},{4,5},{5,4},{6,7},{7,6},{8,9},{9,8},{10,11... | collective-permute-start | bytes 1105928 | tf_op jit(solution)/shard_map/ppermute | solution.py:61
  4.6 0.0 collective-permute-done.refs_4_
  4.6 0.4 shard_map.59
  5.0 1.8 %collective-permute-start.1 = (bf16[160,1152]{1,0:T(8,128)(2,1)S(1)}, bf16[160,1152]{1,0:T(8,128)(2,1)S(1)}, u32[]{:S(2)}, u32[]{:S(2)}) collective-permute-start(bf16[160,1152]{1,0:T(8,128)(2,1)S(1)} %get-tuple-element.28), channel_id=1, source_target_pairs={{0,4},{1,17},{2,6},{3,19},{4,8},{5,21},{6,10},{7,23},{8,12},{9,25}... | collective-permute-start | bytes 1105928 | tf_op jit(solution)/shard_map/ppermute | solution.py:48
  6.8 2.2 %collective-permute-start.4 = (bf16[160,1152]{1,0:T(8,128)(2,1)S(1)}, bf16[160,1152]{1,0:T(8,128)(2,1)S(1)}, u32[]{:S(2)}, u32[]{:S(2)}) collective-permute-start(bf16[160,1152]{1,0:T(8,128)(2,1)S(1)} %get-tuple-element.27), channel_id=1, source_target_pairs={{0,12},{1,49},{2,14},{3,51},{4,0},{5,53},{6,2},{7,55},{8,4},{9,57}... | collective-permute-start | bytes 1105928 | tf_op jit(solution)/shard_map/ppermute | solution.py:48
  9.0 2.7 %collective-permute-start.5 = (bf16[320,1152]{1,0:T(8,128)(2,1)S(1)}, bf16[320,1152]{1,0:T(8,128)(2,1)S(1)}, u32[]{:S(2)}, u32[]{:S(2)}) collective-permute-start(bf16[320,1152]{1,0:T(8,128)(2,1)S(1)} %get-tuple-element.24.refs_2_), channel_id=1, source_target_pairs={{0,2},{1,67},{2,0},{3,65},{4,6},{5,71},{6,4},{7,69},{8,10},{9,75},... | collective-permute-start | bytes 2211848 | tf_op jit(solution)/shard_map/ppermute | solution.py:57
  11.8 0.0 collective-permute-start.2
  11.8 0.1 constant_dynamic-update-slice_fusion.13
  11.8 2.7 %collective-permute-start.3 = (bf16[160,1152]{1,0:T(8,128)(2,1)S(1)}, bf16[160,1152]{1,0:T(8,128)(2,1)S(1)}, u32[]{:S(2)}, u32[]{:S(2)}) collective-permute-start(bf16[160,1152]{1,0:T(8,128)(2,1)S(1)} %get-tuple-element.28), channel_id=1, source_target_pairs={{0,12},{1,49},{2,14},{3,51},{4,0},{5,53},{6,2},{7,55},{8,4},{9,57}... | collective-permute-start | bytes 1105928 | tf_op jit(solution)/shard_map/ppermute | solution.py:48
  14.6 0.0 collective-permute-done.1
  14.6 0.0 collective-permute-start.6
  14.6 0.0 collective-permute-done.4
  14.6 2.7 %collective-permute-start.7 = (bf16[160,1152]{1,0:T(8,128)(2,1)S(1)}, bf16[160,1152]{1,0:T(8,128)(2,1)S(1)}, u32[]{:S(2)}, u32[]{:S(2)}) collective-permute-start(bf16[160,1152]{1,0:T(8,128)(2,1)S(1)} %collective-permute-done.4), channel_id=1, source_target_pairs={{0,12},{1,49},{2,14},{3,51},{4,0},{5,53},{6,2},{7,55},{8,4},{9,57}... | collective-permute-start | bytes 1105928 | tf_op jit(solution)/shard_map/ppermute | solution.py:48
  17.2 0.1 constant_dynamic-update-slice_fusion.12
  17.3 2.3 %collective-permute-done.2 = bf16[160,1152]{1,0:T(8,128)(2,1)S(1)} collective-permute-done((bf16[160,1152]{1,0:T(8,128)(2,1)S(1)}, bf16[160,1152]{1,0:T(8,128)(2,1)S(1)}, u32[]{:S(2)}, u32[]{:S(2)}) %collective-permute-start.2) | collective-permute-done | bytes 368672 | tf_op jit(solution)/shard_map/ppermute | solution.py:48
  19.6 0.1 constant_dynamic-update-slice_fusion.11
  19.7 0.1 constant_dynamic-update-slice_fusion.10
  19.8 0.1 constant_dynamic-update-slice_fusion.9
  19.9 1.0 %collective-permute-done.5.refs_5_ = bf16[320,1152]{1,0:T(8,128)(2,1)S(1)} collective-permute-done((bf16[320,1152]{1,0:T(8,128)(2,1)S(1)}, bf16[320,1152]{1,0:T(8,128)(2,1)S(1)}, u32[]{:S(2)}, u32[]{:S(2)}) %collective-permute-start.5) | collective-permute-done | bytes 737312 | tf_op jit(solution)/shard_map/ppermute | solution.py:57
  20.9 0.1 constant_dynamic-update-slice_fusion.8
  21.0 0.1 collective-permute-start.12
  21.1 3.4 %collective-permute-start.9 = (bf16[320,1152]{1,0:T(8,128)(2,1)S(1)}, bf16[320,1152]{1,0:T(8,128)(2,1)S(1)}, u32[]{:S(2)}, u32[]{:S(2)}) collective-permute-start(bf16[320,1152]{1,0:T(8,128)(2,1)S(1)} %collective-permute-done.5.refs_5_), channel_id=1, source_target_pairs={{0,12},{1,49},{2,14},{3,51},{4,0},{5,53},{6,2},{7,55},{8,4},{9,57}... | collective-permute-start | bytes 2211848 | tf_op jit(solution)/shard_map/ppermute | solution.py:48
  24.5 0.0 collective-permute-done.6
  24.5 2.7 %collective-permute-start.10 = (bf16[160,1152]{1,0:T(8,128)(2,1)S(1)}, bf16[160,1152]{1,0:T(8,128)(2,1)S(1)}, u32[]{:S(2)}, u32[]{:S(2)}) collective-permute-start(bf16[160,1152]{1,0:T(8,128)(2,1)S(1)} %collective-permute-done.6), channel_id=1, source_target_pairs={{0,2},{1,67},{2,0},{3,65},{4,6},{5,71},{6,4},{7,69},{8,10},{9,75},... | collective-permute-start | bytes 1105928 | tf_op jit(solution)/shard_map/ppermute | solution.py:57
  27.2 0.0 collective-permute-done.7
  27.2 0.1 collective-permute-start.11
  27.3 0.1 constant_dynamic-update-slice_fusion.19
  27.4 0.1 constant_dynamic-update-slice_fusion.18
  27.4 5.0 %collective-permute-done.8.refs_7_ = bf16[320,1152]{1,0:T(8,128)(2,1)S(1)} collective-permute-done((bf16[320,1152]{1,0:T(8,128)(2,1)S(1)}, bf16[320,1152]{1,0:T(8,128)(2,1)S(1)}, u32[]{:S(2)}, u32[]{:S(2)}) %collective-permute-start.8) | collective-permute-done | bytes 737312 | tf_op jit(solution)/shard_map/ppermute | solution.py:48
  32.5 0.1 constant_dynamic-update-slice_fusion.17
  32.5 0.3 collective-permute-done.9.refs_8_
  32.9 0.1 constant_dynamic-update-slice_fusion.16
  33.0 0.1 constant_dynamic-update-slice_fusion.15
  33.1 3.0 %collective-permute-done.11 = bf16[160,1152]{1,0:T(8,128)(2,1)S(1)} collective-permute-done((bf16[160,1152]{1,0:T(8,128)(2,1)S(1)}, bf16[160,1152]{1,0:T(8,128)(2,1)S(1)}, u32[]{:S(2)}, u32[]{:S(2)}) %collective-permute-start.11) | collective-permute-done | bytes 368672 | tf_op jit(solution)/shard_map/ppermute | solution.py:57
  36.1 0.1 constant_dynamic-update-slice_fusion.14
  36.1 0.3 collective-permute-start.13
  36.4 0.0 collective-permute-done.12.refs_10_.refs_3_.refs_7_.refs_6_.refs_5_
  36.4 5.6 %shard_map.60 = (bf16[2,1280,512]{2,1,0:T(8,128)(2,1)S(1)}, f32[2,640,1152]{2,1,0:T(8,128)S(1)}) custom-call(s32[1]{0:T(128)} %bitcast.refs_2_.refs_0_, f32[8,128]{1,0:T(8,128)S(1)} %get-tuple-element.22.refs_1_, bf16[320,1152]{1,0:T(8,128)(2,1)S(1)} %get-tuple-element.24.refs_2_, bf16[320,1152]{1,0:T(8,128)(2,1)S(1)} %get-tuple-element.59.refs_3_, ...), custom_call_target="tpu_custom_call" | custom-call | flops 4529848320 | bytes 1048576 | tf_op jit(solution)/shard_map/pallas_call | solution.py:290
  42.0 0.0 collective-permute-done.13.refs_11_.refs_4_.refs_8_.refs_7_.refs_6_
  42.0 3.9 %shard_map.61.refs_13_.refs_6_.refs_5_.refs_4_ = bf16[2,1280,512]{2,1,0:T(8,128)(2,1)S(1)} custom-call(s32[1]{0:T(128)} %bitcast.refs_2_.refs_0_, f32[8,128]{1,0:T(8,128)S(1)} %get-tuple-element.22.refs_1_, bf16[320,1152]{1,0:T(8,128)(2,1)S(1)} %get-tuple-element.24.refs_2_, bf16[320,1152]{1,0:T(8,128)(2,1)S(1)} %get-tuple-element.59.refs_3_, ...), custom_call_target="tpu_custom_call" | custom-call | flops 3019898880 | bytes 1048576 | tf_op jit(solution)/shard_map/pallas_call | solution.py:290
  45.9 0.8 collective-permute-start.16
  46.7 6.4 %shard_map.62 = (f32[2,320,1152]{2,1,0:T(8,128)S(1)}, f32[2,480,1152]{2,1,0:T(8,128)S(1)}, bf16[2,1280,512]{2,1,0:T(8,128)(2,1)S(1)}, bf16[2,1280,256]{2,1,0:T(8,128)(2,1)S(1)}) custom-call(s32[1]{0:T(128)} %bitcast.refs_2_.refs_0_, f32[8,128]{1,0:T(8,128)S(1)} %get-tuple-element.22.refs_1_, bf16[320,1152]{1,0:T(8,128)(2,1)S(1)} %get-tuple-element.24.refs_2_, ...), custom_call_target="tpu_custom_call" | custom-call | flops 6039797760 | bytes 1048576 | tf_op jit(solution)/shard_map/pallas_call | solution.py:290
  53.2 0.1 collective-permute-start.14
  53.3 0.5 collective-permute-start.15
  53.8 3.7 %shard_map.63 = (bf16[320,1152]{1,0:T(8,128)(2,1)S(1)}, bf16[320,1152]{1,0:T(8,128)(2,1)S(1)}, bf16[320,1152]{1,0:T(8,128)(2,1)S(1)}, f32[2,32,1152]{2,1,0:T(8,128)S(1)}) custom-call(s32[1]{0:T(128)} %bitcast.refs_2_.refs_0_, bf16[2,1280,512]{2,1,0:T(8,128)(2,1)S(1)} %collective-permute-done.16.refs_1_, f32[2,480,1152]{2,1,0:T(8,128)S(1)} %get-tuple-element.33.refs_2_, ...), custom_call_target="tpu_custom_call" | custom-call | flops 3774873600 | bytes 1048576 | tf_op jit(solution)/shard_map/pallas_call | solution.py:290
  57.4 2.6 %collective-permute-start.17 = (bf16[320,1152]{1,0:T(8,128)(2,1)S(1)}, bf16[320,1152]{1,0:T(8,128)(2,1)S(1)}, u32[]{:S(2)}, u32[]{:S(2)}) collective-permute-start(bf16[320,1152]{1,0:T(8,128)(2,1)S(1)} %get-tuple-element.37), channel_id=1, source_target_pairs={{0,12},{1,49},{2,14},{3,51},{4,0},{5,53},{6,2},{7,55},{8,4},{9,57}... | collective-permute-start | bytes 2211848 | tf_op jit(solution)/shard_map/ppermute | solution.py:48
  60.0 2.7 %collective-permute-start.19 = (bf16[320,1152]{1,0:T(8,128)(2,1)S(1)}, bf16[320,1152]{1,0:T(8,128)(2,1)S(1)}, u32[]{:S(2)}, u32[]{:S(2)}) collective-permute-start(bf16[320,1152]{1,0:T(8,128)(2,1)S(1)} %get-tuple-element.40), channel_id=1, source_target_pairs={{0,2},{1,67},{2,0},{3,65},{4,6},{5,71},{6,4},{7,69},{8,10},{9,75},... | collective-permute-start | bytes 2211848 | tf_op jit(solution)/shard_map/ppermute | solution.py:57
  62.8 4.7 %shard_map.64 = (bf16[320,1152]{1,0:T(8,128)(2,1)S(1)}, bf16[320,1152]{1,0:T(8,128)(2,1)S(1)}, bf16[320,1152]{1,0:T(8,128)(2,1)S(1)}) custom-call(s32[1]{0:T(128)} %bitcast.refs_2_.refs_0_, bf16[2,1280,512]{2,1,0:T(8,128)(2,1)S(1)} %collective-permute-done.14.refs_1_, bf16[2,1280,256]{2,1,0:T(8,128)(2,1)S(1)} %collective-permute-done.15.refs_2_.refs_1_, ...), custom_call_target="tpu_custom_call" | custom-call | flops 3019898880 | bytes 1048576 | tf_op jit(solution)/shard_map/pallas_call | solution.py:290
  67.5 2.7 %collective-permute-start.21 = (bf16[320,1152]{1,0:T(8,128)(2,1)S(1)}, bf16[320,1152]{1,0:T(8,128)(2,1)S(1)}, u32[]{:S(2)}, u32[]{:S(2)}) collective-permute-start(bf16[320,1152]{1,0:T(8,128)(2,1)S(1)} %get-tuple-element.39.refs_3_), channel_id=1, source_target_pairs={{0,12},{1,49},{2,14},{3,51},{4,0},{5,53},{6,2},{7,55},{8,4},{9,57}... | collective-permute-start | bytes 2211848 | tf_op jit(solution)/shard_map/ppermute | solution.py:48
  70.2 1.6 %collective-permute-done.18.refs_2_ = bf16[320,1152]{1,0:T(8,128)(2,1)S(1)} collective-permute-done((bf16[320,1152]{1,0:T(8,128)(2,1)S(1)}, bf16[320,1152]{1,0:T(8,128)(2,1)S(1)}, u32[]{:S(2)}, u32[]{:S(2)}) %collective-permute-start.18) | collective-permute-done | bytes 737312 | tf_op jit(solution)/shard_map/ppermute | solution.py:48
  71.8 0.3 shard_map.65.refs_8_
  72.1 1.8 %shard_map.66.refs_0_ = bf16[320,1152]{1,0:T(8,128)(2,1)S(1)} custom-call(s32[1]{0:T(128)} %bitcast.refs_2_.refs_0_, bf16[2,1280,256]{2,1,0:T(8,128)(2,1)S(1)} %collective-permute-done.15.refs_2_.refs_1_, f32[2,32,1152]{2,1,0:T(8,128)S(1)} %get-tuple-element.34.refs_2_, f32[2,640,1152]{2,1,0:T(8,128)S(1)} %get-tuple-element.30.refs_14_.refs_3_, ...), custom_call_target="tpu_custom_call" | custom-call | flops 1509949440 | bytes 1048576 | tf_op jit(solution)/shard_map/pallas_call | solution.py:290
  73.9 0.2 shard_map.67.refs_7_
  74.1 0.1 collective-permute-start.20
  74.2 2.8 %collective-permute-start.23 = (bf16[320,1152]{1,0:T(8,128)(2,1)S(1)}, bf16[320,1152]{1,0:T(8,128)(2,1)S(1)}, u32[]{:S(2)}, u32[]{:S(2)}) collective-permute-start(bf16[320,1152]{1,0:T(8,128)(2,1)S(1)} %shard_map.65.refs_8_), channel_id=1, source_target_pairs={{0,2},{1,67},{2,0},{3,65},{4,6},{5,71},{6,4},{7,69},{8,10},{9,75},... | collective-permute-start | bytes 2211848 | tf_op jit(solution)/shard_map/ppermute | solution.py:57
  77.0 3.0 %shard_map.68.refs_3_ = f32[320,1152]{1,0:T(8,128)S(1)} custom-call(s32[1]{0:T(128)} %bitcast.refs_2_.refs_0_, bf16[2,1280,512]{2,1,0:T(8,128)(2,1)S(1)} %collective-permute-done.14.refs_1_, bf16[2,1280,512]{2,1,0:T(8,128)(2,1)S(1)} %get-tuple-element.29.refs_12_.refs_4_.refs_2_, bf16[2,1280,256]{2,1,0:T(8,128)(2,1)S(1)} %get-tuple-element.32.refs_5_.refs_4_.refs_3_, ...), custom_call_target="tpu_custom_call" | custom-call | flops 1887436800 | bytes 1048576 | tf_op jit(solution)/shard_map/pallas_call | solution.py:290
  80.0 6.5 %collective-permute-done.21.refs_5_ = bf16[320,1152]{1,0:T(8,128)(2,1)S(1)} collective-permute-done((bf16[320,1152]{1,0:T(8,128)(2,1)S(1)}, bf16[320,1152]{1,0:T(8,128)(2,1)S(1)}, u32[]{:S(2)}, u32[]{:S(2)}) %collective-permute-start.21) | collective-permute-done | bytes 737312 | tf_op jit(solution)/shard_map/ppermute | solution.py:48
  86.5 3.1 %collective-permute-done.22.refs_6_ = bf16[320,1152]{1,0:T(8,128)(2,1)S(1)} collective-permute-done((bf16[320,1152]{1,0:T(8,128)(2,1)S(1)}, bf16[320,1152]{1,0:T(8,128)(2,1)S(1)}, u32[]{:S(2)}, u32[]{:S(2)}) %collective-permute-start.22) | collective-permute-done | bytes 737312 | tf_op jit(solution)/shard_map/ppermute | solution.py:48
  89.7 0.5 shard_map.69.refs_8_
  90.2 0.1 collective-permute-start.24
  90.2 0.5 shard_map.70
  90.7 1.2 %collective-permute-done.24 = bf16[160,1152]{1,0:T(8,128)(2,1)S(1)} collective-permute-done((bf16[160,1152]{1,0:T(8,128)(2,1)S(1)}, bf16[160,1152]{1,0:T(8,128)(2,1)S(1)}, u32[]{:S(2)}, u32[]{:S(2)}) %collective-permute-start.24) | collective-permute-done | bytes 368672 | tf_op jit(solution)/shard_map/ppermute | solution.py:61
  91.9 0.9 %broadcast_select_fusion = (bf16[160,1152]{1,0:T(8,128)(2,1)}, bf16[160,1152]{1,0:T(8,128)(2,1)}) fusion(bf16[160,1152]{1,0:T(8,128)(2,1)S(1)} %collective-permute-done.24, bf16[160,1152]{1,0:T(8,128)(2,1)S(1)} %shard_map.70, pred[]{:T(512)S(6)} %eq.3), kind=kLoop, calls=%fused_computation | loop fusion | flops 368640 | bytes 1474561 | tf_op jit(solution)/shard_map/jit(_where)/select_n | solution.py:462
  (12 shorter events, 0.0 us)
Async XLA Ops:
  1.8 2.8 %collective-permute-start = (bf16[160,1152]{1,0:T(8,128)(2,1)S(1)}, bf16[160,1152]{1,0:T(8,128)(2,1)S(1)}, u32[]{:S(2)}, u32[]{:S(2)}) collective-permute-start(bf16[160,1152]{1,0:T(8,128)(2,1)S(1)} %get-tuple-element.44), channel_id=1, source_target_pairs={{0,1},{1,0},{2,3},{3,2},{4,5},{5,4},{6,7},{7,6},{8,9},{9,8},{10,11... | collective-permute-start | bytes 1105928 | tf_op jit(solution)/shard_map/ppermute | solution.py:61
  5.0 9.5 %collective-permute-start.1 = (bf16[160,1152]{1,0:T(8,128)(2,1)S(1)}, bf16[160,1152]{1,0:T(8,128)(2,1)S(1)}, u32[]{:S(2)}, u32[]{:S(2)}) collective-permute-start(bf16[160,1152]{1,0:T(8,128)(2,1)S(1)} %get-tuple-element.28), channel_id=1, source_target_pairs={{0,4},{1,17},{2,6},{3,19},{4,8},{5,21},{6,10},{7,23},{8,12},{9,25}... | collective-permute-start | bytes 1105928 | tf_op jit(solution)/shard_map/ppermute | solution.py:48
  6.8 7.8 %collective-permute-start.4 = (bf16[160,1152]{1,0:T(8,128)(2,1)S(1)}, bf16[160,1152]{1,0:T(8,128)(2,1)S(1)}, u32[]{:S(2)}, u32[]{:S(2)}) collective-permute-start(bf16[160,1152]{1,0:T(8,128)(2,1)S(1)} %get-tuple-element.27), channel_id=1, source_target_pairs={{0,12},{1,49},{2,14},{3,51},{4,0},{5,53},{6,2},{7,55},{8,4},{9,57}... | collective-permute-start | bytes 1105928 | tf_op jit(solution)/shard_map/ppermute | solution.py:48
  9.0 11.9 %collective-permute-start.5 = (bf16[320,1152]{1,0:T(8,128)(2,1)S(1)}, bf16[320,1152]{1,0:T(8,128)(2,1)S(1)}, u32[]{:S(2)}, u32[]{:S(2)}) collective-permute-start(bf16[320,1152]{1,0:T(8,128)(2,1)S(1)} %get-tuple-element.24.refs_2_), channel_id=1, source_target_pairs={{0,2},{1,67},{2,0},{3,65},{4,6},{5,71},{6,4},{7,69},{8,10},{9,75},... | collective-permute-start | bytes 2211848 | tf_op jit(solution)/shard_map/ppermute | solution.py:57
  11.8 7.9 %collective-permute-start.2 = (bf16[160,1152]{1,0:T(8,128)(2,1)S(1)}, bf16[160,1152]{1,0:T(8,128)(2,1)S(1)}, u32[]{:S(2)}, u32[]{:S(2)}) collective-permute-start(bf16[160,1152]{1,0:T(8,128)(2,1)S(1)} %get-tuple-element.27), channel_id=1, source_target_pairs={{0,4},{1,17},{2,6},{3,19},{4,8},{5,21},{6,10},{7,23},{8,12},{9,25}... | collective-permute-start | bytes 1105928 | tf_op jit(solution)/shard_map/ppermute | solution.py:48
  11.8 7.9 %collective-permute-start.3 = (bf16[160,1152]{1,0:T(8,128)(2,1)S(1)}, bf16[160,1152]{1,0:T(8,128)(2,1)S(1)}, u32[]{:S(2)}, u32[]{:S(2)}) collective-permute-start(bf16[160,1152]{1,0:T(8,128)(2,1)S(1)} %get-tuple-element.28), channel_id=1, source_target_pairs={{0,12},{1,49},{2,14},{3,51},{4,0},{5,53},{6,2},{7,55},{8,4},{9,57}... | collective-permute-start | bytes 1105928 | tf_op jit(solution)/shard_map/ppermute | solution.py:48
  14.6 9.9 %collective-permute-start.6 = (bf16[160,1152]{1,0:T(8,128)(2,1)S(1)}, bf16[160,1152]{1,0:T(8,128)(2,1)S(1)}, u32[]{:S(2)}, u32[]{:S(2)}) collective-permute-start(bf16[160,1152]{1,0:T(8,128)(2,1)S(1)} %collective-permute-done.1), channel_id=1, source_target_pairs={{0,4},{1,17},{2,6},{3,19},{4,8},{5,21},{6,10},{7,23},{8,12},{9,25}... | collective-permute-start | bytes 1105928 | tf_op jit(solution)/shard_map/ppermute | solution.py:48
  14.6 12.6 %collective-permute-start.7 = (bf16[160,1152]{1,0:T(8,128)(2,1)S(1)}, bf16[160,1152]{1,0:T(8,128)(2,1)S(1)}, u32[]{:S(2)}, u32[]{:S(2)}) collective-permute-start(bf16[160,1152]{1,0:T(8,128)(2,1)S(1)} %collective-permute-done.4), channel_id=1, source_target_pairs={{0,12},{1,49},{2,14},{3,51},{4,0},{5,53},{6,2},{7,55},{8,4},{9,57}... | collective-permute-start | bytes 1105928 | tf_op jit(solution)/shard_map/ppermute | solution.py:48
  20.9 11.5 %collective-permute-start.8 = (bf16[320,1152]{1,0:T(8,128)(2,1)S(1)}, bf16[320,1152]{1,0:T(8,128)(2,1)S(1)}, u32[]{:S(2)}, u32[]{:S(2)}) collective-permute-start(bf16[320,1152]{1,0:T(8,128)(2,1)S(1)} %collective-permute-done.5.refs_5_), channel_id=1, source_target_pairs={{0,4},{1,17},{2,6},{3,19},{4,8},{5,21},{6,10},{7,23},{8,12},{9,25}... | collective-permute-start | bytes 2211848 | tf_op jit(solution)/shard_map/ppermute | solution.py:48
  21.0 15.4 %collective-permute-start.12 = (bf16[1280,1152]{1,0:T(8,128)(2,1)S(1)}, bf16[1280,1152]{1,0:T(8,128)(2,1)S(1)}, u32[]{:S(2)}, u32[]{:S(2)}) collective-permute-start(bf16[1280,1152]{1,0:T(8,128)(2,1)S(1)} %constant_dynamic-update-slice_fusion.8), channel_id=1, source_target_pairs={{0,1},{1,0},{2,3},{3,2},{4,5},{5,4},{6,7},{7,6},{8,9},{9,8},{10,11... | collective-permute-start | bytes 8847368 | tf_op jit(solution)/shard_map/ppermute | solution.py:61
  21.1 11.8 %collective-permute-start.9 = (bf16[320,1152]{1,0:T(8,128)(2,1)S(1)}, bf16[320,1152]{1,0:T(8,128)(2,1)S(1)}, u32[]{:S(2)}, u32[]{:S(2)}) collective-permute-start(bf16[320,1152]{1,0:T(8,128)(2,1)S(1)} %collective-permute-done.5.refs_5_), channel_id=1, source_target_pairs={{0,12},{1,49},{2,14},{3,51},{4,0},{5,53},{6,2},{7,55},{8,4},{9,57}... | collective-permute-start | bytes 2211848 | tf_op jit(solution)/shard_map/ppermute | solution.py:48
  24.5 8.5 %collective-permute-start.10 = (bf16[160,1152]{1,0:T(8,128)(2,1)S(1)}, bf16[160,1152]{1,0:T(8,128)(2,1)S(1)}, u32[]{:S(2)}, u32[]{:S(2)}) collective-permute-start(bf16[160,1152]{1,0:T(8,128)(2,1)S(1)} %collective-permute-done.6), channel_id=1, source_target_pairs={{0,2},{1,67},{2,0},{3,65},{4,6},{5,71},{6,4},{7,69},{8,10},{9,75},... | collective-permute-start | bytes 1105928 | tf_op jit(solution)/shard_map/ppermute | solution.py:57
  27.2 8.8 %collective-permute-start.11 = (bf16[160,1152]{1,0:T(8,128)(2,1)S(1)}, bf16[160,1152]{1,0:T(8,128)(2,1)S(1)}, u32[]{:S(2)}, u32[]{:S(2)}) collective-permute-start(bf16[160,1152]{1,0:T(8,128)(2,1)S(1)} %collective-permute-done.7), channel_id=1, source_target_pairs={{0,2},{1,67},{2,0},{3,65},{4,6},{5,71},{6,4},{7,69},{8,10},{9,75},... | collective-permute-start | bytes 1105928 | tf_op jit(solution)/shard_map/ppermute | solution.py:57
  36.1 5.9 %collective-permute-start.13 = (bf16[1280,1152]{1,0:T(8,128)(2,1)S(1)}, bf16[1280,1152]{1,0:T(8,128)(2,1)S(1)}, u32[]{:S(2)}, u32[]{:S(2)}) collective-permute-start(bf16[1280,1152]{1,0:T(8,128)(2,1)S(1)} %get-tuple-element.46), channel_id=1, source_target_pairs={{0,1},{1,0},{2,3},{3,2},{4,5},{5,4},{6,7},{7,6},{8,9},{9,8},{10,11... | collective-permute-start | bytes 8847368 | tf_op jit(solution)/shard_map/ppermute | solution.py:61
  45.9 7.8 %collective-permute-start.16 = (bf16[2,1280,512]{2,1,0:T(8,128)(2,1)S(1)}, bf16[2,1280,512]{2,1,0:T(8,128)(2,1)S(1)}, u32[]{:S(2)}, u32[]{:S(2)}) collective-permute-start(bf16[2,1280,512]{2,1,0:T(8,128)(2,1)S(1)} %shard_map.61.refs_13_.refs_6_.refs_5_.refs_4_), channel_id=1, source_target_pairs={{0,1},{1,0},{2,3},{3,2},{4,5},{5,4},{6,7},{7,6},{8,9},{9,8},{10,11... | collective-permute-start | bytes 7864328 | tf_op jit(solution)/shard_map/ppermute | solution.py:61
  53.2 9.6 %collective-permute-start.14 = (bf16[2,1280,512]{2,1,0:T(8,128)(2,1)S(1)}, bf16[2,1280,512]{2,1,0:T(8,128)(2,1)S(1)}, u32[]{:S(2)}, u32[]{:S(2)}) collective-permute-start(bf16[2,1280,512]{2,1,0:T(8,128)(2,1)S(1)} %get-tuple-element.31), channel_id=1, source_target_pairs={{0,1},{1,0},{2,3},{3,2},{4,5},{5,4},{6,7},{7,6},{8,9},{9,8},{10,11... | collective-permute-start | bytes 7864328 | tf_op jit(solution)/shard_map/ppermute | solution.py:61
  53.3 9.5 %collective-permute-start.15 = (bf16[2,1280,256]{2,1,0:T(8,128)(2,1)S(1)}, bf16[2,1280,256]{2,1,0:T(8,128)(2,1)S(1)}, u32[]{:S(2)}, u32[]{:S(2)}) collective-permute-start(bf16[2,1280,256]{2,1,0:T(8,128)(2,1)S(1)} %get-tuple-element.32.refs_5_.refs_4_.refs_3_), channel_id=1, source_target_pairs={{0,1},{1,0},{2,3},{3,2},{4,5},{5,4},{6,7},{7,6},{8,9},{9,8},{10,11... | collective-permute-start | bytes 3932168 | tf_op jit(solution)/shard_map/ppermute | solution.py:61
  57.4 12.8 %collective-permute-start.17 = (bf16[320,1152]{1,0:T(8,128)(2,1)S(1)}, bf16[320,1152]{1,0:T(8,128)(2,1)S(1)}, u32[]{:S(2)}, u32[]{:S(2)}) collective-permute-start(bf16[320,1152]{1,0:T(8,128)(2,1)S(1)} %get-tuple-element.37), channel_id=1, source_target_pairs={{0,12},{1,49},{2,14},{3,51},{4,0},{5,53},{6,2},{7,55},{8,4},{9,57}... | collective-permute-start | bytes 2211848 | tf_op jit(solution)/shard_map/ppermute | solution.py:48
  60.0 11.8 %collective-permute-start.18 = (bf16[320,1152]{1,0:T(8,128)(2,1)S(1)}, bf16[320,1152]{1,0:T(8,128)(2,1)S(1)}, u32[]{:S(2)}, u32[]{:S(2)}) collective-permute-start(bf16[320,1152]{1,0:T(8,128)(2,1)S(1)} %get-tuple-element.38), channel_id=1, source_target_pairs={{0,4},{1,17},{2,6},{3,19},{4,8},{5,21},{6,10},{7,23},{8,12},{9,25}... | collective-permute-start | bytes 2211848 | tf_op jit(solution)/shard_map/ppermute | solution.py:48
  60.0 13.9 %collective-permute-start.19 = (bf16[320,1152]{1,0:T(8,128)(2,1)S(1)}, bf16[320,1152]{1,0:T(8,128)(2,1)S(1)}, u32[]{:S(2)}, u32[]{:S(2)}) collective-permute-start(bf16[320,1152]{1,0:T(8,128)(2,1)S(1)} %get-tuple-element.40), channel_id=1, source_target_pairs={{0,2},{1,67},{2,0},{3,65},{4,6},{5,71},{6,4},{7,69},{8,10},{9,75},... | collective-permute-start | bytes 2211848 | tf_op jit(solution)/shard_map/ppermute | solution.py:57
  67.5 19.0 %collective-permute-start.21 = (bf16[320,1152]{1,0:T(8,128)(2,1)S(1)}, bf16[320,1152]{1,0:T(8,128)(2,1)S(1)}, u32[]{:S(2)}, u32[]{:S(2)}) collective-permute-start(bf16[320,1152]{1,0:T(8,128)(2,1)S(1)} %get-tuple-element.39.refs_3_), channel_id=1, source_target_pairs={{0,12},{1,49},{2,14},{3,51},{4,0},{5,53},{6,2},{7,55},{8,4},{9,57}... | collective-permute-start | bytes 2211848 | tf_op jit(solution)/shard_map/ppermute | solution.py:48
  70.2 19.4 %collective-permute-start.22 = (bf16[320,1152]{1,0:T(8,128)(2,1)S(1)}, bf16[320,1152]{1,0:T(8,128)(2,1)S(1)}, u32[]{:S(2)}, u32[]{:S(2)}) collective-permute-start(bf16[320,1152]{1,0:T(8,128)(2,1)S(1)} %get-tuple-element.41), channel_id=1, source_target_pairs={{0,4},{1,17},{2,6},{3,19},{4,8},{5,21},{6,10},{7,23},{8,12},{9,25}... | collective-permute-start | bytes 2211848 | tf_op jit(solution)/shard_map/ppermute | solution.py:48
  74.1 15.6 %collective-permute-start.20 = (bf16[320,1152]{1,0:T(8,128)(2,1)S(1)}, bf16[320,1152]{1,0:T(8,128)(2,1)S(1)}, u32[]{:S(2)}, u32[]{:S(2)}) collective-permute-start(bf16[320,1152]{1,0:T(8,128)(2,1)S(1)} %shard_map.67.refs_7_), channel_id=1, source_target_pairs={{0,8},{1,33},{2,10},{3,35},{4,12},{5,37},{6,14},{7,39},{8,0},{9,41... | collective-permute-start | bytes 2211848 | tf_op jit(solution)/shard_map/ppermute | solution.py:48
  74.2 15.5 %collective-permute-start.23 = (bf16[320,1152]{1,0:T(8,128)(2,1)S(1)}, bf16[320,1152]{1,0:T(8,128)(2,1)S(1)}, u32[]{:S(2)}, u32[]{:S(2)}) collective-permute-start(bf16[320,1152]{1,0:T(8,128)(2,1)S(1)} %shard_map.65.refs_8_), channel_id=1, source_target_pairs={{0,2},{1,67},{2,0},{3,65},{4,6},{5,71},{6,4},{7,69},{8,10},{9,75},... | collective-permute-start | bytes 2211848 | tf_op jit(solution)/shard_map/ppermute | solution.py:57
  90.2 1.8 %collective-permute-start.24 = (bf16[160,1152]{1,0:T(8,128)(2,1)S(1)}, bf16[160,1152]{1,0:T(8,128)(2,1)S(1)}, u32[]{:S(2)}, u32[]{:S(2)}) collective-permute-start(bf16[160,1152]{1,0:T(8,128)(2,1)S(1)} %shard_map.69.refs_8_), channel_id=1, source_target_pairs={{0,1},{1,0},{2,3},{3,2},{4,5},{5,4},{6,7},{7,6},{8,9},{9,8},{10,11... | collective-permute-start | bytes 1105928 | tf_op jit(solution)/shard_map/ppermute | solution.py:61

commit v16 on v15

--- a/solution.py
+++ b/solution.py
@@ -227,17 +227,25 @@
 
 
 def near_kernel(pieces, core_ref, low_ref, high_ref, part_ref, *refs):
-    weights_refs, other = refs[:3], places_of(refs[3 : 3 + pieces])
-    sums = places_of(refs[3 + pieces :])
+    other, sums = places_of(refs[:pieces]), places_of(refs[pieces:])
     first = rows // 128 * 128
     count = low_ref.shape[2]
     columns = [(low_ref, first, count - first), (high_ref, 0, 4 * rows - count)]
     for half in range(2):
         total = received(core_ref[0], half, columns, other)[rows - first :]
+        store_chips(sums[:2], half * rows, 0, total[: 2 * rows] + part_ref[half])
+        store_chips(sums[2:], half * rows, 0, total[2 * rows :])
+
+
+def across_kernel(pieces, core_ref, *refs):
+    weights_refs, parts = refs[:3], refs[3:6]
+    other, sums = places_of(refs[6 : 6 + pieces]), places_of(refs[6 + pieces :])
+    for half in range(2):
         other_rows = stacked(other, opposite_rows(core_ref[0], half))
-        own = own_product(half, 3 * rows, rows, weights_refs, other_rows)
-        store_chips(sums[:2], half * rows, 0, total[: 2 * rows] + part_ref[half])
-        store_chips(sums[2:], half * rows, 0, total[2 * rows :] + own)
+        total = own_product(half, 3 * rows, rows, weights_refs, other_rows)
+        for part in parts:
+            total = total + part[pl.ds(half * rows, rows), :].astype(jnp.float32)
+        store_chips(sums, half * rows, 0, total)
 
 
 def distant_kernel(pieces, core_ref, high_ref, tail_ref, begun_ref, *refs):
@@ -415,10 +423,17 @@
         functools.partial(near_kernel, len(other)),
         [block] * 3,
         (cores,),
-        (near_received, edge_received, near_part, *weights, *other),
+        (near_received, edge_received, near_part, *other),
         8 * share,
     )
-    (across_total,) = add([(near_sums[2], arrived[0], arrived[1])], (near_sums[0],))
+    (across_total,) = call(
+        functools.partial(across_kernel, len(other)),
+        [block],
+        (cores,),
+        (*weights, near_sums[2], arrived[0], arrived[1], *other),
+        2 * share,
+        (near_sums[0],),
+    )
     (distant_sum,) = call(
         functools.partial(distant_kernel, len(other)),
         [block],

time: 93 us -> 92.8 us (level)
  waiting for transfers between devices: 24.2 us -> 23 us
where the time goes in v16:
time: 92.8 us; the launch traced here: 92.6 us
  starting transfers between devices  33.3 us (36%)
  Pallas kernels  31.1 us (34%)
  waiting for transfers between devices  23 us (25%)
  between operations  2.14 us (2%)
  other arithmetic  2.1 us (2%)
    pallas_call x12, Pallas kernels, call(): pl.pallas_call(body, in_specs=[pl.BlockSpec(memory_space=pltpu.SMEM)] * l...  31.1 us
    ppermute x13, starting transfers between devices, ring(): return lax.ppermute(value, axes, ring_move(steps))  18.5 us
    ppermute x13, waiting for transfers between devices, ring(): return lax.ppermute(value, axes, ring_move(steps))  18.1 us
    ppermute x5, starting transfers between devices, pair(): return lax.ppermute(value, axes, pairs_of(move))  11.1 us
    ppermute x5, waiting for transfers between devices, pair(): return lax.ppermute(value, axes, pairs_of(move))  4.03 us
    ppermute x7, starting transfers between devices, swap(): return lax.ppermute(value, 'core', [(0, 1), (1, 0)])  3.78 us
  transfers between devices with their start and end apart: 25, of which 9 were waited for; matrix products, arithmetic and copies ran while one was open for 1% of the time, Pallas kernels for 28%

profile of v16, /device:TPU:1, one launch (start us, length us, event | category | flops | bytes accessed | tf_op | source)
XLA Modules:
  0.0 92.6 jit_solution(10561827908154689914)
XLA Ops:
  0.6 1.2 %broadcast_select_fusion.2 = (bf16[160,1152]{1,0:T(8,128)(2,1)S(1)}, bf16[160,1152]{1,0:T(8,128)(2,1)S(1)}) fusion(bf16[160,1152]{1,0:T(8,128)(2,1)} %param.5, bf16[160,1152]{1,0:T(8,128)(2,1)} %param.4, pred[]{:T(512)S(6)} %eq.3), kind=kLoop, calls=%fused_computation.2 | loop fusion | flops 368640 | bytes 1474561 | tf_op jit(solution)/shard_map/jit(_where)/select_n | solution.py:353
  1.8 1.5 %collective-permute-start = (bf16[160,1152]{1,0:T(8,128)(2,1)S(1)}, bf16[160,1152]{1,0:T(8,128)(2,1)S(1)}, u32[]{:S(2)}, u32[]{:S(2)}) collective-permute-start(bf16[160,1152]{1,0:T(8,128)(2,1)S(1)} %get-tuple-element.44), channel_id=1, source_target_pairs={{0,1},{1,0},{2,3},{3,2},{4,5},{5,4},{6,7},{7,6},{8,9},{9,8},{10,11... | collective-permute-start | bytes 1105928 | tf_op jit(solution)/shard_map/ppermute | solution.py:61
  4.6 0.0 collective-permute-done.refs_4_
  4.6 0.4 shard_map.59
  5.0 1.8 %collective-permute-start.1 = (bf16[160,1152]{1,0:T(8,128)(2,1)S(1)}, bf16[160,1152]{1,0:T(8,128)(2,1)S(1)}, u32[]{:S(2)}, u32[]{:S(2)}) collective-permute-start(bf16[160,1152]{1,0:T(8,128)(2,1)S(1)} %get-tuple-element.28), channel_id=1, source_target_pairs={{0,4},{1,17},{2,6},{3,19},{4,8},{5,21},{6,10},{7,23},{8,12},{9,25}... | collective-permute-start | bytes 1105928 | tf_op jit(solution)/shard_map/ppermute | solution.py:48
  6.8 2.2 %collective-permute-start.4 = (bf16[160,1152]{1,0:T(8,128)(2,1)S(1)}, bf16[160,1152]{1,0:T(8,128)(2,1)S(1)}, u32[]{:S(2)}, u32[]{:S(2)}) collective-permute-start(bf16[160,1152]{1,0:T(8,128)(2,1)S(1)} %get-tuple-element.27), channel_id=1, source_target_pairs={{0,12},{1,49},{2,14},{3,51},{4,0},{5,53},{6,2},{7,55},{8,4},{9,57}... | collective-permute-start | bytes 1105928 | tf_op jit(solution)/shard_map/ppermute | solution.py:48
  9.0 2.7 %collective-permute-start.5 = (bf16[320,1152]{1,0:T(8,128)(2,1)S(1)}, bf16[320,1152]{1,0:T(8,128)(2,1)S(1)}, u32[]{:S(2)}, u32[]{:S(2)}) collective-permute-start(bf16[320,1152]{1,0:T(8,128)(2,1)S(1)} %get-tuple-element.24.refs_2_), channel_id=1, source_target_pairs={{0,2},{1,67},{2,0},{3,65},{4,6},{5,71},{6,4},{7,69},{8,10},{9,75},... | collective-permute-start | bytes 2211848 | tf_op jit(solution)/shard_map/ppermute | solution.py:57
  11.8 0.1 constant_dynamic-update-slice_fusion.13
  11.8 2.7 %collective-permute-start.3 = (bf16[160,1152]{1,0:T(8,128)(2,1)S(1)}, bf16[160,1152]{1,0:T(8,128)(2,1)S(1)}, u32[]{:S(2)}, u32[]{:S(2)}) collective-permute-start(bf16[160,1152]{1,0:T(8,128)(2,1)S(1)} %get-tuple-element.28), channel_id=1, source_target_pairs={{0,12},{1,49},{2,14},{3,51},{4,0},{5,53},{6,2},{7,55},{8,4},{9,57}... | collective-permute-start | bytes 1105928 | tf_op jit(solution)/shard_map/ppermute | solution.py:48
  14.6 0.0 collective-permute-start.6
  14.6 0.0 collective-permute-done.4
  14.6 2.7 %collective-permute-start.7 = (bf16[160,1152]{1,0:T(8,128)(2,1)S(1)}, bf16[160,1152]{1,0:T(8,128)(2,1)S(1)}, u32[]{:S(2)}, u32[]{:S(2)}) collective-permute-start(bf16[160,1152]{1,0:T(8,128)(2,1)S(1)} %collective-permute-done.4), channel_id=1, source_target_pairs={{0,12},{1,49},{2,14},{3,51},{4,0},{5,53},{6,2},{7,55},{8,4},{9,57}... | collective-permute-start | bytes 1105928 | tf_op jit(solution)/shard_map/ppermute | solution.py:48
  17.2 0.1 constant_dynamic-update-slice_fusion.12
  17.3 2.3 %collective-permute-done.2 = bf16[160,1152]{1,0:T(8,128)(2,1)S(1)} collective-permute-done((bf16[160,1152]{1,0:T(8,128)(2,1)S(1)}, bf16[160,1152]{1,0:T(8,128)(2,1)S(1)}, u32[]{:S(2)}, u32[]{:S(2)}) %collective-permute-start.2) | collective-permute-done | bytes 368672 | tf_op jit(solution)/shard_map/ppermute | solution.py:48
  19.6 0.1 constant_dynamic-update-slice_fusion.11
  19.7 0.0 collective-permute-done.3
  19.7 0.1 constant_dynamic-update-slice_fusion.10
  19.8 0.1 constant_dynamic-update-slice_fusion.9
  19.9 1.0 %collective-permute-done.5.refs_5_ = bf16[320,1152]{1,0:T(8,128)(2,1)S(1)} collective-permute-done((bf16[320,1152]{1,0:T(8,128)(2,1)S(1)}, bf16[320,1152]{1,0:T(8,128)(2,1)S(1)}, u32[]{:S(2)}, u32[]{:S(2)}) %collective-permute-start.5) | collective-permute-done | bytes 737312 | tf_op jit(solution)/shard_map/ppermute | solution.py:57
  20.9 0.0 collective-permute-start.8
  20.9 0.1 constant_dynamic-update-slice_fusion.8
  21.0 0.1 collective-permute-start.12
  21.1 3.4 %collective-permute-start.9 = (bf16[320,1152]{1,0:T(8,128)(2,1)S(1)}, bf16[320,1152]{1,0:T(8,128)(2,1)S(1)}, u32[]{:S(2)}, u32[]{:S(2)}) collective-permute-start(bf16[320,1152]{1,0:T(8,128)(2,1)S(1)} %collective-permute-done.5.refs_5_), channel_id=1, source_target_pairs={{0,12},{1,49},{2,14},{3,51},{4,0},{5,53},{6,2},{7,55},{8,4},{9,57}... | collective-permute-start | bytes 2211848 | tf_op jit(solution)/shard_map/ppermute | solution.py:48
  24.5 2.7 %collective-permute-start.10 = (bf16[160,1152]{1,0:T(8,128)(2,1)S(1)}, bf16[160,1152]{1,0:T(8,128)(2,1)S(1)}, u32[]{:S(2)}, u32[]{:S(2)}) collective-permute-start(bf16[160,1152]{1,0:T(8,128)(2,1)S(1)} %collective-permute-done.6), channel_id=1, source_target_pairs={{0,2},{1,67},{2,0},{3,65},{4,6},{5,71},{6,4},{7,69},{8,10},{9,75},... | collective-permute-start | bytes 1105928 | tf_op jit(solution)/shard_map/ppermute | solution.py:57
  27.2 0.1 collective-permute-start.11
  27.3 0.1 constant_dynamic-update-slice_fusion.19
  27.4 0.1 constant_dynamic-update-slice_fusion.18
  27.4 5.0 %collective-permute-done.8.refs_7_ = bf16[320,1152]{1,0:T(8,128)(2,1)S(1)} collective-permute-done((bf16[320,1152]{1,0:T(8,128)(2,1)S(1)}, bf16[320,1152]{1,0:T(8,128)(2,1)S(1)}, u32[]{:S(2)}, u32[]{:S(2)}) %collective-permute-start.8) | collective-permute-done | bytes 737312 | tf_op jit(solution)/shard_map/ppermute | solution.py:48
  32.5 0.1 constant_dynamic-update-slice_fusion.17
  32.6 0.3 collective-permute-done.9.refs_8_
  32.9 0.1 constant_dynamic-update-slice_fusion.16
  33.0 0.0 collective-permute-done.10
  33.0 0.1 constant_dynamic-update-slice_fusion.15
  33.1 3.0 %collective-permute-done.11 = bf16[160,1152]{1,0:T(8,128)(2,1)S(1)} collective-permute-done((bf16[160,1152]{1,0:T(8,128)(2,1)S(1)}, bf16[160,1152]{1,0:T(8,128)(2,1)S(1)}, u32[]{:S(2)}, u32[]{:S(2)}) %collective-permute-start.11) | collective-permute-done | bytes 368672 | tf_op jit(solution)/shard_map/ppermute | solution.py:57
  36.1 0.1 constant_dynamic-update-slice_fusion.14
  36.1 0.3 collective-permute-start.13
  36.4 0.0 collective-permute-done.12.refs_10_.refs_3_.refs_4_.refs_7_.refs_6_.refs_5_
  36.4 5.6 %shard_map.60 = (bf16[2,1280,512]{2,1,0:T(8,128)(2,1)S(1)}, f32[2,640,1152]{2,1,0:T(8,128)S(1)}) custom-call(s32[1]{0:T(128)} %bitcast.refs_2_.refs_0_, f32[8,128]{1,0:T(8,128)S(1)} %get-tuple-element.22.refs_1_, bf16[320,1152]{1,0:T(8,128)(2,1)S(1)} %get-tuple-element.24.refs_2_, bf16[320,1152]{1,0:T(8,128)(2,1)S(1)} %get-tuple-element.59.refs_3_, ...), custom_call_target="tpu_custom_call" | custom-call | flops 4529848320 | bytes 1048576 | tf_op jit(solution)/shard_map/pallas_call | solution.py:298
  42.1 3.9 %shard_map.61.refs_13_.refs_3_.refs_5_.refs_4_ = bf16[2,1280,512]{2,1,0:T(8,128)(2,1)S(1)} custom-call(s32[1]{0:T(128)} %bitcast.refs_2_.refs_0_, f32[8,128]{1,0:T(8,128)S(1)} %get-tuple-element.22.refs_1_, bf16[320,1152]{1,0:T(8,128)(2,1)S(1)} %get-tuple-element.24.refs_2_, bf16[320,1152]{1,0:T(8,128)(2,1)S(1)} %get-tuple-element.59.refs_3_, ...), custom_call_target="tpu_custom_call" | custom-call | flops 3019898880 | bytes 1048576 | tf_op jit(solution)/shard_map/pallas_call | solution.py:298
  46.0 0.8 collective-permute-start.16
  46.8 6.5 %shard_map.62 = (f32[2,320,1152]{2,1,0:T(8,128)S(1)}, f32[2,480,1152]{2,1,0:T(8,128)S(1)}, bf16[2,1280,512]{2,1,0:T(8,128)(2,1)S(1)}, bf16[2,1280,256]{2,1,0:T(8,128)(2,1)S(1)}) custom-call(s32[1]{0:T(128)} %bitcast.refs_2_.refs_0_, f32[8,128]{1,0:T(8,128)S(1)} %get-tuple-element.22.refs_1_, bf16[320,1152]{1,0:T(8,128)(2,1)S(1)} %get-tuple-element.24.refs_2_, ...), custom_call_target="tpu_custom_call" | custom-call | flops 6039797760 | bytes 1048576 | tf_op jit(solution)/shard_map/pallas_call | solution.py:298
  53.3 0.1 collective-permute-start.14
  53.5 0.4 collective-permute-start.15
  53.9 3.7 %shard_map.63 = (bf16[320,1152]{1,0:T(8,128)(2,1)S(1)}, bf16[320,1152]{1,0:T(8,128)(2,1)S(1)}, bf16[320,1152]{1,0:T(8,128)(2,1)S(1)}, f32[2,32,1152]{2,1,0:T(8,128)S(1)}) custom-call(s32[1]{0:T(128)} %bitcast.refs_2_.refs_0_, bf16[2,1280,512]{2,1,0:T(8,128)(2,1)S(1)} %collective-permute-done.16.refs_1_, f32[2,480,1152]{2,1,0:T(8,128)S(1)} %get-tuple-element.33.refs_2_, ...), custom_call_target="tpu_custom_call" | custom-call | flops 3774873600 | bytes 1048576 | tf_op jit(solution)/shard_map/pallas_call | solution.py:298
  57.6 2.6 %collective-permute-start.17 = (bf16[320,1152]{1,0:T(8,128)(2,1)S(1)}, bf16[320,1152]{1,0:T(8,128)(2,1)S(1)}, u32[]{:S(2)}, u32[]{:S(2)}) collective-permute-start(bf16[320,1152]{1,0:T(8,128)(2,1)S(1)} %get-tuple-element.37), channel_id=1, source_target_pairs={{0,12},{1,49},{2,14},{3,51},{4,0},{5,53},{6,2},{7,55},{8,4},{9,57}... | collective-permute-start | bytes 2211848 | tf_op jit(solution)/shard_map/ppermute | solution.py:48
  60.2 2.7 %collective-permute-start.19 = (bf16[320,1152]{1,0:T(8,128)(2,1)S(1)}, bf16[320,1152]{1,0:T(8,128)(2,1)S(1)}, u32[]{:S(2)}, u32[]{:S(2)}) collective-permute-start(bf16[320,1152]{1,0:T(8,128)(2,1)S(1)} %get-tuple-element.40), channel_id=1, source_target_pairs={{0,2},{1,67},{2,0},{3,65},{4,6},{5,71},{6,4},{7,69},{8,10},{9,75},... | collective-permute-start | bytes 2211848 | tf_op jit(solution)/shard_map/ppermute | solution.py:57
  62.9 0.0 collective-permute-done.15.refs_2_.refs_1_
  62.9 0.0 collective-permute-done.14.refs_1_
  62.9 3.6 %shard_map.64 = (bf16[320,1152]{1,0:T(8,128)(2,1)S(1)}, bf16[320,1152]{1,0:T(8,128)(2,1)S(1)}, bf16[320,1152]{1,0:T(8,128)(2,1)S(1)}) custom-call(s32[1]{0:T(128)} %bitcast.refs_2_.refs_0_, bf16[2,1280,512]{2,1,0:T(8,128)(2,1)S(1)} %collective-permute-done.14.refs_1_, bf16[2,1280,256]{2,1,0:T(8,128)(2,1)S(1)} %collective-permute-done.15.refs_2_.refs_1_, ...), custom_call_target="tpu_custom_call" | custom-call | flops 3019898880 | bytes 1048576 | tf_op jit(solution)/shard_map/pallas_call | solution.py:298
  66.6 3.0 %collective-permute-start.21 = (bf16[320,1152]{1,0:T(8,128)(2,1)S(1)}, bf16[320,1152]{1,0:T(8,128)(2,1)S(1)}, u32[]{:S(2)}, u32[]{:S(2)}) collective-permute-start(bf16[320,1152]{1,0:T(8,128)(2,1)S(1)} %get-tuple-element.39.refs_9_), channel_id=1, source_target_pairs={{0,12},{1,49},{2,14},{3,51},{4,0},{5,53},{6,2},{7,55},{8,4},{9,57}... | collective-permute-start | bytes 2211848 | tf_op jit(solution)/shard_map/ppermute | solution.py:48
  69.6 2.4 %collective-permute-done.18.refs_6_ = bf16[320,1152]{1,0:T(8,128)(2,1)S(1)} collective-permute-done((bf16[320,1152]{1,0:T(8,128)(2,1)S(1)}, bf16[320,1152]{1,0:T(8,128)(2,1)S(1)}, u32[]{:S(2)}, u32[]{:S(2)}) %collective-permute-start.18) | collective-permute-done | bytes 737312 | tf_op jit(solution)/shard_map/ppermute | solution.py:48
  72.0 1.4 %shard_map.65.refs_8_ = bf16[320,1152]{1,0:T(8,128)(2,1)S(1)} custom-call(s32[1]{0:T(128)} %bitcast.refs_2_.refs_0_, bf16[2,1280,512]{2,1,0:T(8,128)(2,1)S(1)} %get-tuple-element.29.refs_12_.refs_1_.refs_2_, bf16[2,1280,256]{2,1,0:T(8,128)(2,1)S(1)} %get-tuple-element.32.refs_2_.refs_4_.refs_3_, ...), custom_call_target="tpu_custom_call" | custom-call | flops 754974720 | bytes 1048576 | tf_op jit(solution)/shard_map/pallas_call | solution.py:298
  73.5 1.8 %shard_map.66.refs_0_ = bf16[320,1152]{1,0:T(8,128)(2,1)S(1)} custom-call(s32[1]{0:T(128)} %bitcast.refs_2_.refs_0_, bf16[2,1280,256]{2,1,0:T(8,128)(2,1)S(1)} %collective-permute-done.15.refs_2_.refs_1_, f32[2,32,1152]{2,1,0:T(8,128)S(1)} %get-tuple-element.34.refs_2_, f32[2,640,1152]{2,1,0:T(8,128)S(1)} %get-tuple-element.30.refs_14_.refs_3_, ...), custom_call_target="tpu_custom_call" | custom-call | flops 1509949440 | bytes 1048576 | tf_op jit(solution)/shard_map/pallas_call | solution.py:298
  75.2 0.2 shard_map.67.refs_7_
  75.4 0.1 collective-permute-start.20
  75.5 2.8 %collective-permute-start.23 = (bf16[320,1152]{1,0:T(8,128)(2,1)S(1)}, bf16[320,1152]{1,0:T(8,128)(2,1)S(1)}, u32[]{:S(2)}, u32[]{:S(2)}) collective-permute-start(bf16[320,1152]{1,0:T(8,128)(2,1)S(1)} %shard_map.65.refs_8_), channel_id=1, source_target_pairs={{0,2},{1,67},{2,0},{3,65},{4,6},{5,71},{6,4},{7,69},{8,10},{9,75},... | collective-permute-start | bytes 2211848 | tf_op jit(solution)/shard_map/ppermute | solution.py:57
  78.3 3.0 %shard_map.68.refs_3_ = f32[320,1152]{1,0:T(8,128)S(1)} custom-call(s32[1]{0:T(128)} %bitcast.refs_2_.refs_0_, bf16[2,1280,512]{2,1,0:T(8,128)(2,1)S(1)} %collective-permute-done.14.refs_1_, bf16[2,1280,512]{2,1,0:T(8,128)(2,1)S(1)} %get-tuple-element.29.refs_12_.refs_1_.refs_2_, bf16[2,1280,256]{2,1,0:T(8,128)(2,1)S(1)} %get-tuple-element.32.refs_2_.refs_4_.refs_3_, ...), custom_call_target="tpu_custom_call" | custom-call | flops 1887436800 | bytes 1048576 | tf_op jit(solution)/shard_map/pallas_call | solution.py:298
  81.3 4.6 %collective-permute-done.21.refs_5_ = bf16[320,1152]{1,0:T(8,128)(2,1)S(1)} collective-permute-done((bf16[320,1152]{1,0:T(8,128)(2,1)S(1)}, bf16[320,1152]{1,0:T(8,128)(2,1)S(1)}, u32[]{:S(2)}, u32[]{:S(2)}) %collective-permute-start.21) | collective-permute-done | bytes 737312 | tf_op jit(solution)/shard_map/ppermute | solution.py:48
  85.9 3.4 %collective-permute-done.22.refs_6_ = bf16[320,1152]{1,0:T(8,128)(2,1)S(1)} collective-permute-done((bf16[320,1152]{1,0:T(8,128)(2,1)S(1)}, bf16[320,1152]{1,0:T(8,128)(2,1)S(1)}, u32[]{:S(2)}, u32[]{:S(2)}) %collective-permute-start.22) | collective-permute-done | bytes 737312 | tf_op jit(solution)/shard_map/ppermute | solution.py:48
  89.3 0.5 shard_map.69.refs_8_
  89.8 0.6 collective-permute-start.24
  90.4 0.5 shard_map.70
  90.9 0.8 collective-permute-done.24
  91.7 0.9 %broadcast_select_fusion = (bf16[160,1152]{1,0:T(8,128)(2,1)}, bf16[160,1152]{1,0:T(8,128)(2,1)}) fusion(bf16[160,1152]{1,0:T(8,128)(2,1)S(1)} %collective-permute-done.24, bf16[160,1152]{1,0:T(8,128)(2,1)S(1)} %shard_map.70, pred[]{:T(512)S(6)} %eq.3), kind=kLoop, calls=%fused_computation | loop fusion | flops 368640 | bytes 1474561 | tf_op jit(solution)/shard_map/jit(_where)/select_n | solution.py:477
  (12 shorter events, 0.0 us)
Async XLA Ops:
  1.8 2.8 %collective-permute-start = (bf16[160,1152]{1,0:T(8,128)(2,1)S(1)}, bf16[160,1152]{1,0:T(8,128)(2,1)S(1)}, u32[]{:S(2)}, u32[]{:S(2)}) collective-permute-start(bf16[160,1152]{1,0:T(8,128)(2,1)S(1)} %get-tuple-element.44), channel_id=1, source_target_pairs={{0,1},{1,0},{2,3},{3,2},{4,5},{5,4},{6,7},{7,6},{8,9},{9,8},{10,11... | collective-permute-start | bytes 1105928 | tf_op jit(solution)/shard_map/ppermute | solution.py:61
  5.0 9.5 %collective-permute-start.1 = (bf16[160,1152]{1,0:T(8,128)(2,1)S(1)}, bf16[160,1152]{1,0:T(8,128)(2,1)S(1)}, u32[]{:S(2)}, u32[]{:S(2)}) collective-permute-start(bf16[160,1152]{1,0:T(8,128)(2,1)S(1)} %get-tuple-element.28), channel_id=1, source_target_pairs={{0,4},{1,17},{2,6},{3,19},{4,8},{5,21},{6,10},{7,23},{8,12},{9,25}... | collective-permute-start | bytes 1105928 | tf_op jit(solution)/shard_map/ppermute | solution.py:48
  6.8 7.8 %collective-permute-start.4 = (bf16[160,1152]{1,0:T(8,128)(2,1)S(1)}, bf16[160,1152]{1,0:T(8,128)(2,1)S(1)}, u32[]{:S(2)}, u32[]{:S(2)}) collective-permute-start(bf16[160,1152]{1,0:T(8,128)(2,1)S(1)} %get-tuple-element.27), channel_id=1, source_target_pairs={{0,12},{1,49},{2,14},{3,51},{4,0},{5,53},{6,2},{7,55},{8,4},{9,57}... | collective-permute-start | bytes 1105928 | tf_op jit(solution)/shard_map/ppermute | solution.py:48
  9.0 11.9 %collective-permute-start.5 = (bf16[320,1152]{1,0:T(8,128)(2,1)S(1)}, bf16[320,1152]{1,0:T(8,128)(2,1)S(1)}, u32[]{:S(2)}, u32[]{:S(2)}) collective-permute-start(bf16[320,1152]{1,0:T(8,128)(2,1)S(1)} %get-tuple-element.24.refs_2_), channel_id=1, source_target_pairs={{0,2},{1,67},{2,0},{3,65},{4,6},{5,71},{6,4},{7,69},{8,10},{9,75},... | collective-permute-start | bytes 2211848 | tf_op jit(solution)/shard_map/ppermute | solution.py:57
  11.8 7.9 %collective-permute-start.2 = (bf16[160,1152]{1,0:T(8,128)(2,1)S(1)}, bf16[160,1152]{1,0:T(8,128)(2,1)S(1)}, u32[]{:S(2)}, u32[]{:S(2)}) collective-permute-start(bf16[160,1152]{1,0:T(8,128)(2,1)S(1)} %get-tuple-element.27), channel_id=1, source_target_pairs={{0,4},{1,17},{2,6},{3,19},{4,8},{5,21},{6,10},{7,23},{8,12},{9,25}... | collective-permute-start | bytes 1105928 | tf_op jit(solution)/shard_map/ppermute | solution.py:48
  11.8 7.9 %collective-permute-start.3 = (bf16[160,1152]{1,0:T(8,128)(2,1)S(1)}, bf16[160,1152]{1,0:T(8,128)(2,1)S(1)}, u32[]{:S(2)}, u32[]{:S(2)}) collective-permute-start(bf16[160,1152]{1,0:T(8,128)(2,1)S(1)} %get-tuple-element.28), channel_id=1, source_target_pairs={{0,12},{1,49},{2,14},{3,51},{4,0},{5,53},{6,2},{7,55},{8,4},{9,57}... | collective-permute-start | bytes 1105928 | tf_op jit(solution)/shard_map/ppermute | solution.py:48
  14.6 9.9 %collective-permute-start.6 = (bf16[160,1152]{1,0:T(8,128)(2,1)S(1)}, bf16[160,1152]{1,0:T(8,128)(2,1)S(1)}, u32[]{:S(2)}, u32[]{:S(2)}) collective-permute-start(bf16[160,1152]{1,0:T(8,128)(2,1)S(1)} %collective-permute-done.1), channel_id=1, source_target_pairs={{0,4},{1,17},{2,6},{3,19},{4,8},{5,21},{6,10},{7,23},{8,12},{9,25}... | collective-permute-start | bytes 1105928 | tf_op jit(solution)/shard_map/ppermute | solution.py:48
  14.6 12.6 %collective-permute-start.7 = (bf16[160,1152]{1,0:T(8,128)(2,1)S(1)}, bf16[160,1152]{1,0:T(8,128)(2,1)S(1)}, u32[]{:S(2)}, u32[]{:S(2)}) collective-permute-start(bf16[160,1152]{1,0:T(8,128)(2,1)S(1)} %collective-permute-done.4), channel_id=1, source_target_pairs={{0,12},{1,49},{2,14},{3,51},{4,0},{5,53},{6,2},{7,55},{8,4},{9,57}... | collective-permute-start | bytes 1105928 | tf_op jit(solution)/shard_map/ppermute | solution.py:48
  20.9 11.6 %collective-permute-start.8 = (bf16[320,1152]{1,0:T(8,128)(2,1)S(1)}, bf16[320,1152]{1,0:T(8,128)(2,1)S(1)}, u32[]{:S(2)}, u32[]{:S(2)}) collective-permute-start(bf16[320,1152]{1,0:T(8,128)(2,1)S(1)} %collective-permute-done.5.refs_5_), channel_id=1, source_target_pairs={{0,4},{1,17},{2,6},{3,19},{4,8},{5,21},{6,10},{7,23},{8,12},{9,25}... | collective-permute-start | bytes 2211848 | tf_op jit(solution)/shard_map/ppermute | solution.py:48
  21.0 15.4 %collective-permute-start.12 = (bf16[1280,1152]{1,0:T(8,128)(2,1)S(1)}, bf16[1280,1152]{1,0:T(8,128)(2,1)S(1)}, u32[]{:S(2)}, u32[]{:S(2)}) collective-permute-start(bf16[1280,1152]{1,0:T(8,128)(2,1)S(1)} %constant_dynamic-update-slice_fusion.8), channel_id=1, source_target_pairs={{0,1},{1,0},{2,3},{3,2},{4,5},{5,4},{6,7},{7,6},{8,9},{9,8},{10,11... | collective-permute-start | bytes 8847368 | tf_op jit(solution)/shard_map/ppermute | solution.py:61
  21.1 11.8 %collective-permute-start.9 = (bf16[320,1152]{1,0:T(8,128)(2,1)S(1)}, bf16[320,1152]{1,0:T(8,128)(2,1)S(1)}, u32[]{:S(2)}, u32[]{:S(2)}) collective-permute-start(bf16[320,1152]{1,0:T(8,128)(2,1)S(1)} %collective-permute-done.5.refs_5_), channel_id=1, source_target_pairs={{0,12},{1,49},{2,14},{3,51},{4,0},{5,53},{6,2},{7,55},{8,4},{9,57}... | collective-permute-start | bytes 2211848 | tf_op jit(solution)/shard_map/ppermute | solution.py:48
  24.5 8.5 %collective-permute-start.10 = (bf16[160,1152]{1,0:T(8,128)(2,1)S(1)}, bf16[160,1152]{1,0:T(8,128)(2,1)S(1)}, u32[]{:S(2)}, u32[]{:S(2)}) collective-permute-start(bf16[160,1152]{1,0:T(8,128)(2,1)S(1)} %collective-permute-done.6), channel_id=1, source_target_pairs={{0,2},{1,67},{2,0},{3,65},{4,6},{5,71},{6,4},{7,69},{8,10},{9,75},... | collective-permute-start | bytes 1105928 | tf_op jit(solution)/shard_map/ppermute | solution.py:57
  27.2 8.8 %collective-permute-start.11 = (bf16[160,1152]{1,0:T(8,128)(2,1)S(1)}, bf16[160,1152]{1,0:T(8,128)(2,1)S(1)}, u32[]{:S(2)}, u32[]{:S(2)}) collective-permute-start(bf16[160,1152]{1,0:T(8,128)(2,1)S(1)} %collective-permute-done.7), channel_id=1, source_target_pairs={{0,2},{1,67},{2,0},{3,65},{4,6},{5,71},{6,4},{7,69},{8,10},{9,75},... | collective-permute-start | bytes 1105928 | tf_op jit(solution)/shard_map/ppermute | solution.py:57
  36.1 5.9 %collective-permute-start.13 = (bf16[1280,1152]{1,0:T(8,128)(2,1)S(1)}, bf16[1280,1152]{1,0:T(8,128)(2,1)S(1)}, u32[]{:S(2)}, u32[]{:S(2)}) collective-permute-start(bf16[1280,1152]{1,0:T(8,128)(2,1)S(1)} %get-tuple-element.46), channel_id=1, source_target_pairs={{0,1},{1,0},{2,3},{3,2},{4,5},{5,4},{6,7},{7,6},{8,9},{9,8},{10,11... | collective-permute-start | bytes 8847368 | tf_op jit(solution)/shard_map/ppermute | solution.py:61
  46.0 7.9 %collective-permute-start.16 = (bf16[2,1280,512]{2,1,0:T(8,128)(2,1)S(1)}, bf16[2,1280,512]{2,1,0:T(8,128)(2,1)S(1)}, u32[]{:S(2)}, u32[]{:S(2)}) collective-permute-start(bf16[2,1280,512]{2,1,0:T(8,128)(2,1)S(1)} %shard_map.61.refs_13_.refs_3_.refs_5_.refs_4_), channel_id=1, source_target_pairs={{0,1},{1,0},{2,3},{3,2},{4,5},{5,4},{6,7},{7,6},{8,9},{9,8},{10,11... | collective-permute-start | bytes 7864328 | tf_op jit(solution)/shard_map/ppermute | solution.py:61
  53.3 9.6 %collective-permute-start.14 = (bf16[2,1280,512]{2,1,0:T(8,128)(2,1)S(1)}, bf16[2,1280,512]{2,1,0:T(8,128)(2,1)S(1)}, u32[]{:S(2)}, u32[]{:S(2)}) collective-permute-start(bf16[2,1280,512]{2,1,0:T(8,128)(2,1)S(1)} %get-tuple-element.31), channel_id=1, source_target_pairs={{0,1},{1,0},{2,3},{3,2},{4,5},{5,4},{6,7},{7,6},{8,9},{9,8},{10,11... | collective-permute-start | bytes 7864328 | tf_op jit(solution)/shard_map/ppermute | solution.py:61
  53.5 9.5 %collective-permute-start.15 = (bf16[2,1280,256]{2,1,0:T(8,128)(2,1)S(1)}, bf16[2,1280,256]{2,1,0:T(8,128)(2,1)S(1)}, u32[]{:S(2)}, u32[]{:S(2)}) collective-permute-start(bf16[2,1280,256]{2,1,0:T(8,128)(2,1)S(1)} %get-tuple-element.32.refs_2_.refs_4_.refs_3_), channel_id=1, source_target_pairs={{0,1},{1,0},{2,3},{3,2},{4,5},{5,4},{6,7},{7,6},{8,9},{9,8},{10,11... | collective-permute-start | bytes 3932168 | tf_op jit(solution)/shard_map/ppermute | solution.py:61
  57.6 12.0 %collective-permute-start.17 = (bf16[320,1152]{1,0:T(8,128)(2,1)S(1)}, bf16[320,1152]{1,0:T(8,128)(2,1)S(1)}, u32[]{:S(2)}, u32[]{:S(2)}) collective-permute-start(bf16[320,1152]{1,0:T(8,128)(2,1)S(1)} %get-tuple-element.37), channel_id=1, source_target_pairs={{0,12},{1,49},{2,14},{3,51},{4,0},{5,53},{6,2},{7,55},{8,4},{9,57}... | collective-permute-start | bytes 2211848 | tf_op jit(solution)/shard_map/ppermute | solution.py:48
  60.2 11.8 %collective-permute-start.18 = (bf16[320,1152]{1,0:T(8,128)(2,1)S(1)}, bf16[320,1152]{1,0:T(8,128)(2,1)S(1)}, u32[]{:S(2)}, u32[]{:S(2)}) collective-permute-start(bf16[320,1152]{1,0:T(8,128)(2,1)S(1)} %get-tuple-element.38), channel_id=1, source_target_pairs={{0,4},{1,17},{2,6},{3,19},{4,8},{5,21},{6,10},{7,23},{8,12},{9,25}... | collective-permute-start | bytes 2211848 | tf_op jit(solution)/shard_map/ppermute | solution.py:48
  60.2 15.0 %collective-permute-start.19 = (bf16[320,1152]{1,0:T(8,128)(2,1)S(1)}, bf16[320,1152]{1,0:T(8,128)(2,1)S(1)}, u32[]{:S(2)}, u32[]{:S(2)}) collective-permute-start(bf16[320,1152]{1,0:T(8,128)(2,1)S(1)} %get-tuple-element.40), channel_id=1, source_target_pairs={{0,2},{1,67},{2,0},{3,65},{4,6},{5,71},{6,4},{7,69},{8,10},{9,75},... | collective-permute-start | bytes 2211848 | tf_op jit(solution)/shard_map/ppermute | solution.py:57
  66.6 19.3 %collective-permute-start.21 = (bf16[320,1152]{1,0:T(8,128)(2,1)S(1)}, bf16[320,1152]{1,0:T(8,128)(2,1)S(1)}, u32[]{:S(2)}, u32[]{:S(2)}) collective-permute-start(bf16[320,1152]{1,0:T(8,128)(2,1)S(1)} %get-tuple-element.39.refs_9_), channel_id=1, source_target_pairs={{0,12},{1,49},{2,14},{3,51},{4,0},{5,53},{6,2},{7,55},{8,4},{9,57}... | collective-permute-start | bytes 2211848 | tf_op jit(solution)/shard_map/ppermute | solution.py:48
  69.6 19.7 %collective-permute-start.22 = (bf16[320,1152]{1,0:T(8,128)(2,1)S(1)}, bf16[320,1152]{1,0:T(8,128)(2,1)S(1)}, u32[]{:S(2)}, u32[]{:S(2)}) collective-permute-start(bf16[320,1152]{1,0:T(8,128)(2,1)S(1)} %get-tuple-element.41), channel_id=1, source_target_pairs={{0,4},{1,17},{2,6},{3,19},{4,8},{5,21},{6,10},{7,23},{8,12},{9,25}... | collective-permute-start | bytes 2211848 | tf_op jit(solution)/shard_map/ppermute | solution.py:48
  75.4 13.9 %collective-permute-start.20 = (bf16[320,1152]{1,0:T(8,128)(2,1)S(1)}, bf16[320,1152]{1,0:T(8,128)(2,1)S(1)}, u32[]{:S(2)}, u32[]{:S(2)}) collective-permute-start(bf16[320,1152]{1,0:T(8,128)(2,1)S(1)} %shard_map.67.refs_7_), channel_id=1, source_target_pairs={{0,8},{1,33},{2,10},{3,35},{4,12},{5,37},{6,14},{7,39},{8,0},{9,41... | collective-permute-start | bytes 2211848 | tf_op jit(solution)/shard_map/ppermute | solution.py:48
  75.5 13.8 %collective-permute-start.23 = (bf16[320,1152]{1,0:T(8,128)(2,1)S(1)}, bf16[320,1152]{1,0:T(8,128)(2,1)S(1)}, u32[]{:S(2)}, u32[]{:S(2)}) collective-permute-start(bf16[320,1152]{1,0:T(8,128)(2,1)S(1)} %shard_map.65.refs_8_), channel_id=1, source_target_pairs={{0,2},{1,67},{2,0},{3,65},{4,6},{5,71},{6,4},{7,69},{8,10},{9,75},... | collective-permute-start | bytes 2211848 | tf_op jit(solution)/shard_map/ppermute | solution.py:57
  89.8 1.9 %collective-permute-start.24 = (bf16[160,1152]{1,0:T(8,128)(2,1)S(1)}, bf16[160,1152]{1,0:T(8,128)(2,1)S(1)}, u32[]{:S(2)}, u32[]{:S(2)}) collective-permute-start(bf16[160,1152]{1,0:T(8,128)(2,1)S(1)} %shard_map.69.refs_8_), channel_id=1, source_target_pairs={{0,1},{1,0},{2,3},{3,2},{4,5},{5,4},{6,7},{7,6},{8,9},{9,8},{10,11... | collective-permute-start | bytes 1105928 | tf_op jit(solution)/shard_map/ppermute | solution.py:61
